TPU v7x, 32 devices: a whole 2x2x4 slice. The times are simulated.
32 devices in a mesh: lat: 2 (over core), lon: 16 (over z, y, x).
Axes of the slice: x: 2, y: 2, z: 4, core: 2. Of those that a mesh axis runs over, the one named last changes fastest.
Arguments:
- fields: bfloat16 [2, 8, 640, 384], P(None, 'lat', None, 'lon'), may hold values from -6 to 6
- kernel: bfloat16 [5, 8, 3, 3, 64, 64], P(None, 'lat'), may hold values from -0.25 to 0.25
- band_low: int32 [5, 8], replicated, may hold values from -2 to 0
- block_shift: int32 [8, 3], replicated, may hold values from -3 to 3
- mix_weight: bfloat16 [5, 640, 640], P(None, 'lon'), may hold values from -0.109375 to 0.109375
Outputs:
- mixed: bfloat16 [2, 8, 384, 640], P(None, 'lat', 'lon')
All inputs are finite; a program needn't handle non-finite values.
Results may differ from a plain program's by a relative error of at most 0.005.
Values may be sent and summed in bfloat16 or wider, within the bound.
No kernel may reach another device: no remote copies, remote signals or barrier semaphores. Data moves between devices by JAX's collectives and lax.ppermute only.
A program may use at most 128 MiB of HBM per device.

v0:
```python
import jax
import jax.numpy as jnp
from jax import lax
from jax.sharding import PartitionSpec as P

BL = 64


def from_behind(block, axis, distance):
    devices = range(lax.axis_size(axis))
    route = [(i - distance, i) for i in devices if i - distance in devices]
    return lax.ppermute(block, axis, route)


def take_row(row_blocks, row_index):
    return jnp.take(row_blocks, row_index, axis=2)


def accumulate(source, weights, low_table, shift_table, first_row, first_slot, window):
    members, count, pieces, cells = source.shape
    nblocks = cells // BL
    taps = weights.shape[2]
    blocks = source.reshape(members, count, pieces, nblocks, BL)
    lane_ids = jnp.arange(nblocks, dtype=jnp.int32)
    index = (lane_ids[None, None, :] + shift_table[:, :, None]) % nblocks
    picked = jax.vmap(take_row, in_axes=(1, 0), out_axes=1)(blocks, index)
    row_ids = jnp.arange(count, dtype=jnp.int32)
    tap_ids = jnp.arange(taps, dtype=jnp.int32)
    slot_ids = jnp.arange(window, dtype=jnp.int32)
    target = (
        first_row
        - first_slot
        + row_ids[None, :, None]
        + low_table[:, :, None]
        + tap_ids[None, None, :]
    )
    select = (target[:, None, :, :] == slot_ids[None, :, None, None]).astype(jnp.float32)
    effective = jnp.einsum("kwrt,krtjpq->kwrjpq", select, weights.astype(jnp.float32)).astype(
        jnp.bfloat16
    )
    return jnp.einsum(
        "ercjbp,kwrjpq->kwecbq", picked, effective, preferred_element_type=jnp.float32
    )


def per_device(fields, kernel, band_low, block_shift, mix_weight):
    local_rows = fields.shape[1]
    pieces = lax.all_to_all(fields, "lon", split_axis=2, concat_axis=3, tiled=True)
    start = lax.axis_index("lat") * local_rows
    low_padded = jnp.pad(band_low, ((0, 0), (2, 2)))
    shift_padded = jnp.pad(block_shift, ((2, 2), (0, 0)))
    low_rows = lax.dynamic_slice_in_dim(low_padded, start + 2, local_rows, 1)
    shift_rows = lax.dynamic_slice_in_dim(shift_padded, start + 2, local_rows, 0)
    partial_value = accumulate(
        pieces, kernel, low_rows, shift_rows, start, start - 2, local_rows + 4
    )
    below = from_behind(partial_value[:, local_rows + 2 :], "lat", 1)
    above = from_behind(partial_value[:, :2], "lat", -1)
    filler = jnp.zeros(
        (partial_value.shape[0], local_rows - 2) + partial_value.shape[2:], jnp.float32
    )
    owned = partial_value[:, 2 : local_rows + 2]
    owned = owned + jnp.concatenate([below, filler], axis=1)
    owned = owned + jnp.concatenate([filler, above], axis=1)
    bases, window, members, channel_part, nblocks, width = owned.shape
    conv = owned.astype(jnp.bfloat16).reshape(bases, window, members, channel_part, nblocks * width)
    conv_pixels = lax.all_to_all(conv, "lon", split_axis=4, concat_axis=3, tiled=True)
    summed = jnp.einsum(
        "klecn,kcd->elnd",
        conv_pixels,
        lax.all_gather(mix_weight, "lon", axis=1, tiled=True),
        preferred_element_type=jnp.float32,
    )
    return jax.nn.gelu(summed, approximate=False).astype(jnp.bfloat16)


def solution(mesh):
    placed = (
        P(None, "lat", None, "lon"),
        P(None, "lat", None, None, None, None),
        P(),
        P(),
        P(None, "lon", None),
    )
    return jax.shard_map(
        per_device,
        mesh=mesh,
        in_specs=placed,
        out_specs=P(None, "lat", "lon", None),
        check_vma=False,
    )
```

profile of v0, /device:TPU:0, one launch (start us, length us, event | category | flops | bytes accessed | tf_op | source)
XLA Modules:
  0.0 150.2 jit_solution(8655199147472661944)
XLA Ops:
  6.5 0.0 copy-start
  6.5 0.0 copy-start.2
  6.5 0.0 copy-start.1
  6.5 0.0 all-gather.2.cloned.1.call-start
  6.5 0.7 all-gather.2.cloned.1.call-update
  7.3 2.6 %copy.19 = bf16[2,4,640,24]{3,1,0,2:T(4,128)(2,1)} copy(bf16[2,4,640,24]{2,3,1,0:T(8,128)(2,1)} %param.5) | data formatting | bytes 491520 | tf_op args[0]
  9.8 4.7 %reshape.71 = bf16[16,2,3840]{2,1,0:T(2,128)(2,1)} reshape(bf16[640,2,4,24]{3,2,1,0:T(4,128)(2,1)} %bitcast.124) | data formatting | bytes 491520
  14.6 8.3 %all-to-all-start = ((bf16[16,2,3840]{2,1,0:T(2,128)(2,1)}), bf16[16,2,3840]{2,1,0:T(2,128)(2,1)S(1)}, u32[]{:S(2)}, u32[]{:S(2)}) async-start(bf16[16,2,3840]{2,1,0:T(2,128)(2,1)} %reshape.71), calls=%async_computation | async-start | bytes 491520 | tf_op jit(solution)/shard_map/all_to_all | solution.py:48
  22.9 0.0 copy-done.2
  22.9 0.1 pad_dynamic-slice_fusion
  23.0 0.1 copy.18
  23.1 0.0 copy-done.1
  23.1 0.1 dynamic-slice_add_fusion
  23.2 0.1 fusion.39
  23.3 0.1 iota_add_fusion
  23.4 0.1 compare_and_fusion
  23.5 0.1 reshape.59
  23.5 0.0 copy-done
  23.6 5.5 %convert_bitcast_fusion = bf16[5,8,4,3,64,64,1,1]{5,1,4,3,2,0,7,6:T(8,128)(2,1)} fusion(bf16[5,4,3,3,64,64]{5,4,3,2,1,0:T(8,128)(2,1)S(1)} %copy-done, s32[5,4,3]{2,1,0:T(4,128)S(1)} %iota_add_fusion), kind=kOutput, calls=%fused_computation.3 | convolution fusion | flops 13763040 | bytes 5406960 | tf_op jit(solution)/shard_map/kwrt,krtjpq->kwrjpq/dot_general | solution.py:38
  29.0 7.2 %all-to-all-done = bf16[16,2,3840]{2,1,0:T(2,128)(2,1)S(1)} async-done(((bf16[16,2,3840]{2,1,0:T(2,128)(2,1)}), bf16[16,2,3840]{2,1,0:T(2,128)(2,1)S(1)}, u32[]{:S(2)}, u32[]{:S(2)}) %all-to-all-start) | async-done | bytes 245792 | tf_op jit(solution)/shard_map/all_to_all | solution.py:48
  36.3 3.0 %reshape.72 = bf16[640,2,4,24]{3,2,1,0:T(4,128)(2,1)} reshape(bf16[16,2,3840]{2,1,0:T(2,128)(2,1)S(1)} %all-to-all-done) | data formatting | bytes 491520
  39.3 3.4 %copy.20 = bf16[2,4,16,40,24]{3,4,2,1,0:T(8,128)(2,1)} copy(bf16[2,4,16,40,24]{4,1,0,3,2:T(4,128)(2,1)} %bitcast.123) | data formatting | bytes 491520 | tf_op jit(solution)/shard_map/all_to_all | solution.py:48
  42.7 1.5 copy.21
  44.1 2.5 %gather_fusion = bf16[72,2,40,64]{3,2,1,0:T(8,128)(2,1)} fusion(bf16[4,2,40,6,64]{4,2,3,1,0:T(8,128)(2,1)S(1)} %bitcast.122, s32[72]{0:T(128)S(1)} %reshape.59), kind=kCustom, calls=%fused_computation | custom fusion | bytes 1475136 | tf_op jit(solution)/shard_map/vmap(jit(_take))/gather | solution.py:16
  46.6 8.0 %fusion.7 = f32[5,8,2,40,6,64]{5,3,4,2,1,0:T(8,128)S(1)} fusion(bf16[5,8,4,3,64,64,1,1]{5,1,4,3,2,0,7,6:T(8,128)(2,1)} %convert_bitcast_fusion, bf16[4,3,6,2,40,64]{5,4,3,2,1,0:T(8,128)(2,1)} %bitcast.126, pred[4,3,6]{2,1,0:T(4,128)(4,1)S(1)} %compare_and_fusion), kind=kOutput, calls=%fused_computation.10 | convolution fusion | flops 1887805440 | bytes 9584712 | tf_op jit(solution)/shard_map/ercjbp,kwrjpq->kwecbq/dot_general | solution.py:41
  54.7 0.3 fusion.46
  55.0 1.4 collective-permute-start
  56.5 1.5 collective-permute-start.1
  57.9 2.6 %collective-permute-done = f32[5,2,2,40,6,64]{5,3,4,2,1,0:T(8,128)S(1)} collective-permute-done((f32[5,2,2,40,6,64]{5,3,4,2,1,0:T(8,128)S(1)}, f32[5,2,2,40,6,64]{5,3,4,2,1,0:T(8,128)S(1)}, u32[]{:S(2)}, u32[]{:S(2)}) %collective-permute-start) | collective-permute-done | bytes 1228832 | tf_op jit(solution)/shard_map/ppermute | solution.py:12
  60.6 2.4 %collective-permute-done.1 = f32[5,2,2,40,6,64]{5,3,4,2,1,0:T(8,128)S(1)} collective-permute-done((f32[5,2,2,40,6,64]{5,3,4,2,1,0:T(8,128)S(1)}, f32[5,2,2,40,6,64]{5,3,4,2,1,0:T(8,128)S(1)}, u32[]{:S(2)}, u32[]{:S(2)}) %collective-permute-start.1) | collective-permute-done | bytes 1228832 | tf_op jit(solution)/shard_map/ppermute | solution.py:12
  63.0 2.1 %fusion.3 = bf16[5,4,2,40,6,64]{5,3,4,2,1,0:T(8,128)(2,1)} fusion(f32[5,8,2,40,6,64]{5,3,4,2,1,0:T(8,128)S(1)} %fusion.7, f32[5,2,2,40,6,64]{5,3,4,2,1,0:T(8,128)S(1)} %collective-permute-done.1, f32[5,2,2,40,6,64]{5,3,4,2,1,0:T(8,128)S(1)} %collective-permute-done), kind=kLoop, calls=%fused_computation.6 | loop fusion | flops 1843200 | bytes 6144000 | tf_op jit(solution)/shard_map/convert_element_type | solution.py:66
  65.1 8.9 %copy.40 = bf16[5,4,2,40,6,64]{3,2,1,0,5,4:T(2,128)(2,1)} copy(bf16[5,4,2,40,6,64]{5,3,4,2,1,0:T(8,128)(2,1)} %fusion.3) | data formatting | bytes 2457600 | tf_op jit(solution)/shard_map/reshape | solution.py:66
  74.0 7.6 %reshape.73 = bf16[16,2,19200]{2,1,0:T(2,128)(2,1)} reshape(bf16[384,5,4,2,40]{4,3,2,1,0:T(2,128)(2,1)} %bitcast.119) | data formatting | bytes 2457600
  81.6 35.9 %all_to_all.33 = bf16[16,2,19200]{2,1,0:T(2,128)(2,1)} all-to-all(bf16[16,2,19200]{2,1,0:T(2,128)(2,1)} %reshape.73), channel_id=1, replica_groups=mesh['lat'=2,'lon'=16] {'lon'}, dimensions={0} | all-to-all | bytes 2457600 | tf_op jit(solution)/shard_map/all_to_all | solution.py:67
  117.5 7.9 %reshape.74 = bf16[384,5,4,2,40]{4,3,2,1,0:T(2,128)(2,1)} reshape(bf16[16,2,19200]{2,1,0:T(2,128)(2,1)} %all_to_all.33) | data formatting | bytes 2457600
  125.4 3.0 %copy.27 = bf16[5,4,2,40,384]{3,4,2,1,0:T(8,128)(2,1)S(1)} copy(bf16[5,4,2,40,384]{3,2,1,0,4:T(2,128)(2,1)} %bitcast.120) | data formatting | bytes 2457600 | tf_op jit(solution)/shard_map/all_to_all | solution.py:67
  128.4 2.8 %copy.28 = bf16[5,4,2,16,40,24]{4,3,5,0,2,1:T(8,128)(2,1)} copy(bf16[5,4,2,16,40,24]{4,5,3,2,1,0:T(8,128)(2,1)S(1)} %bitcast.121) | data formatting | bytes 2457600 | tf_op jit(solution)/shard_map/all_to_all | solution.py:67
  131.2 6.8 %all_to_all.30 = bf16[5,4,2,640,24]{3,4,0,2,1:T(8,128)(2,1)} reshape(bf16[5,4,2,16,40,24]{4,3,5,0,2,1:T(8,128)(2,1)} %copy.28) | data formatting | bytes 2457600 | tf_op jit(solution)/shard_map/all_to_all | solution.py:67
  138.0 0.0 all-gather.2.cloned.1.call-done
  138.0 4.7 %fusion.16 = bf16[2,4,24,640]{3,2,0,1:T(8,128)(2,1)S(1)} fusion(bf16[5,4,2,640,24]{3,4,0,2,1:T(8,128)(2,1)} %all_to_all.30, bf16[5,640,640]{2,1,0:T(8,128)(2,1)} %all-gather.2.cloned.1.call-done), kind=kOutput, calls=%fused_computation.17 | convolution fusion | flops 794419200 | bytes 5570560 | tf_op jit(solution)/shard_map/klecn,kcd->elnd/dot_general | solution.py:68
  142.6 0.7 copy.29
  (1 shorter events, 0.0 us)
Async XLA Ops:
  6.5 17.0 %copy-start = (bf16[5,4,3,3,64,64]{5,4,3,2,1,0:T(8,128)(2,1)S(1)}, bf16[5,4,3,3,64,64]{5,4,3,2,1,0:T(8,128)(2,1)}, u32[]{:S(2)}) copy-start(bf16[5,4,3,3,64,64]{5,4,3,2,1,0:T(8,128)(2,1)} %param.6) | copy-start | bytes 4423684
  6.5 16.4 %copy-start.2 = (s32[8,3]{0,1:T(4,128)S(1)}, s32[8,3]{0,1:T(4,128)}, u32[]{:S(2)}) copy-start(s32[8,3]{0,1:T(4,128)} %param.8) | copy-start | bytes 292
  6.5 16.6 %copy-start.1 = (s32[5,8]{1,0:T(8,128)S(1)}, s32[5,8]{1,0:T(8,128)}, u32[]{:S(2)}) copy-start(s32[5,8]{1,0:T(8,128)} %param.7) | copy-start | bytes 484
  6.5 131.4 %all-gather.2.cloned.1.call-start = ((), (), s32[]{:S(2)}) async-start(), calls=%async_computation.2 | async-start | bytes 4352000 | tf_op jit(solution)/shard_map/all_gather | solution.py:71
  14.6 21.7 %all-to-all-start = ((bf16[16,2,3840]{2,1,0:T(2,128)(2,1)}), bf16[16,2,3840]{2,1,0:T(2,128)(2,1)S(1)}, u32[]{:S(2)}, u32[]{:S(2)}) async-start(bf16[16,2,3840]{2,1,0:T(2,128)(2,1)} %reshape.71), calls=%async_computation | async-start | bytes 491520 | tf_op jit(solution)/shard_map/all_to_all | solution.py:48
  55.0 5.6 %collective-permute-start = (f32[5,2,2,40,6,64]{5,3,4,2,1,0:T(8,128)S(1)}, f32[5,2,2,40,6,64]{5,3,4,2,1,0:T(8,128)S(1)}, u32[]{:S(2)}, u32[]{:S(2)}) collective-permute-start(f32[5,2,2,40,6,64]{5,3,4,2,1,0:T(8,128)S(1)} %get-tuple-element.5), channel_id=1, source_target_pairs={{0,16},{1,17},{2,18},{3,19},{4,20},{5,21},{6,22},{7,23},{8,24},{9,... | collective-permute-start | bytes 3686408 | tf_op jit(solution)/shard_map/ppermute | solution.py:12
  56.5 6.6 %collective-permute-start.1 = (f32[5,2,2,40,6,64]{5,3,4,2,1,0:T(8,128)S(1)}, f32[5,2,2,40,6,64]{5,3,4,2,1,0:T(8,128)S(1)}, u32[]{:S(2)}, u32[]{:S(2)}) collective-permute-start(f32[5,2,2,40,6,64]{5,3,4,2,1,0:T(8,128)S(1)} %get-tuple-element.6), channel_id=1, source_target_pairs={{16,0},{17,1},{18,2},{19,3},{20,4},{21,5},{22,6},{23,7},{24,8},{25... | collective-permute-start | bytes 3686408 | tf_op jit(solution)/shard_map/ppermute | solution.py:12
Sparse Core Ops, SparseCore 0:
  10.1 79.6 all-gather.1
where the time goes:
time: 151 us; the launch traced here: 150 us
  local copies, waits for them, and re-layouts  56 us (37%)
  blocking collectives  35.9 us (24%)
  matrix products  18.2 us (12%)
  between operations  13.5 us (9%)
  waiting for transfers between devices  13 us (9%)
  starting transfers between devices  11.2 us (7%)
  other arithmetic  2.39 us (2%)
    all_to_all x1, blocking collectives, per_device(): lax.all_to_all(conv, 'lon', split_axis=4, concat_axis=3, tiled=True)  35.9 us
    unnamed x11, local copies, waits for them, and re-layouts  25.8 us
    all_to_all x3, local copies, waits for them, and re-layouts, per_device(): lax.all_to_all(conv, 'lon', split_axis=4, concat_axis=3, tiled=True)  12.6 us
    reshape x1, local copies, waits for them, and re-layouts, per_device(): owned.astype(jnp.bfloat16)  8.9 us
    all_to_all x1, starting transfers between devices, per_device(): lax.all_to_all(fields, 'lon', split_axis=2, concat_axis=3, tiled=True)  8.31 us
    dot_general x1, matrix products, accumulate(): jnp.einsum('ercjbp,kwrjpq->kwecbq', picked, effective, preferred_element_...  8.03 us
    all_to_all x1, waiting for transfers between devices, per_device(): lax.all_to_all(fields, 'lon', split_axis=2, concat_axis=3, tiled=True)  7.24 us
    dot_general x1, matrix products, accumulate(): jnp.einsum('kwrt,krtjpq->kwrjpq', select, weights.astype(jnp.float32))  5.49 us
  transfers between devices with their start and end apart: 4, of which 3 were waited for; matrix products, arithmetic and copies ran while one was open for 43% of the time, Pallas kernels for 0%

commit v1 on v0

v1 whole, which is shorter than its diff:
```python
import functools
import math

import jax
import jax.numpy as jnp
from jax import lax
from jax.experimental import pallas as pl
from jax.experimental.pallas import tpu as pltpu
from jax.sharding import Mesh
from jax.sharding import PartitionSpec as P

HALO = 2
VMEM = pltpu.VMEM
LIMIT = 48 * 1024 * 1024


def pack_kernel(groups, owners, x_ref, out_ref):
    members, rows, cells, channels = x_ref.shape
    width = channels // (groups * owners)
    for e in range(members):
        for q in range(groups):
            parts = [
                x_ref[e, i, :, (p * groups + q) * width : (p * groups + q + 1) * width]
                for i in range(rows)
                for p in range(owners)
            ]
            block = jnp.concatenate(parts, axis=-1)
            for p in range(owners):
                out_ref[e, p, q] = block


def pack(x, groups, owners):
    members, rows, cells, channels = x.shape
    return pl.pallas_call(
        functools.partial(pack_kernel, groups, owners),
        out_shape=jax.ShapeDtypeStruct((members, owners, groups, cells, rows * channels // groups), x.dtype),
        in_specs=[pl.BlockSpec(memory_space=VMEM)],
        out_specs=pl.BlockSpec(memory_space=VMEM),
        compiler_params=pltpu.CompilerParams(vmem_limit_bytes=LIMIT),
        name="pack",
    )(x)


def conv_mix_kernel(bases, taps, slots, halo, sub, low_ref, shift_ref, place_ref, fields_ref, *refs):
    late = fields_ref.shape[1]
    weight_refs = refs[:late]
    mix_ref = refs[late]
    outs = refs[late + 1 : -2]
    field_rows, total = refs[-2:]
    owners, _, span, _ = fields_ref.shape
    channels = mix_ref.shape[1]
    rows = weight_refs[0].shape[0]
    block = weight_refs[0].shape[2]
    nblocks = owners * span // block
    member, owner = place_ref[0], place_ref[1]

    total[...] = jnp.zeros_like(total)
    for s in range(late):
        lat = lax.rem(member + s, late)
        for r in range(rows):
            for p in range(owners):
                field_rows[r, p * span : (p + 1) * span] = fields_ref[
                    p, lat, :, r * channels : (r + 1) * channels
                ]
        for r in range(rows):
            row = lat * rows + r
            for piece in range(span // sub):
                cell = owner * span + piece * sub
                b = lax.div(cell, block)
                q = pl.multiple_of(lax.rem(cell, block), sub)
                chosen = []
                for j in range(slots):
                    source = lax.rem(b + shift_ref[row, j] + nblocks, nblocks)
                    chosen.append(field_rows[r, pl.ds(pl.multiple_of(source * block, block), block)])
                picked = jnp.concatenate(chosen, axis=0)
                lhs = weight_refs[s][r, :, pl.ds(q, sub), :].reshape(bases * taps * sub, slots * block)
                product = jnp.dot(lhs, picked, preferred_element_type=jnp.float32)
                for k in range(bases):
                    first = row + low_ref[k, row] + HALO
                    for t in range(taps):
                        at = (k * taps + t) * sub
                        total[k, first + t, piece * sub : (piece + 1) * sub] += product[at : at + sub]
    main = outs[0]
    _, groups, _, cells, _ = main.shape
    for o in range(-halo, late * rows + halo):
        mixed = sum(
            jnp.dot(total[k, o + HALO].astype(jnp.bfloat16), mix_ref[k], preferred_element_type=jnp.float32)
            for k in range(bases)
        )
        for q in range(groups):
            value = mixed[q * cells : (q + 1) * cells].astype(jnp.bfloat16)
            if 0 <= o < late * rows:
                main[o // rows, q, o % rows] = value
            else:
                outs[1][o + halo if o < 0 else o + halo - late * rows, q] = value


def conv_mix(low, shift, place, fields, weights, mix, halo, groups, block):
    bases, all_rows = low.shape
    slots = shift.shape[1]
    owners, late, span, _ = fields.shape
    rows = all_rows // late
    channels, width = mix.shape[1:]
    taps = weights[0].shape[1] // bases
    sub = math.gcd(span, block)
    shapes = [jax.ShapeDtypeStruct((late, groups, rows, span // groups, width), jnp.bfloat16)]
    if halo:
        shapes.append(jax.ShapeDtypeStruct((2 * halo, groups, span // groups, width), jnp.bfloat16))
    smem = pl.BlockSpec(memory_space=pltpu.SMEM)
    vmem = pl.BlockSpec(memory_space=VMEM)
    return pl.pallas_call(
        functools.partial(conv_mix_kernel, bases, taps, slots, halo, sub),
        out_shape=shapes,
        in_specs=[smem] * 3 + [vmem] * (2 + late),
        out_specs=[vmem] * len(shapes),
        scratch_shapes=[
            VMEM((rows, owners * span, channels), jnp.bfloat16),
            VMEM((bases, all_rows + 2 * HALO, span, channels), jnp.float32),
        ],
        compiler_params=pltpu.CompilerParams(vmem_limit_bytes=LIMIT),
        name="conv_mix",
    )(low, shift, place, fields, *weights, mix)


def per_device(sizes, fields, kernel, band_low, block_shift, mix_weight):
    halves, late, owners, groups = sizes
    members, rows, channels, cells = fields.shape
    bases, _, taps, slots, block, _ = kernel.shape
    all_rows = late * rows
    halo = HALO if halves > 1 else 0

    packed = pack(fields.transpose(0, 1, 3, 2), groups, owners)
    packed = packed.reshape((late * owners * groups,) + packed.shape[3:])
    spread = lax.all_to_all(packed, ("late", "lonp", "lonq"), split_axis=0, concat_axis=0, tiled=True)
    spread = spread.reshape(late, owners, groups * cells, -1).transpose(1, 0, 2, 3)

    own = kernel.transpose(1, 0, 2, 5, 3, 4).reshape(rows, bases * taps, block, slots * block)
    weights = [own]
    for s in range(1, late):
        route = [((i + s) % late, i) for i in range(late)]
        weights.append(lax.ppermute(own, "late", route))
    mix = lax.all_gather(mix_weight, "lonp", axis=1, tiled=True)

    start = lax.axis_index("lath") * all_rows
    low = lax.dynamic_slice_in_dim(band_low, start, all_rows, 1)
    shift = lax.dynamic_slice_in_dim(block_shift, start, all_rows, 0)
    place = jnp.stack([lax.axis_index("late"), lax.axis_index("lonp")]).astype(jnp.int32)
    partial, *beyond = conv_mix(low, shift, place, spread, weights, mix, halo, groups, block)
    if halo:
        beyond = beyond[0]
        below = lax.ppermute(beyond[halo:], "lath", [(i, i + 1) for i in range(halves - 1)])
        above = lax.ppermute(beyond[:halo], "lath", [(i + 1, i) for i in range(halves - 1)])
        body = partial.transpose(0, 2, 1, 3, 4).reshape((all_rows,) + beyond.shape[1:])
        body = body.astype(jnp.float32)
        body = body.at[:halo].add(below.astype(jnp.float32)).at[-halo:].add(above.astype(jnp.float32))
        body = body.astype(jnp.bfloat16).reshape((late, rows) + beyond.shape[1:])
        partial = body.transpose(0, 2, 1, 3, 4)
    partial = partial.reshape(late * groups, rows * cells, -1)
    parts = lax.all_to_all(partial, ("late", "lonq"), split_axis=0, concat_axis=0, tiled=True)
    parts = parts.reshape(members, groups, rows, cells, -1)
    summed = jnp.sum(parts.astype(jnp.float32), axis=1)
    return jax.nn.gelu(summed, approximate=False).astype(jnp.bfloat16)


def solution(mesh):
    lat, lon = mesh.shape["lat"], mesh.shape["lon"]
    groups = max(g for g in range(1, lon + 1) if lon % g == 0 and g * g <= lon)

    def whole(fields, kernel, band_low, block_shift, mix_weight):
        late = fields.shape[0]
        sizes = (lat // late, late, lon // groups, groups)
        split = Mesh(mesh.devices.reshape(sizes), ("lath", "late", "lonp", "lonq"))
        rows, cells = ("lath", "late"), ("lonp", "lonq")
        return jax.shard_map(
            functools.partial(per_device, sizes),
            mesh=split,
            in_specs=(
                P(None, rows, None, cells),
                P(None, rows, None, None, None, None),
                P(),
                P(),
                P(None, cells, None),
            ),
            out_specs=P(None, rows, cells, None),
            check_vma=False,
        )(fields, kernel, band_low, block_shift, mix_weight)

    return whole
```

time: 151 us -> 78.3 us (0.52)
  local copies, waits for them, and re-layouts: 56 us -> 8.03 us
  matrix products: 18.2 us -> 0 us
  blocking collectives: 35.9 us -> 52.6 us
  between operations: 13.5 us -> 0.07 us
  waiting for transfers between devices: 13 us -> 0.01 us
  Pallas kernels: 0 us -> 7.55 us
  starting transfers between devices: 11.2 us -> 7.66 us
    all_gather x0 -> x1, blocking collectives: none -> 34.8 us  [per_device(): mix = lax.all_gather(mix_weight, 'lonp', axis=1, tiled=True)]
    unnamed x11, local copies, waits for them, and re-layouts: 25.8 us -> 1.04 us
    dot_general x3 -> x0, matrix products: 18.2 us -> none  [the longest x1 8.03 us: accumulate(): jnp.einsum('ercjbp,kwrjpq->kwecbq', picked, effective, preferred_element_...]
    all_to_all x1, blocking collectives: 35.9 us -> 17.9 us  [per_device(): lax.all_to_all(partial, ('late', 'lonq'), split_axis=0, concat_axis=0, ti...]
    all_to_all x4 -> x0, local copies, waits for them, and re-layouts: 16 us -> none  [the longest x3 12.6 us: per_device(): lax.all_to_all(conv, 'lon', split_axis=4, concat_axis=3, tiled=True)]
    pallas_call x0 -> x2, Pallas kernels: none -> 7.55 us  [the longest x1 6.21 us: conv_mix(): pl.pallas_call(functools.partial(conv_mix_kernel, bases, taps, slots, hal...]
    all_to_all x1, waiting for transfers between devices: 7.24 us -> 0.01 us  [per_device(): lax.all_to_all(packed, ('late', 'lonp', 'lonq'), split_axis=0, concat_axi...]
    reshape x2, local copies, waits for them, and re-layouts: 10.4 us -> 4.61 us  [the longest x1 3.32 us: per_device(): kernel.transpose(1, 0, 2, 5, 3, 4)]
  transfers between devices with their start and end apart: 4 -> 2, of which waited for: 3 -> 0; matrix products, arithmetic and copies ran while one was open for 43% -> 9% of each run, Pallas kernels for 0% -> 0%
where the time goes in v1:
time: 78.3 us; the launch traced here: 77.9 us
  blocking collectives  52.6 us (67%)
  local copies, waits for them, and re-layouts  8.03 us (10%)
  starting transfers between devices  7.66 us (10%)
  Pallas kernels  7.55 us (10%)
  other arithmetic  1.97 us (3%)
    all_gather x1, blocking collectives, per_device(): mix = lax.all_gather(mix_weight, 'lonp', axis=1, tiled=True)  34.8 us
    all_to_all x1, blocking collectives, per_device(): lax.all_to_all(partial, ('late', 'lonq'), split_axis=0, concat_axis=0, ti...  17.9 us
    all_to_all x1, starting transfers between devices, per_device(): lax.all_to_all(packed, ('late', 'lonp', 'lonq'), split_axis=0, concat_axi...  7.41 us
    pallas_call x1, Pallas kernels, conv_mix(): pl.pallas_call(functools.partial(conv_mix_kernel, bases, taps, slots, hal...  6.21 us
    reshape x1, local copies, waits for them, and re-layouts, per_device(): kernel.transpose(1, 0, 2, 5, 3, 4)  3.32 us
    transpose x1, local copies, waits for them, and re-layouts, per_device(): kernel.transpose(1, 0, 2, 5, 3, 4)  2.38 us
    convert_element_type x1, other arithmetic, per_device(): return jax.nn.gelu(summed, approximate=False).astype(jnp.bfloat16)  1.76 us
  transfers between devices with their start and end apart: 2, of which 0 were waited for; matrix products, arithmetic and copies ran while one was open for 9% of the time, Pallas kernels for 0%

profile of v1, /device:TPU:0, one launch (start us, length us, event | category | flops | bytes accessed | tf_op | source)
XLA Modules:
  0.0 77.9 jit_solution(17344165774489097640)
XLA Ops:
  0.0 0.0 copy-start
  0.0 0.9 %copy-done = bf16[2,4,640,24]{2,3,1,0:T(8,128)(2,1)S(1)} copy-done((bf16[2,4,640,24]{2,3,1,0:T(8,128)(2,1)S(1)}, bf16[2,4,640,24]{2,3,1,0:T(8,128)(2,1)}, u32[]{:S(2)}) %copy-start) | copy-done | bytes 245784
  0.9 0.0 copy-start.2
  0.9 1.3 %pack.1 = bf16[2,4,4,24,640]{4,3,2,1,0:T(8,128)(2,1)} custom-call(bf16[2,4,24,640]{3,2,1,0:T(8,128)(2,1)S(1)} %bitcast.15), custom_call_target="tpu_custom_call" | custom-call | tf_op jit(solution)/shard_map/pack/pallas_call | solution.py:34
  2.3 7.4 %all-to-all-start = ((bf16[32,24,640]{2,1,0:T(8,128)(2,1)}), bf16[32,24,640]{2,1,0:T(8,128)(2,1)}, u32[]{:S(2)}, u32[]{:S(2)}) async-start(bf16[32,24,640]{2,1,0:T(8,128)(2,1)} %bitcast.3), calls=%async_computation | async-start | bytes 1966080 | tf_op jit(solution)/shard_map/all_to_all | solution.py:134
  9.7 0.0 copy-done.2
  9.7 2.4 %copy.9 = bf16[4,5,3,64,3,64]{3,5,4,2,1,0:T(8,128)(2,1)} copy(bf16[4,5,3,64,3,64]{3,5,4,2,0,1:T(8,128)(2,1)S(1)} %bitcast.18) | data formatting | bytes 2949120 | tf_op jit(solution)/shard_map/transpose | solution.py:137
  12.1 0.0 copy-start.4
  12.1 0.0 copy-start.3
  12.1 3.3 %copy.12.refs_0_ = bf16[4,15,64,192]{3,2,1,0:T(8,128)(2,1)S(1)} copy(bf16[4,15,64,192]{2,3,1,0:T(8,128)(2,1)} %bitcast.16) | data formatting | bytes 2949120 | tf_op jit(solution)/shard_map/reshape | solution.py:137
  15.4 0.0 copy-start.1
  15.4 0.3 collective-permute-start
  15.7 0.0 copy-done.4
  15.7 0.1 copy.11.shift_ref
  15.8 0.1 pad_add_fusion.place_ref
  15.9 0.0 copy-done.3
  15.9 34.8 %all_gather.3.refs_2_ = bf16[5,160,640]{2,1,0:T(8,128)(2,1)S(1)} all-gather(bf16[5,40,640]{2,1,0:T(8,128)(2,1)S(1)} %copy-done.3), channel_id=1, replica_groups=mesh['lath'=1,'late'=2,'lonp'=4,'lonq'=4] {'lonp'}, dimensions={1}, use_global_device_ids=true | all-gather | bytes 1280000 | tf_op jit(solution)/shard_map/all_gather | solution.py:142
  50.6 0.0 all-to-all-done
  50.6 1.3 %copy.14 = bf16[2,4,96,640]{3,2,0,1:T(8,128)(2,1)S(1)} copy(bf16[2,4,96,640]{3,2,1,0:T(8,128)(2,1)} %bitcast.4) | data formatting | bytes 1966080 | tf_op jit(solution)/shard_map/reshape | solution.py:135
  51.9 0.0 collective-permute-done.refs_1_
  51.9 0.0 copy-done.1
  51.9 6.2 %conv_mix.1 = bf16[2,4,4,24,640]{4,3,2,1,0:T(8,128)(2,1)S(1)} custom-call(s32[5,8]{1,0:T(8,128)S(1)} %copy-done.1, s32[8,3]{1,0:T(8,128)S(1)} %copy.11.shift_ref, s32[2]{0:T(128)S(1)} %pad_add_fusion.place_ref, bf16[4,2,96,640]{3,2,1,0:T(8,128)(2,1)S(1)} %bitcast.13, bf16[4,15,64,192]{3,2,1,0:T(8,128)(2,1)S(1)} %copy.12.refs_0_, ...), custom_call_target="tpu_custom_call" | custom-call | tf_op jit(solution)/shard_map/conv_mix/pallas_call | solution.py:111
  58.2 17.9 %all_to_all.10 = bf16[8,96,640]{2,1,0:T(8,128)(2,1)S(1)} all-to-all(bf16[8,96,640]{2,1,0:T(8,128)(2,1)S(1)} %bitcast.14), channel_id=1, replica_groups=mesh['lath'=1,'late'=2,'lonp'=4,'lonq'=4] {'late','lonq'}, dimensions={0} | all-to-all | bytes 1966080 | tf_op jit(solution)/shard_map/all_to_all | solution.py:159
  76.0 0.1 convert_reduce_fusion
  76.2 1.8 %fusion.2 = bf16[2,4,24,640]{3,2,1,0:T(8,128)(2,1)} fusion(f32[2,4,24,640]{3,2,1,0:T(8,128)S(1)} %convert_reduce_fusion), kind=kLoop, calls=%fused_computation.5 | loop fusion | flops 7987200 | bytes 737280 | tf_op jit(solution)/shard_map/convert_element_type | solution.py:162
Async XLA Ops:
  0.0 0.9 %copy-start = (bf16[2,4,640,24]{2,3,1,0:T(8,128)(2,1)S(1)}, bf16[2,4,640,24]{2,3,1,0:T(8,128)(2,1)}, u32[]{:S(2)}) copy-start(bf16[2,4,640,24]{2,3,1,0:T(8,128)(2,1)} %param.5) | copy-start | bytes 737284
  0.9 8.8 %copy-start.2 = (bf16[5,4,3,3,64,64]{5,4,3,2,1,0:T(8,128)(2,1)S(1)}, bf16[5,4,3,3,64,64]{5,4,3,2,1,0:T(8,128)(2,1)}, u32[]{:S(2)}) copy-start(bf16[5,4,3,3,64,64]{5,4,3,2,1,0:T(8,128)(2,1)} %param.6) | copy-start | bytes 4423684
  2.3 48.3 %all-to-all-start = ((bf16[32,24,640]{2,1,0:T(8,128)(2,1)}), bf16[32,24,640]{2,1,0:T(8,128)(2,1)}, u32[]{:S(2)}, u32[]{:S(2)}) async-start(bf16[32,24,640]{2,1,0:T(8,128)(2,1)} %bitcast.3), calls=%async_computation | async-start | bytes 1966080 | tf_op jit(solution)/shard_map/all_to_all | solution.py:134
  12.1 3.6 %copy-start.4 = (s32[8,3]{0,1:T(4,128)S(1)}, s32[8,3]{0,1:T(4,128)}, u32[]{:S(2)}) copy-start(s32[8,3]{0,1:T(4,128)} %param.8) | copy-start | bytes 292
  12.1 3.8 %copy-start.3 = (bf16[5,40,640]{2,1,0:T(8,128)(2,1)S(1)}, bf16[5,40,640]{2,1,0:T(8,128)(2,1)}, u32[]{:S(2)}) copy-start(bf16[5,40,640]{2,1,0:T(8,128)(2,1)} %param.9) | copy-start | bytes 768004
  15.4 36.5 %copy-start.1 = (s32[5,8]{1,0:T(8,128)S(1)}, s32[5,8]{1,0:T(8,128)}, u32[]{:S(2)}) copy-start(s32[5,8]{1,0:T(8,128)} %low_ref) | copy-start | bytes 484
  15.4 36.5 %collective-permute-start = (bf16[4,15,64,192]{3,2,1,0:T(8,128)(2,1)S(1)}, bf16[4,15,64,192]{3,2,1,0:T(8,128)(2,1)}, u32[]{:S(2)}, u32[]{:S(2)}) collective-permute-start(bf16[4,15,64,192]{3,2,1,0:T(8,128)(2,1)S(1)} %copy.12.refs_0_), channel_id=1, source_target_pairs={{16,0},{0,16},{17,1},{1,17},{18,2},{2,18},{19,3},{3,19},{20,4},{4,... | collective-permute-start | bytes 4423688 | tf_op jit(solution)/shard_map/ppermute | solution.py:141

commit v2 on v1

v2 whole, which is shorter than its diff:
```python
import functools
import math

import jax
import jax.numpy as jnp
from jax import lax
from jax.experimental import pallas as pl
from jax.experimental.pallas import tpu as pltpu
from jax.sharding import Mesh
from jax.sharding import PartitionSpec as P

HALO = 2
LANES = 128
VMEM = pltpu.VMEM
LIMIT = 48 * 1024 * 1024
SMEM_SPEC = pl.BlockSpec(memory_space=pltpu.SMEM)
VMEM_SPEC = pl.BlockSpec(memory_space=VMEM)


def partner(index, distance, size):
    if size & (size - 1) == 0:
        return index ^ distance
    return (distance - index) % size


def partner_in_kernel(index, distance, size):
    if size & (size - 1) == 0:
        return lax.bitwise_xor(index, distance)
    return lax.rem(distance - index + size, size)


def trade(x, axis, distance, size):
    return lax.ppermute(x, axis, [(i, partner(i, distance, size)) for i in range(size)])


def pack_kernel(groups, owners, x_ref, out_ref):
    members, rows, cells, channels = x_ref.shape
    width = channels // (groups * owners)
    for e in range(members):
        for q in range(groups):
            parts = [
                x_ref[e, i, :, (p * groups + q) * width : (p * groups + q + 1) * width]
                for i in range(rows)
                for p in range(owners)
            ]
            out_ref[e, q] = jnp.concatenate(parts, axis=-1)


def pack(x, groups, owners):
    members, rows, cells, channels = x.shape
    return pl.pallas_call(
        functools.partial(pack_kernel, groups, owners),
        out_shape=jax.ShapeDtypeStruct((members, groups, cells, rows * channels // groups), x.dtype),
        in_specs=[VMEM_SPEC],
        out_specs=VMEM_SPEC,
        compiler_params=pltpu.CompilerParams(vmem_limit_bytes=LIMIT),
        name="pack",
    )(x)


def added(refs, *at):
    value = refs[0][at]
    for ref in refs[1:]:
        value = value + ref[at]
    return value


def conv_mix_kernel(geometry, counts, low_ref, shift_ref, place_ref, *refs):
    bases, taps, slots, halo, sub, groups = geometry
    refs = list(refs)
    field_slots = [[refs.pop(0) for _ in range(n)] for n in counts[0]]
    weight_refs = [refs.pop(0) for _ in range(counts[1])]
    mix_slots = [[refs.pop(0) for _ in range(n)] for n in counts[2]]
    field_rows, total, mix_all, mixed = refs[-4:]
    outs = refs[:-4]
    late, span, _ = field_slots[0][0].shape
    owners = len(field_slots)
    depth, width = mix_slots[0][0].shape[1:]
    channels = owners * depth
    padded = total.shape[-1]
    rows, _, block, _ = weight_refs[0].shape
    nblocks = owners * span // block
    cells = span // groups
    member, owner, group = place_ref[0], place_ref[1], place_ref[2]

    total[...] = jnp.zeros_like(total)
    field_rows[...] = jnp.zeros_like(field_rows)
    for s in range(late):
        lat = partner_in_kernel(member, s, late)
        for d, slot in enumerate(field_slots):
            base = pl.multiple_of(partner_in_kernel(owner, d, owners) * span, sub)
            value = added(slot, lat)
            for r in range(rows):
                field_rows[r, pl.ds(base, span), :channels] = value[:, r * channels : (r + 1) * channels]

        def one_row(r, carry):
            row = lat * rows + r
            for piece in range(span // sub):
                cell = owner * span + piece * sub
                b = lax.div(cell, block)
                q = pl.multiple_of(lax.rem(cell, block), sub)
                chosen = []
                for j in range(slots):
                    source = lax.rem(b + shift_ref[row, j] + nblocks, nblocks)
                    chosen.append(field_rows[r, pl.ds(pl.multiple_of(source * block, block), block)])
                picked = jnp.concatenate(chosen, axis=0)
                lhs = weight_refs[s][r, :, pl.ds(q, sub), :].reshape(bases * taps * sub, slots * block)
                product = jnp.dot(lhs, picked, preferred_element_type=jnp.float32)
                for k in range(bases):
                    first = row + low_ref[k, row] + HALO
                    for t in range(taps):
                        at = (k * taps + t) * sub
                        total[k, first + t, piece * sub : (piece + 1) * sub] += product[at : at + sub]
            return carry

        lax.fori_loop(0, rows, one_row, 0)

    for d, slot in enumerate(mix_slots):
        for k in range(bases):
            mix_all[place_ref[3 + d], k] = added(slot, k)
    fill = jnp.zeros((padded - channels, width), jnp.bfloat16)
    matrix = jnp.concatenate(
        [x for k in range(bases) for x in [mix_all[p, k] for p in range(owners)] + [fill]], axis=0
    )

    def one_out(first, count):
        at = pl.ds(first + HALO, count)
        lhs = [total[k, at].astype(jnp.bfloat16).reshape(count * span, padded) for k in range(bases)]
        product = jnp.dot(jnp.concatenate(lhs, axis=-1), matrix, preferred_element_type=jnp.float32)
        return product.reshape(count, span, width)

    for lat in range(late):
        mixed[lat * rows : (lat + 1) * rows] = one_out(lat * rows, rows)
    for dl in range(late):
        lat = partner_in_kernel(member, dl, late)
        for dq in range(groups):
            start = pl.multiple_of(partner_in_kernel(group, dq, groups) * cells, 8 if cells % 8 == 0 else cells)
            for r in range(rows):
                outs[dl * groups + dq][r] = mixed[lat * rows + r, pl.ds(start, cells)].astype(jnp.bfloat16)
    if halo:
        for side, first in enumerate((-halo, late * rows)):
            outs[-1][side] = one_out(first, halo).astype(jnp.bfloat16)


def conv_mix(low, shift, place, fields, weights, mix, halo, groups, block):
    bases, all_rows = low.shape
    slots = shift.shape[1]
    late, span, _ = fields[0][0].shape
    owners = len(fields)
    rows = all_rows // late
    depth, width = mix[0][0].shape[1:]
    padded = -(-owners * depth // LANES) * LANES
    taps = weights[0].shape[1] // bases
    sub = math.gcd(span, block)
    shapes = [jax.ShapeDtypeStruct((rows, span // groups, width), jnp.bfloat16)] * (late * groups)
    if halo:
        shapes.append(jax.ShapeDtypeStruct((2, halo, span, width), jnp.bfloat16))
    operands = [x for slot in fields for x in slot] + weights + [x for slot in mix for x in slot]
    counts = ([len(s) for s in fields], len(weights), [len(s) for s in mix])
    return pl.pallas_call(
        functools.partial(conv_mix_kernel, (bases, taps, slots, halo, sub, groups), counts),
        out_shape=shapes,
        in_specs=[SMEM_SPEC] * 3 + [VMEM_SPEC] * len(operands),
        out_specs=[VMEM_SPEC] * len(shapes),
        scratch_shapes=[
            VMEM((rows, owners * span, padded), jnp.bfloat16),
            VMEM((bases, all_rows + 2 * HALO, span, padded), jnp.float32),
            VMEM((owners, bases, depth, width), jnp.bfloat16),
            VMEM((all_rows, span, width), jnp.float32),
        ],
        compiler_params=pltpu.CompilerParams(vmem_limit_bytes=LIMIT),
        name="conv_mix",
    )(low, shift, place, *operands)


def finish_kernel(groups, place_ref, *refs):
    out_ref = refs[-1]
    late = out_ref.shape[0]
    for dl in range(late):
        total = refs[dl * groups][...].astype(jnp.float32)
        for dq in range(1, groups):
            total += refs[dl * groups + dq][...].astype(jnp.float32)
        value = total * (1.0 + lax.erf(total * (0.5**0.5))) * 0.5
        out_ref[partner_in_kernel(place_ref[0], dl, late)] = value.astype(jnp.bfloat16)


def finish(place, parts, groups):
    return pl.pallas_call(
        functools.partial(finish_kernel, groups),
        out_shape=jax.ShapeDtypeStruct((len(parts) // groups,) + parts[0].shape, jnp.bfloat16),
        in_specs=[SMEM_SPEC] + [VMEM_SPEC] * len(parts),
        out_specs=VMEM_SPEC,
        compiler_params=pltpu.CompilerParams(vmem_limit_bytes=LIMIT),
        name="finish",
    )(place, *parts)


def gather_fields(x, owners):
    if owners == 4:
        two = lax.ppermute(x, "lonp", [(0, 2), (2, 0), (1, 3), (3, 1)])
        one = lax.ppermute(x, "lonp", [(0, 1), (1, 0), (2, 3), (3, 2)])
        middle = lax.ppermute(x, "lonp", [(1, 2), (2, 1)])
        passed = lax.ppermute(two, "lonp", [(1, 0), (2, 3)])
        return [[x], [one], [two], [middle, passed]]
    return [[x]] + [[trade(x, "lonp", d, owners)] for d in range(1, owners)]


def gather_mix(x, late, owners):
    core, own = lax.axis_index("late"), lax.axis_index("lonp")
    if owners == 4 and late == 2:
        def both(pairs_first, pairs_second):
            return [(a, b) for a, b in pairs_first] + [(4 + a, 4 + b) for a, b in pairs_second]

        near, far = [(0, 1), (1, 0), (2, 3), (3, 2)], [(0, 2), (2, 0), (1, 3), (3, 1)]
        fetched = lax.ppermute(x, ("late", "lonp"), both(near, far))
        other = trade(fetched, "late", 1, late)
        source = jnp.where(core == 0, x, fetched)
        third = lax.ppermute(source, ("late", "lonp"), both([(1, 2), (2, 1)], [(1, 0), (2, 3)]))
        copied = lax.ppermute(third, ("late", "lonp"), [(1, 5), (2, 6), (4, 0), (7, 3)])
        return [[x], [fetched], [other], [third, copied]], [own, own ^ (1 + core), own ^ (2 - core), own ^ 3]
    slots = [[x]] + [[trade(x, "lonp", d, owners)] for d in range(1, owners)]
    return slots, [partner(own, d, owners) for d in range(owners)]


def per_device(sizes, fields, kernel, band_low, block_shift, mix_weight):
    halves, late, owners, groups = sizes
    members, rows, channels, cells = fields.shape
    bases, _, taps, slots, block, _ = kernel.shape
    all_rows = late * rows
    halo = HALO if halves > 1 else 0

    mix, origins = gather_mix(mix_weight, late, owners)
    packed = pack(fields.transpose(0, 1, 3, 2), groups, owners)
    packed = packed.reshape((late * groups,) + packed.shape[2:])
    spread = lax.all_to_all(packed, ("late", "lonq"), split_axis=0, concat_axis=0, tiled=True)
    gathered = gather_fields(spread.reshape(late, groups * cells, -1), owners)

    own = kernel.transpose(1, 0, 2, 5, 3, 4).reshape(rows, bases * taps, block, slots * block)
    weights = [own] + [trade(own, "late", s, late) for s in range(1, late)]

    start = lax.axis_index("lath") * all_rows
    low = lax.dynamic_slice_in_dim(band_low, start, all_rows, 1)
    shift = lax.dynamic_slice_in_dim(block_shift, start, all_rows, 0)
    place = [lax.axis_index("late"), lax.axis_index("lonp"), lax.axis_index("lonq")] + origins
    place = jnp.stack(place).astype(jnp.int32)
    partial = conv_mix(low, shift, place, gathered, weights, mix, halo, groups, block)
    if halo:
        *partial, beyond = partial
        below = lax.ppermute(beyond[1], "lath", [(i, i + 1) for i in range(halves - 1)])
        above = lax.ppermute(beyond[0], "lath", [(i + 1, i) for i in range(halves - 1)])
        filler = jnp.zeros((all_rows - 2 * halo,) + below.shape[1:], below.dtype)
        extra = jnp.concatenate([below, filler, above], axis=0).reshape(late, rows, groups, cells, -1)
        for dl in range(late):
            lat = partner(lax.axis_index("late"), dl, late)
            for dq in range(groups):
                group = partner(lax.axis_index("lonq"), dq, groups)
                partial[dl * groups + dq] += extra[lat, :, group]
    parts = [
        lax.ppermute(
            partial[dl * groups + dq],
            ("late", "lonq"),
            [
                (l * groups + q, partner(l, dl, late) * groups + partner(q, dq, groups))
                for l in range(late)
                for q in range(groups)
            ],
        )
        if dl or dq
        else partial[0]
        for dl in range(late)
        for dq in range(groups)
    ]
    return finish(place, parts, groups)


def solution(mesh):
    lat, lon = mesh.shape["lat"], mesh.shape["lon"]
    groups = max(g for g in range(1, lon + 1) if lon % g == 0 and g * g <= lon)

    def whole(fields, kernel, band_low, block_shift, mix_weight):
        late = fields.shape[0]
        sizes = (lat // late, late, lon // groups, groups)
        split = Mesh(mesh.devices.reshape(sizes), ("lath", "late", "lonp", "lonq"))
        rows, cells = ("lath", "late"), ("lonp", "lonq")
        return jax.shard_map(
            functools.partial(per_device, sizes),
            mesh=split,
            in_specs=(
                P(None, rows, None, cells),
                P(None, rows, None, None, None, None),
                P(),
                P(),
                P(None, cells, None),
            ),
            out_specs=P(None, rows, cells, None),
            check_vma=False,
        )(fields, kernel, band_low, block_shift, mix_weight)

    return whole
```

time: 78.3 us -> 79.2 us (1.011)
  blocking collectives: 52.6 us -> 0 us
  waiting for transfers between devices: 0.01 us -> 27 us
  starting transfers between devices: 7.66 us -> 31.7 us
  Pallas kernels: 7.55 us -> 10.6 us
  other arithmetic: 1.97 us -> 0.03 us
  local copies, waits for them, and re-layouts: 8.03 us -> 9.29 us
    all_gather x1 -> x0, blocking collectives: 34.8 us -> none  [per_device(): mix = lax.all_gather(mix_weight, 'lonp', axis=1, tiled=True)]
    ppermute x1 -> x16, starting transfers between devices: 0.25 us -> 27.2 us  [the longest x1 11.2 us: gather_fields(): one = lax.ppermute(x, 'lonp', [(0, 1), (1, 0), (2, 3), (3, 2)])]
    ppermute x1 -> x16, waiting for transfers between devices: 0.01 us -> 22.4 us  [the longest x7 8.93 us: per_device(): lax.ppermute(partial[dl * groups + dq], ('late', 'lonq'), [(l * groups +...]
    all_to_all x1 -> x0, blocking collectives: 17.9 us -> none  [per_device(): lax.all_to_all(partial, ('late', 'lonq'), split_axis=0, concat_axis=0, ti...]
    all_to_all x1, waiting for transfers between devices: 0.01 us -> 4.63 us  [per_device(): lax.all_to_all(packed, ('late', 'lonq'), split_axis=0, concat_axis=0, til...]
    pallas_call x1 -> x2, Pallas kernels: 6.21 us -> 9.53 us  [the longest x1 8.08 us: conv_mix(): pl.pallas_call(functools.partial(conv_mix_kernel, (bases, taps, slots, ha...]
    all_to_all x1, starting transfers between devices: 7.41 us -> 4.48 us  [per_device(): lax.all_to_all(packed, ('late', 'lonq'), split_axis=0, concat_axis=0, til...]
    transpose x1, local copies, waits for them, and re-layouts: 2.38 us -> 4.15 us  [per_device(): kernel.transpose(1, 0, 2, 5, 3, 4)]
  transfers between devices with their start and end apart: 2 -> 17, of which waited for: 0 -> 10; matrix products, arithmetic and copies ran while one was open for 9% -> 0% of each run, Pallas kernels for 0% -> 1%
where the time goes in v2:
time: 79.2 us; the launch traced here: 78.8 us
  starting transfers between devices  31.7 us (40%)
  waiting for transfers between devices  27 us (34%)
  Pallas kernels  10.6 us (13%)
  local copies, waits for them, and re-layouts  9.29 us (12%)
    ppermute x1, starting transfers between devices, gather_fields(): one = lax.ppermute(x, 'lonp', [(0, 1), (1, 0), (2, 3), (3, 2)])  11.2 us
    ppermute x7, waiting for transfers between devices, per_device(): lax.ppermute(partial[dl * groups + dq], ('late', 'lonq'), [(l * groups +...  8.93 us
    pallas_call x1, Pallas kernels, conv_mix(): pl.pallas_call(functools.partial(conv_mix_kernel, (bases, taps, slots, ha...  8.08 us
    ppermute x1, waiting for transfers between devices, gather_fields(): passed = lax.ppermute(two, 'lonp', [(1, 0), (2, 3)])  5.17 us
    all_to_all x1, waiting for transfers between devices, per_device(): lax.all_to_all(packed, ('late', 'lonq'), split_axis=0, concat_axis=0, til...  4.63 us
    ppermute x7, starting transfers between devices, per_device(): lax.ppermute(partial[dl * groups + dq], ('late', 'lonq'), [(l * groups +...  4.6 us
    all_to_all x1, starting transfers between devices, per_device(): lax.all_to_all(packed, ('late', 'lonq'), split_axis=0, concat_axis=0, til...  4.48 us
    ppermute x1, starting transfers between devices, gather_fields(): two = lax.ppermute(x, 'lonp', [(0, 2), (2, 0), (1, 3), (3, 1)])  4.34 us
  transfers between devices with their start and end apart: 17, of which 10 were waited for; matrix products, arithmetic and copies ran while one was open for 0% of the time, Pallas kernels for 1%

profile of v2, /device:TPU:0, one launch (start us, length us, event | category | flops | bytes accessed | tf_op | source)
XLA Modules:
  0.0 78.8 jit_solution(18241480096256762668)
XLA Ops:
  0.0 4.1 %copy.8 = bf16[4,5,3,64,3,64]{3,5,4,2,1,0:T(8,128)(2,1)} copy(bf16[4,5,3,64,3,64]{3,5,4,2,0,1:T(8,128)(2,1)} %bitcast.17) | data formatting | bytes 2949120 | tf_op jit(solution)/shard_map/transpose | solution.py:238
  4.2 3.3 %copy.11.refs_5_ = bf16[4,15,64,192]{3,2,1,0:T(8,128)(2,1)S(1)} copy(bf16[4,15,64,192]{2,3,1,0:T(8,128)(2,1)} %bitcast.16) | data formatting | bytes 2949120 | tf_op jit(solution)/shard_map/reshape | solution.py:238
  7.5 0.5 collective-permute-start.4
  8.0 0.0 copy-done
  8.0 2.7 %collective-permute-start.5 = (bf16[5,40,640]{2,1,0:T(8,128)(2,1)S(1)}, bf16[5,40,640]{2,1,0:T(8,128)(2,1)S(1)}, u32[]{:S(2)}, u32[]{:S(2)}) collective-permute-start(bf16[5,40,640]{2,1,0:T(8,128)(2,1)S(1)} %copy-done), channel_id=1, source_target_pairs={{0,4},{4,0},{8,12},{12,8},{16,24},{24,16},{20,28},{28,20},{1,5},{5... | collective-permute-start | bytes 768008 | tf_op jit(solution)/shard_map/ppermute | solution.py:215
  10.7 0.0 copy-done.1
  10.7 1.1 %pack.1 = bf16[2,4,24,640]{3,2,1,0:T(8,128)(2,1)} custom-call(bf16[2,4,24,640]{3,2,1,0:T(8,128)(2,1)S(1)} %bitcast.15), custom_call_target="tpu_custom_call" | custom-call | tf_op jit(solution)/shard_map/pack/pallas_call | solution.py:51
  11.8 4.5 %all-to-all-start = ((bf16[8,24,640]{2,1,0:T(8,128)(2,1)}), bf16[8,24,640]{2,1,0:T(8,128)(2,1)S(1)}, u32[]{:S(2)}, u32[]{:S(2)}) async-start(bf16[8,24,640]{2,1,0:T(8,128)(2,1)} %bitcast.7), calls=%async_computation | async-start | bytes 491520 | tf_op jit(solution)/shard_map/all_to_all | solution.py:235
  16.3 1.1 %collective-permute-done.5.refs_8_ = bf16[5,40,640]{2,1,0:T(8,128)(2,1)S(1)} collective-permute-done((bf16[5,40,640]{2,1,0:T(8,128)(2,1)S(1)}, bf16[5,40,640]{2,1,0:T(8,128)(2,1)S(1)}, u32[]{:S(2)}, u32[]{:S(2)}) %collective-permute-start.5) | collective-permute-done | bytes 256032 | tf_op jit(solution)/shard_map/ppermute | solution.py:215
  17.4 0.7 collective-permute-start.7
  18.1 4.6 %all-to-all-done = bf16[8,24,640]{2,1,0:T(8,128)(2,1)S(1)} async-done(((bf16[8,24,640]{2,1,0:T(8,128)(2,1)}), bf16[8,24,640]{2,1,0:T(8,128)(2,1)S(1)}, u32[]{:S(2)}, u32[]{:S(2)}) %all-to-all-start) | async-done | bytes 245792 | tf_op jit(solution)/shard_map/all_to_all | solution.py:235
  22.7 0.7 collective-permute-start.2
  23.4 4.3 %collective-permute-start.1 = (bf16[2,96,640]{2,1,0:T(8,128)(2,1)S(1)}, bf16[2,96,640]{2,1,0:T(8,128)(2,1)}, u32[]{:S(2)}, u32[]{:S(2)}) collective-permute-start(bf16[2,96,640]{2,1,0:T(8,128)(2,1)S(1)} %bitcast.12), channel_id=1, source_target_pairs={{0,8},{8,0},{4,12},{12,4},{1,9},{9,1},{5,13},{13,5},{2,10},{10,2},... | collective-permute-start | bytes 737288 | tf_op jit(solution)/shard_map/ppermute | solution.py:200
  27.7 0.0 collective-permute-start.6
  27.7 0.0 collective-permute-done.7.refs_10_
  27.7 1.3 %collective-permute-start.8 = (bf16[5,40,640]{2,1,0:T(8,128)(2,1)S(1)}, bf16[5,40,640]{2,1,0:T(8,128)(2,1)S(1)}, u32[]{:S(2)}, u32[]{:S(2)}) collective-permute-start(bf16[5,40,640]{2,1,0:T(8,128)(2,1)S(1)} %collective-permute-done.7.refs_10_), channel_id=1, source_target_pairs={{4,20},{8,24},{16,0},{28,12},{5,21},{9,25},{17,1},{29,13},{6,22},{... | collective-permute-start | bytes 768008 | tf_op jit(solution)/shard_map/ppermute | solution.py:219
  29.0 0.0 collective-permute-done.2.refs_3_
  29.0 0.0 copy-start.2
  29.0 0.7 copy-done.2
  29.7 11.2 %collective-permute-start = (bf16[2,96,640]{2,1,0:T(8,128)(2,1)S(1)}, bf16[2,96,640]{2,1,0:T(8,128)(2,1)}, u32[]{:S(2)}, u32[]{:S(2)}) collective-permute-start(bf16[2,96,640]{2,1,0:T(8,128)(2,1)S(1)} %bitcast.13), channel_id=1, source_target_pairs={{0,4},{4,0},{8,12},{12,8},{1,5},{5,1},{9,13},{13,9},{2,6},{6,2},{1... | collective-permute-start | bytes 737288 | tf_op jit(solution)/shard_map/ppermute | solution.py:201
  40.9 3.4 %collective-permute-done.1.refs_2_ = bf16[2,96,640]{2,1,0:T(8,128)(2,1)} collective-permute-done((bf16[2,96,640]{2,1,0:T(8,128)(2,1)S(1)}, bf16[2,96,640]{2,1,0:T(8,128)(2,1)}, u32[]{:S(2)}, u32[]{:S(2)}) %collective-permute-start.1) | collective-permute-done | bytes 245792 | tf_op jit(solution)/shard_map/ppermute | solution.py:200
  44.3 1.3 %collective-permute-start.3 = (bf16[2,96,640]{2,1,0:T(8,128)(2,1)}, bf16[2,96,640]{2,1,0:T(8,128)(2,1)}, u32[]{:S(2)}, u32[]{:S(2)}) collective-permute-start(bf16[2,96,640]{2,1,0:T(8,128)(2,1)} %collective-permute-done.1.refs_2_), channel_id=1, source_target_pairs={{4,0},{8,12},{5,1},{9,13},{6,2},{10,14},{7,3},{11,15},{20,16},{24,... | collective-permute-start | bytes 737288 | tf_op jit(solution)/shard_map/ppermute | solution.py:203
  45.6 0.0 copy-done.5
  45.6 0.1 copy.10.shift_ref
  45.7 0.1 stack.28.place_ref
  45.8 3.8 %collective-permute-done.refs_1_ = bf16[2,96,640]{2,1,0:T(8,128)(2,1)} collective-permute-done((bf16[2,96,640]{2,1,0:T(8,128)(2,1)S(1)}, bf16[2,96,640]{2,1,0:T(8,128)(2,1)}, u32[]{:S(2)}, u32[]{:S(2)}) %collective-permute-start) | collective-permute-done | bytes 245792 | tf_op jit(solution)/shard_map/ppermute | solution.py:201
  49.6 0.0 collective-permute-done.6.refs_9_
  49.6 5.2 %collective-permute-done.3.refs_4_ = bf16[2,96,640]{2,1,0:T(8,128)(2,1)} collective-permute-done((bf16[2,96,640]{2,1,0:T(8,128)(2,1)}, bf16[2,96,640]{2,1,0:T(8,128)(2,1)}, u32[]{:S(2)}, u32[]{:S(2)}) %collective-permute-start.3) | collective-permute-done | bytes 245792 | tf_op jit(solution)/shard_map/ppermute | solution.py:203
  54.8 0.0 collective-permute-done.8.refs_11_
  54.8 0.0 collective-permute-done.4.refs_6_
  54.8 0.0 copy-start.3
  54.8 0.9 %copy-done.3 = bf16[2,96,640]{2,1,0:T(8,128)(2,1)S(1)} copy-done((bf16[2,96,640]{2,1,0:T(8,128)(2,1)S(1)}, bf16[2,96,640]{2,1,0:T(8,128)(2,1)}, u32[]{:S(2)}) %copy-start.3) | copy-done | bytes 245784
  55.7 8.1 %conv_mix.1 = (bf16[4,24,640]{2,1,0:T(8,128)(2,1)S(1)}, bf16[4,24,640]{2,1,0:T(8,128)(2,1)S(1)}, bf16[4,24,640]{2,1,0:T(8,128)(2,1)S(1)}, bf16[4,24,640]{2,1,0:T...) custom-call(s32[5,8]{1,0:T(8,128)S(1)} %copy-done.4, ...), custom_call_target="tpu_custom_call" | custom-call | tf_op jit(solution)/shard_map/conv_mix/pallas_call | solution.py:160
  63.8 0.9 %collective-permute-start.9 = (bf16[4,24,640]{2,1,0:T(8,128)(2,1)S(1)}, bf16[4,24,640]{2,1,0:T(8,128)(2,1)S(1)}, u32[]{:S(2)}, u32[]{:S(2)}) collective-permute-start(bf16[4,24,640]{2,1,0:T(8,128)(2,1)S(1)} %get-tuple-element.14), channel_id=1, source_target_pairs={{0,1},{1,0},{2,3},{3,2},{16,17},{17,16},{18,19},{19,18},{4,5},{5,4... | collective-permute-start | bytes 368648 | tf_op jit(solution)/shard_map/ppermute | solution.py:259
  64.7 0.9 %collective-permute-start.10 = (bf16[4,24,640]{2,1,0:T(8,128)(2,1)S(1)}, bf16[4,24,640]{2,1,0:T(8,128)(2,1)S(1)}, u32[]{:S(2)}, u32[]{:S(2)}) collective-permute-start(bf16[4,24,640]{2,1,0:T(8,128)(2,1)S(1)} %get-tuple-element.15), channel_id=1, source_target_pairs={{0,2},{1,3},{2,0},{3,1},{16,18},{17,19},{18,16},{19,17},{4,6},{5,7... | collective-permute-start | bytes 368648 | tf_op jit(solution)/shard_map/ppermute | solution.py:259
  65.6 1.8 %collective-permute-start.11 = (bf16[4,24,640]{2,1,0:T(8,128)(2,1)S(1)}, bf16[4,24,640]{2,1,0:T(8,128)(2,1)S(1)}, u32[]{:S(2)}, u32[]{:S(2)}) collective-permute-start(bf16[4,24,640]{2,1,0:T(8,128)(2,1)S(1)} %get-tuple-element.16), channel_id=1, source_target_pairs={{0,3},{1,2},{2,1},{3,0},{16,19},{17,18},{18,17},{19,16},{4,7},{5,6... | collective-permute-start | bytes 368648 | tf_op jit(solution)/shard_map/ppermute | solution.py:259
  67.4 0.0 collective-permute-start.12
  67.4 0.9 %collective-permute-start.13 = (bf16[4,24,640]{2,1,0:T(8,128)(2,1)S(1)}, bf16[4,24,640]{2,1,0:T(8,128)(2,1)S(1)}, u32[]{:S(2)}, u32[]{:S(2)}) collective-permute-start(bf16[4,24,640]{2,1,0:T(8,128)(2,1)S(1)} %get-tuple-element.18), channel_id=1, source_target_pairs={{0,17},{1,16},{2,19},{3,18},{16,1},{17,0},{18,3},{19,2},{4,21},{5,... | collective-permute-start | bytes 368648 | tf_op jit(solution)/shard_map/ppermute | solution.py:259
  68.3 1.6 %collective-permute-done.9.refs_1_ = bf16[4,24,640]{2,1,0:T(8,128)(2,1)S(1)} collective-permute-done((bf16[4,24,640]{2,1,0:T(8,128)(2,1)S(1)}, bf16[4,24,640]{2,1,0:T(8,128)(2,1)S(1)}, u32[]{:S(2)}, u32[]{:S(2)}) %collective-permute-start.9) | collective-permute-done | bytes 122912 | tf_op jit(solution)/shard_map/ppermute | solution.py:259
  69.9 0.0 collective-permute-start.14
  69.9 1.5 %collective-permute-done.10.refs_2_ = bf16[4,24,640]{2,1,0:T(8,128)(2,1)S(1)} collective-permute-done((bf16[4,24,640]{2,1,0:T(8,128)(2,1)S(1)}, bf16[4,24,640]{2,1,0:T(8,128)(2,1)S(1)}, u32[]{:S(2)}, u32[]{:S(2)}) %collective-permute-start.10) | collective-permute-done | bytes 122912 | tf_op jit(solution)/shard_map/ppermute | solution.py:259
  71.4 0.1 collective-permute-start.15
  71.5 1.1 %collective-permute-done.11.refs_3_ = bf16[4,24,640]{2,1,0:T(8,128)(2,1)S(1)} collective-permute-done((bf16[4,24,640]{2,1,0:T(8,128)(2,1)S(1)}, bf16[4,24,640]{2,1,0:T(8,128)(2,1)S(1)}, u32[]{:S(2)}, u32[]{:S(2)}) %collective-permute-start.11) | collective-permute-done | bytes 122912 | tf_op jit(solution)/shard_map/ppermute | solution.py:259
  72.6 0.0 collective-permute-done.12.refs_4_
  72.6 0.4 collective-permute-done.13.refs_5_
  73.0 4.3 %collective-permute-done.14.refs_6_ = bf16[4,24,640]{2,1,0:T(8,128)(2,1)S(1)} collective-permute-done((bf16[4,24,640]{2,1,0:T(8,128)(2,1)S(1)}, bf16[4,24,640]{2,1,0:T(8,128)(2,1)S(1)}, u32[]{:S(2)}, u32[]{:S(2)}) %collective-permute-start.14) | collective-permute-done | bytes 122912 | tf_op jit(solution)/shard_map/ppermute | solution.py:259
  77.3 0.0 collective-permute-done.15.refs_7_
  77.3 1.4 %finish.1 = bf16[2,4,24,640]{3,2,1,0:T(8,128)(2,1)} custom-call(s32[7]{0:T(128)S(1)} %stack.28.place_ref, bf16[4,24,640]{2,1,0:T(8,128)(2,1)S(1)} %get-tuple-element.13.refs_0_, bf16[4,24,640]{2,1,0:T(8,128)(2,1)S(1)} %collective-permute-done.9.refs_1_, bf16[4,24,640]{2,1,0:T(8,128)(2,1)S(1)} %collective-permute-done.10.refs_2_, ...), custom_call_target="tpu_custom_call" | custom-call | tf_op jit(solution)/shard_map/finish/pallas_call | solution.py:188
  (6 shorter events, 0.0 us)
Async XLA Ops:
  4.1 3.9 %copy-start = (bf16[5,40,640]{2,1,0:T(8,128)(2,1)S(1)}, bf16[5,40,640]{2,1,0:T(8,128)(2,1)}, u32[]{:S(2)}) copy-start(bf16[5,40,640]{2,1,0:T(8,128)(2,1)} %refs_7_.1) | copy-start | bytes 768004
  4.2 6.5 %copy-start.1 = (bf16[2,4,640,24]{2,3,1,0:T(8,128)(2,1)S(1)}, bf16[2,4,640,24]{2,3,1,0:T(8,128)(2,1)}, u32[]{:S(2)}) copy-start(bf16[2,4,640,24]{2,3,1,0:T(8,128)(2,1)} %param.5) | copy-start | bytes 737284
  4.2 41.5 %copy-start.5 = (s32[8,3]{0,1:T(4,128)S(1)}, s32[8,3]{0,1:T(4,128)}, u32[]{:S(2)}) copy-start(s32[8,3]{0,1:T(4,128)} %param.8) | copy-start | bytes 292
  4.2 50.6 %copy-start.4 = (s32[5,8]{1,0:T(8,128)S(1)}, s32[5,8]{1,0:T(8,128)}, u32[]{:S(2)}) copy-start(s32[5,8]{1,0:T(8,128)} %low_ref) | copy-start | bytes 484
  7.5 47.3 %collective-permute-start.4 = (bf16[4,15,64,192]{3,2,1,0:T(8,128)(2,1)S(1)}, bf16[4,15,64,192]{3,2,1,0:T(8,128)(2,1)}, u32[]{:S(2)}, u32[]{:S(2)}) collective-permute-start(bf16[4,15,64,192]{3,2,1,0:T(8,128)(2,1)S(1)} %copy.11.refs_5_), channel_id=1, source_target_pairs={{0,16},{16,0},{1,17},{17,1},{2,18},{18,2},{3,19},{19,3},{4,20},{20... | collective-permute-start | bytes 4423688 | tf_op jit(solution)/shard_map/ppermute | solution.py:33
  8.0 9.3 %collective-permute-start.5 = (bf16[5,40,640]{2,1,0:T(8,128)(2,1)S(1)}, bf16[5,40,640]{2,1,0:T(8,128)(2,1)S(1)}, u32[]{:S(2)}, u32[]{:S(2)}) collective-permute-start(bf16[5,40,640]{2,1,0:T(8,128)(2,1)S(1)} %copy-done), channel_id=1, source_target_pairs={{0,4},{4,0},{8,12},{12,8},{16,24},{24,16},{20,28},{28,20},{1,5},{5... | collective-permute-start | bytes 768008 | tf_op jit(solution)/shard_map/ppermute | solution.py:215
  11.8 10.9 %all-to-all-start = ((bf16[8,24,640]{2,1,0:T(8,128)(2,1)}), bf16[8,24,640]{2,1,0:T(8,128)(2,1)S(1)}, u32[]{:S(2)}, u32[]{:S(2)}) async-start(bf16[8,24,640]{2,1,0:T(8,128)(2,1)} %bitcast.7), calls=%async_computation | async-start | bytes 491520 | tf_op jit(solution)/shard_map/all_to_all | solution.py:235
  17.4 10.3 %collective-permute-start.7 = (bf16[5,40,640]{2,1,0:T(8,128)(2,1)S(1)}, bf16[5,40,640]{2,1,0:T(8,128)(2,1)S(1)}, u32[]{:S(2)}, u32[]{:S(2)}) collective-permute-start(bf16[5,40,640]{2,1,0:T(8,128)(2,1)S(1)} %broadcast_select_fusion), channel_id=1, source_target_pairs={{4,8},{8,4},{20,16},{24,28},{5,9},{9,5},{21,17},{25,29},{6,10},{10... | collective-permute-start | bytes 768008 | tf_op jit(solution)/shard_map/ppermute | solution.py:218
  22.7 6.3 %collective-permute-start.2 = (bf16[2,96,640]{2,1,0:T(8,128)(2,1)S(1)}, bf16[2,96,640]{2,1,0:T(8,128)(2,1)S(1)}, u32[]{:S(2)}, u32[]{:S(2)}) collective-permute-start(bf16[2,96,640]{2,1,0:T(8,128)(2,1)S(1)} %bitcast.11), channel_id=1, source_target_pairs={{4,8},{8,4},{5,9},{9,5},{6,10},{10,6},{7,11},{11,7},{20,24},{24,20... | collective-permute-start | bytes 737288 | tf_op jit(solution)/shard_map/ppermute | solution.py:202
  23.4 21.0 %collective-permute-start.1 = (bf16[2,96,640]{2,1,0:T(8,128)(2,1)S(1)}, bf16[2,96,640]{2,1,0:T(8,128)(2,1)}, u32[]{:S(2)}, u32[]{:S(2)}) collective-permute-start(bf16[2,96,640]{2,1,0:T(8,128)(2,1)S(1)} %bitcast.12), channel_id=1, source_target_pairs={{0,8},{8,0},{4,12},{12,4},{1,9},{9,1},{5,13},{13,5},{2,10},{10,2},... | collective-permute-start | bytes 737288 | tf_op jit(solution)/shard_map/ppermute | solution.py:200
  27.7 21.9 %collective-permute-start.6 = (bf16[5,40,640]{2,1,0:T(8,128)(2,1)S(1)}, bf16[5,40,640]{2,1,0:T(8,128)(2,1)S(1)}, u32[]{:S(2)}, u32[]{:S(2)}) collective-permute-start(bf16[5,40,640]{2,1,0:T(8,128)(2,1)S(1)} %collective-permute-done.5.refs_8_), channel_id=1, source_target_pairs={{0,16},{16,0},{1,17},{17,1},{2,18},{18,2},{3,19},{19,3},{4,20},{20... | collective-permute-start | bytes 768008 | tf_op jit(solution)/shard_map/ppermute | solution.py:33
  27.7 27.1 %collective-permute-start.8 = (bf16[5,40,640]{2,1,0:T(8,128)(2,1)S(1)}, bf16[5,40,640]{2,1,0:T(8,128)(2,1)S(1)}, u32[]{:S(2)}, u32[]{:S(2)}) collective-permute-start(bf16[5,40,640]{2,1,0:T(8,128)(2,1)S(1)} %collective-permute-done.7.refs_10_), channel_id=1, source_target_pairs={{4,20},{8,24},{16,0},{28,12},{5,21},{9,25},{17,1},{29,13},{6,22},{... | collective-permute-start | bytes 768008 | tf_op jit(solution)/shard_map/ppermute | solution.py:219
  29.0 0.7 copy-start.2
  29.7 19.9 %collective-permute-start = (bf16[2,96,640]{2,1,0:T(8,128)(2,1)S(1)}, bf16[2,96,640]{2,1,0:T(8,128)(2,1)}, u32[]{:S(2)}, u32[]{:S(2)}) collective-permute-start(bf16[2,96,640]{2,1,0:T(8,128)(2,1)S(1)} %bitcast.13), channel_id=1, source_target_pairs={{0,4},{4,0},{8,12},{12,8},{1,5},{5,1},{9,13},{13,9},{2,6},{6,2},{1... | collective-permute-start | bytes 737288 | tf_op jit(solution)/shard_map/ppermute | solution.py:201
  44.3 10.4 %collective-permute-start.3 = (bf16[2,96,640]{2,1,0:T(8,128)(2,1)}, bf16[2,96,640]{2,1,0:T(8,128)(2,1)}, u32[]{:S(2)}, u32[]{:S(2)}) collective-permute-start(bf16[2,96,640]{2,1,0:T(8,128)(2,1)} %collective-permute-done.1.refs_2_), channel_id=1, source_target_pairs={{4,0},{8,12},{5,1},{9,13},{6,2},{10,14},{7,3},{11,15},{20,16},{24,... | collective-permute-start | bytes 737288 | tf_op jit(solution)/shard_map/ppermute | solution.py:203
  54.8 0.9 %copy-start.3 = (bf16[2,96,640]{2,1,0:T(8,128)(2,1)S(1)}, bf16[2,96,640]{2,1,0:T(8,128)(2,1)}, u32[]{:S(2)}) copy-start(bf16[2,96,640]{2,1,0:T(8,128)(2,1)} %copy-done.2) | copy-start | bytes 737284
  63.8 6.1 %collective-permute-start.9 = (bf16[4,24,640]{2,1,0:T(8,128)(2,1)S(1)}, bf16[4,24,640]{2,1,0:T(8,128)(2,1)S(1)}, u32[]{:S(2)}, u32[]{:S(2)}) collective-permute-start(bf16[4,24,640]{2,1,0:T(8,128)(2,1)S(1)} %get-tuple-element.14), channel_id=1, source_target_pairs={{0,1},{1,0},{2,3},{3,2},{16,17},{17,16},{18,19},{19,18},{4,5},{5,4... | collective-permute-start | bytes 368648 | tf_op jit(solution)/shard_map/ppermute | solution.py:259
  64.7 6.7 %collective-permute-start.10 = (bf16[4,24,640]{2,1,0:T(8,128)(2,1)S(1)}, bf16[4,24,640]{2,1,0:T(8,128)(2,1)S(1)}, u32[]{:S(2)}, u32[]{:S(2)}) collective-permute-start(bf16[4,24,640]{2,1,0:T(8,128)(2,1)S(1)} %get-tuple-element.15), channel_id=1, source_target_pairs={{0,2},{1,3},{2,0},{3,1},{16,18},{17,19},{18,16},{19,17},{4,6},{5,7... | collective-permute-start | bytes 368648 | tf_op jit(solution)/shard_map/ppermute | solution.py:259
  65.6 7.0 %collective-permute-start.11 = (bf16[4,24,640]{2,1,0:T(8,128)(2,1)S(1)}, bf16[4,24,640]{2,1,0:T(8,128)(2,1)S(1)}, u32[]{:S(2)}, u32[]{:S(2)}) collective-permute-start(bf16[4,24,640]{2,1,0:T(8,128)(2,1)S(1)} %get-tuple-element.16), channel_id=1, source_target_pairs={{0,3},{1,2},{2,1},{3,0},{16,19},{17,18},{18,17},{19,16},{4,7},{5,6... | collective-permute-start | bytes 368648 | tf_op jit(solution)/shard_map/ppermute | solution.py:259
  67.4 5.3 %collective-permute-start.12 = (bf16[4,24,640]{2,1,0:T(8,128)(2,1)S(1)}, bf16[4,24,640]{2,1,0:T(8,128)(2,1)S(1)}, u32[]{:S(2)}, u32[]{:S(2)}) collective-permute-start(bf16[4,24,640]{2,1,0:T(8,128)(2,1)S(1)} %get-tuple-element.17), channel_id=1, source_target_pairs={{0,16},{1,17},{2,18},{3,19},{16,0},{17,1},{18,2},{19,3},{4,20},{5,... | collective-permute-start | bytes 368648 | tf_op jit(solution)/shard_map/ppermute | solution.py:259
  67.4 5.7 %collective-permute-start.13 = (bf16[4,24,640]{2,1,0:T(8,128)(2,1)S(1)}, bf16[4,24,640]{2,1,0:T(8,128)(2,1)S(1)}, u32[]{:S(2)}, u32[]{:S(2)}) collective-permute-start(bf16[4,24,640]{2,1,0:T(8,128)(2,1)S(1)} %get-tuple-element.18), channel_id=1, source_target_pairs={{0,17},{1,16},{2,19},{3,18},{16,1},{17,0},{18,3},{19,2},{4,21},{5,... | collective-permute-start | bytes 368648 | tf_op jit(solution)/shard_map/ppermute | solution.py:259
  69.9 7.5 %collective-permute-start.14 = (bf16[4,24,640]{2,1,0:T(8,128)(2,1)S(1)}, bf16[4,24,640]{2,1,0:T(8,128)(2,1)S(1)}, u32[]{:S(2)}, u32[]{:S(2)}) collective-permute-start(bf16[4,24,640]{2,1,0:T(8,128)(2,1)S(1)} %get-tuple-element.19), channel_id=1, source_target_pairs={{0,18},{1,19},{2,16},{3,17},{16,2},{17,3},{18,0},{19,1},{4,22},{5,... | collective-permute-start | bytes 368648 | tf_op jit(solution)/shard_map/ppermute | solution.py:259
  71.4 5.9 %collective-permute-start.15 = (bf16[4,24,640]{2,1,0:T(8,128)(2,1)S(1)}, bf16[4,24,640]{2,1,0:T(8,128)(2,1)S(1)}, u32[]{:S(2)}, u32[]{:S(2)}) collective-permute-start(bf16[4,24,640]{2,1,0:T(8,128)(2,1)S(1)} %get-tuple-element.20), channel_id=1, source_target_pairs={{0,19},{1,18},{2,17},{3,16},{16,3},{17,2},{18,1},{19,0},{4,23},{5,... | collective-permute-start | bytes 368648 | tf_op jit(solution)/shard_map/ppermute | solution.py:259

commit v3 on v2

--- a/solution.py
+++ b/solution.py
@@ -12,7 +12,7 @@
 HALO = 2
 LANES = 128
 VMEM = pltpu.VMEM
-LIMIT = 48 * 1024 * 1024
+LIMIT = 24 * 1024 * 1024
 SMEM_SPEC = pl.BlockSpec(memory_space=pltpu.SMEM)
 VMEM_SPEC = pl.BlockSpec(memory_space=VMEM)
 
@@ -195,31 +195,49 @@
     )(place, *parts)
 
 
-def gather_fields(x, owners):
-    if owners == 4:
-        two = lax.ppermute(x, "lonp", [(0, 2), (2, 0), (1, 3), (3, 1)])
-        one = lax.ppermute(x, "lonp", [(0, 1), (1, 0), (2, 3), (3, 2)])
-        middle = lax.ppermute(x, "lonp", [(1, 2), (2, 1)])
-        passed = lax.ppermute(two, "lonp", [(1, 0), (2, 3)])
-        return [[x], [one], [two], [middle, passed]]
-    return [[x]] + [[trade(x, "lonp", d, owners)] for d in range(1, owners)]
-
-
-def gather_mix(x, late, owners):
+def chain(*cores):
+    return [(4 * c + a, 4 * c + b) for c, pairs in enumerate(cores) for a, b in pairs]
+
+
+NEAR = [(0, 1), (1, 0), (2, 3), (3, 2)]
+FAR = [(0, 2), (2, 0), (1, 3), (3, 1)]
+MIDDLE = [(1, 2), (2, 1)]
+ENDS = [(1, 0), (2, 3)]
+
+
+def both_kernels(kernel, late):
+    bases, rows, taps, slots, block, _ = kernel.shape
+    own = kernel.transpose(1, 0, 2, 5, 3, 4).reshape(rows, bases * taps, block, slots * block)
+    return [own] + [trade(own, "late", s, late) for s in range(1, late)]
+
+
+def gather(packed, kernel, mix, late, groups, owners):
     core, own = lax.axis_index("late"), lax.axis_index("lonp")
-    if owners == 4 and late == 2:
-        def both(pairs_first, pairs_second):
-            return [(a, b) for a, b in pairs_first] + [(4 + a, 4 + b) for a, b in pairs_second]
-
-        near, far = [(0, 1), (1, 0), (2, 3), (3, 2)], [(0, 2), (2, 0), (1, 3), (3, 1)]
-        fetched = lax.ppermute(x, ("late", "lonp"), both(near, far))
-        other = trade(fetched, "late", 1, late)
-        source = jnp.where(core == 0, x, fetched)
-        third = lax.ppermute(source, ("late", "lonp"), both([(1, 2), (2, 1)], [(1, 0), (2, 3)]))
-        copied = lax.ppermute(third, ("late", "lonp"), [(1, 5), (2, 6), (4, 0), (7, 3)])
-        return [[x], [fetched], [other], [third, copied]], [own, own ^ (1 + core), own ^ (2 - core), own ^ 3]
-    slots = [[x]] + [[trade(x, "lonp", d, owners)] for d in range(1, owners)]
-    return slots, [partner(own, d, owners) for d in range(owners)]
+    chained = owners == 4 and late == 2
+    if chained:
+        mix, packed = lax.optimization_barrier((mix, packed))
+        fetched = lax.ppermute(mix, ("late", "lonp"), chain(NEAR, FAR))
+    cells = packed.shape[1]
+    x = lax.all_to_all(packed, ("late", "lonq"), split_axis=0, concat_axis=0, tiled=True)
+    x = x.reshape(late, groups * cells, -1)
+    if not chained:
+        weights = both_kernels(kernel, late)
+        fields = [[x]] + [[trade(x, "lonp", d, owners)] for d in range(1, owners)]
+        mixes = [[mix]] + [[trade(mix, "lonp", d, owners)] for d in range(1, owners)]
+        return fields, weights, mixes, [partner(own, d, owners) for d in range(owners)]
+    two = lax.ppermute(x, "lonp", FAR)
+    one = lax.ppermute(x, "lonp", NEAR)
+    other = trade(fetched, "late", 1, late)
+    source = jnp.where(core == 0, mix, fetched)
+    third = lax.ppermute(source, ("late", "lonp"), chain(MIDDLE, ENDS))
+    copied = lax.ppermute(third, ("late", "lonp"), [(1, 5), (2, 6), (4, 0), (7, 3)])
+    kernel, third = lax.optimization_barrier((kernel, third))
+    weights = both_kernels(kernel, late)
+    late_x, two, other, third = lax.optimization_barrier((x, two, other, third))
+    middle = lax.ppermute(late_x, "lonp", MIDDLE)
+    passed = lax.ppermute(two, "lonp", ENDS)
+    origins = [own, own ^ (1 + core), own ^ (2 - core), own ^ 3]
+    return [[x], [one], [two], [middle, passed]], weights, [[mix], [fetched], [other], [third, copied]], origins
 
 
 def per_device(sizes, fields, kernel, band_low, block_shift, mix_weight):
@@ -229,14 +247,9 @@
     all_rows = late * rows
     halo = HALO if halves > 1 else 0
 
-    mix, origins = gather_mix(mix_weight, late, owners)
     packed = pack(fields.transpose(0, 1, 3, 2), groups, owners)
     packed = packed.reshape((late * groups,) + packed.shape[2:])
-    spread = lax.all_to_all(packed, ("late", "lonq"), split_axis=0, concat_axis=0, tiled=True)
-    gathered = gather_fields(spread.reshape(late, groups * cells, -1), owners)
-
-    own = kernel.transpose(1, 0, 2, 5, 3, 4).reshape(rows, bases * taps, block, slots * block)
-    weights = [own] + [trade(own, "late", s, late) for s in range(1, late)]
+    gathered, weights, mix, origins = gather(packed, kernel, mix_weight, late, groups, owners)
 
     start = lax.axis_index("lath") * all_rows
     low = lax.dynamic_slice_in_dim(band_low, start, all_rows, 1)

time: 79.2 us -> 87 us (1.098)
  waiting for transfers between devices: 27 us -> 38.6 us
  starting transfers between devices: 31.7 us -> 27.7 us
  other arithmetic: 0.03 us -> 0.98 us
    ppermute x7, waiting for transfers between devices: 13.5 us -> 24.8 us  [the longest x1 9.75 us: gather(): two = lax.ppermute(x, 'lonp', FAR)]
    ppermute x7, starting transfers between devices: 22.1 us -> 12.5 us  [the longest x1 4.22 us: gather(): two = lax.ppermute(x, 'lonp', FAR)]
    ppermute x2, starting transfers between devices: 0.52 us -> 6.37 us  [trade(): lax.ppermute(x, axis, [(i, partner(i, distance, size)) for i in range(siz...]
    all_to_all x1, waiting for transfers between devices: 4.63 us -> 5.92 us  [gather(): lax.all_to_all(packed, ('late', 'lonq'), split_axis=0, concat_axis=0, til...]
    ppermute x7, waiting for transfers between devices: 8.93 us -> 7.85 us  [per_device(): lax.ppermute(partial[dl * groups + dq], ('late', 'lonq'), [(l * groups +...]
    select_n x1, other arithmetic: 0.03 us -> 0.98 us  [gather(): source = jnp.where(core == 0, mix, fetched)]
  transfers between devices with their start and end apart: 17 -> 17, of which waited for: 10 -> 8; matrix products, arithmetic and copies ran while one was open for 0% -> 0% of each run, Pallas kernels for 1% -> 0%
where the time goes in v3:
time: 87 us; the launch traced here: 86.6 us
  waiting for transfers between devices  38.6 us (44%)
  starting transfers between devices  27.7 us (32%)
  Pallas kernels  10.6 us (12%)
  local copies, waits for them, and re-layouts  8.6 us (10%)
  other arithmetic  0.98 us (1%)
    ppermute x1, waiting for transfers between devices, gather(): two = lax.ppermute(x, 'lonp', FAR)  9.75 us
    ppermute x1, waiting for transfers between devices, gather(): passed = lax.ppermute(two, 'lonp', ENDS)  8.15 us
    pallas_call x1, Pallas kernels, conv_mix(): pl.pallas_call(functools.partial(conv_mix_kernel, (bases, taps, slots, ha...  8.11 us
    ppermute x7, waiting for transfers between devices, per_device(): lax.ppermute(partial[dl * groups + dq], ('late', 'lonq'), [(l * groups +...  7.85 us
    ppermute x1, waiting for transfers between devices, gather(): fetched = lax.ppermute(mix, ('late', 'lonp'), chain(NEAR, FAR))  6.87 us
    ppermute x2, starting transfers between devices, trade(): lax.ppermute(x, axis, [(i, partner(i, distance, size)) for i in range(siz...  6.37 us
    all_to_all x1, waiting for transfers between devices, gather(): lax.all_to_all(packed, ('late', 'lonq'), split_axis=0, concat_axis=0, til...  5.92 us
    ppermute x7, starting transfers between devices, per_device(): lax.ppermute(partial[dl * groups + dq], ('late', 'lonq'), [(l * groups +...  5.04 us
  transfers between devices with their start and end apart: 17, of which 8 were waited for; matrix products, arithmetic and copies ran while one was open for 0% of the time, Pallas kernels for 0%

profile of v3, /device:TPU:0, one launch (start us, length us, event | category | flops | bytes accessed | tf_op | source)
XLA Modules:
  0.0 86.6 jit_solution(15243396791059554786)
XLA Ops:
  0.0 0.0 copy-start.1
  0.0 0.9 %copy-done.1 = bf16[2,4,640,24]{2,3,1,0:T(8,128)(2,1)S(1)} copy-done((bf16[2,4,640,24]{2,3,1,0:T(8,128)(2,1)S(1)}, bf16[2,4,640,24]{2,3,1,0:T(8,128)(2,1)}, u32[]{:S(2)}) %copy-start.1) | copy-done | bytes 245784
  0.9 1.1 %pack.1 = bf16[2,4,24,640]{3,2,1,0:T(8,128)(2,1)} custom-call(bf16[2,4,24,640]{3,2,1,0:T(8,128)(2,1)S(1)} %bitcast.15), custom_call_target="tpu_custom_call" | custom-call | tf_op jit(solution)/shard_map/pack/pallas_call | solution.py:51
  2.0 3.0 %collective-permute-start.2 = (bf16[5,40,640]{2,1,0:T(8,128)(2,1)}, bf16[5,40,640]{2,1,0:T(8,128)(2,1)S(1)}, u32[]{:S(2)}, u32[]{:S(2)}) collective-permute-start(bf16[5,40,640]{2,1,0:T(8,128)(2,1)} %refs_7_), channel_id=1, source_target_pairs={{0,4},{4,0},{8,12},{12,8},{16,24},{24,16},{20,28},{28,20},{1,5},{5... | collective-permute-start | bytes 768008 | tf_op jit(solution)/shard_map/ppermute | solution.py:219
  5.1 6.9 %collective-permute-done.2.refs_8_ = bf16[5,40,640]{2,1,0:T(8,128)(2,1)S(1)} collective-permute-done((bf16[5,40,640]{2,1,0:T(8,128)(2,1)}, bf16[5,40,640]{2,1,0:T(8,128)(2,1)S(1)}, u32[]{:S(2)}, u32[]{:S(2)}) %collective-permute-start.2) | collective-permute-done | bytes 256032 | tf_op jit(solution)/shard_map/ppermute | solution.py:219
  11.9 1.0 %broadcast_select_fusion = bf16[5,40,640]{2,1,0:T(8,128)(2,1)S(1)} fusion(bf16[5,40,640]{2,1,0:T(8,128)(2,1)} %refs_7_, bf16[5,40,640]{2,1,0:T(8,128)(2,1)S(1)} %collective-permute-done.2.refs_8_, pred[]{:T(512)S(6)} %eq.3), kind=kLoop, calls=%fused_computation | loop fusion | flops 128000 | bytes 768001 | tf_op jit(solution)/shard_map/jit(_where)/select_n | solution.py:231
  12.9 0.7 collective-permute-start.4
  13.6 0.0 collective-permute-done.4.refs_10_
  13.6 4.2 %copy.8 = bf16[4,5,3,64,3,64]{3,5,4,2,1,0:T(8,128)(2,1)} copy(bf16[4,5,3,64,3,64]{3,5,4,2,0,1:T(8,128)(2,1)} %bitcast.17) | data formatting | bytes 2949120 | tf_op jit(solution)/shard_map/transpose | solution.py:210
  17.8 0.0 copy-start.3
  17.8 3.3 %copy.11.refs_5_ = bf16[4,15,64,192]{3,2,1,0:T(8,128)(2,1)S(1)} copy(bf16[4,15,64,192]{2,3,1,0:T(8,128)(2,1)} %bitcast.16) | data formatting | bytes 2949120 | tf_op jit(solution)/shard_map/reshape | solution.py:210
  21.1 5.9 %collective-permute-start.7 = (bf16[4,15,64,192]{3,2,1,0:T(8,128)(2,1)S(1)}, bf16[4,15,64,192]{3,2,1,0:T(8,128)(2,1)}, u32[]{:S(2)}, u32[]{:S(2)}) collective-permute-start(bf16[4,15,64,192]{3,2,1,0:T(8,128)(2,1)S(1)} %copy.11.refs_5_), channel_id=1, source_target_pairs={{0,16},{16,0},{1,17},{17,1},{2,18},{18,2},{3,19},{19,3},{4,20},{20... | collective-permute-start | bytes 4423688 | tf_op jit(solution)/shard_map/ppermute | solution.py:33
  27.0 3.7 %all-to-all-start = ((bf16[8,24,640]{2,1,0:T(8,128)(2,1)}), bf16[8,24,640]{2,1,0:T(8,128)(2,1)S(1)}, u32[]{:S(2)}, u32[]{:S(2)}) async-start(bf16[8,24,640]{2,1,0:T(8,128)(2,1)} %bitcast.7), calls=%async_computation | async-start | bytes 491520 | tf_op jit(solution)/shard_map/all_to_all | solution.py:221
  30.7 0.5 collective-permute-start.3
  31.2 5.9 %all-to-all-done = bf16[8,24,640]{2,1,0:T(8,128)(2,1)S(1)} async-done(((bf16[8,24,640]{2,1,0:T(8,128)(2,1)}), bf16[8,24,640]{2,1,0:T(8,128)(2,1)S(1)}, u32[]{:S(2)}, u32[]{:S(2)}) %all-to-all-start) | async-done | bytes 245792 | tf_op jit(solution)/shard_map/all_to_all | solution.py:221
  37.1 4.2 %collective-permute-start.1 = (bf16[2,96,640]{2,1,0:T(8,128)(2,1)S(1)}, bf16[2,96,640]{2,1,0:T(8,128)(2,1)}, u32[]{:S(2)}, u32[]{:S(2)}) collective-permute-start(bf16[2,96,640]{2,1,0:T(8,128)(2,1)S(1)} %bitcast.11), channel_id=1, source_target_pairs={{0,8},{8,0},{4,12},{12,4},{1,9},{9,1},{5,13},{13,5},{2,10},{10,2},... | collective-permute-start | bytes 737288 | tf_op jit(solution)/shard_map/ppermute | solution.py:228
  41.3 1.3 %collective-permute-start.8 = (bf16[5,40,640]{2,1,0:T(8,128)(2,1)S(1)}, bf16[5,40,640]{2,1,0:T(8,128)(2,1)S(1)}, u32[]{:S(2)}, u32[]{:S(2)}) collective-permute-start(bf16[5,40,640]{2,1,0:T(8,128)(2,1)S(1)} %collective-permute-done.4.refs_10_), channel_id=1, source_target_pairs={{4,20},{8,24},{16,0},{28,12},{5,21},{9,25},{17,1},{29,13},{6,22},{... | collective-permute-start | bytes 768008 | tf_op jit(solution)/shard_map/ppermute | solution.py:233
  42.6 0.7 collective-permute-start
  43.3 9.8 %collective-permute-done.1.refs_2_ = bf16[2,96,640]{2,1,0:T(8,128)(2,1)} collective-permute-done((bf16[2,96,640]{2,1,0:T(8,128)(2,1)S(1)}, bf16[2,96,640]{2,1,0:T(8,128)(2,1)}, u32[]{:S(2)}, u32[]{:S(2)}) %collective-permute-start.1) | collective-permute-done | bytes 245792 | tf_op jit(solution)/shard_map/ppermute | solution.py:228
  53.1 0.0 collective-permute-done.3.refs_9_
  53.1 1.4 %collective-permute-start.5 = (bf16[2,96,640]{2,1,0:T(8,128)(2,1)S(1)}, bf16[2,96,640]{2,1,0:T(8,128)(2,1)}, u32[]{:S(2)}, u32[]{:S(2)}) collective-permute-start(bf16[2,96,640]{2,1,0:T(8,128)(2,1)S(1)} %bitcast.13), channel_id=1, source_target_pairs={{4,8},{8,4},{5,9},{9,5},{6,10},{10,6},{7,11},{11,7},{20,24},{24,20... | collective-permute-start | bytes 737288 | tf_op jit(solution)/shard_map/ppermute | solution.py:237
  54.5 1.3 %collective-permute-start.6 = (bf16[2,96,640]{2,1,0:T(8,128)(2,1)}, bf16[2,96,640]{2,1,0:T(8,128)(2,1)}, u32[]{:S(2)}, u32[]{:S(2)}) collective-permute-start(bf16[2,96,640]{2,1,0:T(8,128)(2,1)} %collective-permute-done.1.refs_2_), channel_id=1, source_target_pairs={{4,0},{8,12},{5,1},{9,13},{6,2},{10,14},{7,3},{11,15},{20,16},{24,... | collective-permute-start | bytes 737288 | tf_op jit(solution)/shard_map/ppermute | solution.py:238
  55.8 0.0 copy-done.3
  55.8 0.1 copy.10.shift_ref
  55.8 0.1 stack.28.place_ref
  55.9 0.0 collective-permute-done.refs_1_
  55.9 0.0 collective-permute-done.5.refs_3_
  55.9 8.2 %collective-permute-done.6.refs_4_ = bf16[2,96,640]{2,1,0:T(8,128)(2,1)} collective-permute-done((bf16[2,96,640]{2,1,0:T(8,128)(2,1)}, bf16[2,96,640]{2,1,0:T(8,128)(2,1)}, u32[]{:S(2)}, u32[]{:S(2)}) %collective-permute-start.6) | collective-permute-done | bytes 245792 | tf_op jit(solution)/shard_map/ppermute | solution.py:238
  64.1 0.0 collective-permute-done.8.refs_11_
  64.1 0.0 collective-permute-done.7.refs_6_
  64.1 0.0 copy-done
  64.1 0.0 copy-done.2
  64.1 8.1 %conv_mix.1 = (bf16[4,24,640]{2,1,0:T(8,128)(2,1)S(1)}, bf16[4,24,640]{2,1,0:T(8,128)(2,1)S(1)}, bf16[4,24,640]{2,1,0:T(8,128)(2,1)S(1)}, bf16[4,24,640]{2,1,0:T...) custom-call(s32[5,8]{1,0:T(8,128)S(1)} %copy-done.2, ...), custom_call_target="tpu_custom_call" | custom-call | tf_op jit(solution)/shard_map/conv_mix/pallas_call | solution.py:160
  72.2 0.8 collective-permute-start.9
  73.1 0.1 collective-permute-start.10
  73.1 2.6 %collective-permute-start.11 = (bf16[4,24,640]{2,1,0:T(8,128)(2,1)S(1)}, bf16[4,24,640]{2,1,0:T(8,128)(2,1)S(1)}, u32[]{:S(2)}, u32[]{:S(2)}) collective-permute-start(bf16[4,24,640]{2,1,0:T(8,128)(2,1)S(1)} %get-tuple-element.32), channel_id=1, source_target_pairs={{0,3},{1,2},{2,1},{3,0},{16,19},{17,18},{18,17},{19,16},{4,7},{5,6... | collective-permute-start | bytes 368648 | tf_op jit(solution)/shard_map/ppermute | solution.py:272
  75.8 0.0 collective-permute-start.12
  75.8 0.9 %collective-permute-start.13 = (bf16[4,24,640]{2,1,0:T(8,128)(2,1)S(1)}, bf16[4,24,640]{2,1,0:T(8,128)(2,1)S(1)}, u32[]{:S(2)}, u32[]{:S(2)}) collective-permute-start(bf16[4,24,640]{2,1,0:T(8,128)(2,1)S(1)} %get-tuple-element.34), channel_id=1, source_target_pairs={{0,17},{1,16},{2,19},{3,18},{16,1},{17,0},{18,3},{19,2},{4,21},{5,... | collective-permute-start | bytes 368648 | tf_op jit(solution)/shard_map/ppermute | solution.py:272
  76.7 1.1 %collective-permute-done.9.refs_1_ = bf16[4,24,640]{2,1,0:T(8,128)(2,1)S(1)} collective-permute-done((bf16[4,24,640]{2,1,0:T(8,128)(2,1)S(1)}, bf16[4,24,640]{2,1,0:T(8,128)(2,1)S(1)}, u32[]{:S(2)}, u32[]{:S(2)}) %collective-permute-start.9) | collective-permute-done | bytes 122912 | tf_op jit(solution)/shard_map/ppermute | solution.py:272
  77.8 0.0 collective-permute-start.14
  77.8 1.9 %collective-permute-done.10.refs_2_ = bf16[4,24,640]{2,1,0:T(8,128)(2,1)S(1)} collective-permute-done((bf16[4,24,640]{2,1,0:T(8,128)(2,1)S(1)}, bf16[4,24,640]{2,1,0:T(8,128)(2,1)S(1)}, u32[]{:S(2)}, u32[]{:S(2)}) %collective-permute-start.10) | collective-permute-done | bytes 122912 | tf_op jit(solution)/shard_map/ppermute | solution.py:272
  79.7 0.6 collective-permute-start.15
  80.3 0.0 collective-permute-done.11.refs_3_
  80.3 0.0 collective-permute-done.12.refs_4_
  80.3 1.0 %collective-permute-done.13.refs_5_ = bf16[4,24,640]{2,1,0:T(8,128)(2,1)S(1)} collective-permute-done((bf16[4,24,640]{2,1,0:T(8,128)(2,1)S(1)}, bf16[4,24,640]{2,1,0:T(8,128)(2,1)S(1)}, u32[]{:S(2)}, u32[]{:S(2)}) %collective-permute-start.13) | collective-permute-done | bytes 122912 | tf_op jit(solution)/shard_map/ppermute | solution.py:272
  81.4 3.8 %collective-permute-done.14.refs_6_ = bf16[4,24,640]{2,1,0:T(8,128)(2,1)S(1)} collective-permute-done((bf16[4,24,640]{2,1,0:T(8,128)(2,1)S(1)}, bf16[4,24,640]{2,1,0:T(8,128)(2,1)S(1)}, u32[]{:S(2)}, u32[]{:S(2)}) %collective-permute-start.14) | collective-permute-done | bytes 122912 | tf_op jit(solution)/shard_map/ppermute | solution.py:272
  85.1 0.0 collective-permute-done.15.refs_7_
  85.1 1.4 %finish.1 = bf16[2,4,24,640]{3,2,1,0:T(8,128)(2,1)} custom-call(s32[7]{0:T(128)S(1)} %stack.28.place_ref, bf16[4,24,640]{2,1,0:T(8,128)(2,1)S(1)} %get-tuple-element.29.refs_0_, bf16[4,24,640]{2,1,0:T(8,128)(2,1)S(1)} %collective-permute-done.9.refs_1_, bf16[4,24,640]{2,1,0:T(8,128)(2,1)S(1)} %collective-permute-done.10.refs_2_, ...), custom_call_target="tpu_custom_call" | custom-call | tf_op jit(solution)/shard_map/finish/pallas_call | solution.py:188
  (2 shorter events, 0.0 us)
Async XLA Ops:
  0.0 0.9 %copy-start.1 = (bf16[2,4,640,24]{2,3,1,0:T(8,128)(2,1)S(1)}, bf16[2,4,640,24]{2,3,1,0:T(8,128)(2,1)}, u32[]{:S(2)}) copy-start(bf16[2,4,640,24]{2,3,1,0:T(8,128)(2,1)} %param.5) | copy-start | bytes 737284
  2.0 9.9 %collective-permute-start.2 = (bf16[5,40,640]{2,1,0:T(8,128)(2,1)}, bf16[5,40,640]{2,1,0:T(8,128)(2,1)S(1)}, u32[]{:S(2)}, u32[]{:S(2)}) collective-permute-start(bf16[5,40,640]{2,1,0:T(8,128)(2,1)} %refs_7_), channel_id=1, source_target_pairs={{0,4},{4,0},{8,12},{12,8},{16,24},{24,16},{20,28},{28,20},{1,5},{5... | collective-permute-start | bytes 768008 | tf_op jit(solution)/shard_map/ppermute | solution.py:219
  12.9 0.7 collective-permute-start.4
  17.8 38.0 %copy-start.3 = (s32[8,3]{0,1:T(4,128)S(1)}, s32[8,3]{0,1:T(4,128)}, u32[]{:S(2)}) copy-start(s32[8,3]{0,1:T(4,128)} %param.8) | copy-start | bytes 292
  17.8 46.3 %copy-start = (bf16[5,40,640]{2,1,0:T(8,128)(2,1)S(1)}, bf16[5,40,640]{2,1,0:T(8,128)(2,1)}, u32[]{:S(2)}) copy-start(bf16[5,40,640]{2,1,0:T(8,128)(2,1)} %refs_7_) | copy-start | bytes 768004
  17.8 46.3 %copy-start.2 = (s32[5,8]{1,0:T(8,128)S(1)}, s32[5,8]{1,0:T(8,128)}, u32[]{:S(2)}) copy-start(s32[5,8]{1,0:T(8,128)} %low_ref) | copy-start | bytes 484
  21.1 43.0 %collective-permute-start.7 = (bf16[4,15,64,192]{3,2,1,0:T(8,128)(2,1)S(1)}, bf16[4,15,64,192]{3,2,1,0:T(8,128)(2,1)}, u32[]{:S(2)}, u32[]{:S(2)}) collective-permute-start(bf16[4,15,64,192]{3,2,1,0:T(8,128)(2,1)S(1)} %copy.11.refs_5_), channel_id=1, source_target_pairs={{0,16},{16,0},{1,17},{17,1},{2,18},{18,2},{3,19},{19,3},{4,20},{20... | collective-permute-start | bytes 4423688 | tf_op jit(solution)/shard_map/ppermute | solution.py:33
  27.0 10.2 %all-to-all-start = ((bf16[8,24,640]{2,1,0:T(8,128)(2,1)}), bf16[8,24,640]{2,1,0:T(8,128)(2,1)S(1)}, u32[]{:S(2)}, u32[]{:S(2)}) async-start(bf16[8,24,640]{2,1,0:T(8,128)(2,1)} %bitcast.7), calls=%async_computation | async-start | bytes 491520 | tf_op jit(solution)/shard_map/all_to_all | solution.py:221
  30.7 22.4 %collective-permute-start.3 = (bf16[5,40,640]{2,1,0:T(8,128)(2,1)S(1)}, bf16[5,40,640]{2,1,0:T(8,128)(2,1)S(1)}, u32[]{:S(2)}, u32[]{:S(2)}) collective-permute-start(bf16[5,40,640]{2,1,0:T(8,128)(2,1)S(1)} %collective-permute-done.2.refs_8_), channel_id=1, source_target_pairs={{0,16},{16,0},{1,17},{17,1},{2,18},{18,2},{3,19},{19,3},{4,20},{20... | collective-permute-start | bytes 768008 | tf_op jit(solution)/shard_map/ppermute | solution.py:33
  37.1 16.0 %collective-permute-start.1 = (bf16[2,96,640]{2,1,0:T(8,128)(2,1)S(1)}, bf16[2,96,640]{2,1,0:T(8,128)(2,1)}, u32[]{:S(2)}, u32[]{:S(2)}) collective-permute-start(bf16[2,96,640]{2,1,0:T(8,128)(2,1)S(1)} %bitcast.11), channel_id=1, source_target_pairs={{0,8},{8,0},{4,12},{12,4},{1,9},{9,1},{5,13},{13,5},{2,10},{10,2},... | collective-permute-start | bytes 737288 | tf_op jit(solution)/shard_map/ppermute | solution.py:228
  41.3 22.8 %collective-permute-start.8 = (bf16[5,40,640]{2,1,0:T(8,128)(2,1)S(1)}, bf16[5,40,640]{2,1,0:T(8,128)(2,1)S(1)}, u32[]{:S(2)}, u32[]{:S(2)}) collective-permute-start(bf16[5,40,640]{2,1,0:T(8,128)(2,1)S(1)} %collective-permute-done.4.refs_10_), channel_id=1, source_target_pairs={{4,20},{8,24},{16,0},{28,12},{5,21},{9,25},{17,1},{29,13},{6,22},{... | collective-permute-start | bytes 768008 | tf_op jit(solution)/shard_map/ppermute | solution.py:233
  42.6 13.3 %collective-permute-start = (bf16[2,96,640]{2,1,0:T(8,128)(2,1)S(1)}, bf16[2,96,640]{2,1,0:T(8,128)(2,1)}, u32[]{:S(2)}, u32[]{:S(2)}) collective-permute-start(bf16[2,96,640]{2,1,0:T(8,128)(2,1)S(1)} %bitcast.12), channel_id=1, source_target_pairs={{0,4},{4,0},{8,12},{12,8},{1,5},{5,1},{9,13},{13,9},{2,6},{6,2},{1... | collective-permute-start | bytes 737288 | tf_op jit(solution)/shard_map/ppermute | solution.py:229
  53.1 2.8 %collective-permute-start.5 = (bf16[2,96,640]{2,1,0:T(8,128)(2,1)S(1)}, bf16[2,96,640]{2,1,0:T(8,128)(2,1)}, u32[]{:S(2)}, u32[]{:S(2)}) collective-permute-start(bf16[2,96,640]{2,1,0:T(8,128)(2,1)S(1)} %bitcast.13), channel_id=1, source_target_pairs={{4,8},{8,4},{5,9},{9,5},{6,10},{10,6},{7,11},{11,7},{20,24},{24,20... | collective-permute-start | bytes 737288 | tf_op jit(solution)/shard_map/ppermute | solution.py:237
  54.5 9.6 %collective-permute-start.6 = (bf16[2,96,640]{2,1,0:T(8,128)(2,1)}, bf16[2,96,640]{2,1,0:T(8,128)(2,1)}, u32[]{:S(2)}, u32[]{:S(2)}) collective-permute-start(bf16[2,96,640]{2,1,0:T(8,128)(2,1)} %collective-permute-done.1.refs_2_), channel_id=1, source_target_pairs={{4,0},{8,12},{5,1},{9,13},{6,2},{10,14},{7,3},{11,15},{20,16},{24,... | collective-permute-start | bytes 737288 | tf_op jit(solution)/shard_map/ppermute | solution.py:238
  72.2 5.6 %collective-permute-start.9 = (bf16[4,24,640]{2,1,0:T(8,128)(2,1)S(1)}, bf16[4,24,640]{2,1,0:T(8,128)(2,1)S(1)}, u32[]{:S(2)}, u32[]{:S(2)}) collective-permute-start(bf16[4,24,640]{2,1,0:T(8,128)(2,1)S(1)} %get-tuple-element.30), channel_id=1, source_target_pairs={{0,1},{1,0},{2,3},{3,2},{16,17},{17,16},{18,19},{19,18},{4,5},{5,4... | collective-permute-start | bytes 368648 | tf_op jit(solution)/shard_map/ppermute | solution.py:272
  73.1 6.7 %collective-permute-start.10 = (bf16[4,24,640]{2,1,0:T(8,128)(2,1)S(1)}, bf16[4,24,640]{2,1,0:T(8,128)(2,1)S(1)}, u32[]{:S(2)}, u32[]{:S(2)}) collective-permute-start(bf16[4,24,640]{2,1,0:T(8,128)(2,1)S(1)} %get-tuple-element.31), channel_id=1, source_target_pairs={{0,2},{1,3},{2,0},{3,1},{16,18},{17,19},{18,16},{19,17},{4,6},{5,7... | collective-permute-start | bytes 368648 | tf_op jit(solution)/shard_map/ppermute | solution.py:272
  73.1 7.2 %collective-permute-start.11 = (bf16[4,24,640]{2,1,0:T(8,128)(2,1)S(1)}, bf16[4,24,640]{2,1,0:T(8,128)(2,1)S(1)}, u32[]{:S(2)}, u32[]{:S(2)}) collective-permute-start(bf16[4,24,640]{2,1,0:T(8,128)(2,1)S(1)} %get-tuple-element.32), channel_id=1, source_target_pairs={{0,3},{1,2},{2,1},{3,0},{16,19},{17,18},{18,17},{19,16},{4,7},{5,6... | collective-permute-start | bytes 368648 | tf_op jit(solution)/shard_map/ppermute | solution.py:272
  75.8 4.5 %collective-permute-start.12 = (bf16[4,24,640]{2,1,0:T(8,128)(2,1)S(1)}, bf16[4,24,640]{2,1,0:T(8,128)(2,1)S(1)}, u32[]{:S(2)}, u32[]{:S(2)}) collective-permute-start(bf16[4,24,640]{2,1,0:T(8,128)(2,1)S(1)} %get-tuple-element.33), channel_id=1, source_target_pairs={{0,16},{1,17},{2,18},{3,19},{16,0},{17,1},{18,2},{19,3},{4,20},{5,... | collective-permute-start | bytes 368648 | tf_op jit(solution)/shard_map/ppermute | solution.py:272
  75.8 5.6 %collective-permute-start.13 = (bf16[4,24,640]{2,1,0:T(8,128)(2,1)S(1)}, bf16[4,24,640]{2,1,0:T(8,128)(2,1)S(1)}, u32[]{:S(2)}, u32[]{:S(2)}) collective-permute-start(bf16[4,24,640]{2,1,0:T(8,128)(2,1)S(1)} %get-tuple-element.34), channel_id=1, source_target_pairs={{0,17},{1,16},{2,19},{3,18},{16,1},{17,0},{18,3},{19,2},{4,21},{5,... | collective-permute-start | bytes 368648 | tf_op jit(solution)/shard_map/ppermute | solution.py:272
  77.8 7.3 %collective-permute-start.14 = (bf16[4,24,640]{2,1,0:T(8,128)(2,1)S(1)}, bf16[4,24,640]{2,1,0:T(8,128)(2,1)S(1)}, u32[]{:S(2)}, u32[]{:S(2)}) collective-permute-start(bf16[4,24,640]{2,1,0:T(8,128)(2,1)S(1)} %get-tuple-element.35), channel_id=1, source_target_pairs={{0,18},{1,19},{2,16},{3,17},{16,2},{17,3},{18,0},{19,1},{4,22},{5,... | collective-permute-start | bytes 368648 | tf_op jit(solution)/shard_map/ppermute | solution.py:272
  79.7 5.4 %collective-permute-start.15 = (bf16[4,24,640]{2,1,0:T(8,128)(2,1)S(1)}, bf16[4,24,640]{2,1,0:T(8,128)(2,1)S(1)}, u32[]{:S(2)}, u32[]{:S(2)}) collective-permute-start(bf16[4,24,640]{2,1,0:T(8,128)(2,1)S(1)} %get-tuple-element.36), channel_id=1, source_target_pairs={{0,19},{1,18},{2,17},{3,16},{16,3},{17,2},{18,1},{19,0},{4,23},{5,... | collective-permute-start | bytes 368648 | tf_op jit(solution)/shard_map/ppermute | solution.py:272

commit v4 on v2

--- a/solution.py
+++ b/solution.py
@@ -12,7 +12,7 @@
 HALO = 2
 LANES = 128
 VMEM = pltpu.VMEM
-LIMIT = 48 * 1024 * 1024
+LIMIT = 24 * 1024 * 1024
 SMEM_SPEC = pl.BlockSpec(memory_space=pltpu.SMEM)
 VMEM_SPEC = pl.BlockSpec(memory_space=VMEM)
 
@@ -43,14 +43,16 @@
                 for i in range(rows)
                 for p in range(owners)
             ]
-            out_ref[e, q] = jnp.concatenate(parts, axis=-1)
+            block = jnp.concatenate(parts, axis=-1)
+            for p in range(owners):
+                out_ref[e, p, q] = block
 
 
 def pack(x, groups, owners):
     members, rows, cells, channels = x.shape
     return pl.pallas_call(
         functools.partial(pack_kernel, groups, owners),
-        out_shape=jax.ShapeDtypeStruct((members, groups, cells, rows * channels // groups), x.dtype),
+        out_shape=jax.ShapeDtypeStruct((members, owners, groups, cells, rows * channels // groups), x.dtype),
         in_specs=[VMEM_SPEC],
         out_specs=VMEM_SPEC,
         compiler_params=pltpu.CompilerParams(vmem_limit_bytes=LIMIT),
@@ -68,13 +70,12 @@
 def conv_mix_kernel(geometry, counts, low_ref, shift_ref, place_ref, *refs):
     bases, taps, slots, halo, sub, groups = geometry
     refs = list(refs)
-    field_slots = [[refs.pop(0) for _ in range(n)] for n in counts[0]]
-    weight_refs = [refs.pop(0) for _ in range(counts[1])]
-    mix_slots = [[refs.pop(0) for _ in range(n)] for n in counts[2]]
+    fields_ref = refs.pop(0)
+    weight_refs = [refs.pop(0) for _ in range(counts[0])]
+    mix_slots = [[refs.pop(0) for _ in range(n)] for n in counts[1]]
     field_rows, total, mix_all, mixed = refs[-4:]
     outs = refs[:-4]
-    late, span, _ = field_slots[0][0].shape
-    owners = len(field_slots)
+    late, owners, span, _ = fields_ref.shape
     depth, width = mix_slots[0][0].shape[1:]
     channels = owners * depth
     padded = total.shape[-1]
@@ -87,11 +88,10 @@
     field_rows[...] = jnp.zeros_like(field_rows)
     for s in range(late):
         lat = partner_in_kernel(member, s, late)
-        for d, slot in enumerate(field_slots):
-            base = pl.multiple_of(partner_in_kernel(owner, d, owners) * span, sub)
-            value = added(slot, lat)
+        for p in range(owners):
+            value = fields_ref[lat, p]
             for r in range(rows):
-                field_rows[r, pl.ds(base, span), :channels] = value[:, r * channels : (r + 1) * channels]
+                field_rows[r, p * span : (p + 1) * span, :channels] = value[:, r * channels : (r + 1) * channels]
 
         def one_row(r, carry):
             row = lat * rows + r
@@ -107,10 +107,9 @@
                 lhs = weight_refs[s][r, :, pl.ds(q, sub), :].reshape(bases * taps * sub, slots * block)
                 product = jnp.dot(lhs, picked, preferred_element_type=jnp.float32)
                 for k in range(bases):
-                    first = row + low_ref[k, row] + HALO
-                    for t in range(taps):
-                        at = (k * taps + t) * sub
-                        total[k, first + t, piece * sub : (piece + 1) * sub] += product[at : at + sub]
+                    at = pl.ds(row + low_ref[k, row] + HALO, taps)
+                    slab = product[k * taps * sub : (k + 1) * taps * sub].reshape(taps, sub, padded)
+                    total[k, at, piece * sub : (piece + 1) * sub] += slab
             return carry
 
         lax.fori_loop(0, rows, one_row, 0)
@@ -145,8 +144,7 @@
 def conv_mix(low, shift, place, fields, weights, mix, halo, groups, block):
     bases, all_rows = low.shape
     slots = shift.shape[1]
-    late, span, _ = fields[0][0].shape
-    owners = len(fields)
+    late, owners, span, _ = fields.shape
     rows = all_rows // late
     depth, width = mix[0][0].shape[1:]
     padded = -(-owners * depth // LANES) * LANES
@@ -155,8 +153,8 @@
     shapes = [jax.ShapeDtypeStruct((rows, span // groups, width), jnp.bfloat16)] * (late * groups)
     if halo:
         shapes.append(jax.ShapeDtypeStruct((2, halo, span, width), jnp.bfloat16))
-    operands = [x for slot in fields for x in slot] + weights + [x for slot in mix for x in slot]
-    counts = ([len(s) for s in fields], len(weights), [len(s) for s in mix])
+    operands = [fields] + weights + [x for slot in mix for x in slot]
+    counts = (len(weights), [len(s) for s in mix])
     return pl.pallas_call(
         functools.partial(conv_mix_kernel, (bases, taps, slots, halo, sub, groups), counts),
         out_shape=shapes,
@@ -195,30 +193,27 @@
     )(place, *parts)
 
 
-def gather_fields(x, owners):
-    if owners == 4:
-        two = lax.ppermute(x, "lonp", [(0, 2), (2, 0), (1, 3), (3, 1)])
-        one = lax.ppermute(x, "lonp", [(0, 1), (1, 0), (2, 3), (3, 2)])
-        middle = lax.ppermute(x, "lonp", [(1, 2), (2, 1)])
-        passed = lax.ppermute(two, "lonp", [(1, 0), (2, 3)])
-        return [[x], [one], [two], [middle, passed]]
-    return [[x]] + [[trade(x, "lonp", d, owners)] for d in range(1, owners)]
-
-
-def gather_mix(x, late, owners):
+def both_kernels(kernel, late):
+    bases, rows, taps, slots, block, _ = kernel.shape
+    own = kernel.transpose(1, 0, 2, 5, 3, 4).reshape(rows, bases * taps, block, slots * block)
+    return [own] + [trade(own, "late", s, late) for s in range(1, late)]
+
+
+def gather_mix(mix, late, owners):
     core, own = lax.axis_index("late"), lax.axis_index("lonp")
     if owners == 4 and late == 2:
-        def both(pairs_first, pairs_second):
-            return [(a, b) for a, b in pairs_first] + [(4 + a, 4 + b) for a, b in pairs_second]
-
-        near, far = [(0, 1), (1, 0), (2, 3), (3, 2)], [(0, 2), (2, 0), (1, 3), (3, 1)]
-        fetched = lax.ppermute(x, ("late", "lonp"), both(near, far))
-        other = trade(fetched, "late", 1, late)
-        source = jnp.where(core == 0, x, fetched)
-        third = lax.ppermute(source, ("late", "lonp"), both([(1, 2), (2, 1)], [(1, 0), (2, 3)]))
-        copied = lax.ppermute(third, ("late", "lonp"), [(1, 5), (2, 6), (4, 0), (7, 3)])
-        return [[x], [fetched], [other], [third, copied]], [own, own ^ (1 + core), own ^ (2 - core), own ^ 3]
-    slots = [[x]] + [[trade(x, "lonp", d, owners)] for d in range(1, owners)]
+        def fetch(distances):
+            route = [
+                (c * owners + p, c * owners + (p ^ d)) for p in range(owners) for c, d in enumerate(distances(p)) if d
+            ]
+            return lax.ppermute(mix, ("late", "lonp"), route)
+
+        first = fetch(lambda p: (1, 2))
+        third = fetch(lambda p: (3, 0) if p in (0, 3) else (0, 3))
+        other = trade(first, "late", 1, late)
+        copied = trade(third, "late", 1, late)
+        return [[mix], [first], [other], [third, copied]], [own, own ^ (1 + core), own ^ (2 - core), own ^ 3]
+    slots = [[mix]] + [[trade(mix, "lonp", d, owners)] for d in range(1, owners)]
     return slots, [partner(own, d, owners) for d in range(owners)]
 
 
@@ -229,21 +224,19 @@
     all_rows = late * rows
     halo = HALO if halves > 1 else 0
 
+    packed = pack(fields.transpose(0, 1, 3, 2), groups, owners)
+    packed = packed.reshape((-1,) + packed.shape[3:])
+    spread = lax.all_to_all(packed, ("late", "lonp", "lonq"), split_axis=0, concat_axis=0, tiled=True)
+    spread = spread.reshape(late, owners, groups * cells, -1)
+    weights = both_kernels(kernel, late)
     mix, origins = gather_mix(mix_weight, late, owners)
-    packed = pack(fields.transpose(0, 1, 3, 2), groups, owners)
-    packed = packed.reshape((late * groups,) + packed.shape[2:])
-    spread = lax.all_to_all(packed, ("late", "lonq"), split_axis=0, concat_axis=0, tiled=True)
-    gathered = gather_fields(spread.reshape(late, groups * cells, -1), owners)
-
-    own = kernel.transpose(1, 0, 2, 5, 3, 4).reshape(rows, bases * taps, block, slots * block)
-    weights = [own] + [trade(own, "late", s, late) for s in range(1, late)]
 
     start = lax.axis_index("lath") * all_rows
     low = lax.dynamic_slice_in_dim(band_low, start, all_rows, 1)
     shift = lax.dynamic_slice_in_dim(block_shift, start, all_rows, 0)
     place = [lax.axis_index("late"), lax.axis_index("lonp"), lax.axis_index("lonq")] + origins
     place = jnp.stack(place).astype(jnp.int32)
-    partial = conv_mix(low, shift, place, gathered, weights, mix, halo, groups, block)
+    partial = conv_mix(low, shift, place, spread, weights, mix, halo, groups, block)
     if halo:
         *partial, beyond = partial
         below = lax.ppermute(beyond[1], "lath", [(i, i + 1) for i in range(halves - 1)])

time: 79.2 us -> 69.2 us (0.87)
  waiting for transfers between devices: 27 us -> 19.2 us
  starting transfers between devices: 31.7 us -> 30 us
    ppermute x7 -> x2, starting transfers between devices: 22.1 us -> 5.93 us  [fetch(): return lax.ppermute(mix, ('late', 'lonp'), route)]
    ppermute x2 -> x3, starting transfers between devices: 0.52 us -> 11 us  [trade(): lax.ppermute(x, axis, [(i, partner(i, distance, size)) for i in range(siz...]
    ppermute x7 -> x2, waiting for transfers between devices: 13.5 us -> 8.39 us  [fetch(): return lax.ppermute(mix, ('late', 'lonp'), route)]
    all_to_all x1, waiting for transfers between devices: 4.63 us -> 0.01 us  [per_device(): lax.all_to_all(packed, ('late', 'lonp', 'lonq'), split_axis=0, concat_axi...]
    all_to_all x1, starting transfers between devices: 4.48 us -> 7.3 us  [per_device(): lax.all_to_all(packed, ('late', 'lonp', 'lonq'), split_axis=0, concat_axi...]
    ppermute x2 -> x3, waiting for transfers between devices: 0.01 us -> 1.7 us  [trade(): lax.ppermute(x, axis, [(i, partner(i, distance, size)) for i in range(siz...]
    ppermute x7, starting transfers between devices: 4.6 us -> 5.7 us  [per_device(): lax.ppermute(partial[dl * groups + dq], ('late', 'lonq'), [(l * groups +...]
    unnamed x13 -> x9, local copies, waits for them, and re-layouts: 1.72 us -> 1.04 us
  transfers between devices with their start and end apart: 17 -> 13, of which waited for: 10 -> 8; matrix products, arithmetic and copies ran while one was open for 0% -> 11% of each run, Pallas kernels for 1% -> 0%
where the time goes in v4:
time: 69.2 us; the launch traced here: 68.5 us
  starting transfers between devices  30 us (43%)
  waiting for transfers between devices  19.2 us (28%)
  Pallas kernels  10.7 us (15%)
  local copies, waits for them, and re-layouts  8.62 us (12%)
    ppermute x3, starting transfers between devices, trade(): lax.ppermute(x, axis, [(i, partner(i, distance, size)) for i in range(siz...  11 us
    ppermute x7, waiting for transfers between devices, per_device(): lax.ppermute(partial[dl * groups + dq], ('late', 'lonq'), [(l * groups +...  9.09 us
    ppermute x2, waiting for transfers between devices, fetch(): return lax.ppermute(mix, ('late', 'lonp'), route)  8.39 us
    pallas_call x1, Pallas kernels, conv_mix(): pl.pallas_call(functools.partial(conv_mix_kernel, (bases, taps, slots, ha...  7.91 us
    all_to_all x1, starting transfers between devices, per_device(): lax.all_to_all(packed, ('late', 'lonp', 'lonq'), split_axis=0, concat_axi...  7.3 us
    ppermute x2, starting transfers between devices, fetch(): return lax.ppermute(mix, ('late', 'lonp'), route)  5.93 us
    ppermute x7, starting transfers between devices, per_device(): lax.ppermute(partial[dl * groups + dq], ('late', 'lonq'), [(l * groups +...  5.7 us
    transpose x1, local copies, waits for them, and re-layouts, both_kernels(): kernel.transpose(1, 0, 2, 5, 3, 4)  4.18 us
  transfers between devices with their start and end apart: 13, of which 8 were waited for; matrix products, arithmetic and copies ran while one was open for 11% of the time, Pallas kernels for 0%

profile of v4, /device:TPU:0, one launch (start us, length us, event | category | flops | bytes accessed | tf_op | source)
XLA Modules:
  0.0 68.5 jit_solution(18319315551474130287)
XLA Ops:
  0.0 0.0 copy-start.1
  0.0 0.9 %copy-done.1 = bf16[2,4,640,24]{2,3,1,0:T(8,128)(2,1)S(1)} copy-done((bf16[2,4,640,24]{2,3,1,0:T(8,128)(2,1)S(1)}, bf16[2,4,640,24]{2,3,1,0:T(8,128)(2,1)}, u32[]{:S(2)}) %copy-start.1) | copy-done | bytes 245784
  0.9 1.3 %pack.1 = bf16[2,4,4,24,640]{4,3,2,1,0:T(8,128)(2,1)} custom-call(bf16[2,4,24,640]{3,2,1,0:T(8,128)(2,1)S(1)} %bitcast.12), custom_call_target="tpu_custom_call" | custom-call | tf_op jit(solution)/shard_map/pack/pallas_call | solution.py:53
  2.3 7.3 %all-to-all-start = ((bf16[32,24,640]{2,1,0:T(8,128)(2,1)}), bf16[32,24,640]{2,1,0:T(8,128)(2,1)S(1)}, u32[]{:S(2)}, u32[]{:S(2)}) async-start(bf16[32,24,640]{2,1,0:T(8,128)(2,1)} %bitcast.7), calls=%async_computation | async-start | bytes 1966080 | tf_op jit(solution)/shard_map/all_to_all | solution.py:229
  9.6 4.2 %copy.8 = bf16[4,5,3,64,3,64]{3,5,4,2,1,0:T(8,128)(2,1)} copy(bf16[4,5,3,64,3,64]{3,5,4,2,0,1:T(8,128)(2,1)} %bitcast.14) | data formatting | bytes 2949120 | tf_op jit(solution)/shard_map/transpose | solution.py:198
  13.8 0.0 copy-start
  13.8 0.0 copy-start.3
  13.8 0.0 copy-start.2
  13.8 3.3 %copy.11.refs_1_ = bf16[4,15,64,192]{3,2,1,0:T(8,128)(2,1)S(1)} copy(bf16[4,15,64,192]{2,3,1,0:T(8,128)(2,1)} %bitcast.13) | data formatting | bytes 2949120 | tf_op jit(solution)/shard_map/reshape | solution.py:198
  17.1 0.3 collective-permute-start
  17.4 0.0 copy-done
  17.4 1.7 %collective-permute-start.1 = (bf16[5,40,640]{2,1,0:T(8,128)(2,1)S(1)}, bf16[5,40,640]{2,1,0:T(8,128)(2,1)S(1)}, u32[]{:S(2)}, u32[]{:S(2)}) collective-permute-start(bf16[5,40,640]{2,1,0:T(8,128)(2,1)S(1)} %copy-done), channel_id=1, source_target_pairs={{0,4},{16,24},{4,0},{20,28},{8,12},{24,16},{12,8},{28,20},{1,5},{1... | collective-permute-start | bytes 768008 | tf_op jit(solution)/shard_map/ppermute | solution.py:209
  19.1 4.3 %collective-permute-start.3 = (bf16[5,40,640]{2,1,0:T(8,128)(2,1)S(1)}, bf16[5,40,640]{2,1,0:T(8,128)(2,1)}, u32[]{:S(2)}, u32[]{:S(2)}) collective-permute-start(bf16[5,40,640]{2,1,0:T(8,128)(2,1)S(1)} %copy-done), channel_id=1, source_target_pairs={{0,12},{20,24},{24,20},{12,0},{1,13},{21,25},{25,21},{13,1},{2,14}... | collective-permute-start | bytes 768008 | tf_op jit(solution)/shard_map/ppermute | solution.py:209
  23.4 8.4 %collective-permute-done.1.refs_4_ = bf16[5,40,640]{2,1,0:T(8,128)(2,1)S(1)} collective-permute-done((bf16[5,40,640]{2,1,0:T(8,128)(2,1)S(1)}, bf16[5,40,640]{2,1,0:T(8,128)(2,1)S(1)}, u32[]{:S(2)}, u32[]{:S(2)}) %collective-permute-start.1) | collective-permute-done | bytes 256032 | tf_op jit(solution)/shard_map/ppermute | solution.py:209
  31.8 10.7 %collective-permute-start.2 = (bf16[5,40,640]{2,1,0:T(8,128)(2,1)S(1)}, bf16[5,40,640]{2,1,0:T(8,128)(2,1)}, u32[]{:S(2)}, u32[]{:S(2)}) collective-permute-start(bf16[5,40,640]{2,1,0:T(8,128)(2,1)S(1)} %collective-permute-done.1.refs_4_), channel_id=1, source_target_pairs={{0,16},{16,0},{1,17},{17,1},{2,18},{18,2},{3,19},{19,3},{4,20},{20... | collective-permute-start | bytes 768008 | tf_op jit(solution)/shard_map/ppermute | solution.py:33
  42.5 0.0 collective-permute-done.3.refs_6_
  42.5 0.0 collective-permute-start.4
  42.5 0.0 copy-done.3
  42.5 0.1 copy.10.shift_ref
  42.6 0.1 stack.28.place_ref
  42.7 1.4 %collective-permute-done.2.refs_5_ = bf16[5,40,640]{2,1,0:T(8,128)(2,1)} collective-permute-done((bf16[5,40,640]{2,1,0:T(8,128)(2,1)S(1)}, bf16[5,40,640]{2,1,0:T(8,128)(2,1)}, u32[]{:S(2)}, u32[]{:S(2)}) %collective-permute-start.2) | collective-permute-done | bytes 256032 | tf_op jit(solution)/shard_map/ppermute | solution.py:33
  44.1 0.3 collective-permute-done.4.refs_7_
  44.4 0.0 collective-permute-done.refs_2_
  44.4 0.0 all-to-all-done
  44.4 0.0 copy-done.2
  44.4 7.9 %conv_mix.1 = (bf16[4,24,640]{2,1,0:T(8,128)(2,1)S(1)}, bf16[4,24,640]{2,1,0:T(8,128)(2,1)S(1)}, bf16[4,24,640]{2,1,0:T(8,128)(2,1)S(1)}, bf16[4,24,640]{2,1,0:T...) custom-call(s32[5,8]{1,0:T(8,128)S(1)} %copy-done.2, ...), custom_call_target="tpu_custom_call" | custom-call | tf_op jit(solution)/shard_map/conv_mix/pallas_call | solution.py:158
  52.3 1.5 %collective-permute-start.5 = (bf16[4,24,640]{2,1,0:T(8,128)(2,1)S(1)}, bf16[4,24,640]{2,1,0:T(8,128)(2,1)S(1)}, u32[]{:S(2)}, u32[]{:S(2)}) collective-permute-start(bf16[4,24,640]{2,1,0:T(8,128)(2,1)S(1)} %get-tuple-element.14), channel_id=1, source_target_pairs={{0,1},{1,0},{2,3},{3,2},{16,17},{17,16},{18,19},{19,18},{4,5},{5,4... | collective-permute-start | bytes 368648 | tf_op jit(solution)/shard_map/ppermute | solution.py:252
  53.8 1.5 %collective-permute-start.6 = (bf16[4,24,640]{2,1,0:T(8,128)(2,1)S(1)}, bf16[4,24,640]{2,1,0:T(8,128)(2,1)S(1)}, u32[]{:S(2)}, u32[]{:S(2)}) collective-permute-start(bf16[4,24,640]{2,1,0:T(8,128)(2,1)S(1)} %get-tuple-element.15), channel_id=1, source_target_pairs={{0,2},{1,3},{2,0},{3,1},{16,18},{17,19},{18,16},{19,17},{4,6},{5,7... | collective-permute-start | bytes 368648 | tf_op jit(solution)/shard_map/ppermute | solution.py:252
  55.3 0.5 collective-permute-start.7
  55.9 0.0 collective-permute-start.8
  55.9 1.6 %collective-permute-start.9 = (bf16[4,24,640]{2,1,0:T(8,128)(2,1)S(1)}, bf16[4,24,640]{2,1,0:T(8,128)(2,1)S(1)}, u32[]{:S(2)}, u32[]{:S(2)}) collective-permute-start(bf16[4,24,640]{2,1,0:T(8,128)(2,1)S(1)} %get-tuple-element.18), channel_id=1, source_target_pairs={{0,17},{1,16},{2,19},{3,18},{16,1},{17,0},{18,3},{19,2},{4,21},{5,... | collective-permute-start | bytes 368648 | tf_op jit(solution)/shard_map/ppermute | solution.py:252
  57.4 0.7 %collective-permute-done.5.refs_1_ = bf16[4,24,640]{2,1,0:T(8,128)(2,1)S(1)} collective-permute-done((bf16[4,24,640]{2,1,0:T(8,128)(2,1)S(1)}, bf16[4,24,640]{2,1,0:T(8,128)(2,1)S(1)}, u32[]{:S(2)}, u32[]{:S(2)}) %collective-permute-start.5) | collective-permute-done | bytes 122912 | tf_op jit(solution)/shard_map/ppermute | solution.py:252
  58.1 0.4 collective-permute-start.10
  58.6 2.5 %collective-permute-done.6.refs_2_ = bf16[4,24,640]{2,1,0:T(8,128)(2,1)S(1)} collective-permute-done((bf16[4,24,640]{2,1,0:T(8,128)(2,1)S(1)}, bf16[4,24,640]{2,1,0:T(8,128)(2,1)S(1)}, u32[]{:S(2)}, u32[]{:S(2)}) %collective-permute-start.6) | collective-permute-done | bytes 122912 | tf_op jit(solution)/shard_map/ppermute | solution.py:252
  61.0 0.1 collective-permute-start.11
  61.2 1.3 %collective-permute-done.7.refs_3_ = bf16[4,24,640]{2,1,0:T(8,128)(2,1)S(1)} collective-permute-done((bf16[4,24,640]{2,1,0:T(8,128)(2,1)S(1)}, bf16[4,24,640]{2,1,0:T(8,128)(2,1)S(1)}, u32[]{:S(2)}, u32[]{:S(2)}) %collective-permute-start.7) | collective-permute-done | bytes 122912 | tf_op jit(solution)/shard_map/ppermute | solution.py:252
  62.5 0.0 collective-permute-done.8.refs_4_
  62.5 0.0 collective-permute-done.9.refs_5_
  62.5 1.9 %collective-permute-done.10.refs_6_ = bf16[4,24,640]{2,1,0:T(8,128)(2,1)S(1)} collective-permute-done((bf16[4,24,640]{2,1,0:T(8,128)(2,1)S(1)}, bf16[4,24,640]{2,1,0:T(8,128)(2,1)S(1)}, u32[]{:S(2)}, u32[]{:S(2)}) %collective-permute-start.10) | collective-permute-done | bytes 122912 | tf_op jit(solution)/shard_map/ppermute | solution.py:252
  64.4 2.6 %collective-permute-done.11.refs_7_ = bf16[4,24,640]{2,1,0:T(8,128)(2,1)S(1)} collective-permute-done((bf16[4,24,640]{2,1,0:T(8,128)(2,1)S(1)}, bf16[4,24,640]{2,1,0:T(8,128)(2,1)S(1)}, u32[]{:S(2)}, u32[]{:S(2)}) %collective-permute-start.11) | collective-permute-done | bytes 122912 | tf_op jit(solution)/shard_map/ppermute | solution.py:252
  67.1 1.4 %finish.1 = bf16[2,4,24,640]{3,2,1,0:T(8,128)(2,1)} custom-call(s32[7]{0:T(128)S(1)} %stack.28.place_ref, bf16[4,24,640]{2,1,0:T(8,128)(2,1)S(1)} %get-tuple-element.13.refs_0_, bf16[4,24,640]{2,1,0:T(8,128)(2,1)S(1)} %collective-permute-done.5.refs_1_, bf16[4,24,640]{2,1,0:T(8,128)(2,1)S(1)} %collective-permute-done.6.refs_2_, ...), custom_call_target="tpu_custom_call" | custom-call | tf_op jit(solution)/shard_map/finish/pallas_call | solution.py:186
Async XLA Ops:
  0.0 0.9 %copy-start.1 = (bf16[2,4,640,24]{2,3,1,0:T(8,128)(2,1)S(1)}, bf16[2,4,640,24]{2,3,1,0:T(8,128)(2,1)}, u32[]{:S(2)}) copy-start(bf16[2,4,640,24]{2,3,1,0:T(8,128)(2,1)} %param.5) | copy-start | bytes 737284
  2.3 42.1 %all-to-all-start = ((bf16[32,24,640]{2,1,0:T(8,128)(2,1)}), bf16[32,24,640]{2,1,0:T(8,128)(2,1)S(1)}, u32[]{:S(2)}, u32[]{:S(2)}) async-start(bf16[32,24,640]{2,1,0:T(8,128)(2,1)} %bitcast.7), calls=%async_computation | async-start | bytes 1966080 | tf_op jit(solution)/shard_map/all_to_all | solution.py:229
  13.8 3.7 %copy-start = (bf16[5,40,640]{2,1,0:T(8,128)(2,1)S(1)}, bf16[5,40,640]{2,1,0:T(8,128)(2,1)}, u32[]{:S(2)}) copy-start(bf16[5,40,640]{2,1,0:T(8,128)(2,1)} %refs_3_.1) | copy-start | bytes 768004
  13.8 28.7 %copy-start.3 = (s32[8,3]{0,1:T(4,128)S(1)}, s32[8,3]{0,1:T(4,128)}, u32[]{:S(2)}) copy-start(s32[8,3]{0,1:T(4,128)} %param.8) | copy-start | bytes 292
  13.8 30.6 %copy-start.2 = (s32[5,8]{1,0:T(8,128)S(1)}, s32[5,8]{1,0:T(8,128)}, u32[]{:S(2)}) copy-start(s32[5,8]{1,0:T(8,128)} %low_ref) | copy-start | bytes 484
  17.1 27.2 %collective-permute-start = (bf16[4,15,64,192]{3,2,1,0:T(8,128)(2,1)S(1)}, bf16[4,15,64,192]{3,2,1,0:T(8,128)(2,1)}, u32[]{:S(2)}, u32[]{:S(2)}) collective-permute-start(bf16[4,15,64,192]{3,2,1,0:T(8,128)(2,1)S(1)} %copy.11.refs_1_), channel_id=1, source_target_pairs={{0,16},{16,0},{1,17},{17,1},{2,18},{18,2},{3,19},{19,3},{4,20},{20... | collective-permute-start | bytes 4423688 | tf_op jit(solution)/shard_map/ppermute | solution.py:33
  17.4 14.3 %collective-permute-start.1 = (bf16[5,40,640]{2,1,0:T(8,128)(2,1)S(1)}, bf16[5,40,640]{2,1,0:T(8,128)(2,1)S(1)}, u32[]{:S(2)}, u32[]{:S(2)}) collective-permute-start(bf16[5,40,640]{2,1,0:T(8,128)(2,1)S(1)} %copy-done), channel_id=1, source_target_pairs={{0,4},{16,24},{4,0},{20,28},{8,12},{24,16},{12,8},{28,20},{1,5},{1... | collective-permute-start | bytes 768008 | tf_op jit(solution)/shard_map/ppermute | solution.py:209
  19.1 23.4 %collective-permute-start.3 = (bf16[5,40,640]{2,1,0:T(8,128)(2,1)S(1)}, bf16[5,40,640]{2,1,0:T(8,128)(2,1)}, u32[]{:S(2)}, u32[]{:S(2)}) collective-permute-start(bf16[5,40,640]{2,1,0:T(8,128)(2,1)S(1)} %copy-done), channel_id=1, source_target_pairs={{0,12},{20,24},{24,20},{12,0},{1,13},{21,25},{25,21},{13,1},{2,14}... | collective-permute-start | bytes 768008 | tf_op jit(solution)/shard_map/ppermute | solution.py:209
  31.8 12.3 %collective-permute-start.2 = (bf16[5,40,640]{2,1,0:T(8,128)(2,1)S(1)}, bf16[5,40,640]{2,1,0:T(8,128)(2,1)}, u32[]{:S(2)}, u32[]{:S(2)}) collective-permute-start(bf16[5,40,640]{2,1,0:T(8,128)(2,1)S(1)} %collective-permute-done.1.refs_4_), channel_id=1, source_target_pairs={{0,16},{16,0},{1,17},{17,1},{2,18},{18,2},{3,19},{19,3},{4,20},{20... | collective-permute-start | bytes 768008 | tf_op jit(solution)/shard_map/ppermute | solution.py:33
  42.5 1.9 %collective-permute-start.4 = (bf16[5,40,640]{2,1,0:T(8,128)(2,1)}, bf16[5,40,640]{2,1,0:T(8,128)(2,1)}, u32[]{:S(2)}, u32[]{:S(2)}) collective-permute-start(bf16[5,40,640]{2,1,0:T(8,128)(2,1)} %collective-permute-done.3.refs_6_), channel_id=1, source_target_pairs={{0,16},{16,0},{1,17},{17,1},{2,18},{18,2},{3,19},{19,3},{4,20},{20... | collective-permute-start | bytes 768008 | tf_op jit(solution)/shard_map/ppermute | solution.py:33
  52.3 5.8 %collective-permute-start.5 = (bf16[4,24,640]{2,1,0:T(8,128)(2,1)S(1)}, bf16[4,24,640]{2,1,0:T(8,128)(2,1)S(1)}, u32[]{:S(2)}, u32[]{:S(2)}) collective-permute-start(bf16[4,24,640]{2,1,0:T(8,128)(2,1)S(1)} %get-tuple-element.14), channel_id=1, source_target_pairs={{0,1},{1,0},{2,3},{3,2},{16,17},{17,16},{18,19},{19,18},{4,5},{5,4... | collective-permute-start | bytes 368648 | tf_op jit(solution)/shard_map/ppermute | solution.py:252
  53.8 7.2 %collective-permute-start.6 = (bf16[4,24,640]{2,1,0:T(8,128)(2,1)S(1)}, bf16[4,24,640]{2,1,0:T(8,128)(2,1)S(1)}, u32[]{:S(2)}, u32[]{:S(2)}) collective-permute-start(bf16[4,24,640]{2,1,0:T(8,128)(2,1)S(1)} %get-tuple-element.15), channel_id=1, source_target_pairs={{0,2},{1,3},{2,0},{3,1},{16,18},{17,19},{18,16},{19,17},{4,6},{5,7... | collective-permute-start | bytes 368648 | tf_op jit(solution)/shard_map/ppermute | solution.py:252
  55.3 7.2 %collective-permute-start.7 = (bf16[4,24,640]{2,1,0:T(8,128)(2,1)S(1)}, bf16[4,24,640]{2,1,0:T(8,128)(2,1)S(1)}, u32[]{:S(2)}, u32[]{:S(2)}) collective-permute-start(bf16[4,24,640]{2,1,0:T(8,128)(2,1)S(1)} %get-tuple-element.16), channel_id=1, source_target_pairs={{0,3},{1,2},{2,1},{3,0},{16,19},{17,18},{18,17},{19,16},{4,7},{5,6... | collective-permute-start | bytes 368648 | tf_op jit(solution)/shard_map/ppermute | solution.py:252
  55.9 6.6 %collective-permute-start.8 = (bf16[4,24,640]{2,1,0:T(8,128)(2,1)S(1)}, bf16[4,24,640]{2,1,0:T(8,128)(2,1)S(1)}, u32[]{:S(2)}, u32[]{:S(2)}) collective-permute-start(bf16[4,24,640]{2,1,0:T(8,128)(2,1)S(1)} %get-tuple-element.17), channel_id=1, source_target_pairs={{0,16},{1,17},{2,18},{3,19},{16,0},{17,1},{18,2},{19,3},{4,20},{5,... | collective-permute-start | bytes 368648 | tf_op jit(solution)/shard_map/ppermute | solution.py:252
  55.9 6.6 %collective-permute-start.9 = (bf16[4,24,640]{2,1,0:T(8,128)(2,1)S(1)}, bf16[4,24,640]{2,1,0:T(8,128)(2,1)S(1)}, u32[]{:S(2)}, u32[]{:S(2)}) collective-permute-start(bf16[4,24,640]{2,1,0:T(8,128)(2,1)S(1)} %get-tuple-element.18), channel_id=1, source_target_pairs={{0,17},{1,16},{2,19},{3,18},{16,1},{17,0},{18,3},{19,2},{4,21},{5,... | collective-permute-start | bytes 368648 | tf_op jit(solution)/shard_map/ppermute | solution.py:252
  58.1 6.3 %collective-permute-start.10 = (bf16[4,24,640]{2,1,0:T(8,128)(2,1)S(1)}, bf16[4,24,640]{2,1,0:T(8,128)(2,1)S(1)}, u32[]{:S(2)}, u32[]{:S(2)}) collective-permute-start(bf16[4,24,640]{2,1,0:T(8,128)(2,1)S(1)} %get-tuple-element.19), channel_id=1, source_target_pairs={{0,18},{1,19},{2,16},{3,17},{16,2},{17,3},{18,0},{19,1},{4,22},{5,... | collective-permute-start | bytes 368648 | tf_op jit(solution)/shard_map/ppermute | solution.py:252
  61.0 6.1 %collective-permute-start.11 = (bf16[4,24,640]{2,1,0:T(8,128)(2,1)S(1)}, bf16[4,24,640]{2,1,0:T(8,128)(2,1)S(1)}, u32[]{:S(2)}, u32[]{:S(2)}) collective-permute-start(bf16[4,24,640]{2,1,0:T(8,128)(2,1)S(1)} %get-tuple-element.20), channel_id=1, source_target_pairs={{0,19},{1,18},{2,17},{3,16},{16,3},{17,2},{18,1},{19,0},{4,23},{5,... | collective-permute-start | bytes 368648 | tf_op jit(solution)/shard_map/ppermute | solution.py:252

commit v5 on v4

--- a/solution.py
+++ b/solution.py
@@ -33,26 +33,26 @@
     return lax.ppermute(x, axis, [(i, partner(i, distance, size)) for i in range(size)])
 
 
-def pack_kernel(groups, owners, x_ref, out_ref):
+def pack_kernel(parts, x_ref, out_ref):
     members, rows, cells, channels = x_ref.shape
-    width = channels // (groups * owners)
+    na, nb, nc, nd = parts
+    width = channels // (na * nb * nc * nd)
     for e in range(members):
-        for q in range(groups):
-            parts = [
-                x_ref[e, i, :, (p * groups + q) * width : (p * groups + q + 1) * width]
-                for i in range(rows)
-                for p in range(owners)
-            ]
-            block = jnp.concatenate(parts, axis=-1)
-            for p in range(owners):
-                out_ref[e, p, q] = block
-
-
-def pack(x, groups, owners):
+        for b in range(nb):
+            for d in range(nd):
+                firsts = [(((a * nb + b) * nc + c) * nd + d) * width for a in range(na) for c in range(nc)]
+                taken = [x_ref[e, i, :, at : at + width] for i in range(rows) for at in firsts]
+                block = jnp.concatenate(taken, axis=-1)
+                for a in range(na):
+                    out_ref[e, a, b, d] = block
+
+
+def pack(x, parts):
     members, rows, cells, channels = x.shape
+    na, nb, _, nd = parts
     return pl.pallas_call(
-        functools.partial(pack_kernel, groups, owners),
-        out_shape=jax.ShapeDtypeStruct((members, owners, groups, cells, rows * channels // groups), x.dtype),
+        functools.partial(pack_kernel, parts),
+        out_shape=jax.ShapeDtypeStruct((members, na, nb, nd, cells, rows * channels // (nb * nd)), x.dtype),
         in_specs=[VMEM_SPEC],
         out_specs=VMEM_SPEC,
         compiler_params=pltpu.CompilerParams(vmem_limit_bytes=LIMIT),
@@ -70,33 +70,41 @@
 def conv_mix_kernel(geometry, counts, low_ref, shift_ref, place_ref, *refs):
     bases, taps, slots, halo, sub, groups = geometry
     refs = list(refs)
-    fields_ref = refs.pop(0)
-    weight_refs = [refs.pop(0) for _ in range(counts[0])]
-    mix_slots = [[refs.pop(0) for _ in range(n)] for n in counts[1]]
+    field_refs = [refs.pop(0) for _ in range(counts[0])]
+    weight_refs = [refs.pop(0) for _ in range(counts[1])]
+    mix_slots = [[refs.pop(0) for _ in range(n)] for n in counts[2]]
     field_rows, total, mix_all, mixed = refs[-4:]
     outs = refs[:-4]
-    late, owners, span, _ = fields_ref.shape
+    late, na, nb, stripe, _ = field_refs[0].shape
+    nc = len(field_refs)
+    span = nb * stripe
+    owners = len(mix_slots)
     depth, width = mix_slots[0][0].shape[1:]
     channels = owners * depth
     padded = total.shape[-1]
     rows, _, block, _ = weight_refs[0].shape
-    nblocks = owners * span // block
+    nblocks = field_rows.shape[1] // block
     cells = span // groups
-    member, owner, group = place_ref[0], place_ref[1], place_ref[2]
+    member, place_a, place_c, group = [place_ref[i] for i in range(4)]
 
     total[...] = jnp.zeros_like(total)
     field_rows[...] = jnp.zeros_like(field_rows)
     for s in range(late):
         lat = partner_in_kernel(member, s, late)
-        for p in range(owners):
-            value = fields_ref[lat, p]
-            for r in range(rows):
-                field_rows[r, p * span : (p + 1) * span, :channels] = value[:, r * channels : (r + 1) * channels]
+        for a in range(na):
+            for b in range(nb):
+                for dc, ref in enumerate(field_refs):
+                    stripe_at = (a * nb + b) * nc + partner_in_kernel(place_c, dc, nc)
+                    at = pl.ds(pl.multiple_of(stripe_at * stripe, sub), stripe)
+                    value = ref[lat, a, b]
+                    for r in range(rows):
+                        field_rows[r, at, :channels] = value[:, r * channels : (r + 1) * channels]
 
         def one_row(r, carry):
             row = lat * rows + r
             for piece in range(span // sub):
-                cell = owner * span + piece * sub
+                b_at, in_stripe = divmod(piece * sub, stripe)
+                cell = ((place_a * nb + b_at) * nc + place_c) * stripe + in_stripe
                 b = lax.div(cell, block)
                 q = pl.multiple_of(lax.rem(cell, block), sub)
                 chosen = []
@@ -116,7 +124,7 @@
 
     for d, slot in enumerate(mix_slots):
         for k in range(bases):
-            mix_all[place_ref[3 + d], k] = added(slot, k)
+            mix_all[place_ref[4 + d], k] = added(slot, k)
     fill = jnp.zeros((padded - channels, width), jnp.bfloat16)
     matrix = jnp.concatenate(
         [x for k in range(bases) for x in [mix_all[p, k] for p in range(owners)] + [fill]], axis=0
@@ -144,24 +152,27 @@
 def conv_mix(low, shift, place, fields, weights, mix, halo, groups, block):
     bases, all_rows = low.shape
     slots = shift.shape[1]
-    late, owners, span, _ = fields.shape
+    late, na, nb, stripe, _ = fields[0].shape
+    span = nb * stripe
+    longitudes = na * len(fields) * span
+    owners = len(mix)
     rows = all_rows // late
     depth, width = mix[0][0].shape[1:]
     padded = -(-owners * depth // LANES) * LANES
     taps = weights[0].shape[1] // bases
-    sub = math.gcd(span, block)
+    sub = math.gcd(stripe, block)
     shapes = [jax.ShapeDtypeStruct((rows, span // groups, width), jnp.bfloat16)] * (late * groups)
     if halo:
         shapes.append(jax.ShapeDtypeStruct((2, halo, span, width), jnp.bfloat16))
-    operands = [fields] + weights + [x for slot in mix for x in slot]
-    counts = (len(weights), [len(s) for s in mix])
+    operands = fields + weights + [x for slot in mix for x in slot]
+    counts = (len(fields), len(weights), [len(s) for s in mix])
     return pl.pallas_call(
         functools.partial(conv_mix_kernel, (bases, taps, slots, halo, sub, groups), counts),
         out_shape=shapes,
         in_specs=[SMEM_SPEC] * 3 + [VMEM_SPEC] * len(operands),
         out_specs=[VMEM_SPEC] * len(shapes),
         scratch_shapes=[
-            VMEM((rows, owners * span, padded), jnp.bfloat16),
+            VMEM((rows, longitudes, padded), jnp.bfloat16),
             VMEM((bases, all_rows + 2 * HALO, span, padded), jnp.float32),
             VMEM((owners, bases, depth, width), jnp.bfloat16),
             VMEM((all_rows, span, width), jnp.float32),
@@ -199,42 +210,42 @@
     return [own] + [trade(own, "late", s, late) for s in range(1, late)]
 
 
-def gather_mix(mix, late, owners):
-    core, own = lax.axis_index("late"), lax.axis_index("lonp")
-    if owners == 4 and late == 2:
-        def fetch(distances):
-            route = [
-                (c * owners + p, c * owners + (p ^ d)) for p in range(owners) for c, d in enumerate(distances(p)) if d
-            ]
-            return lax.ppermute(mix, ("late", "lonp"), route)
-
-        first = fetch(lambda p: (1, 2))
-        third = fetch(lambda p: (3, 0) if p in (0, 3) else (0, 3))
+def gather_mix(mix, late, na, nc):
+    core, own = lax.axis_index("late"), lax.axis_index("a") * nc + lax.axis_index("c")
+    owners = na * nc
+    if na == nc == late == 2:
+        route = [(p, p ^ 2) for p in range(4)] + [(4 + p, 4 + (p ^ 1)) for p in range(4)]
+        first = lax.ppermute(mix, ("late", "a", "c"), route)
+        third = lax.ppermute(mix, ("late", "a", "c"), [(4 + p, 4 + (p ^ 3)) for p in range(4)])
         other = trade(first, "late", 1, late)
-        copied = trade(third, "late", 1, late)
-        return [[mix], [first], [other], [third, copied]], [own, own ^ (1 + core), own ^ (2 - core), own ^ 3]
-    slots = [[mix]] + [[trade(mix, "lonp", d, owners)] for d in range(1, owners)]
+        copied = lax.ppermute(third, "late", [(1, 0)])
+        return [[mix], [first], [other], [third, copied]], [own, own ^ (2 - core), own ^ (1 + core), own ^ 3]
+    slots = [[mix]] + [[trade(mix, ("a", "c"), d, owners)] for d in range(1, owners)]
     return slots, [partner(own, d, owners) for d in range(owners)]
 
 
 def per_device(sizes, fields, kernel, band_low, block_shift, mix_weight):
-    halves, late, owners, groups = sizes
+    halves, late, na, nb, nc, nd = sizes
+    groups = nb * nd
     members, rows, channels, cells = fields.shape
-    bases, _, taps, slots, block, _ = kernel.shape
+    block = kernel.shape[-1]
     all_rows = late * rows
     halo = HALO if halves > 1 else 0
 
-    packed = pack(fields.transpose(0, 1, 3, 2), groups, owners)
-    packed = packed.reshape((-1,) + packed.shape[3:])
-    spread = lax.all_to_all(packed, ("late", "lonp", "lonq"), split_axis=0, concat_axis=0, tiled=True)
-    spread = spread.reshape(late, owners, groups * cells, -1)
+    packed = pack(fields.transpose(0, 1, 3, 2), sizes[2:])
+    packed = packed.reshape((-1,) + packed.shape[4:])
+    spread = lax.all_to_all(packed, ("late", "a", "b", "d"), split_axis=0, concat_axis=0, tiled=True)
     weights = both_kernels(kernel, late)
-    mix, origins = gather_mix(mix_weight, late, owners)
+    mix_weight, spread = lax.optimization_barrier((mix_weight, spread))
+    spread = spread.reshape(late, na, nb, nd * cells, -1)
+    spread = [spread] + [trade(spread, "c", s, nc) for s in range(1, nc)]
+    mix, origins = gather_mix(mix_weight, late, na, nc)
 
     start = lax.axis_index("lath") * all_rows
     low = lax.dynamic_slice_in_dim(band_low, start, all_rows, 1)
     shift = lax.dynamic_slice_in_dim(block_shift, start, all_rows, 0)
-    place = [lax.axis_index("late"), lax.axis_index("lonp"), lax.axis_index("lonq")] + origins
+    group = lax.axis_index("b") * nd + lax.axis_index("d")
+    place = [lax.axis_index("late"), lax.axis_index("a"), lax.axis_index("c"), group] + origins
     place = jnp.stack(place).astype(jnp.int32)
     partial = conv_mix(low, shift, place, spread, weights, mix, halo, groups, block)
     if halo:
@@ -246,12 +257,11 @@
         for dl in range(late):
             lat = partner(lax.axis_index("late"), dl, late)
             for dq in range(groups):
-                group = partner(lax.axis_index("lonq"), dq, groups)
-                partial[dl * groups + dq] += extra[lat, :, group]
+                partial[dl * groups + dq] += extra[lat, :, partner(group, dq, groups)]
     parts = [
         lax.ppermute(
             partial[dl * groups + dq],
-            ("late", "lonq"),
+            ("late", "b", "d"),
             [
                 (l * groups + q, partner(l, dl, late) * groups + partner(q, dq, groups))
                 for l in range(late)
@@ -268,13 +278,13 @@
 
 def solution(mesh):
     lat, lon = mesh.shape["lat"], mesh.shape["lon"]
-    groups = max(g for g in range(1, lon + 1) if lon % g == 0 and g * g <= lon)
+    halves = [2 if lon % 8 == 0 else 1] * 3
 
     def whole(fields, kernel, band_low, block_shift, mix_weight):
         late = fields.shape[0]
-        sizes = (lat // late, late, lon // groups, groups)
-        split = Mesh(mesh.devices.reshape(sizes), ("lath", "late", "lonp", "lonq"))
-        rows, cells = ("lath", "late"), ("lonp", "lonq")
+        sizes = (lat // late, late, lon // math.prod(halves), *halves)
+        split = Mesh(mesh.devices.reshape(sizes), ("lath", "late", "a", "b", "c", "d"))
+        rows, cells = ("lath", "late"), ("a", "b", "c", "d")
         return jax.shard_map(
             functools.partial(per_device, sizes),
             mesh=split,

time: 69.2 us -> 74.5 us (1.077)
  blocking collectives: 0 us -> 21.9 us
  starting transfers between devices: 30 us -> 13.4 us
  waiting for transfers between devices: 19.2 us -> 21.4 us
  Pallas kernels: 10.7 us -> 9.71 us
  local copies, waits for them, and re-layouts: 8.62 us -> 7.7 us
    all_to_all x0 -> x1, blocking collectives: none -> 21.9 us  [per_device(): lax.all_to_all(packed, ('late', 'a', 'b', 'd'), split_axis=0, concat_axis...]
    ppermute x3, starting transfers between devices: 11 us -> 3.31 us  [trade(): lax.ppermute(x, axis, [(i, partner(i, distance, size)) for i in range(siz...]
    all_to_all x1 -> x0, starting transfers between devices: 7.3 us -> none  [per_device(): lax.all_to_all(packed, ('late', 'lonp', 'lonq'), split_axis=0, concat_axi...]
    ppermute x9 -> x10, waiting for transfers between devices: 17.5 us -> 20.3 us  [the longest x1 12.5 us: gather_mix(): first = lax.ppermute(mix, ('late', 'a', 'c'), route)]
    ppermute x9 -> x10, starting transfers between devices: 11.6 us -> 10.1 us  [the longest x7 8.11 us: per_device(): lax.ppermute(partial[dl * groups + dq], ('late', 'b', 'd'), [(l * groups...]
    pallas_call x1, Pallas kernels: 1.35 us -> 0.39 us  [pack(): pl.pallas_call(functools.partial(pack_kernel, parts), out_shape=jax.Shape...]
    unnamed x9, local copies, waits for them, and re-layouts: 1.04 us -> 0.1 us
  transfers between devices with their start and end apart: 13 -> 13, of which waited for: 8 -> 8; matrix products, arithmetic and copies ran while one was open for 11% -> 0% of each run, Pallas kernels for 0% -> 1%
where the time goes in v5:
time: 74.5 us; the launch traced here: 74.2 us
  blocking collectives  21.9 us (29%)
  waiting for transfers between devices  21.4 us (29%)
  starting transfers between devices  13.4 us (18%)
  Pallas kernels  9.71 us (13%)
  local copies, waits for them, and re-layouts  7.7 us (10%)
    all_to_all x1, blocking collectives, per_device(): lax.all_to_all(packed, ('late', 'a', 'b', 'd'), split_axis=0, concat_axis...  21.9 us
    ppermute x1, waiting for transfers between devices, gather_mix(): first = lax.ppermute(mix, ('late', 'a', 'c'), route)  12.5 us
    ppermute x7, starting transfers between devices, per_device(): lax.ppermute(partial[dl * groups + dq], ('late', 'b', 'd'), [(l * groups...  8.11 us
    pallas_call x1, Pallas kernels, conv_mix(): pl.pallas_call(functools.partial(conv_mix_kernel, (bases, taps, slots, ha...  7.87 us
    ppermute x7, waiting for transfers between devices, per_device(): lax.ppermute(partial[dl * groups + dq], ('late', 'b', 'd'), [(l * groups...  7.55 us
    transpose x1, local copies, waits for them, and re-layouts, both_kernels(): kernel.transpose(1, 0, 2, 5, 3, 4)  4.18 us
    reshape x1, local copies, waits for them, and re-layouts, both_kernels(): kernel.transpose(1, 0, 2, 5, 3, 4)  3.34 us
    ppermute x3, starting transfers between devices, trade(): lax.ppermute(x, axis, [(i, partner(i, distance, size)) for i in range(siz...  3.31 us
  transfers between devices with their start and end apart: 13, of which 8 were waited for; matrix products, arithmetic and copies ran while one was open for 0% of the time, Pallas kernels for 1%

profile of v5, /device:TPU:0, one launch (start us, length us, event | category | flops | bytes accessed | tf_op | source)
XLA Modules:
  0.0 74.2 jit_solution(4910223561103048597)
XLA Ops:
  0.0 4.2 %copy.8 = bf16[4,5,3,64,3,64]{3,5,4,2,1,0:T(8,128)(2,1)} copy(bf16[4,5,3,64,3,64]{3,5,4,2,0,1:T(8,128)(2,1)} %bitcast.18) | data formatting | bytes 2949120 | tf_op jit(solution)/shard_map/transpose | solution.py:209
  4.2 0.0 copy-start.1
  4.2 0.0 copy-start
  4.2 0.0 copy-start.3
  4.2 0.0 copy-start.2
  4.2 3.3 %copy.11.refs_2_ = bf16[4,15,64,192]{3,2,1,0:T(8,128)(2,1)S(1)} copy(bf16[4,15,64,192]{2,3,1,0:T(8,128)(2,1)} %bitcast.17) | data formatting | bytes 2949120 | tf_op jit(solution)/shard_map/reshape | solution.py:209
  7.5 0.5 collective-permute-start.1
  8.1 0.0 copy-done.1
  8.1 0.4 pack.1
  8.5 21.9 %all_to_all.5 = bf16[16,24,640]{2,1,0:T(8,128)(2,1)S(1)} all-to-all(bf16[16,24,640]{2,1,0:T(8,128)(2,1)S(1)} %bitcast.15), channel_id=1, replica_groups=mesh['lath'=1,'late'=2,'a'=2,'b'=2,'c'=2,'d'=2] {'late','a','b','d'}, dimensions={0} | all-to-all | bytes 983040 | tf_op jit(solution)/shard_map/all_to_all | solution.py:237
  30.4 0.0 copy-done
  30.4 0.7 collective-permute-start.4
  31.1 0.1 collective-permute-start.2
  31.2 1.6 %collective-permute-start = (bf16[2,2,2,48,640]{4,3,2,1,0:T(8,128)(2,1)S(1)}, bf16[2,2,2,48,640]{4,3,2,1,0:T(8,128)(2,1)S(1)}, u32[]{:S(2)}, u32[]{:S(2)}) collective-permute-start(bf16[2,2,2,48,640]{4,3,2,1,0:T(8,128)(2,1)S(1)} %bitcast.13), channel_id=1, source_target_pairs={{0,2},{2,0},{1,3},{3,1},{4,6},{6,4},{5,7},{7,5},{8,10},{10,8},{9,1... | collective-permute-start | bytes 1474568 | tf_op jit(solution)/shard_map/ppermute | solution.py:33
  32.7 0.0 collective-permute-done.4.refs_7_
  32.7 1.3 %collective-permute-start.5 = (bf16[5,40,640]{2,1,0:T(8,128)(2,1)S(1)}, bf16[5,40,640]{2,1,0:T(8,128)(2,1)}, u32[]{:S(2)}, u32[]{:S(2)}) collective-permute-start(bf16[5,40,640]{2,1,0:T(8,128)(2,1)S(1)} %collective-permute-done.4.refs_7_), channel_id=1, source_target_pairs={{16,0},{17,1},{18,2},{19,3},{20,4},{21,5},{22,6},{23,7},{24,8},{25... | collective-permute-start | bytes 768008 | tf_op jit(solution)/shard_map/ppermute | solution.py:221
  34.0 12.5 %collective-permute-done.2.refs_5_ = bf16[5,40,640]{2,1,0:T(8,128)(2,1)} collective-permute-done((bf16[5,40,640]{2,1,0:T(8,128)(2,1)S(1)}, bf16[5,40,640]{2,1,0:T(8,128)(2,1)}, u32[]{:S(2)}, u32[]{:S(2)}) %collective-permute-start.2) | collective-permute-done | bytes 256032 | tf_op jit(solution)/shard_map/ppermute | solution.py:218
  46.5 1.2 %collective-permute-start.3 = (bf16[5,40,640]{2,1,0:T(8,128)(2,1)}, bf16[5,40,640]{2,1,0:T(8,128)(2,1)}, u32[]{:S(2)}, u32[]{:S(2)}) collective-permute-start(bf16[5,40,640]{2,1,0:T(8,128)(2,1)} %collective-permute-done.2.refs_5_), channel_id=1, source_target_pairs={{0,16},{16,0},{1,17},{17,1},{2,18},{18,2},{3,19},{19,3},{4,20},{20... | collective-permute-start | bytes 768008 | tf_op jit(solution)/shard_map/ppermute | solution.py:33
  47.7 0.0 copy-done.3
  47.7 0.1 copy.10.shift_ref
  47.8 0.1 stack.35.place_ref
  47.9 0.0 collective-permute-done.refs_1_
  47.9 0.2 collective-permute-done.5.refs_8_
  48.2 1.1 %collective-permute-done.3.refs_6_ = bf16[5,40,640]{2,1,0:T(8,128)(2,1)} collective-permute-done((bf16[5,40,640]{2,1,0:T(8,128)(2,1)}, bf16[5,40,640]{2,1,0:T(8,128)(2,1)}, u32[]{:S(2)}, u32[]{:S(2)}) %collective-permute-start.3) | collective-permute-done | bytes 256032 | tf_op jit(solution)/shard_map/ppermute | solution.py:33
  49.2 0.0 collective-permute-done.1.refs_3_
  49.2 0.0 copy-done.2
  49.2 7.9 %conv_mix.1 = (bf16[4,24,640]{2,1,0:T(8,128)(2,1)S(1)}, bf16[4,24,640]{2,1,0:T(8,128)(2,1)S(1)}, bf16[4,24,640]{2,1,0:T(8,128)(2,1)S(1)}, bf16[4,24,640]{2,1,0:T...) custom-call(s32[5,8]{1,0:T(8,128)S(1)} %copy-done.2, ...), custom_call_target="tpu_custom_call" | custom-call | tf_op jit(solution)/shard_map/conv_mix/pallas_call | solution.py:169
  57.1 0.6 collective-permute-start.6
  57.8 0.0 collective-permute-start.7
  57.8 2.9 %collective-permute-start.8 = (bf16[4,24,640]{2,1,0:T(8,128)(2,1)S(1)}, bf16[4,24,640]{2,1,0:T(8,128)(2,1)S(1)}, u32[]{:S(2)}, u32[]{:S(2)}) collective-permute-start(bf16[4,24,640]{2,1,0:T(8,128)(2,1)S(1)} %get-tuple-element.20), channel_id=1, source_target_pairs={{0,5},{1,4},{4,1},{5,0},{16,21},{17,20},{20,17},{21,16},{2,7},{3,6... | collective-permute-start | bytes 368648 | tf_op jit(solution)/shard_map/ppermute | solution.py:262
  60.7 0.6 collective-permute-start.9
  61.3 1.0 %collective-permute-start.10 = (bf16[4,24,640]{2,1,0:T(8,128)(2,1)S(1)}, bf16[4,24,640]{2,1,0:T(8,128)(2,1)S(1)}, u32[]{:S(2)}, u32[]{:S(2)}) collective-permute-start(bf16[4,24,640]{2,1,0:T(8,128)(2,1)S(1)} %get-tuple-element.22), channel_id=1, source_target_pairs={{0,17},{1,16},{4,21},{5,20},{16,1},{17,0},{20,5},{21,4},{2,19},{3,... | collective-permute-start | bytes 368648 | tf_op jit(solution)/shard_map/ppermute | solution.py:262
  62.2 0.8 %collective-permute-done.6.refs_1_ = bf16[4,24,640]{2,1,0:T(8,128)(2,1)S(1)} collective-permute-done((bf16[4,24,640]{2,1,0:T(8,128)(2,1)S(1)}, bf16[4,24,640]{2,1,0:T(8,128)(2,1)S(1)}, u32[]{:S(2)}, u32[]{:S(2)}) %collective-permute-start.6) | collective-permute-done | bytes 122912 | tf_op jit(solution)/shard_map/ppermute | solution.py:262
  63.0 0.5 collective-permute-start.11
  63.5 0.0 collective-permute-done.7.refs_2_
  63.5 2.5 %collective-permute-start.12 = (bf16[4,24,640]{2,1,0:T(8,128)(2,1)S(1)}, bf16[4,24,640]{2,1,0:T(8,128)(2,1)S(1)}, u32[]{:S(2)}, u32[]{:S(2)}) collective-permute-start(bf16[4,24,640]{2,1,0:T(8,128)(2,1)S(1)} %get-tuple-element.24), channel_id=1, source_target_pairs={{0,21},{1,20},{4,17},{5,16},{16,5},{17,4},{20,1},{21,0},{2,23},{3,... | collective-permute-start | bytes 368648 | tf_op jit(solution)/shard_map/ppermute | solution.py:262
  66.0 1.4 %collective-permute-done.8.refs_3_ = bf16[4,24,640]{2,1,0:T(8,128)(2,1)S(1)} collective-permute-done((bf16[4,24,640]{2,1,0:T(8,128)(2,1)S(1)}, bf16[4,24,640]{2,1,0:T(8,128)(2,1)S(1)}, u32[]{:S(2)}, u32[]{:S(2)}) %collective-permute-start.8) | collective-permute-done | bytes 122912 | tf_op jit(solution)/shard_map/ppermute | solution.py:262
  67.4 0.0 collective-permute-done.9.refs_4_
  67.4 1.9 %collective-permute-done.10.refs_5_ = bf16[4,24,640]{2,1,0:T(8,128)(2,1)S(1)} collective-permute-done((bf16[4,24,640]{2,1,0:T(8,128)(2,1)S(1)}, bf16[4,24,640]{2,1,0:T(8,128)(2,1)S(1)}, u32[]{:S(2)}, u32[]{:S(2)}) %collective-permute-start.10) | collective-permute-done | bytes 122912 | tf_op jit(solution)/shard_map/ppermute | solution.py:262
  69.3 0.1 collective-permute-done.11.refs_6_
  69.4 3.4 %collective-permute-done.12.refs_7_ = bf16[4,24,640]{2,1,0:T(8,128)(2,1)S(1)} collective-permute-done((bf16[4,24,640]{2,1,0:T(8,128)(2,1)S(1)}, bf16[4,24,640]{2,1,0:T(8,128)(2,1)S(1)}, u32[]{:S(2)}, u32[]{:S(2)}) %collective-permute-start.12) | collective-permute-done | bytes 122912 | tf_op jit(solution)/shard_map/ppermute | solution.py:262
  72.8 1.4 %finish.1 = bf16[2,4,24,640]{3,2,1,0:T(8,128)(2,1)} custom-call(s32[8]{0:T(128)S(1)} %stack.35.place_ref, bf16[4,24,640]{2,1,0:T(8,128)(2,1)S(1)} %get-tuple-element.17.refs_0_, bf16[4,24,640]{2,1,0:T(8,128)(2,1)S(1)} %collective-permute-done.6.refs_1_, bf16[4,24,640]{2,1,0:T(8,128)(2,1)S(1)} %collective-permute-done.7.refs_2_, ...), custom_call_target="tpu_custom_call" | custom-call | tf_op jit(solution)/shard_map/finish/pallas_call | solution.py:197
Async XLA Ops:
  4.2 3.9 %copy-start.1 = (bf16[2,4,640,24]{2,3,1,0:T(8,128)(2,1)S(1)}, bf16[2,4,640,24]{2,3,1,0:T(8,128)(2,1)}, u32[]{:S(2)}) copy-start(bf16[2,4,640,24]{2,3,1,0:T(8,128)(2,1)} %param.5) | copy-start | bytes 737284
  4.2 26.2 %copy-start = (bf16[5,40,640]{2,1,0:T(8,128)(2,1)S(1)}, bf16[5,40,640]{2,1,0:T(8,128)(2,1)}, u32[]{:S(2)}) copy-start(bf16[5,40,640]{2,1,0:T(8,128)(2,1)} %refs_4_) | copy-start | bytes 768004
  4.2 43.6 %copy-start.3 = (s32[8,3]{0,1:T(4,128)S(1)}, s32[8,3]{0,1:T(4,128)}, u32[]{:S(2)}) copy-start(s32[8,3]{0,1:T(4,128)} %param.8) | copy-start | bytes 292
  4.2 45.1 %copy-start.2 = (s32[5,8]{1,0:T(8,128)S(1)}, s32[5,8]{1,0:T(8,128)}, u32[]{:S(2)}) copy-start(s32[5,8]{1,0:T(8,128)} %low_ref) | copy-start | bytes 484
  7.5 41.7 %collective-permute-start.1 = (bf16[4,15,64,192]{3,2,1,0:T(8,128)(2,1)S(1)}, bf16[4,15,64,192]{3,2,1,0:T(8,128)(2,1)}, u32[]{:S(2)}, u32[]{:S(2)}) collective-permute-start(bf16[4,15,64,192]{3,2,1,0:T(8,128)(2,1)S(1)} %copy.11.refs_2_), channel_id=1, source_target_pairs={{0,16},{16,0},{1,17},{17,1},{2,18},{18,2},{3,19},{19,3},{4,20},{20... | collective-permute-start | bytes 4423688 | tf_op jit(solution)/shard_map/ppermute | solution.py:33
  30.4 2.3 %collective-permute-start.4 = (bf16[5,40,640]{2,1,0:T(8,128)(2,1)S(1)}, bf16[5,40,640]{2,1,0:T(8,128)(2,1)S(1)}, u32[]{:S(2)}, u32[]{:S(2)}) collective-permute-start(bf16[5,40,640]{2,1,0:T(8,128)(2,1)S(1)} %copy-done), channel_id=1, source_target_pairs={{16,26},{18,24},{24,18},{26,16},{17,27},{19,25},{25,19},{27,17},{2... | collective-permute-start | bytes 768008 | tf_op jit(solution)/shard_map/ppermute | solution.py:219
  31.1 15.5 %collective-permute-start.2 = (bf16[5,40,640]{2,1,0:T(8,128)(2,1)S(1)}, bf16[5,40,640]{2,1,0:T(8,128)(2,1)}, u32[]{:S(2)}, u32[]{:S(2)}) collective-permute-start(bf16[5,40,640]{2,1,0:T(8,128)(2,1)S(1)} %copy-done), channel_id=1, source_target_pairs={{0,8},{2,10},{8,0},{10,2},{16,18},{18,16},{24,26},{26,24},{1,9},{3... | collective-permute-start | bytes 768008 | tf_op jit(solution)/shard_map/ppermute | solution.py:218
  31.2 16.8 %collective-permute-start = (bf16[2,2,2,48,640]{4,3,2,1,0:T(8,128)(2,1)S(1)}, bf16[2,2,2,48,640]{4,3,2,1,0:T(8,128)(2,1)S(1)}, u32[]{:S(2)}, u32[]{:S(2)}) collective-permute-start(bf16[2,2,2,48,640]{4,3,2,1,0:T(8,128)(2,1)S(1)} %bitcast.13), channel_id=1, source_target_pairs={{0,2},{2,0},{1,3},{3,1},{4,6},{6,4},{5,7},{7,5},{8,10},{10,8},{9,1... | collective-permute-start | bytes 1474568 | tf_op jit(solution)/shard_map/ppermute | solution.py:33
  32.7 15.4 %collective-permute-start.5 = (bf16[5,40,640]{2,1,0:T(8,128)(2,1)S(1)}, bf16[5,40,640]{2,1,0:T(8,128)(2,1)}, u32[]{:S(2)}, u32[]{:S(2)}) collective-permute-start(bf16[5,40,640]{2,1,0:T(8,128)(2,1)S(1)} %collective-permute-done.4.refs_7_), channel_id=1, source_target_pairs={{16,0},{17,1},{18,2},{19,3},{20,4},{21,5},{22,6},{23,7},{24,8},{25... | collective-permute-start | bytes 768008 | tf_op jit(solution)/shard_map/ppermute | solution.py:221
  46.5 2.7 %collective-permute-start.3 = (bf16[5,40,640]{2,1,0:T(8,128)(2,1)}, bf16[5,40,640]{2,1,0:T(8,128)(2,1)}, u32[]{:S(2)}, u32[]{:S(2)}) collective-permute-start(bf16[5,40,640]{2,1,0:T(8,128)(2,1)} %collective-permute-done.2.refs_5_), channel_id=1, source_target_pairs={{0,16},{16,0},{1,17},{17,1},{2,18},{18,2},{3,19},{19,3},{4,20},{20... | collective-permute-start | bytes 768008 | tf_op jit(solution)/shard_map/ppermute | solution.py:33
  57.1 5.9 %collective-permute-start.6 = (bf16[4,24,640]{2,1,0:T(8,128)(2,1)S(1)}, bf16[4,24,640]{2,1,0:T(8,128)(2,1)S(1)}, u32[]{:S(2)}, u32[]{:S(2)}) collective-permute-start(bf16[4,24,640]{2,1,0:T(8,128)(2,1)S(1)} %get-tuple-element.18), channel_id=1, source_target_pairs={{0,1},{1,0},{4,5},{5,4},{16,17},{17,16},{20,21},{21,20},{2,3},{3,2... | collective-permute-start | bytes 368648 | tf_op jit(solution)/shard_map/ppermute | solution.py:262
  57.8 5.8 %collective-permute-start.7 = (bf16[4,24,640]{2,1,0:T(8,128)(2,1)S(1)}, bf16[4,24,640]{2,1,0:T(8,128)(2,1)S(1)}, u32[]{:S(2)}, u32[]{:S(2)}) collective-permute-start(bf16[4,24,640]{2,1,0:T(8,128)(2,1)S(1)} %get-tuple-element.19), channel_id=1, source_target_pairs={{0,4},{1,5},{4,0},{5,1},{16,20},{17,21},{20,16},{21,17},{2,6},{3,7... | collective-permute-start | bytes 368648 | tf_op jit(solution)/shard_map/ppermute | solution.py:262
  57.8 9.7 %collective-permute-start.8 = (bf16[4,24,640]{2,1,0:T(8,128)(2,1)S(1)}, bf16[4,24,640]{2,1,0:T(8,128)(2,1)S(1)}, u32[]{:S(2)}, u32[]{:S(2)}) collective-permute-start(bf16[4,24,640]{2,1,0:T(8,128)(2,1)S(1)} %get-tuple-element.20), channel_id=1, source_target_pairs={{0,5},{1,4},{4,1},{5,0},{16,21},{17,20},{20,17},{21,16},{2,7},{3,6... | collective-permute-start | bytes 368648 | tf_op jit(solution)/shard_map/ppermute | solution.py:262
  60.7 6.7 %collective-permute-start.9 = (bf16[4,24,640]{2,1,0:T(8,128)(2,1)S(1)}, bf16[4,24,640]{2,1,0:T(8,128)(2,1)S(1)}, u32[]{:S(2)}, u32[]{:S(2)}) collective-permute-start(bf16[4,24,640]{2,1,0:T(8,128)(2,1)S(1)} %get-tuple-element.21), channel_id=1, source_target_pairs={{0,16},{1,17},{4,20},{5,21},{16,0},{17,1},{20,4},{21,5},{2,18},{3,... | collective-permute-start | bytes 368648 | tf_op jit(solution)/shard_map/ppermute | solution.py:262
  61.3 8.1 %collective-permute-start.10 = (bf16[4,24,640]{2,1,0:T(8,128)(2,1)S(1)}, bf16[4,24,640]{2,1,0:T(8,128)(2,1)S(1)}, u32[]{:S(2)}, u32[]{:S(2)}) collective-permute-start(bf16[4,24,640]{2,1,0:T(8,128)(2,1)S(1)} %get-tuple-element.22), channel_id=1, source_target_pairs={{0,17},{1,16},{4,21},{5,20},{16,1},{17,0},{20,5},{21,4},{2,19},{3,... | collective-permute-start | bytes 368648 | tf_op jit(solution)/shard_map/ppermute | solution.py:262
  63.0 6.4 %collective-permute-start.11 = (bf16[4,24,640]{2,1,0:T(8,128)(2,1)S(1)}, bf16[4,24,640]{2,1,0:T(8,128)(2,1)S(1)}, u32[]{:S(2)}, u32[]{:S(2)}) collective-permute-start(bf16[4,24,640]{2,1,0:T(8,128)(2,1)S(1)} %get-tuple-element.23), channel_id=1, source_target_pairs={{0,20},{1,21},{4,16},{5,17},{16,4},{17,5},{20,0},{21,1},{2,22},{3,... | collective-permute-start | bytes 368648 | tf_op jit(solution)/shard_map/ppermute | solution.py:262
  63.5 9.3 %collective-permute-start.12 = (bf16[4,24,640]{2,1,0:T(8,128)(2,1)S(1)}, bf16[4,24,640]{2,1,0:T(8,128)(2,1)S(1)}, u32[]{:S(2)}, u32[]{:S(2)}) collective-permute-start(bf16[4,24,640]{2,1,0:T(8,128)(2,1)S(1)} %get-tuple-element.24), channel_id=1, source_target_pairs={{0,21},{1,20},{4,17},{5,16},{16,5},{17,4},{20,1},{21,0},{2,23},{3,... | collective-permute-start | bytes 368648 | tf_op jit(solution)/shard_map/ppermute | solution.py:262

commit v6 on v4

--- a/solution.py
+++ b/solution.py
@@ -112,7 +112,7 @@
                     total[k, at, piece * sub : (piece + 1) * sub] += slab
             return carry
 
-        lax.fori_loop(0, rows, one_row, 0)
+        lax.fori_loop(0, rows, one_row, 0, unroll=True)
 
     for d, slot in enumerate(mix_slots):
         for k in range(bases):
@@ -199,7 +199,7 @@
     return [own] + [trade(own, "late", s, late) for s in range(1, late)]
 
 
-def gather_mix(mix, late, owners):
+def gather_mix(mix, kernel, late, owners):
     core, own = lax.axis_index("late"), lax.axis_index("lonp")
     if owners == 4 and late == 2:
         def fetch(distances):
@@ -210,11 +210,12 @@
 
         first = fetch(lambda p: (1, 2))
         third = fetch(lambda p: (3, 0) if p in (0, 3) else (0, 3))
+        kernel, first, third = lax.optimization_barrier((kernel, first, third))
         other = trade(first, "late", 1, late)
         copied = trade(third, "late", 1, late)
-        return [[mix], [first], [other], [third, copied]], [own, own ^ (1 + core), own ^ (2 - core), own ^ 3]
+        return [[mix], [first], [other], [third, copied]], [own, own ^ (1 + core), own ^ (2 - core), own ^ 3], kernel
     slots = [[mix]] + [[trade(mix, "lonp", d, owners)] for d in range(1, owners)]
-    return slots, [partner(own, d, owners) for d in range(owners)]
+    return slots, [partner(own, d, owners) for d in range(owners)], kernel
 
 
 def per_device(sizes, fields, kernel, band_low, block_shift, mix_weight):
@@ -228,8 +229,8 @@
     packed = packed.reshape((-1,) + packed.shape[3:])
     spread = lax.all_to_all(packed, ("late", "lonp", "lonq"), split_axis=0, concat_axis=0, tiled=True)
     spread = spread.reshape(late, owners, groups * cells, -1)
+    mix, origins, kernel = gather_mix(mix_weight, kernel, late, owners)
     weights = both_kernels(kernel, late)
-    mix, origins = gather_mix(mix_weight, late, owners)
 
     start = lax.axis_index("lath") * all_rows
     low = lax.dynamic_slice_in_dim(band_low, start, all_rows, 1)

time: 69.2 us -> 80.2 us (1.16)
  waiting for transfers between devices: 19.2 us -> 35.8 us
  starting transfers between devices: 30 us -> 23.7 us
  local copies, waits for them, and re-layouts: 8.62 us -> 10.3 us
  Pallas kernels: 10.7 us -> 9.37 us
    ppermute x2, waiting for transfers between devices: 8.39 us -> 22.7 us  [fetch(): return lax.ppermute(mix, ('late', 'lonp'), route)]
    ppermute x3, starting transfers between devices: 11 us -> 4.62 us  [trade(): lax.ppermute(x, axis, [(i, partner(i, distance, size)) for i in range(siz...]
    ppermute x3, waiting for transfers between devices: 1.7 us -> 4 us  [trade(): lax.ppermute(x, axis, [(i, partner(i, distance, size)) for i in range(siz...]
    unnamed x9 -> x13, local copies, waits for them, and re-layouts: 1.04 us -> 2.72 us
    pallas_call x1, Pallas kernels: 7.91 us -> 6.57 us  [conv_mix(): pl.pallas_call(functools.partial(conv_mix_kernel, (bases, taps, slots, ha...]
  transfers between devices with their start and end apart: 13 -> 13, of which waited for: 8 -> 9; matrix products, arithmetic and copies ran while one was open for 11% -> 10% of each run, Pallas kernels for 0% -> 0%
where the time goes in v6:
time: 80.2 us; the launch traced here: 79.3 us
  waiting for transfers between devices  35.8 us (45%)
  starting transfers between devices  23.7 us (30%)
  local copies, waits for them, and re-layouts  10.3 us (13%)
  Pallas kernels  9.37 us (12%)
    ppermute x2, waiting for transfers between devices, fetch(): return lax.ppermute(mix, ('late', 'lonp'), route)  22.7 us
    ppermute x7, waiting for transfers between devices, per_device(): lax.ppermute(partial[dl * groups + dq], ('late', 'lonq'), [(l * groups +...  9.12 us
    all_to_all x1, starting transfers between devices, per_device(): lax.all_to_all(packed, ('late', 'lonp', 'lonq'), split_axis=0, concat_axi...  7.3 us
    pallas_call x1, Pallas kernels, conv_mix(): pl.pallas_call(functools.partial(conv_mix_kernel, (bases, taps, slots, ha...  6.57 us
    ppermute x2, starting transfers between devices, fetch(): return lax.ppermute(mix, ('late', 'lonp'), route)  6.1 us
    ppermute x7, starting transfers between devices, per_device(): lax.ppermute(partial[dl * groups + dq], ('late', 'lonq'), [(l * groups +...  5.69 us
    ppermute x3, starting transfers between devices, trade(): lax.ppermute(x, axis, [(i, partner(i, distance, size)) for i in range(siz...  4.62 us
    transpose x1, local copies, waits for them, and re-layouts, both_kernels(): kernel.transpose(1, 0, 2, 5, 3, 4)  4.16 us
  transfers between devices with their start and end apart: 13, of which 9 were waited for; matrix products, arithmetic and copies ran while one was open for 10% of the time, Pallas kernels for 0%

profile of v6, /device:TPU:0, one launch (start us, length us, event | category | flops | bytes accessed | tf_op | source)
XLA Modules:
  0.0 79.3 jit_solution(3523943081733694911)
XLA Ops:
  0.0 0.0 copy-start
  0.0 0.0 copy-start.3
  0.0 1.0 %copy-done.3 = bf16[2,4,640,24]{2,3,1,0:T(8,128)(2,1)S(1)} copy-done((bf16[2,4,640,24]{2,3,1,0:T(8,128)(2,1)S(1)}, bf16[2,4,640,24]{2,3,1,0:T(8,128)(2,1)}, u32[]{:S(2)}) %copy-start.3) | copy-done | bytes 245784
  1.0 1.4 %pack.1 = bf16[2,4,4,24,640]{4,3,2,1,0:T(8,128)(2,1)} custom-call(bf16[2,4,24,640]{3,2,1,0:T(8,128)(2,1)S(1)} %bitcast.12), custom_call_target="tpu_custom_call" | custom-call | tf_op jit(solution)/shard_map/pack/pallas_call | solution.py:53
  2.3 7.3 %all-to-all-start = ((bf16[32,24,640]{2,1,0:T(8,128)(2,1)}), bf16[32,24,640]{2,1,0:T(8,128)(2,1)S(1)}, u32[]{:S(2)}, u32[]{:S(2)}) async-start(bf16[32,24,640]{2,1,0:T(8,128)(2,1)} %bitcast.7), calls=%async_computation | async-start | bytes 1966080 | tf_op jit(solution)/shard_map/all_to_all | solution.py:230
  9.6 0.0 copy-done
  9.7 1.8 %collective-permute-start = (bf16[5,40,640]{2,1,0:T(8,128)(2,1)S(1)}, bf16[5,40,640]{2,1,0:T(8,128)(2,1)S(1)}, u32[]{:S(2)}, u32[]{:S(2)}) collective-permute-start(bf16[5,40,640]{2,1,0:T(8,128)(2,1)S(1)} %copy-done), channel_id=1, source_target_pairs={{0,4},{16,24},{4,0},{20,28},{8,12},{24,16},{12,8},{28,20},{1,5},{1... | collective-permute-start | bytes 768008 | tf_op jit(solution)/shard_map/ppermute | solution.py:209
  11.5 4.3 %collective-permute-start.1 = (bf16[5,40,640]{2,1,0:T(8,128)(2,1)S(1)}, bf16[5,40,640]{2,1,0:T(8,128)(2,1)S(1)}, u32[]{:S(2)}, u32[]{:S(2)}) collective-permute-start(bf16[5,40,640]{2,1,0:T(8,128)(2,1)S(1)} %copy-done), channel_id=1, source_target_pairs={{0,12},{20,24},{24,20},{12,0},{1,13},{21,25},{25,21},{13,1},{2,14}... | collective-permute-start | bytes 768008 | tf_op jit(solution)/shard_map/ppermute | solution.py:209
  15.8 16.0 %collective-permute-done.refs_4_ = bf16[5,40,640]{2,1,0:T(8,128)(2,1)S(1)} collective-permute-done((bf16[5,40,640]{2,1,0:T(8,128)(2,1)S(1)}, bf16[5,40,640]{2,1,0:T(8,128)(2,1)S(1)}, u32[]{:S(2)}, u32[]{:S(2)}) %collective-permute-start) | collective-permute-done | bytes 256032 | tf_op jit(solution)/shard_map/ppermute | solution.py:209
  31.8 6.7 %collective-permute-done.1.refs_6_ = bf16[5,40,640]{2,1,0:T(8,128)(2,1)S(1)} collective-permute-done((bf16[5,40,640]{2,1,0:T(8,128)(2,1)S(1)}, bf16[5,40,640]{2,1,0:T(8,128)(2,1)S(1)}, u32[]{:S(2)}, u32[]{:S(2)}) %collective-permute-start.1) | collective-permute-done | bytes 256032 | tf_op jit(solution)/shard_map/ppermute | solution.py:209
  38.5 0.0 copy-start.1
  38.5 0.7 copy-done.1
  39.2 4.2 %copy.8 = bf16[4,5,3,64,3,64]{3,5,4,2,1,0:T(8,128)(2,1)} copy(bf16[4,5,3,64,3,64]{3,5,4,2,0,1:T(8,128)(2,1)} %bitcast.14) | data formatting | bytes 2949120 | tf_op jit(solution)/shard_map/transpose | solution.py:198
  43.4 0.0 copy-start.5
  43.4 0.0 copy-start.4
  43.4 3.3 %copy.11.refs_1_ = bf16[4,15,64,192]{3,2,1,0:T(8,128)(2,1)S(1)} copy(bf16[4,15,64,192]{2,3,1,0:T(8,128)(2,1)} %bitcast.13) | data formatting | bytes 2949120 | tf_op jit(solution)/shard_map/reshape | solution.py:198
  46.7 4.1 %collective-permute-start.2 = (bf16[4,15,64,192]{3,2,1,0:T(8,128)(2,1)S(1)}, bf16[4,15,64,192]{3,2,1,0:T(8,128)(2,1)}, u32[]{:S(2)}, u32[]{:S(2)}) collective-permute-start(bf16[4,15,64,192]{3,2,1,0:T(8,128)(2,1)S(1)} %copy.11.refs_1_), channel_id=1, source_target_pairs={{0,16},{16,0},{1,17},{17,1},{2,18},{18,2},{3,19},{19,3},{4,20},{20... | collective-permute-start | bytes 4423688 | tf_op jit(solution)/shard_map/ppermute | solution.py:33
  50.8 0.1 collective-permute-start.3
  50.9 0.4 collective-permute-start.4
  51.3 0.0 copy-done.5
  51.3 0.1 copy.10.shift_ref
  51.4 0.1 stack.28.place_ref
  51.5 3.8 %collective-permute-done.3.refs_5_ = bf16[5,40,640]{2,1,0:T(8,128)(2,1)} collective-permute-done((bf16[5,40,640]{2,1,0:T(8,128)(2,1)S(1)}, bf16[5,40,640]{2,1,0:T(8,128)(2,1)}, u32[]{:S(2)}, u32[]{:S(2)}) %collective-permute-start.3) | collective-permute-done | bytes 256032 | tf_op jit(solution)/shard_map/ppermute | solution.py:33
  55.2 0.2 collective-permute-done.4.refs_7_
  55.5 0.0 collective-permute-done.2.refs_2_
  55.5 0.0 all-to-all-done
  55.5 0.0 copy-done.4
  55.5 0.0 copy-start.2
  55.5 0.9 %copy-done.2 = bf16[5,40,640]{2,1,0:T(8,128)(2,1)S(1)} copy-done((bf16[5,40,640]{2,1,0:T(8,128)(2,1)S(1)}, bf16[5,40,640]{2,1,0:T(8,128)(2,1)}, u32[]{:S(2)}) %copy-start.2) | copy-done | bytes 256024
  56.4 6.6 %conv_mix.1 = (bf16[4,24,640]{2,1,0:T(8,128)(2,1)S(1)}, bf16[4,24,640]{2,1,0:T(8,128)(2,1)S(1)}, bf16[4,24,640]{2,1,0:T(8,128)(2,1)S(1)}, bf16[4,24,640]{2,1,0:T...) custom-call(s32[5,8]{1,0:T(8,128)S(1)} %copy-done.4, ...), custom_call_target="tpu_custom_call" | custom-call | tf_op jit(solution)/shard_map/conv_mix/pallas_call | solution.py:158
  63.0 1.5 %collective-permute-start.5 = (bf16[4,24,640]{2,1,0:T(8,128)(2,1)S(1)}, bf16[4,24,640]{2,1,0:T(8,128)(2,1)S(1)}, u32[]{:S(2)}, u32[]{:S(2)}) collective-permute-start(bf16[4,24,640]{2,1,0:T(8,128)(2,1)S(1)} %get-tuple-element.20), channel_id=1, source_target_pairs={{0,1},{1,0},{2,3},{3,2},{16,17},{17,16},{18,19},{19,18},{4,5},{5,4... | collective-permute-start | bytes 368648 | tf_op jit(solution)/shard_map/ppermute | solution.py:253
  64.5 1.5 %collective-permute-start.6 = (bf16[4,24,640]{2,1,0:T(8,128)(2,1)S(1)}, bf16[4,24,640]{2,1,0:T(8,128)(2,1)S(1)}, u32[]{:S(2)}, u32[]{:S(2)}) collective-permute-start(bf16[4,24,640]{2,1,0:T(8,128)(2,1)S(1)} %get-tuple-element.21), channel_id=1, source_target_pairs={{0,2},{1,3},{2,0},{3,1},{16,18},{17,19},{18,16},{19,17},{4,6},{5,7... | collective-permute-start | bytes 368648 | tf_op jit(solution)/shard_map/ppermute | solution.py:253
  66.0 0.5 collective-permute-start.7
  66.6 0.0 collective-permute-start.8
  66.6 1.6 %collective-permute-start.9 = (bf16[4,24,640]{2,1,0:T(8,128)(2,1)S(1)}, bf16[4,24,640]{2,1,0:T(8,128)(2,1)S(1)}, u32[]{:S(2)}, u32[]{:S(2)}) collective-permute-start(bf16[4,24,640]{2,1,0:T(8,128)(2,1)S(1)} %get-tuple-element.24), channel_id=1, source_target_pairs={{0,17},{1,16},{2,19},{3,18},{16,1},{17,0},{18,3},{19,2},{4,21},{5,... | collective-permute-start | bytes 368648 | tf_op jit(solution)/shard_map/ppermute | solution.py:253
  68.1 0.7 collective-permute-done.5.refs_1_
  68.9 0.4 collective-permute-start.10
  69.3 2.5 %collective-permute-done.6.refs_2_ = bf16[4,24,640]{2,1,0:T(8,128)(2,1)S(1)} collective-permute-done((bf16[4,24,640]{2,1,0:T(8,128)(2,1)S(1)}, bf16[4,24,640]{2,1,0:T(8,128)(2,1)S(1)}, u32[]{:S(2)}, u32[]{:S(2)}) %collective-permute-start.6) | collective-permute-done | bytes 122912 | tf_op jit(solution)/shard_map/ppermute | solution.py:253
  71.8 0.1 collective-permute-start.11
  71.9 1.3 %collective-permute-done.7.refs_3_ = bf16[4,24,640]{2,1,0:T(8,128)(2,1)S(1)} collective-permute-done((bf16[4,24,640]{2,1,0:T(8,128)(2,1)S(1)}, bf16[4,24,640]{2,1,0:T(8,128)(2,1)S(1)}, u32[]{:S(2)}, u32[]{:S(2)}) %collective-permute-start.7) | collective-permute-done | bytes 122912 | tf_op jit(solution)/shard_map/ppermute | solution.py:253
  73.2 0.0 collective-permute-done.8.refs_4_
  73.2 0.0 collective-permute-done.9.refs_5_
  73.2 2.0 %collective-permute-done.10.refs_6_ = bf16[4,24,640]{2,1,0:T(8,128)(2,1)S(1)} collective-permute-done((bf16[4,24,640]{2,1,0:T(8,128)(2,1)S(1)}, bf16[4,24,640]{2,1,0:T(8,128)(2,1)S(1)}, u32[]{:S(2)}, u32[]{:S(2)}) %collective-permute-start.10) | collective-permute-done | bytes 122912 | tf_op jit(solution)/shard_map/ppermute | solution.py:253
  75.1 2.7 %collective-permute-done.11.refs_7_ = bf16[4,24,640]{2,1,0:T(8,128)(2,1)S(1)} collective-permute-done((bf16[4,24,640]{2,1,0:T(8,128)(2,1)S(1)}, bf16[4,24,640]{2,1,0:T(8,128)(2,1)S(1)}, u32[]{:S(2)}, u32[]{:S(2)}) %collective-permute-start.11) | collective-permute-done | bytes 122912 | tf_op jit(solution)/shard_map/ppermute | solution.py:253
  77.8 1.4 %finish.1 = bf16[2,4,24,640]{3,2,1,0:T(8,128)(2,1)} custom-call(s32[7]{0:T(128)S(1)} %stack.28.place_ref, bf16[4,24,640]{2,1,0:T(8,128)(2,1)S(1)} %get-tuple-element.19.refs_0_, bf16[4,24,640]{2,1,0:T(8,128)(2,1)S(1)} %collective-permute-done.5.refs_1_, bf16[4,24,640]{2,1,0:T(8,128)(2,1)S(1)} %collective-permute-done.6.refs_2_, ...), custom_call_target="tpu_custom_call" | custom-call | tf_op jit(solution)/shard_map/finish/pallas_call | solution.py:186
Async XLA Ops:
  0.0 9.7 %copy-start = (bf16[5,40,640]{2,1,0:T(8,128)(2,1)S(1)}, bf16[5,40,640]{2,1,0:T(8,128)(2,1)}, u32[]{:S(2)}) copy-start(bf16[5,40,640]{2,1,0:T(8,128)(2,1)} %refs_3_.1) | copy-start | bytes 768004
  0.0 1.0 %copy-start.3 = (bf16[2,4,640,24]{2,3,1,0:T(8,128)(2,1)S(1)}, bf16[2,4,640,24]{2,3,1,0:T(8,128)(2,1)}, u32[]{:S(2)}) copy-start(bf16[2,4,640,24]{2,3,1,0:T(8,128)(2,1)} %param.5) | copy-start | bytes 737284
  2.3 53.1 %all-to-all-start = ((bf16[32,24,640]{2,1,0:T(8,128)(2,1)}), bf16[32,24,640]{2,1,0:T(8,128)(2,1)S(1)}, u32[]{:S(2)}, u32[]{:S(2)}) async-start(bf16[32,24,640]{2,1,0:T(8,128)(2,1)} %bitcast.7), calls=%async_computation | async-start | bytes 1966080 | tf_op jit(solution)/shard_map/all_to_all | solution.py:230
  9.7 22.1 %collective-permute-start = (bf16[5,40,640]{2,1,0:T(8,128)(2,1)S(1)}, bf16[5,40,640]{2,1,0:T(8,128)(2,1)S(1)}, u32[]{:S(2)}, u32[]{:S(2)}) collective-permute-start(bf16[5,40,640]{2,1,0:T(8,128)(2,1)S(1)} %copy-done), channel_id=1, source_target_pairs={{0,4},{16,24},{4,0},{20,28},{8,12},{24,16},{12,8},{28,20},{1,5},{1... | collective-permute-start | bytes 768008 | tf_op jit(solution)/shard_map/ppermute | solution.py:209
  11.5 27.0 %collective-permute-start.1 = (bf16[5,40,640]{2,1,0:T(8,128)(2,1)S(1)}, bf16[5,40,640]{2,1,0:T(8,128)(2,1)S(1)}, u32[]{:S(2)}, u32[]{:S(2)}) collective-permute-start(bf16[5,40,640]{2,1,0:T(8,128)(2,1)S(1)} %copy-done), channel_id=1, source_target_pairs={{0,12},{20,24},{24,20},{12,0},{1,13},{21,25},{25,21},{13,1},{2,14}... | collective-permute-start | bytes 768008 | tf_op jit(solution)/shard_map/ppermute | solution.py:209
  38.5 0.7 copy-start.1
  43.4 7.9 %copy-start.5 = (s32[8,3]{0,1:T(4,128)S(1)}, s32[8,3]{0,1:T(4,128)}, u32[]{:S(2)}) copy-start(s32[8,3]{0,1:T(4,128)} %param.8) | copy-start | bytes 292
  43.4 12.1 %copy-start.4 = (s32[5,8]{1,0:T(8,128)S(1)}, s32[5,8]{1,0:T(8,128)}, u32[]{:S(2)}) copy-start(s32[5,8]{1,0:T(8,128)} %low_ref) | copy-start | bytes 484
  46.7 8.8 %collective-permute-start.2 = (bf16[4,15,64,192]{3,2,1,0:T(8,128)(2,1)S(1)}, bf16[4,15,64,192]{3,2,1,0:T(8,128)(2,1)}, u32[]{:S(2)}, u32[]{:S(2)}) collective-permute-start(bf16[4,15,64,192]{3,2,1,0:T(8,128)(2,1)S(1)} %copy.11.refs_1_), channel_id=1, source_target_pairs={{0,16},{16,0},{1,17},{17,1},{2,18},{18,2},{3,19},{19,3},{4,20},{20... | collective-permute-start | bytes 4423688 | tf_op jit(solution)/shard_map/ppermute | solution.py:33
  50.8 4.5 %collective-permute-start.3 = (bf16[5,40,640]{2,1,0:T(8,128)(2,1)S(1)}, bf16[5,40,640]{2,1,0:T(8,128)(2,1)}, u32[]{:S(2)}, u32[]{:S(2)}) collective-permute-start(bf16[5,40,640]{2,1,0:T(8,128)(2,1)S(1)} %collective-permute-done.refs_4_), channel_id=1, source_target_pairs={{0,16},{16,0},{1,17},{17,1},{2,18},{18,2},{3,19},{19,3},{4,20},{20... | collective-permute-start | bytes 768008 | tf_op jit(solution)/shard_map/ppermute | solution.py:33
  50.9 4.6 %collective-permute-start.4 = (bf16[5,40,640]{2,1,0:T(8,128)(2,1)}, bf16[5,40,640]{2,1,0:T(8,128)(2,1)}, u32[]{:S(2)}, u32[]{:S(2)}) collective-permute-start(bf16[5,40,640]{2,1,0:T(8,128)(2,1)} %copy-done.1), channel_id=1, source_target_pairs={{0,16},{16,0},{1,17},{17,1},{2,18},{18,2},{3,19},{19,3},{4,20},{20... | collective-permute-start | bytes 768008 | tf_op jit(solution)/shard_map/ppermute | solution.py:33
  55.5 0.9 %copy-start.2 = (bf16[5,40,640]{2,1,0:T(8,128)(2,1)S(1)}, bf16[5,40,640]{2,1,0:T(8,128)(2,1)}, u32[]{:S(2)}) copy-start(bf16[5,40,640]{2,1,0:T(8,128)(2,1)} %copy-done.1) | copy-start | bytes 768004
  63.0 5.9 %collective-permute-start.5 = (bf16[4,24,640]{2,1,0:T(8,128)(2,1)S(1)}, bf16[4,24,640]{2,1,0:T(8,128)(2,1)S(1)}, u32[]{:S(2)}, u32[]{:S(2)}) collective-permute-start(bf16[4,24,640]{2,1,0:T(8,128)(2,1)S(1)} %get-tuple-element.20), channel_id=1, source_target_pairs={{0,1},{1,0},{2,3},{3,2},{16,17},{17,16},{18,19},{19,18},{4,5},{5,4... | collective-permute-start | bytes 368648 | tf_op jit(solution)/shard_map/ppermute | solution.py:253
  64.5 7.2 %collective-permute-start.6 = (bf16[4,24,640]{2,1,0:T(8,128)(2,1)S(1)}, bf16[4,24,640]{2,1,0:T(8,128)(2,1)S(1)}, u32[]{:S(2)}, u32[]{:S(2)}) collective-permute-start(bf16[4,24,640]{2,1,0:T(8,128)(2,1)S(1)} %get-tuple-element.21), channel_id=1, source_target_pairs={{0,2},{1,3},{2,0},{3,1},{16,18},{17,19},{18,16},{19,17},{4,6},{5,7... | collective-permute-start | bytes 368648 | tf_op jit(solution)/shard_map/ppermute | solution.py:253
  66.0 7.2 %collective-permute-start.7 = (bf16[4,24,640]{2,1,0:T(8,128)(2,1)S(1)}, bf16[4,24,640]{2,1,0:T(8,128)(2,1)S(1)}, u32[]{:S(2)}, u32[]{:S(2)}) collective-permute-start(bf16[4,24,640]{2,1,0:T(8,128)(2,1)S(1)} %get-tuple-element.22), channel_id=1, source_target_pairs={{0,3},{1,2},{2,1},{3,0},{16,19},{17,18},{18,17},{19,16},{4,7},{5,6... | collective-permute-start | bytes 368648 | tf_op jit(solution)/shard_map/ppermute | solution.py:253
  66.6 6.6 %collective-permute-start.8 = (bf16[4,24,640]{2,1,0:T(8,128)(2,1)S(1)}, bf16[4,24,640]{2,1,0:T(8,128)(2,1)S(1)}, u32[]{:S(2)}, u32[]{:S(2)}) collective-permute-start(bf16[4,24,640]{2,1,0:T(8,128)(2,1)S(1)} %get-tuple-element.23), channel_id=1, source_target_pairs={{0,16},{1,17},{2,18},{3,19},{16,0},{17,1},{18,2},{19,3},{4,20},{5,... | collective-permute-start | bytes 368648 | tf_op jit(solution)/shard_map/ppermute | solution.py:253
  66.6 6.6 %collective-permute-start.9 = (bf16[4,24,640]{2,1,0:T(8,128)(2,1)S(1)}, bf16[4,24,640]{2,1,0:T(8,128)(2,1)S(1)}, u32[]{:S(2)}, u32[]{:S(2)}) collective-permute-start(bf16[4,24,640]{2,1,0:T(8,128)(2,1)S(1)} %get-tuple-element.24), channel_id=1, source_target_pairs={{0,17},{1,16},{2,19},{3,18},{16,1},{17,0},{18,3},{19,2},{4,21},{5,... | collective-permute-start | bytes 368648 | tf_op jit(solution)/shard_map/ppermute | solution.py:253
  68.9 6.3 %collective-permute-start.10 = (bf16[4,24,640]{2,1,0:T(8,128)(2,1)S(1)}, bf16[4,24,640]{2,1,0:T(8,128)(2,1)S(1)}, u32[]{:S(2)}, u32[]{:S(2)}) collective-permute-start(bf16[4,24,640]{2,1,0:T(8,128)(2,1)S(1)} %get-tuple-element.25), channel_id=1, source_target_pairs={{0,18},{1,19},{2,16},{3,17},{16,2},{17,3},{18,0},{19,1},{4,22},{5,... | collective-permute-start | bytes 368648 | tf_op jit(solution)/shard_map/ppermute | solution.py:253
  71.8 6.1 %collective-permute-start.11 = (bf16[4,24,640]{2,1,0:T(8,128)(2,1)S(1)}, bf16[4,24,640]{2,1,0:T(8,128)(2,1)S(1)}, u32[]{:S(2)}, u32[]{:S(2)}) collective-permute-start(bf16[4,24,640]{2,1,0:T(8,128)(2,1)S(1)} %get-tuple-element.26), channel_id=1, source_target_pairs={{0,19},{1,18},{2,17},{3,16},{16,3},{17,2},{18,1},{19,0},{4,23},{5,... | collective-permute-start | bytes 368648 | tf_op jit(solution)/shard_map/ppermute | solution.py:253

commit v7 on v5

--- a/solution.py
+++ b/solution.py
@@ -120,7 +120,7 @@
                     total[k, at, piece * sub : (piece + 1) * sub] += slab
             return carry
 
-        lax.fori_loop(0, rows, one_row, 0)
+        lax.fori_loop(0, rows, one_row, 0, unroll=2)
 
     for d, slot in enumerate(mix_slots):
         for k in range(bases):
@@ -210,15 +210,16 @@
     return [own] + [trade(own, "late", s, late) for s in range(1, late)]
 
 
-def gather_mix(mix, late, na, nc):
+def gather_mix(mix, spread, late, na, nc):
     core, own = lax.axis_index("late"), lax.axis_index("a") * nc + lax.axis_index("c")
     owners = na * nc
     if na == nc == late == 2:
         route = [(p, p ^ 2) for p in range(4)] + [(4 + p, 4 + (p ^ 1)) for p in range(4)]
         first = lax.ppermute(mix, ("late", "a", "c"), route)
         third = lax.ppermute(mix, ("late", "a", "c"), [(4 + p, 4 + (p ^ 3)) for p in range(4)])
-        other = trade(first, "late", 1, late)
-        copied = lax.ppermute(third, "late", [(1, 0)])
+        first_late, third_late, _ = lax.optimization_barrier((first, third, spread))
+        other = trade(first_late, "late", 1, late)
+        copied = lax.ppermute(third_late, "late", [(1, 0)])
         return [[mix], [first], [other], [third, copied]], [own, own ^ (2 - core), own ^ (1 + core), own ^ 3]
     slots = [[mix]] + [[trade(mix, ("a", "c"), d, owners)] for d in range(1, owners)]
     return slots, [partner(own, d, owners) for d in range(owners)]
@@ -236,10 +237,10 @@
     packed = packed.reshape((-1,) + packed.shape[4:])
     spread = lax.all_to_all(packed, ("late", "a", "b", "d"), split_axis=0, concat_axis=0, tiled=True)
     weights = both_kernels(kernel, late)
-    mix_weight, spread = lax.optimization_barrier((mix_weight, spread))
+    arrived = spread
     spread = spread.reshape(late, na, nb, nd * cells, -1)
     spread = [spread] + [trade(spread, "c", s, nc) for s in range(1, nc)]
-    mix, origins = gather_mix(mix_weight, late, na, nc)
+    mix, origins = gather_mix(mix_weight, arrived, late, na, nc)
 
     start = lax.axis_index("lath") * all_rows
     low = lax.dynamic_slice_in_dim(band_low, start, all_rows, 1)

time: 74.5 us -> 73.5 us (0.987)
  blocking collectives: 21.9 us -> 0 us
  waiting for transfers between devices: 21.4 us -> 33.8 us
  starting transfers between devices: 13.4 us -> 21.7 us
    all_to_all x1 -> x0, blocking collectives: 21.9 us -> none  [per_device(): lax.all_to_all(packed, ('late', 'a', 'b', 'd'), split_axis=0, concat_axis...]
    all_to_all x0 -> x1, waiting for transfers between devices: none -> 16.5 us  [per_device(): lax.all_to_all(packed, ('late', 'a', 'b', 'd'), split_axis=0, concat_axis...]
    ppermute x1, waiting for transfers between devices: 12.5 us -> 3.25 us  [gather_mix(): first = lax.ppermute(mix, ('late', 'a', 'c'), route)]
    all_to_all x0 -> x1, starting transfers between devices: none -> 7.02 us  [per_device(): lax.all_to_all(packed, ('late', 'a', 'b', 'd'), split_axis=0, concat_axis...]
    ppermute x3, waiting for transfers between devices: 1.08 us -> 4.97 us  [trade(): lax.ppermute(x, axis, [(i, partner(i, distance, size)) for i in range(siz...]
    ppermute x1, starting transfers between devices: 0.07 us -> 2.89 us  [gather_mix(): first = lax.ppermute(mix, ('late', 'a', 'c'), route)]
    ppermute x1, waiting for transfers between devices: 0.25 us -> 2.26 us  [gather_mix(): copied = lax.ppermute(third_late, 'late', [(1, 0)])]
    ppermute x7, starting transfers between devices: 8.11 us -> 6.77 us  [per_device(): lax.ppermute(partial[dl * groups + dq], ('late', 'b', 'd'), [(l * groups...]
  transfers between devices with their start and end apart: 13 -> 14, of which waited for: 8 -> 9; matrix products, arithmetic and copies ran while one was open for 0% -> 0% of each run, Pallas kernels for 1% -> 2%
where the time goes in v7:
time: 73.5 us; the launch traced here: 73.1 us
  waiting for transfers between devices  33.8 us (46%)
  starting transfers between devices  21.7 us (30%)
  Pallas kernels  9.83 us (13%)
  local copies, waits for them, and re-layouts  7.69 us (10%)
    all_to_all x1, waiting for transfers between devices, per_device(): lax.all_to_all(packed, ('late', 'a', 'b', 'd'), split_axis=0, concat_axis...  16.5 us
    pallas_call x1, Pallas kernels, conv_mix(): pl.pallas_call(functools.partial(conv_mix_kernel, (bases, taps, slots, ha...  7.21 us
    all_to_all x1, starting transfers between devices, per_device(): lax.all_to_all(packed, ('late', 'a', 'b', 'd'), split_axis=0, concat_axis...  7.02 us
    ppermute x7, waiting for transfers between devices, per_device(): lax.ppermute(partial[dl * groups + dq], ('late', 'b', 'd'), [(l * groups...  6.8 us
    ppermute x7, starting transfers between devices, per_device(): lax.ppermute(partial[dl * groups + dq], ('late', 'b', 'd'), [(l * groups...  6.77 us
    ppermute x3, waiting for transfers between devices, trade(): lax.ppermute(x, axis, [(i, partner(i, distance, size)) for i in range(siz...  4.97 us
    transpose x1, local copies, waits for them, and re-layouts, both_kernels(): kernel.transpose(1, 0, 2, 5, 3, 4)  4.17 us
    reshape x1, local copies, waits for them, and re-layouts, both_kernels(): kernel.transpose(1, 0, 2, 5, 3, 4)  3.34 us
  transfers between devices with their start and end apart: 14, of which 9 were waited for; matrix products, arithmetic and copies ran while one was open for 0% of the time, Pallas kernels for 2%

profile of v7, /device:TPU:0, one launch (start us, length us, event | category | flops | bytes accessed | tf_op | source)
XLA Modules:
  0.0 73.1 jit_solution(12694588183075806689)
XLA Ops:
  0.0 4.2 %copy.8 = bf16[4,5,3,64,3,64]{3,5,4,2,1,0:T(8,128)(2,1)} copy(bf16[4,5,3,64,3,64]{3,5,4,2,0,1:T(8,128)(2,1)} %bitcast.17) | data formatting | bytes 2949120 | tf_op jit(solution)/shard_map/transpose | solution.py:209
  4.2 0.0 copy-start.1
  4.2 0.0 copy-start
  4.2 0.0 copy-start.3
  4.2 0.0 copy-start.2
  4.2 3.3 %copy.11.refs_2_ = bf16[4,15,64,192]{3,2,1,0:T(8,128)(2,1)S(1)} copy(bf16[4,15,64,192]{2,3,1,0:T(8,128)(2,1)} %bitcast.16) | data formatting | bytes 2949120 | tf_op jit(solution)/shard_map/reshape | solution.py:209
  7.5 0.5 collective-permute-start.1
  8.0 0.0 copy-done.1
  8.0 1.2 %pack.1 = bf16[2,2,2,2,24,640]{5,4,3,2,1,0:T(8,128)(2,1)} custom-call(bf16[2,4,24,640]{3,2,1,0:T(8,128)(2,1)S(1)} %bitcast.15), custom_call_target="tpu_custom_call" | custom-call | tf_op jit(solution)/shard_map/pack/pallas_call | solution.py:53
  9.2 7.0 %all-to-all-start = ((bf16[16,24,640]{2,1,0:T(8,128)(2,1)}), bf16[16,24,640]{2,1,0:T(8,128)(2,1)S(1)}, u32[]{:S(2)}, u32[]{:S(2)}) async-start(bf16[16,24,640]{2,1,0:T(8,128)(2,1)} %bitcast.9), calls=%async_computation | async-start | bytes 983040 | tf_op jit(solution)/shard_map/all_to_all | solution.py:238
  16.2 0.0 copy-done
  16.3 2.9 %collective-permute-start.2 = (bf16[5,40,640]{2,1,0:T(8,128)(2,1)S(1)}, bf16[5,40,640]{2,1,0:T(8,128)(2,1)S(1)}, u32[]{:S(2)}, u32[]{:S(2)}) collective-permute-start(bf16[5,40,640]{2,1,0:T(8,128)(2,1)S(1)} %copy-done), channel_id=1, source_target_pairs={{0,8},{2,10},{8,0},{10,2},{16,18},{18,16},{24,26},{26,24},{1,9},{3... | collective-permute-start | bytes 768008 | tf_op jit(solution)/shard_map/ppermute | solution.py:218
  19.1 1.4 %collective-permute-start.3 = (bf16[5,40,640]{2,1,0:T(8,128)(2,1)S(1)}, bf16[5,40,640]{2,1,0:T(8,128)(2,1)}, u32[]{:S(2)}, u32[]{:S(2)}) collective-permute-start(bf16[5,40,640]{2,1,0:T(8,128)(2,1)S(1)} %copy-done), channel_id=1, source_target_pairs={{16,26},{18,24},{24,18},{26,16},{17,27},{19,25},{25,19},{27,17},{2... | collective-permute-start | bytes 768008 | tf_op jit(solution)/shard_map/ppermute | solution.py:219
  20.5 16.5 %all-to-all-done = bf16[16,24,640]{2,1,0:T(8,128)(2,1)S(1)} async-done(((bf16[16,24,640]{2,1,0:T(8,128)(2,1)}), bf16[16,24,640]{2,1,0:T(8,128)(2,1)S(1)}, u32[]{:S(2)}, u32[]{:S(2)}) %all-to-all-start) | async-done | bytes 491552 | tf_op jit(solution)/shard_map/all_to_all | solution.py:238
  37.0 1.5 %collective-permute-start = (bf16[2,2,2,48,640]{4,3,2,1,0:T(8,128)(2,1)S(1)}, bf16[2,2,2,48,640]{4,3,2,1,0:T(8,128)(2,1)S(1)}, u32[]{:S(2)}, u32[]{:S(2)}) collective-permute-start(bf16[2,2,2,48,640]{4,3,2,1,0:T(8,128)(2,1)S(1)} %bitcast.13), channel_id=1, source_target_pairs={{0,2},{2,0},{1,3},{3,1},{4,6},{6,4},{5,7},{7,5},{8,10},{10,8},{9,1... | collective-permute-start | bytes 1474568 | tf_op jit(solution)/shard_map/ppermute | solution.py:33
  38.5 3.3 %collective-permute-done.2.refs_5_ = bf16[5,40,640]{2,1,0:T(8,128)(2,1)S(1)} collective-permute-done((bf16[5,40,640]{2,1,0:T(8,128)(2,1)S(1)}, bf16[5,40,640]{2,1,0:T(8,128)(2,1)S(1)}, u32[]{:S(2)}, u32[]{:S(2)}) %collective-permute-start.2) | collective-permute-done | bytes 256032 | tf_op jit(solution)/shard_map/ppermute | solution.py:218
  41.8 0.0 collective-permute-done.3.refs_7_
  41.8 0.4 collective-permute-start.4
  42.2 1.3 %collective-permute-start.5 = (bf16[5,40,640]{2,1,0:T(8,128)(2,1)}, bf16[5,40,640]{2,1,0:T(8,128)(2,1)}, u32[]{:S(2)}, u32[]{:S(2)}) collective-permute-start(bf16[5,40,640]{2,1,0:T(8,128)(2,1)} %collective-permute-done.3.refs_7_), channel_id=1, source_target_pairs={{16,0},{17,1},{18,2},{19,3},{20,4},{21,5},{22,6},{23,7},{24,8},{25... | collective-permute-start | bytes 768008 | tf_op jit(solution)/shard_map/ppermute | solution.py:222
  43.5 0.0 copy-done.3
  43.5 0.1 copy.10.shift_ref
  43.6 0.1 stack.35.place_ref
  43.7 0.0 collective-permute-done.4.refs_6_
  43.7 2.3 %collective-permute-done.5.refs_8_ = bf16[5,40,640]{2,1,0:T(8,128)(2,1)} collective-permute-done((bf16[5,40,640]{2,1,0:T(8,128)(2,1)}, bf16[5,40,640]{2,1,0:T(8,128)(2,1)}, u32[]{:S(2)}, u32[]{:S(2)}) %collective-permute-start.5) | collective-permute-done | bytes 256032 | tf_op jit(solution)/shard_map/ppermute | solution.py:222
  45.9 5.0 %collective-permute-done.refs_1_ = bf16[2,2,2,48,640]{4,3,2,1,0:T(8,128)(2,1)S(1)} collective-permute-done((bf16[2,2,2,48,640]{4,3,2,1,0:T(8,128)(2,1)S(1)}, bf16[2,2,2,48,640]{4,3,2,1,0:T(8,128)(2,1)S(1)}, u32[]{:S(2)}, u32[]{:S(2)}) %collective-permute-start) | collective-permute-done | bytes 491552 | tf_op jit(solution)/shard_map/ppermute | solution.py:33
  50.9 0.0 collective-permute-done.1.refs_3_
  50.9 0.0 copy-done.2
  50.9 7.2 %conv_mix.1 = (bf16[4,24,640]{2,1,0:T(8,128)(2,1)S(1)}, bf16[4,24,640]{2,1,0:T(8,128)(2,1)S(1)}, bf16[4,24,640]{2,1,0:T(8,128)(2,1)S(1)}, bf16[4,24,640]{2,1,0:T...) custom-call(s32[5,8]{1,0:T(8,128)S(1)} %copy-done.2, ...), custom_call_target="tpu_custom_call" | custom-call | tf_op jit(solution)/shard_map/conv_mix/pallas_call | solution.py:169
  58.1 1.1 %collective-permute-start.6 = (bf16[4,24,640]{2,1,0:T(8,128)(2,1)S(1)}, bf16[4,24,640]{2,1,0:T(8,128)(2,1)S(1)}, u32[]{:S(2)}, u32[]{:S(2)}) collective-permute-start(bf16[4,24,640]{2,1,0:T(8,128)(2,1)S(1)} %get-tuple-element.18), channel_id=1, source_target_pairs={{0,1},{1,0},{4,5},{5,4},{16,17},{17,16},{20,21},{21,20},{2,3},{3,2... | collective-permute-start | bytes 368648 | tf_op jit(solution)/shard_map/ppermute | solution.py:263
  59.2 0.0 collective-permute-start.7
  59.2 2.5 %collective-permute-start.8 = (bf16[4,24,640]{2,1,0:T(8,128)(2,1)S(1)}, bf16[4,24,640]{2,1,0:T(8,128)(2,1)S(1)}, u32[]{:S(2)}, u32[]{:S(2)}) collective-permute-start(bf16[4,24,640]{2,1,0:T(8,128)(2,1)S(1)} %get-tuple-element.20), channel_id=1, source_target_pairs={{0,5},{1,4},{4,1},{5,0},{16,21},{17,20},{20,17},{21,16},{2,7},{3,6... | collective-permute-start | bytes 368648 | tf_op jit(solution)/shard_map/ppermute | solution.py:263
  61.7 0.0 collective-permute-start.9
  61.7 1.1 %collective-permute-start.10 = (bf16[4,24,640]{2,1,0:T(8,128)(2,1)S(1)}, bf16[4,24,640]{2,1,0:T(8,128)(2,1)S(1)}, u32[]{:S(2)}, u32[]{:S(2)}) collective-permute-start(bf16[4,24,640]{2,1,0:T(8,128)(2,1)S(1)} %get-tuple-element.22), channel_id=1, source_target_pairs={{0,17},{1,16},{4,21},{5,20},{16,1},{17,0},{20,5},{21,4},{2,19},{3,... | collective-permute-start | bytes 368648 | tf_op jit(solution)/shard_map/ppermute | solution.py:263
  62.8 1.6 %collective-permute-done.6.refs_1_ = bf16[4,24,640]{2,1,0:T(8,128)(2,1)S(1)} collective-permute-done((bf16[4,24,640]{2,1,0:T(8,128)(2,1)S(1)}, bf16[4,24,640]{2,1,0:T(8,128)(2,1)S(1)}, u32[]{:S(2)}, u32[]{:S(2)}) %collective-permute-start.6) | collective-permute-done | bytes 122912 | tf_op jit(solution)/shard_map/ppermute | solution.py:263
  64.4 0.0 collective-permute-start.11
  64.4 0.1 collective-permute-done.7.refs_2_
  64.5 2.1 %collective-permute-start.12 = (bf16[4,24,640]{2,1,0:T(8,128)(2,1)S(1)}, bf16[4,24,640]{2,1,0:T(8,128)(2,1)S(1)}, u32[]{:S(2)}, u32[]{:S(2)}) collective-permute-start(bf16[4,24,640]{2,1,0:T(8,128)(2,1)S(1)} %get-tuple-element.24), channel_id=1, source_target_pairs={{0,21},{1,20},{4,17},{5,16},{16,5},{17,4},{20,1},{21,0},{2,23},{3,... | collective-permute-start | bytes 368648 | tf_op jit(solution)/shard_map/ppermute | solution.py:263
  66.6 0.0 collective-permute-done.8.refs_3_
  66.6 0.0 collective-permute-done.9.refs_4_
  66.6 2.3 %collective-permute-done.10.refs_5_ = bf16[4,24,640]{2,1,0:T(8,128)(2,1)S(1)} collective-permute-done((bf16[4,24,640]{2,1,0:T(8,128)(2,1)S(1)}, bf16[4,24,640]{2,1,0:T(8,128)(2,1)S(1)}, u32[]{:S(2)}, u32[]{:S(2)}) %collective-permute-start.10) | collective-permute-done | bytes 122912 | tf_op jit(solution)/shard_map/ppermute | solution.py:263
  68.9 1.0 %collective-permute-done.11.refs_6_ = bf16[4,24,640]{2,1,0:T(8,128)(2,1)S(1)} collective-permute-done((bf16[4,24,640]{2,1,0:T(8,128)(2,1)S(1)}, bf16[4,24,640]{2,1,0:T(8,128)(2,1)S(1)}, u32[]{:S(2)}, u32[]{:S(2)}) %collective-permute-start.11) | collective-permute-done | bytes 122912 | tf_op jit(solution)/shard_map/ppermute | solution.py:263
  69.9 1.8 %collective-permute-done.12.refs_7_ = bf16[4,24,640]{2,1,0:T(8,128)(2,1)S(1)} collective-permute-done((bf16[4,24,640]{2,1,0:T(8,128)(2,1)S(1)}, bf16[4,24,640]{2,1,0:T(8,128)(2,1)S(1)}, u32[]{:S(2)}, u32[]{:S(2)}) %collective-permute-start.12) | collective-permute-done | bytes 122912 | tf_op jit(solution)/shard_map/ppermute | solution.py:263
  71.7 1.4 %finish.1 = bf16[2,4,24,640]{3,2,1,0:T(8,128)(2,1)} custom-call(s32[8]{0:T(128)S(1)} %stack.35.place_ref, bf16[4,24,640]{2,1,0:T(8,128)(2,1)S(1)} %get-tuple-element.17.refs_0_, bf16[4,24,640]{2,1,0:T(8,128)(2,1)S(1)} %collective-permute-done.6.refs_1_, bf16[4,24,640]{2,1,0:T(8,128)(2,1)S(1)} %collective-permute-done.7.refs_2_, ...), custom_call_target="tpu_custom_call" | custom-call | tf_op jit(solution)/shard_map/finish/pallas_call | solution.py:197
Async XLA Ops:
  4.2 3.9 %copy-start.1 = (bf16[2,4,640,24]{2,3,1,0:T(8,128)(2,1)S(1)}, bf16[2,4,640,24]{2,3,1,0:T(8,128)(2,1)}, u32[]{:S(2)}) copy-start(bf16[2,4,640,24]{2,3,1,0:T(8,128)(2,1)} %param.5) | copy-start | bytes 737284
  4.2 12.1 %copy-start = (bf16[5,40,640]{2,1,0:T(8,128)(2,1)S(1)}, bf16[5,40,640]{2,1,0:T(8,128)(2,1)}, u32[]{:S(2)}) copy-start(bf16[5,40,640]{2,1,0:T(8,128)(2,1)} %refs_4_.1) | copy-start | bytes 768004
  4.2 39.3 %copy-start.3 = (s32[8,3]{0,1:T(4,128)S(1)}, s32[8,3]{0,1:T(4,128)}, u32[]{:S(2)}) copy-start(s32[8,3]{0,1:T(4,128)} %param.8) | copy-start | bytes 292
  4.2 46.7 %copy-start.2 = (s32[5,8]{1,0:T(8,128)S(1)}, s32[5,8]{1,0:T(8,128)}, u32[]{:S(2)}) copy-start(s32[5,8]{1,0:T(8,128)} %low_ref) | copy-start | bytes 484
  7.5 43.4 %collective-permute-start.1 = (bf16[4,15,64,192]{3,2,1,0:T(8,128)(2,1)S(1)}, bf16[4,15,64,192]{3,2,1,0:T(8,128)(2,1)}, u32[]{:S(2)}, u32[]{:S(2)}) collective-permute-start(bf16[4,15,64,192]{3,2,1,0:T(8,128)(2,1)S(1)} %copy.11.refs_2_), channel_id=1, source_target_pairs={{0,16},{16,0},{1,17},{17,1},{2,18},{18,2},{3,19},{19,3},{4,20},{20... | collective-permute-start | bytes 4423688 | tf_op jit(solution)/shard_map/ppermute | solution.py:33
  9.2 27.8 %all-to-all-start = ((bf16[16,24,640]{2,1,0:T(8,128)(2,1)}), bf16[16,24,640]{2,1,0:T(8,128)(2,1)S(1)}, u32[]{:S(2)}, u32[]{:S(2)}) async-start(bf16[16,24,640]{2,1,0:T(8,128)(2,1)} %bitcast.9), calls=%async_computation | async-start | bytes 983040 | tf_op jit(solution)/shard_map/all_to_all | solution.py:238
  16.3 25.5 %collective-permute-start.2 = (bf16[5,40,640]{2,1,0:T(8,128)(2,1)S(1)}, bf16[5,40,640]{2,1,0:T(8,128)(2,1)S(1)}, u32[]{:S(2)}, u32[]{:S(2)}) collective-permute-start(bf16[5,40,640]{2,1,0:T(8,128)(2,1)S(1)} %copy-done), channel_id=1, source_target_pairs={{0,8},{2,10},{8,0},{10,2},{16,18},{18,16},{24,26},{26,24},{1,9},{3... | collective-permute-start | bytes 768008 | tf_op jit(solution)/shard_map/ppermute | solution.py:218
  19.1 22.6 %collective-permute-start.3 = (bf16[5,40,640]{2,1,0:T(8,128)(2,1)S(1)}, bf16[5,40,640]{2,1,0:T(8,128)(2,1)}, u32[]{:S(2)}, u32[]{:S(2)}) collective-permute-start(bf16[5,40,640]{2,1,0:T(8,128)(2,1)S(1)} %copy-done), channel_id=1, source_target_pairs={{16,26},{18,24},{24,18},{26,16},{17,27},{19,25},{25,19},{27,17},{2... | collective-permute-start | bytes 768008 | tf_op jit(solution)/shard_map/ppermute | solution.py:219
  37.0 13.9 %collective-permute-start = (bf16[2,2,2,48,640]{4,3,2,1,0:T(8,128)(2,1)S(1)}, bf16[2,2,2,48,640]{4,3,2,1,0:T(8,128)(2,1)S(1)}, u32[]{:S(2)}, u32[]{:S(2)}) collective-permute-start(bf16[2,2,2,48,640]{4,3,2,1,0:T(8,128)(2,1)S(1)} %bitcast.13), channel_id=1, source_target_pairs={{0,2},{2,0},{1,3},{3,1},{4,6},{6,4},{5,7},{7,5},{8,10},{10,8},{9,1... | collective-permute-start | bytes 1474568 | tf_op jit(solution)/shard_map/ppermute | solution.py:33
  41.8 1.9 %collective-permute-start.4 = (bf16[5,40,640]{2,1,0:T(8,128)(2,1)S(1)}, bf16[5,40,640]{2,1,0:T(8,128)(2,1)}, u32[]{:S(2)}, u32[]{:S(2)}) collective-permute-start(bf16[5,40,640]{2,1,0:T(8,128)(2,1)S(1)} %collective-permute-done.2.refs_5_), channel_id=1, source_target_pairs={{0,16},{16,0},{1,17},{17,1},{2,18},{18,2},{3,19},{19,3},{4,20},{20... | collective-permute-start | bytes 768008 | tf_op jit(solution)/shard_map/ppermute | solution.py:33
  42.2 3.8 %collective-permute-start.5 = (bf16[5,40,640]{2,1,0:T(8,128)(2,1)}, bf16[5,40,640]{2,1,0:T(8,128)(2,1)}, u32[]{:S(2)}, u32[]{:S(2)}) collective-permute-start(bf16[5,40,640]{2,1,0:T(8,128)(2,1)} %collective-permute-done.3.refs_7_), channel_id=1, source_target_pairs={{16,0},{17,1},{18,2},{19,3},{20,4},{21,5},{22,6},{23,7},{24,8},{25... | collective-permute-start | bytes 768008 | tf_op jit(solution)/shard_map/ppermute | solution.py:222
  58.1 6.3 %collective-permute-start.6 = (bf16[4,24,640]{2,1,0:T(8,128)(2,1)S(1)}, bf16[4,24,640]{2,1,0:T(8,128)(2,1)S(1)}, u32[]{:S(2)}, u32[]{:S(2)}) collective-permute-start(bf16[4,24,640]{2,1,0:T(8,128)(2,1)S(1)} %get-tuple-element.18), channel_id=1, source_target_pairs={{0,1},{1,0},{4,5},{5,4},{16,17},{17,16},{20,21},{21,20},{2,3},{3,2... | collective-permute-start | bytes 368648 | tf_op jit(solution)/shard_map/ppermute | solution.py:263
  59.2 5.3 %collective-permute-start.7 = (bf16[4,24,640]{2,1,0:T(8,128)(2,1)S(1)}, bf16[4,24,640]{2,1,0:T(8,128)(2,1)S(1)}, u32[]{:S(2)}, u32[]{:S(2)}) collective-permute-start(bf16[4,24,640]{2,1,0:T(8,128)(2,1)S(1)} %get-tuple-element.19), channel_id=1, source_target_pairs={{0,4},{1,5},{4,0},{5,1},{16,20},{17,21},{20,16},{21,17},{2,6},{3,7... | collective-permute-start | bytes 368648 | tf_op jit(solution)/shard_map/ppermute | solution.py:263
  59.2 7.4 %collective-permute-start.8 = (bf16[4,24,640]{2,1,0:T(8,128)(2,1)S(1)}, bf16[4,24,640]{2,1,0:T(8,128)(2,1)S(1)}, u32[]{:S(2)}, u32[]{:S(2)}) collective-permute-start(bf16[4,24,640]{2,1,0:T(8,128)(2,1)S(1)} %get-tuple-element.20), channel_id=1, source_target_pairs={{0,5},{1,4},{4,1},{5,0},{16,21},{17,20},{20,17},{21,16},{2,7},{3,6... | collective-permute-start | bytes 368648 | tf_op jit(solution)/shard_map/ppermute | solution.py:263
  61.7 4.9 %collective-permute-start.9 = (bf16[4,24,640]{2,1,0:T(8,128)(2,1)S(1)}, bf16[4,24,640]{2,1,0:T(8,128)(2,1)S(1)}, u32[]{:S(2)}, u32[]{:S(2)}) collective-permute-start(bf16[4,24,640]{2,1,0:T(8,128)(2,1)S(1)} %get-tuple-element.21), channel_id=1, source_target_pairs={{0,16},{1,17},{4,20},{5,21},{16,0},{17,1},{20,4},{21,5},{2,18},{3,... | collective-permute-start | bytes 368648 | tf_op jit(solution)/shard_map/ppermute | solution.py:263
  61.7 7.3 %collective-permute-start.10 = (bf16[4,24,640]{2,1,0:T(8,128)(2,1)S(1)}, bf16[4,24,640]{2,1,0:T(8,128)(2,1)S(1)}, u32[]{:S(2)}, u32[]{:S(2)}) collective-permute-start(bf16[4,24,640]{2,1,0:T(8,128)(2,1)S(1)} %get-tuple-element.22), channel_id=1, source_target_pairs={{0,17},{1,16},{4,21},{5,20},{16,1},{17,0},{20,5},{21,4},{2,19},{3,... | collective-permute-start | bytes 368648 | tf_op jit(solution)/shard_map/ppermute | solution.py:263
  64.4 5.6 %collective-permute-start.11 = (bf16[4,24,640]{2,1,0:T(8,128)(2,1)S(1)}, bf16[4,24,640]{2,1,0:T(8,128)(2,1)S(1)}, u32[]{:S(2)}, u32[]{:S(2)}) collective-permute-start(bf16[4,24,640]{2,1,0:T(8,128)(2,1)S(1)} %get-tuple-element.23), channel_id=1, source_target_pairs={{0,20},{1,21},{4,16},{5,17},{16,4},{17,5},{20,0},{21,1},{2,22},{3,... | collective-permute-start | bytes 368648 | tf_op jit(solution)/shard_map/ppermute | solution.py:263
  64.5 7.2 %collective-permute-start.12 = (bf16[4,24,640]{2,1,0:T(8,128)(2,1)S(1)}, bf16[4,24,640]{2,1,0:T(8,128)(2,1)S(1)}, u32[]{:S(2)}, u32[]{:S(2)}) collective-permute-start(bf16[4,24,640]{2,1,0:T(8,128)(2,1)S(1)} %get-tuple-element.24), channel_id=1, source_target_pairs={{0,21},{1,20},{4,17},{5,16},{16,5},{17,4},{20,1},{21,0},{2,23},{3,... | collective-permute-start | bytes 368648 | tf_op jit(solution)/shard_map/ppermute | solution.py:263

commit v8 on v4

--- a/solution.py
+++ b/solution.py
@@ -112,7 +112,7 @@
                     total[k, at, piece * sub : (piece + 1) * sub] += slab
             return carry
 
-        lax.fori_loop(0, rows, one_row, 0)
+        lax.fori_loop(0, rows, one_row, 0, unroll=2)
 
     for d, slot in enumerate(mix_slots):
         for k in range(bases):
@@ -199,22 +199,19 @@
     return [own] + [trade(own, "late", s, late) for s in range(1, late)]
 
 
-def gather_mix(mix, late, owners):
+def gather_mix(mix, packed, late, owners):
     core, own = lax.axis_index("late"), lax.axis_index("lonp")
     if owners == 4 and late == 2:
-        def fetch(distances):
-            route = [
-                (c * owners + p, c * owners + (p ^ d)) for p in range(owners) for c, d in enumerate(distances(p)) if d
-            ]
-            return lax.ppermute(mix, ("late", "lonp"), route)
-
-        first = fetch(lambda p: (1, 2))
-        third = fetch(lambda p: (3, 0) if p in (0, 3) else (0, 3))
+        route = [(p, p ^ 1) for p in range(4)] + [(4 + p, 4 + (p ^ 2)) for p in range(4)]
+        first = lax.ppermute(mix, ("late", "lonp"), route)
+        packed, first = lax.optimization_barrier((packed, first))
+        third = lax.ppermute(first, ("late", "lonp"), [(4 + p, 4 + (p ^ 1)) for p in range(4)])
         other = trade(first, "late", 1, late)
-        copied = trade(third, "late", 1, late)
-        return [[mix], [first], [other], [third, copied]], [own, own ^ (1 + core), own ^ (2 - core), own ^ 3]
+        copied = lax.ppermute(third, "late", [(1, 0)])
+        slots, origins = [[mix], [first], [other], [third, copied]], [own, own ^ (1 + core), own ^ (2 - core), own ^ 3]
+        return slots, origins, packed
     slots = [[mix]] + [[trade(mix, "lonp", d, owners)] for d in range(1, owners)]
-    return slots, [partner(own, d, owners) for d in range(owners)]
+    return slots, [partner(own, d, owners) for d in range(owners)], packed
 
 
 def per_device(sizes, fields, kernel, band_low, block_shift, mix_weight):
@@ -226,10 +223,10 @@
 
     packed = pack(fields.transpose(0, 1, 3, 2), groups, owners)
     packed = packed.reshape((-1,) + packed.shape[3:])
+    mix, origins, packed = gather_mix(mix_weight, packed, late, owners)
     spread = lax.all_to_all(packed, ("late", "lonp", "lonq"), split_axis=0, concat_axis=0, tiled=True)
     spread = spread.reshape(late, owners, groups * cells, -1)
     weights = both_kernels(kernel, late)
-    mix, origins = gather_mix(mix_weight, late, owners)
 
     start = lax.axis_index("lath") * all_rows
     low = lax.dynamic_slice_in_dim(band_low, start, all_rows, 1)

time: 69.2 us -> 65.1 us (0.941)
  starting transfers between devices: 30 us -> 18.6 us
  waiting for transfers between devices: 19.2 us -> 27.4 us
  Pallas kernels: 10.7 us -> 9.99 us
    ppermute x3 -> x2, starting transfers between devices: 11 us -> 2.67 us  [trade(): lax.ppermute(x, axis, [(i, partner(i, distance, size)) for i in range(siz...]
    ppermute x2 -> x3, waiting for transfers between devices: 8.39 us -> 13.7 us  [the longest x1 9.13 us: gather_mix(): copied = lax.ppermute(third, 'late', [(1, 0)])]
    all_to_all x1, waiting for transfers between devices: 0.01 us -> 4.5 us  [per_device(): lax.all_to_all(packed, ('late', 'lonp', 'lonq'), split_axis=0, concat_axi...]
    ppermute x7, starting transfers between devices: 5.7 us -> 3.74 us  [per_device(): lax.ppermute(partial[dl * groups + dq], ('late', 'lonq'), [(l * groups +...]
    ppermute x3 -> x2, waiting for transfers between devices: 1.7 us -> 0.01 us  [trade(): lax.ppermute(x, axis, [(i, partner(i, distance, size)) for i in range(siz...]
    all_to_all x1, starting transfers between devices: 7.3 us -> 6.55 us  [per_device(): lax.all_to_all(packed, ('late', 'lonp', 'lonq'), split_axis=0, concat_axi...]
    pallas_call x1, Pallas kernels: 7.91 us -> 7.2 us  [conv_mix(): pl.pallas_call(functools.partial(conv_mix_kernel, (bases, taps, slots, ha...]
    ppermute x2 -> x3, starting transfers between devices: 5.93 us -> 5.67 us  [the longest x1 3.02 us: gather_mix(): first = lax.ppermute(mix, ('late', 'lonp'), route)]
  transfers between devices with their start and end apart: 13 -> 13, of which waited for: 8 -> 8; matrix products, arithmetic and copies ran while one was open for 11% -> 12% of each run, Pallas kernels for 0% -> 2%
where the time goes in v8:
time: 65.1 us; the launch traced here: 64.7 us
  waiting for transfers between devices  27.4 us (42%)
  starting transfers between devices  18.6 us (29%)
  Pallas kernels  9.99 us (15%)
  local copies, waits for them, and re-layouts  8.62 us (13%)
    ppermute x7, waiting for transfers between devices, per_device(): lax.ppermute(partial[dl * groups + dq], ('late', 'lonq'), [(l * groups +...  9.17 us
    ppermute x1, waiting for transfers between devices, gather_mix(): copied = lax.ppermute(third, 'late', [(1, 0)])  9.13 us
    pallas_call x1, Pallas kernels, conv_mix(): pl.pallas_call(functools.partial(conv_mix_kernel, (bases, taps, slots, ha...  7.2 us
    all_to_all x1, starting transfers between devices, per_device(): lax.all_to_all(packed, ('late', 'lonp', 'lonq'), split_axis=0, concat_axi...  6.55 us
    ppermute x1, waiting for transfers between devices, gather_mix(): first = lax.ppermute(mix, ('late', 'lonp'), route)  4.58 us
    all_to_all x1, waiting for transfers between devices, per_device(): lax.all_to_all(packed, ('late', 'lonp', 'lonq'), split_axis=0, concat_axi...  4.5 us
    transpose x1, local copies, waits for them, and re-layouts, both_kernels(): kernel.transpose(1, 0, 2, 5, 3, 4)  4.18 us
    ppermute x7, starting transfers between devices, per_device(): lax.ppermute(partial[dl * groups + dq], ('late', 'lonq'), [(l * groups +...  3.74 us
  transfers between devices with their start and end apart: 13, of which 8 were waited for; matrix products, arithmetic and copies ran while one was open for 12% of the time, Pallas kernels for 2%

profile of v8, /device:TPU:0, one launch (start us, length us, event | category | flops | bytes accessed | tf_op | source)
XLA Modules:
  0.0 64.7 jit_solution(5664692715336016037)
XLA Ops:
  0.0 3.0 %collective-permute-start = (bf16[5,40,640]{2,1,0:T(8,128)(2,1)}, bf16[5,40,640]{2,1,0:T(8,128)(2,1)S(1)}, u32[]{:S(2)}, u32[]{:S(2)}) collective-permute-start(bf16[5,40,640]{2,1,0:T(8,128)(2,1)} %refs_3_.1), channel_id=1, source_target_pairs={{0,4},{4,0},{8,12},{12,8},{16,24},{20,28},{24,16},{28,20},{1,5},{5... | collective-permute-start | bytes 768008 | tf_op jit(solution)/shard_map/ppermute | solution.py:206
  3.0 0.0 copy-start.1
  3.0 0.9 %copy-done.1 = bf16[2,4,640,24]{2,3,1,0:T(8,128)(2,1)S(1)} copy-done((bf16[2,4,640,24]{2,3,1,0:T(8,128)(2,1)S(1)}, bf16[2,4,640,24]{2,3,1,0:T(8,128)(2,1)}, u32[]{:S(2)}) %copy-start.1) | copy-done | bytes 245784
  4.0 1.3 %pack.1 = bf16[2,4,4,24,640]{4,3,2,1,0:T(8,128)(2,1)} custom-call(bf16[2,4,24,640]{3,2,1,0:T(8,128)(2,1)S(1)} %bitcast.12), custom_call_target="tpu_custom_call" | custom-call | tf_op jit(solution)/shard_map/pack/pallas_call | solution.py:53
  5.3 4.6 %collective-permute-done.refs_4_ = bf16[5,40,640]{2,1,0:T(8,128)(2,1)S(1)} collective-permute-done((bf16[5,40,640]{2,1,0:T(8,128)(2,1)}, bf16[5,40,640]{2,1,0:T(8,128)(2,1)S(1)}, u32[]{:S(2)}, u32[]{:S(2)}) %collective-permute-start) | collective-permute-done | bytes 256032 | tf_op jit(solution)/shard_map/ppermute | solution.py:206
  9.9 6.5 %all-to-all-start = ((bf16[32,24,640]{2,1,0:T(8,128)(2,1)}), bf16[32,24,640]{2,1,0:T(8,128)(2,1)S(1)}, u32[]{:S(2)}, u32[]{:S(2)}) async-start(bf16[32,24,640]{2,1,0:T(8,128)(2,1)} %bitcast.7), calls=%async_computation | async-start | bytes 1966080 | tf_op jit(solution)/shard_map/all_to_all | solution.py:227
  16.5 4.2 %copy.8 = bf16[4,5,3,64,3,64]{3,5,4,2,1,0:T(8,128)(2,1)} copy(bf16[4,5,3,64,3,64]{3,5,4,2,0,1:T(8,128)(2,1)} %bitcast.14) | data formatting | bytes 2949120 | tf_op jit(solution)/shard_map/transpose | solution.py:198
  20.6 0.0 copy-start.3
  20.6 0.0 copy-start
  20.6 0.0 copy-start.2
  20.6 3.3 %copy.11.refs_1_ = bf16[4,15,64,192]{3,2,1,0:T(8,128)(2,1)S(1)} copy(bf16[4,15,64,192]{2,3,1,0:T(8,128)(2,1)} %bitcast.13) | data formatting | bytes 2949120 | tf_op jit(solution)/shard_map/reshape | solution.py:198
  24.0 0.3 collective-permute-start.1
  24.3 1.4 %collective-permute-start.3 = (bf16[5,40,640]{2,1,0:T(8,128)(2,1)S(1)}, bf16[5,40,640]{2,1,0:T(8,128)(2,1)}, u32[]{:S(2)}, u32[]{:S(2)}) collective-permute-start(bf16[5,40,640]{2,1,0:T(8,128)(2,1)S(1)} %collective-permute-done.refs_4_), channel_id=1, source_target_pairs={{16,20},{20,16},{24,28},{28,24},{17,21},{21,17},{25,29},{29,25},{1... | collective-permute-start | bytes 768008 | tf_op jit(solution)/shard_map/ppermute | solution.py:208
  25.6 2.4 %collective-permute-start.2 = (bf16[5,40,640]{2,1,0:T(8,128)(2,1)S(1)}, bf16[5,40,640]{2,1,0:T(8,128)(2,1)}, u32[]{:S(2)}, u32[]{:S(2)}) collective-permute-start(bf16[5,40,640]{2,1,0:T(8,128)(2,1)S(1)} %collective-permute-done.refs_4_), channel_id=1, source_target_pairs={{0,16},{16,0},{1,17},{17,1},{2,18},{18,2},{3,19},{19,3},{4,20},{20... | collective-permute-start | bytes 768008 | tf_op jit(solution)/shard_map/ppermute | solution.py:33
  28.0 0.0 collective-permute-done.3.refs_6_
  28.0 1.3 %collective-permute-start.4 = (bf16[5,40,640]{2,1,0:T(8,128)(2,1)}, bf16[5,40,640]{2,1,0:T(8,128)(2,1)}, u32[]{:S(2)}, u32[]{:S(2)}) collective-permute-start(bf16[5,40,640]{2,1,0:T(8,128)(2,1)} %collective-permute-done.3.refs_6_), channel_id=1, source_target_pairs={{16,0},{17,1},{18,2},{19,3},{20,4},{21,5},{22,6},{23,7},{24,8},{25... | collective-permute-start | bytes 768008 | tf_op jit(solution)/shard_map/ppermute | solution.py:210
  29.3 0.0 copy-done.3
  29.3 0.1 copy.10.shift_ref
  29.4 0.1 stack.28.place_ref
  29.5 0.0 collective-permute-done.2.refs_5_
  29.5 9.1 %collective-permute-done.4.refs_7_ = bf16[5,40,640]{2,1,0:T(8,128)(2,1)} collective-permute-done((bf16[5,40,640]{2,1,0:T(8,128)(2,1)}, bf16[5,40,640]{2,1,0:T(8,128)(2,1)}, u32[]{:S(2)}, u32[]{:S(2)}) %collective-permute-start.4) | collective-permute-done | bytes 256032 | tf_op jit(solution)/shard_map/ppermute | solution.py:210
  38.6 0.0 collective-permute-done.1.refs_2_
  38.6 4.5 %all-to-all-done = bf16[32,24,640]{2,1,0:T(8,128)(2,1)S(1)} async-done(((bf16[32,24,640]{2,1,0:T(8,128)(2,1)}), bf16[32,24,640]{2,1,0:T(8,128)(2,1)S(1)}, u32[]{:S(2)}, u32[]{:S(2)}) %all-to-all-start) | async-done | bytes 983072 | tf_op jit(solution)/shard_map/all_to_all | solution.py:227
  43.1 0.0 copy-done
  43.1 0.0 copy-done.2
  43.1 7.2 %conv_mix.1 = (bf16[4,24,640]{2,1,0:T(8,128)(2,1)S(1)}, bf16[4,24,640]{2,1,0:T(8,128)(2,1)S(1)}, bf16[4,24,640]{2,1,0:T(8,128)(2,1)S(1)}, bf16[4,24,640]{2,1,0:T...) custom-call(s32[5,8]{1,0:T(8,128)S(1)} %copy-done.2, ...), custom_call_target="tpu_custom_call" | custom-call | tf_op jit(solution)/shard_map/conv_mix/pallas_call | solution.py:158
  50.3 0.1 collective-permute-start.5
  50.4 0.8 %collective-permute-start.6 = (bf16[4,24,640]{2,1,0:T(8,128)(2,1)S(1)}, bf16[4,24,640]{2,1,0:T(8,128)(2,1)S(1)}, u32[]{:S(2)}, u32[]{:S(2)}) collective-permute-start(bf16[4,24,640]{2,1,0:T(8,128)(2,1)S(1)} %get-tuple-element.19), channel_id=1, source_target_pairs={{0,2},{1,3},{2,0},{3,1},{16,18},{17,19},{18,16},{19,17},{4,6},{5,7... | collective-permute-start | bytes 368648 | tf_op jit(solution)/shard_map/ppermute | solution.py:249
  51.2 2.7 %collective-permute-start.7 = (bf16[4,24,640]{2,1,0:T(8,128)(2,1)S(1)}, bf16[4,24,640]{2,1,0:T(8,128)(2,1)S(1)}, u32[]{:S(2)}, u32[]{:S(2)}) collective-permute-start(bf16[4,24,640]{2,1,0:T(8,128)(2,1)S(1)} %get-tuple-element.20), channel_id=1, source_target_pairs={{0,3},{1,2},{2,1},{3,0},{16,19},{17,18},{18,17},{19,16},{4,7},{5,6... | collective-permute-start | bytes 368648 | tf_op jit(solution)/shard_map/ppermute | solution.py:249
  53.9 0.0 collective-permute-start.8
  53.9 0.2 collective-permute-start.9
  54.1 2.2 %collective-permute-done.5.refs_1_ = bf16[4,24,640]{2,1,0:T(8,128)(2,1)S(1)} collective-permute-done((bf16[4,24,640]{2,1,0:T(8,128)(2,1)S(1)}, bf16[4,24,640]{2,1,0:T(8,128)(2,1)S(1)}, u32[]{:S(2)}, u32[]{:S(2)}) %collective-permute-start.5) | collective-permute-done | bytes 122912 | tf_op jit(solution)/shard_map/ppermute | solution.py:249
  56.3 0.0 collective-permute-start.10
  56.3 1.5 %collective-permute-done.6.refs_2_ = bf16[4,24,640]{2,1,0:T(8,128)(2,1)S(1)} collective-permute-done((bf16[4,24,640]{2,1,0:T(8,128)(2,1)S(1)}, bf16[4,24,640]{2,1,0:T(8,128)(2,1)S(1)}, u32[]{:S(2)}, u32[]{:S(2)}) %collective-permute-start.6) | collective-permute-done | bytes 122912 | tf_op jit(solution)/shard_map/ppermute | solution.py:249
  57.8 0.0 collective-permute-start.11
  57.8 0.3 collective-permute-done.7.refs_3_
  58.1 0.0 collective-permute-done.8.refs_4_
  58.1 1.4 %collective-permute-done.9.refs_5_ = bf16[4,24,640]{2,1,0:T(8,128)(2,1)S(1)} collective-permute-done((bf16[4,24,640]{2,1,0:T(8,128)(2,1)S(1)}, bf16[4,24,640]{2,1,0:T(8,128)(2,1)S(1)}, u32[]{:S(2)}, u32[]{:S(2)}) %collective-permute-start.9) | collective-permute-done | bytes 122912 | tf_op jit(solution)/shard_map/ppermute | solution.py:249
  59.6 3.7 %collective-permute-done.10.refs_6_ = bf16[4,24,640]{2,1,0:T(8,128)(2,1)S(1)} collective-permute-done((bf16[4,24,640]{2,1,0:T(8,128)(2,1)S(1)}, bf16[4,24,640]{2,1,0:T(8,128)(2,1)S(1)}, u32[]{:S(2)}, u32[]{:S(2)}) %collective-permute-start.10) | collective-permute-done | bytes 122912 | tf_op jit(solution)/shard_map/ppermute | solution.py:249
  63.2 0.0 collective-permute-done.11.refs_7_
  63.3 1.4 %finish.1 = bf16[2,4,24,640]{3,2,1,0:T(8,128)(2,1)} custom-call(s32[7]{0:T(128)S(1)} %stack.28.place_ref, bf16[4,24,640]{2,1,0:T(8,128)(2,1)S(1)} %get-tuple-element.17.refs_0_, bf16[4,24,640]{2,1,0:T(8,128)(2,1)S(1)} %collective-permute-done.5.refs_1_, bf16[4,24,640]{2,1,0:T(8,128)(2,1)S(1)} %collective-permute-done.6.refs_2_, ...), custom_call_target="tpu_custom_call" | custom-call | tf_op jit(solution)/shard_map/finish/pallas_call | solution.py:186
Async XLA Ops:
  0.0 9.9 %collective-permute-start = (bf16[5,40,640]{2,1,0:T(8,128)(2,1)}, bf16[5,40,640]{2,1,0:T(8,128)(2,1)S(1)}, u32[]{:S(2)}, u32[]{:S(2)}) collective-permute-start(bf16[5,40,640]{2,1,0:T(8,128)(2,1)} %refs_3_.1), channel_id=1, source_target_pairs={{0,4},{4,0},{8,12},{12,8},{16,24},{20,28},{24,16},{28,20},{1,5},{5... | collective-permute-start | bytes 768008 | tf_op jit(solution)/shard_map/ppermute | solution.py:206
  3.0 0.9 %copy-start.1 = (bf16[2,4,640,24]{2,3,1,0:T(8,128)(2,1)S(1)}, bf16[2,4,640,24]{2,3,1,0:T(8,128)(2,1)}, u32[]{:S(2)}) copy-start(bf16[2,4,640,24]{2,3,1,0:T(8,128)(2,1)} %param.5) | copy-start | bytes 737284
  9.9 33.2 %all-to-all-start = ((bf16[32,24,640]{2,1,0:T(8,128)(2,1)}), bf16[32,24,640]{2,1,0:T(8,128)(2,1)S(1)}, u32[]{:S(2)}, u32[]{:S(2)}) async-start(bf16[32,24,640]{2,1,0:T(8,128)(2,1)} %bitcast.7), calls=%async_computation | async-start | bytes 1966080 | tf_op jit(solution)/shard_map/all_to_all | solution.py:227
  20.6 8.7 %copy-start.3 = (s32[8,3]{0,1:T(4,128)S(1)}, s32[8,3]{0,1:T(4,128)}, u32[]{:S(2)}) copy-start(s32[8,3]{0,1:T(4,128)} %param.8) | copy-start | bytes 292
  20.6 22.5 %copy-start = (bf16[5,40,640]{2,1,0:T(8,128)(2,1)S(1)}, bf16[5,40,640]{2,1,0:T(8,128)(2,1)}, u32[]{:S(2)}) copy-start(bf16[5,40,640]{2,1,0:T(8,128)(2,1)} %refs_3_.1) | copy-start | bytes 768004
  20.6 22.5 %copy-start.2 = (s32[5,8]{1,0:T(8,128)S(1)}, s32[5,8]{1,0:T(8,128)}, u32[]{:S(2)}) copy-start(s32[5,8]{1,0:T(8,128)} %low_ref) | copy-start | bytes 484
  24.0 14.6 %collective-permute-start.1 = (bf16[4,15,64,192]{3,2,1,0:T(8,128)(2,1)S(1)}, bf16[4,15,64,192]{3,2,1,0:T(8,128)(2,1)}, u32[]{:S(2)}, u32[]{:S(2)}) collective-permute-start(bf16[4,15,64,192]{3,2,1,0:T(8,128)(2,1)S(1)} %copy.11.refs_1_), channel_id=1, source_target_pairs={{0,16},{16,0},{1,17},{17,1},{2,18},{18,2},{3,19},{19,3},{4,20},{20... | collective-permute-start | bytes 4423688 | tf_op jit(solution)/shard_map/ppermute | solution.py:33
  24.3 3.7 %collective-permute-start.3 = (bf16[5,40,640]{2,1,0:T(8,128)(2,1)S(1)}, bf16[5,40,640]{2,1,0:T(8,128)(2,1)}, u32[]{:S(2)}, u32[]{:S(2)}) collective-permute-start(bf16[5,40,640]{2,1,0:T(8,128)(2,1)S(1)} %collective-permute-done.refs_4_), channel_id=1, source_target_pairs={{16,20},{20,16},{24,28},{28,24},{17,21},{21,17},{25,29},{29,25},{1... | collective-permute-start | bytes 768008 | tf_op jit(solution)/shard_map/ppermute | solution.py:208
  25.6 3.8 %collective-permute-start.2 = (bf16[5,40,640]{2,1,0:T(8,128)(2,1)S(1)}, bf16[5,40,640]{2,1,0:T(8,128)(2,1)}, u32[]{:S(2)}, u32[]{:S(2)}) collective-permute-start(bf16[5,40,640]{2,1,0:T(8,128)(2,1)S(1)} %collective-permute-done.refs_4_), channel_id=1, source_target_pairs={{0,16},{16,0},{1,17},{17,1},{2,18},{18,2},{3,19},{19,3},{4,20},{20... | collective-permute-start | bytes 768008 | tf_op jit(solution)/shard_map/ppermute | solution.py:33
  28.0 10.6 %collective-permute-start.4 = (bf16[5,40,640]{2,1,0:T(8,128)(2,1)}, bf16[5,40,640]{2,1,0:T(8,128)(2,1)}, u32[]{:S(2)}, u32[]{:S(2)}) collective-permute-start(bf16[5,40,640]{2,1,0:T(8,128)(2,1)} %collective-permute-done.3.refs_6_), channel_id=1, source_target_pairs={{16,0},{17,1},{18,2},{19,3},{20,4},{21,5},{22,6},{23,7},{24,8},{25... | collective-permute-start | bytes 768008 | tf_op jit(solution)/shard_map/ppermute | solution.py:210
  50.3 6.0 %collective-permute-start.5 = (bf16[4,24,640]{2,1,0:T(8,128)(2,1)S(1)}, bf16[4,24,640]{2,1,0:T(8,128)(2,1)S(1)}, u32[]{:S(2)}, u32[]{:S(2)}) collective-permute-start(bf16[4,24,640]{2,1,0:T(8,128)(2,1)S(1)} %get-tuple-element.18), channel_id=1, source_target_pairs={{0,1},{1,0},{2,3},{3,2},{16,17},{17,16},{18,19},{19,18},{4,5},{5,4... | collective-permute-start | bytes 368648 | tf_op jit(solution)/shard_map/ppermute | solution.py:249
  50.4 7.4 %collective-permute-start.6 = (bf16[4,24,640]{2,1,0:T(8,128)(2,1)S(1)}, bf16[4,24,640]{2,1,0:T(8,128)(2,1)S(1)}, u32[]{:S(2)}, u32[]{:S(2)}) collective-permute-start(bf16[4,24,640]{2,1,0:T(8,128)(2,1)S(1)} %get-tuple-element.19), channel_id=1, source_target_pairs={{0,2},{1,3},{2,0},{3,1},{16,18},{17,19},{18,16},{19,17},{4,6},{5,7... | collective-permute-start | bytes 368648 | tf_op jit(solution)/shard_map/ppermute | solution.py:249
  51.2 7.0 %collective-permute-start.7 = (bf16[4,24,640]{2,1,0:T(8,128)(2,1)S(1)}, bf16[4,24,640]{2,1,0:T(8,128)(2,1)S(1)}, u32[]{:S(2)}, u32[]{:S(2)}) collective-permute-start(bf16[4,24,640]{2,1,0:T(8,128)(2,1)S(1)} %get-tuple-element.20), channel_id=1, source_target_pairs={{0,3},{1,2},{2,1},{3,0},{16,19},{17,18},{18,17},{19,16},{4,7},{5,6... | collective-permute-start | bytes 368648 | tf_op jit(solution)/shard_map/ppermute | solution.py:249
  53.9 4.3 %collective-permute-start.8 = (bf16[4,24,640]{2,1,0:T(8,128)(2,1)S(1)}, bf16[4,24,640]{2,1,0:T(8,128)(2,1)S(1)}, u32[]{:S(2)}, u32[]{:S(2)}) collective-permute-start(bf16[4,24,640]{2,1,0:T(8,128)(2,1)S(1)} %get-tuple-element.21), channel_id=1, source_target_pairs={{0,16},{1,17},{2,18},{3,19},{16,0},{17,1},{18,2},{19,3},{4,20},{5,... | collective-permute-start | bytes 368648 | tf_op jit(solution)/shard_map/ppermute | solution.py:249
  53.9 5.7 %collective-permute-start.9 = (bf16[4,24,640]{2,1,0:T(8,128)(2,1)S(1)}, bf16[4,24,640]{2,1,0:T(8,128)(2,1)S(1)}, u32[]{:S(2)}, u32[]{:S(2)}) collective-permute-start(bf16[4,24,640]{2,1,0:T(8,128)(2,1)S(1)} %get-tuple-element.22), channel_id=1, source_target_pairs={{0,17},{1,16},{2,19},{3,18},{16,1},{17,0},{18,3},{19,2},{4,21},{5,... | collective-permute-start | bytes 368648 | tf_op jit(solution)/shard_map/ppermute | solution.py:249
  56.3 7.0 %collective-permute-start.10 = (bf16[4,24,640]{2,1,0:T(8,128)(2,1)S(1)}, bf16[4,24,640]{2,1,0:T(8,128)(2,1)S(1)}, u32[]{:S(2)}, u32[]{:S(2)}) collective-permute-start(bf16[4,24,640]{2,1,0:T(8,128)(2,1)S(1)} %get-tuple-element.23), channel_id=1, source_target_pairs={{0,18},{1,19},{2,16},{3,17},{16,2},{17,3},{18,0},{19,1},{4,22},{5,... | collective-permute-start | bytes 368648 | tf_op jit(solution)/shard_map/ppermute | solution.py:249
  57.8 5.4 %collective-permute-start.11 = (bf16[4,24,640]{2,1,0:T(8,128)(2,1)S(1)}, bf16[4,24,640]{2,1,0:T(8,128)(2,1)S(1)}, u32[]{:S(2)}, u32[]{:S(2)}) collective-permute-start(bf16[4,24,640]{2,1,0:T(8,128)(2,1)S(1)} %get-tuple-element.24), channel_id=1, source_target_pairs={{0,19},{1,18},{2,17},{3,16},{16,3},{17,2},{18,1},{19,0},{4,23},{5,... | collective-permute-start | bytes 368648 | tf_op jit(solution)/shard_map/ppermute | solution.py:249

commit v9 on v8

--- a/solution.py
+++ b/solution.py
@@ -12,7 +12,7 @@
 HALO = 2
 LANES = 128
 VMEM = pltpu.VMEM
-LIMIT = 24 * 1024 * 1024
+LIMIT = 16 * 1024 * 1024
 SMEM_SPEC = pl.BlockSpec(memory_space=pltpu.SMEM)
 VMEM_SPEC = pl.BlockSpec(memory_space=VMEM)
 
@@ -43,16 +43,14 @@
                 for i in range(rows)
                 for p in range(owners)
             ]
-            block = jnp.concatenate(parts, axis=-1)
-            for p in range(owners):
-                out_ref[e, p, q] = block
+            out_ref[e, q] = jnp.concatenate(parts, axis=-1)
 
 
 def pack(x, groups, owners):
     members, rows, cells, channels = x.shape
     return pl.pallas_call(
         functools.partial(pack_kernel, groups, owners),
-        out_shape=jax.ShapeDtypeStruct((members, owners, groups, cells, rows * channels // groups), x.dtype),
+        out_shape=jax.ShapeDtypeStruct((members, groups, cells, rows * channels // groups), x.dtype),
         in_specs=[VMEM_SPEC],
         out_specs=VMEM_SPEC,
         compiler_params=pltpu.CompilerParams(vmem_limit_bytes=LIMIT),
@@ -70,12 +68,13 @@
 def conv_mix_kernel(geometry, counts, low_ref, shift_ref, place_ref, *refs):
     bases, taps, slots, halo, sub, groups = geometry
     refs = list(refs)
-    fields_ref = refs.pop(0)
-    weight_refs = [refs.pop(0) for _ in range(counts[0])]
-    mix_slots = [[refs.pop(0) for _ in range(n)] for n in counts[1]]
+    field_refs = [refs.pop(0) for _ in range(counts[0])]
+    weight_refs = [refs.pop(0) for _ in range(counts[1])]
+    mix_slots = [[refs.pop(0) for _ in range(n)] for n in counts[2]]
     field_rows, total, mix_all, mixed = refs[-4:]
     outs = refs[:-4]
-    late, owners, span, _ = fields_ref.shape
+    late, span, _ = field_refs[0].shape
+    owners = len(field_refs)
     depth, width = mix_slots[0][0].shape[1:]
     channels = owners * depth
     padded = total.shape[-1]
@@ -88,10 +87,11 @@
     field_rows[...] = jnp.zeros_like(field_rows)
     for s in range(late):
         lat = partner_in_kernel(member, s, late)
-        for p in range(owners):
-            value = fields_ref[lat, p]
+        for d, ref in enumerate(field_refs):
+            at = pl.ds(pl.multiple_of(partner_in_kernel(owner, d, owners) * span, sub), span)
+            value = ref[lat]
             for r in range(rows):
-                field_rows[r, p * span : (p + 1) * span, :channels] = value[:, r * channels : (r + 1) * channels]
+                field_rows[r, at, :channels] = value[:, r * channels : (r + 1) * channels]
 
         def one_row(r, carry):
             row = lat * rows + r
@@ -144,7 +144,8 @@
 def conv_mix(low, shift, place, fields, weights, mix, halo, groups, block):
     bases, all_rows = low.shape
     slots = shift.shape[1]
-    late, owners, span, _ = fields.shape
+    late, span, _ = fields[0].shape
+    owners = len(fields)
     rows = all_rows // late
     depth, width = mix[0][0].shape[1:]
     padded = -(-owners * depth // LANES) * LANES
@@ -153,8 +154,8 @@
     shapes = [jax.ShapeDtypeStruct((rows, span // groups, width), jnp.bfloat16)] * (late * groups)
     if halo:
         shapes.append(jax.ShapeDtypeStruct((2, halo, span, width), jnp.bfloat16))
-    operands = [fields] + weights + [x for slot in mix for x in slot]
-    counts = (len(weights), [len(s) for s in mix])
+    operands = fields + weights + [x for slot in mix for x in slot]
+    counts = (len(fields), len(weights), [len(s) for s in mix])
     return pl.pallas_call(
         functools.partial(conv_mix_kernel, (bases, taps, slots, halo, sub, groups), counts),
         out_shape=shapes,
@@ -193,40 +194,65 @@
     )(place, *parts)
 
 
-def both_kernels(kernel, late):
-    bases, rows, taps, slots, block, _ = kernel.shape
-    own = kernel.transpose(1, 0, 2, 5, 3, 4).reshape(rows, bases * taps, block, slots * block)
-    return [own] + [trade(own, "late", s, late) for s in range(1, late)]
-
-
-def gather_mix(mix, packed, late, owners):
+def turn_kernel(x_ref, out_ref):
+    bases, rows, taps, slots, block, _ = x_ref.shape
+    unit = (lax.broadcasted_iota(jnp.int32, (block, block), 0) == lax.broadcasted_iota(jnp.int32, (block, block), 1))
+    unit = unit.astype(jnp.float32).astype(x_ref.dtype)
+
+    def one_row(r, carry):
+        for k in range(bases):
+            for t in range(taps):
+                cells = x_ref[k, r, t].reshape(slots * block, block)
+                turned = lax.dot_general(unit, cells, (((1,), (1,)), ((), ())), preferred_element_type=jnp.float32)
+                out_ref[r, k * taps + t] = turned.astype(out_ref.dtype)
+        return carry
+
+    lax.fori_loop(0, rows, one_row, 0)
+
+
+def turn(x):
+    bases, rows, taps, slots, block, _ = x.shape
+    return pl.pallas_call(
+        turn_kernel,
+        out_shape=jax.ShapeDtypeStruct((rows, bases * taps, block, slots * block), x.dtype),
+        in_specs=[VMEM_SPEC],
+        out_specs=VMEM_SPEC,
+        compiler_params=pltpu.CompilerParams(vmem_limit_bytes=LIMIT),
+        name="turn",
+    )(x)
+
+
+def gather_mix(mix, spread, late, owners):
     core, own = lax.axis_index("late"), lax.axis_index("lonp")
     if owners == 4 and late == 2:
         route = [(p, p ^ 1) for p in range(4)] + [(4 + p, 4 + (p ^ 2)) for p in range(4)]
         first = lax.ppermute(mix, ("late", "lonp"), route)
-        packed, first = lax.optimization_barrier((packed, first))
+        spread, first = lax.optimization_barrier((spread, first))
         third = lax.ppermute(first, ("late", "lonp"), [(4 + p, 4 + (p ^ 1)) for p in range(4)])
         other = trade(first, "late", 1, late)
         copied = lax.ppermute(third, "late", [(1, 0)])
         slots, origins = [[mix], [first], [other], [third, copied]], [own, own ^ (1 + core), own ^ (2 - core), own ^ 3]
-        return slots, origins, packed
+        return slots, origins, spread
     slots = [[mix]] + [[trade(mix, "lonp", d, owners)] for d in range(1, owners)]
-    return slots, [partner(own, d, owners) for d in range(owners)], packed
+    return slots, [partner(own, d, owners) for d in range(owners)], spread
 
 
 def per_device(sizes, fields, kernel, band_low, block_shift, mix_weight):
     halves, late, owners, groups = sizes
     members, rows, channels, cells = fields.shape
-    bases, _, taps, slots, block, _ = kernel.shape
+    block = kernel.shape[-1]
     all_rows = late * rows
     halo = HALO if halves > 1 else 0
 
+    kernels = [kernel] + [trade(kernel, "late", s, late) for s in range(1, late)]
     packed = pack(fields.transpose(0, 1, 3, 2), groups, owners)
-    packed = packed.reshape((-1,) + packed.shape[3:])
-    mix, origins, packed = gather_mix(mix_weight, packed, late, owners)
-    spread = lax.all_to_all(packed, ("late", "lonp", "lonq"), split_axis=0, concat_axis=0, tiled=True)
-    spread = spread.reshape(late, owners, groups * cells, -1)
-    weights = both_kernels(kernel, late)
+    packed = packed.reshape((late * groups,) + packed.shape[2:])
+    spread = lax.all_to_all(packed, ("late", "lonq"), split_axis=0, concat_axis=0, tiled=True)
+    mix, origins, spread = gather_mix(mix_weight, spread, late, owners)
+    *kernels, spread = lax.optimization_barrier((*kernels, spread))
+    weights = [turn(x) for x in kernels]
+    spread = spread.reshape(late, groups * cells, -1)
+    spread = [spread] + [trade(spread, "lonp", d, owners) for d in range(1, owners)]
 
     start = lax.axis_index("lath") * all_rows
     low = lax.dynamic_slice_in_dim(band_low, start, all_rows, 1)

time: 65.1 us -> 66 us (1.014)
  the two profiles are of different devices: /device:TPU:0 before, /device:TPU:9 now
where the time goes in v9:
time: 66 us; the launch traced here: 65.7 us
  waiting for transfers between devices  25.2 us (38%)
  Pallas kernels  13.7 us (21%)
  starting transfers between devices  13.4 us (20%)
  blocking collectives  9.7 us (15%)
  local copies, waits for them, and re-layouts  3.63 us (6%)
    ppermute x7, waiting for transfers between devices, per_device(): lax.ppermute(partial[dl * groups + dq], ('late', 'lonq'), [(l * groups +...  10 us
    ppermute x5, waiting for transfers between devices, trade(): lax.ppermute(x, axis, [(i, partner(i, distance, size)) for i in range(siz...  9.88 us
    all_to_all x1, blocking collectives, per_device(): lax.all_to_all(packed, ('late', 'lonq'), split_axis=0, concat_axis=0, til...  9.7 us
    pallas_call x1, Pallas kernels, conv_mix(): pl.pallas_call(functools.partial(conv_mix_kernel, (bases, taps, slots, ha...  6.97 us
    ppermute x1, waiting for transfers between devices, gather_mix(): lax.ppermute(first, ('late', 'lonp'), [(4 + p, 4 + (p ^ 1)) for p in rang...  5.36 us
    pallas_call x2, Pallas kernels, turn(): pl.pallas_call(turn_kernel, out_shape=jax.ShapeDtypeStruct((rows, bases *...  4.86 us
    ppermute x7, starting transfers between devices, per_device(): lax.ppermute(partial[dl * groups + dq], ('late', 'lonq'), [(l * groups +...  3.64 us
    unnamed x9, local copies, waits for them, and re-layouts  3.54 us
  transfers between devices with their start and end apart: 15, of which 8 were waited for; matrix products, arithmetic and copies ran while one was open for 1% of the time, Pallas kernels for 8%

profile of v9, /device:TPU:9, one launch (start us, length us, event | category | flops | bytes accessed | tf_op | source)
XLA Modules:
  0.0 65.7 jit_solution(927562569230910269)
XLA Ops:
  0.0 0.7 %collective-permute-start = (bf16[5,4,3,3,64,64]{5,4,3,2,1,0:T(8,128)(2,1)}, bf16[5,4,3,3,64,64]{5,4,3,2,1,0:T(8,128)(2,1)S(1)}, u32[]{:S(2)}, u32[]{:S(2)}) collective-permute-start(bf16[5,4,3,3,64,64]{5,4,3,2,1,0:T(8,128)(2,1)} %x_ref), channel_id=1, source_target_pairs={{0,16},{16,0},{1,17},{17,1},{2,18},{18,2},{3,19},{19,3},{4,20},{20... | collective-permute-start | bytes 4423688 | tf_op jit(solution)/shard_map/ppermute | solution.py:33
  0.7 2.3 %collective-permute-start.1 = (bf16[5,40,640]{2,1,0:T(8,128)(2,1)}, bf16[5,40,640]{2,1,0:T(8,128)(2,1)S(1)}, u32[]{:S(2)}, u32[]{:S(2)}) collective-permute-start(bf16[5,40,640]{2,1,0:T(8,128)(2,1)} %refs_6_.1), channel_id=1, source_target_pairs={{0,4},{4,0},{8,12},{12,8},{16,24},{20,28},{24,16},{28,20},{1,5},{5... | collective-permute-start | bytes 768008 | tf_op jit(solution)/shard_map/ppermute | solution.py:229
  3.0 0.0 copy-start.2
  3.0 0.9 %copy-done.2 = bf16[2,4,640,24]{2,3,1,0:T(8,128)(2,1)S(1)} copy-done((bf16[2,4,640,24]{2,3,1,0:T(8,128)(2,1)S(1)}, bf16[2,4,640,24]{2,3,1,0:T(8,128)(2,1)}, u32[]{:S(2)}) %copy-start.2) | copy-done | bytes 245784
  3.9 0.4 pack.1
  4.3 9.7 %all_to_all.5 = bf16[8,24,640]{2,1,0:T(8,128)(2,1)S(1)} all-to-all(bf16[8,24,640]{2,1,0:T(8,128)(2,1)S(1)} %bitcast.13), channel_id=1, replica_groups=mesh['lath'=1,'late'=2,'lonp'=4,'lonq'=4] {'late','lonq'}, dimensions={0} | all-to-all | bytes 491520 | tf_op jit(solution)/shard_map/all_to_all | solution.py:250
  14.0 0.0 collective-permute-done.1.refs_7_
  14.0 2.1 %collective-permute-start.6 = (bf16[5,40,640]{2,1,0:T(8,128)(2,1)S(1)}, bf16[5,40,640]{2,1,0:T(8,128)(2,1)}, u32[]{:S(2)}, u32[]{:S(2)}) collective-permute-start(bf16[5,40,640]{2,1,0:T(8,128)(2,1)S(1)} %collective-permute-done.1.refs_7_), channel_id=1, source_target_pairs={{16,20},{20,16},{24,28},{28,24},{17,21},{21,17},{25,29},{29,25},{1... | collective-permute-start | bytes 768008 | tf_op jit(solution)/shard_map/ppermute | solution.py:231
  16.1 0.1 collective-permute-start.5
  16.2 5.4 %collective-permute-done.6.refs_9_ = bf16[5,40,640]{2,1,0:T(8,128)(2,1)} collective-permute-done((bf16[5,40,640]{2,1,0:T(8,128)(2,1)S(1)}, bf16[5,40,640]{2,1,0:T(8,128)(2,1)}, u32[]{:S(2)}, u32[]{:S(2)}) %collective-permute-start.6) | collective-permute-done | bytes 256032 | tf_op jit(solution)/shard_map/ppermute | solution.py:231
  21.5 2.0 %collective-permute-start.7 = (bf16[5,40,640]{2,1,0:T(8,128)(2,1)}, bf16[5,40,640]{2,1,0:T(8,128)(2,1)}, u32[]{:S(2)}, u32[]{:S(2)}) collective-permute-start(bf16[5,40,640]{2,1,0:T(8,128)(2,1)} %collective-permute-done.6.refs_9_), channel_id=1, source_target_pairs={{16,0},{17,1},{18,2},{19,3},{20,4},{21,5},{22,6},{23,7},{24,8},{25... | collective-permute-start | bytes 768008 | tf_op jit(solution)/shard_map/ppermute | solution.py:233
  23.5 0.0 collective-permute-done.x_ref
  23.5 0.0 collective-permute-start.2
  23.5 1.6 %collective-permute-start.3 = (bf16[2,96,640]{2,1,0:T(8,128)(2,1)S(1)}, bf16[2,96,640]{2,1,0:T(8,128)(2,1)}, u32[]{:S(2)}, u32[]{:S(2)}) collective-permute-start(bf16[2,96,640]{2,1,0:T(8,128)(2,1)S(1)} %bitcast.10), channel_id=1, source_target_pairs={{0,8},{4,12},{8,0},{12,4},{1,9},{5,13},{9,1},{13,5},{2,10},{6,14},... | collective-permute-start | bytes 737288 | tf_op jit(solution)/shard_map/ppermute | solution.py:33
  25.2 1.0 %collective-permute-start.4 = (bf16[2,96,640]{2,1,0:T(8,128)(2,1)S(1)}, bf16[2,96,640]{2,1,0:T(8,128)(2,1)}, u32[]{:S(2)}, u32[]{:S(2)}) collective-permute-start(bf16[2,96,640]{2,1,0:T(8,128)(2,1)S(1)} %bitcast.11), channel_id=1, source_target_pairs={{0,12},{4,8},{8,4},{12,0},{1,13},{5,9},{9,5},{13,1},{2,14},{6,10},... | collective-permute-start | bytes 737288 | tf_op jit(solution)/shard_map/ppermute | solution.py:33
  26.2 0.8 %copy.6.shift_ref = s32[8,3]{1,0:T(8,128)S(1)} copy(s32[8,3]{0,1:T(4,128)} %param.8) | data formatting | bytes 192 | tf_op args[3]
  26.9 0.1 stack.28.place_ref
  27.0 0.0 copy-start
  27.0 1.8 %copy-done = bf16[5,4,3,3,64,64]{5,4,3,2,1,0:T(8,128)(2,1)S(1)} copy-done((bf16[5,4,3,3,64,64]{5,4,3,2,1,0:T(8,128)(2,1)S(1)}, bf16[5,4,3,3,64,64]{5,4,3,2,1,0:T(8,128)(2,1)}, u32[]{:S(2)}) %copy-start) | copy-done | bytes 1474584
  28.9 2.4 %turn.2.refs_4_ = bf16[4,15,64,192]{3,2,1,0:T(8,128)(2,1)S(1)} custom-call(bf16[5,4,3,3,64,64]{5,4,3,2,1,0:T(8,128)(2,1)S(1)} %copy-done), custom_call_target="tpu_custom_call" | custom-call | tf_op jit(solution)/shard_map/turn/pallas_call | solution.py:215
  31.3 0.0 copy-start.1
  31.3 0.0 copy-start.3
  31.3 2.4 %turn.3.refs_5_ = bf16[4,15,64,192]{3,2,1,0:T(8,128)(2,1)S(1)} custom-call(bf16[5,4,3,3,64,64]{5,4,3,2,1,0:T(8,128)(2,1)S(1)} %collective-permute-done.x_ref), custom_call_target="tpu_custom_call" | custom-call | tf_op jit(solution)/shard_map/turn/pallas_call | solution.py:215
  33.7 0.0 collective-permute-done.5.refs_8_
  33.8 0.0 collective-permute-done.7.refs_10_
  33.8 0.0 collective-permute-done.2.refs_1_
  33.8 5.3 %collective-permute-done.3.refs_2_ = bf16[2,96,640]{2,1,0:T(8,128)(2,1)} collective-permute-done((bf16[2,96,640]{2,1,0:T(8,128)(2,1)S(1)}, bf16[2,96,640]{2,1,0:T(8,128)(2,1)}, u32[]{:S(2)}, u32[]{:S(2)}) %collective-permute-start.3) | collective-permute-done | bytes 245792 | tf_op jit(solution)/shard_map/ppermute | solution.py:33
  39.1 4.5 %collective-permute-done.4.refs_3_ = bf16[2,96,640]{2,1,0:T(8,128)(2,1)} collective-permute-done((bf16[2,96,640]{2,1,0:T(8,128)(2,1)S(1)}, bf16[2,96,640]{2,1,0:T(8,128)(2,1)}, u32[]{:S(2)}, u32[]{:S(2)}) %collective-permute-start.4) | collective-permute-done | bytes 245792 | tf_op jit(solution)/shard_map/ppermute | solution.py:33
  43.6 0.0 copy-done.1
  43.6 0.0 copy-done.3
  43.7 7.0 %conv_mix.1 = (bf16[4,24,640]{2,1,0:T(8,128)(2,1)S(1)}, bf16[4,24,640]{2,1,0:T(8,128)(2,1)S(1)}, bf16[4,24,640]{2,1,0:T(8,128)(2,1)S(1)}, bf16[4,24,640]{2,1,0:T...) custom-call(s32[5,8]{1,0:T(8,128)S(1)} %copy-done.3, ...), custom_call_target="tpu_custom_call" | custom-call | tf_op jit(solution)/shard_map/conv_mix/pallas_call | solution.py:159
  50.6 0.6 collective-permute-start.8
  51.2 0.1 collective-permute-start.9
  51.3 2.0 %collective-permute-start.10 = (bf16[4,24,640]{2,1,0:T(8,128)(2,1)S(1)}, bf16[4,24,640]{2,1,0:T(8,128)(2,1)S(1)}, u32[]{:S(2)}, u32[]{:S(2)}) collective-permute-start(bf16[4,24,640]{2,1,0:T(8,128)(2,1)S(1)} %get-tuple-element.26), channel_id=1, source_target_pairs={{0,3},{1,2},{2,1},{3,0},{16,19},{17,18},{18,17},{19,16},{4,7},{5,6... | collective-permute-start | bytes 368648 | tf_op jit(solution)/shard_map/ppermute | solution.py:275
  53.3 0.0 collective-permute-start.11
  53.3 0.9 %collective-permute-start.12 = (bf16[4,24,640]{2,1,0:T(8,128)(2,1)S(1)}, bf16[4,24,640]{2,1,0:T(8,128)(2,1)S(1)}, u32[]{:S(2)}, u32[]{:S(2)}) collective-permute-start(bf16[4,24,640]{2,1,0:T(8,128)(2,1)S(1)} %get-tuple-element.28), channel_id=1, source_target_pairs={{0,17},{1,16},{2,19},{3,18},{16,1},{17,0},{18,3},{19,2},{4,21},{5,... | collective-permute-start | bytes 368648 | tf_op jit(solution)/shard_map/ppermute | solution.py:275
  54.3 1.2 %collective-permute-done.8.refs_1_ = bf16[4,24,640]{2,1,0:T(8,128)(2,1)S(1)} collective-permute-done((bf16[4,24,640]{2,1,0:T(8,128)(2,1)S(1)}, bf16[4,24,640]{2,1,0:T(8,128)(2,1)S(1)}, u32[]{:S(2)}, u32[]{:S(2)}) %collective-permute-start.8) | collective-permute-done | bytes 122912 | tf_op jit(solution)/shard_map/ppermute | solution.py:275
  55.5 0.0 collective-permute-start.13
  55.5 3.1 %collective-permute-done.9.refs_2_ = bf16[4,24,640]{2,1,0:T(8,128)(2,1)S(1)} collective-permute-done((bf16[4,24,640]{2,1,0:T(8,128)(2,1)S(1)}, bf16[4,24,640]{2,1,0:T(8,128)(2,1)S(1)}, u32[]{:S(2)}, u32[]{:S(2)}) %collective-permute-start.9) | collective-permute-done | bytes 122912 | tf_op jit(solution)/shard_map/ppermute | solution.py:275
  58.6 0.0 collective-permute-start.14
  58.6 0.0 collective-permute-done.10.refs_3_
  58.6 0.0 collective-permute-done.11.refs_4_
  58.6 1.5 %collective-permute-done.12.refs_5_ = bf16[4,24,640]{2,1,0:T(8,128)(2,1)S(1)} collective-permute-done((bf16[4,24,640]{2,1,0:T(8,128)(2,1)S(1)}, bf16[4,24,640]{2,1,0:T(8,128)(2,1)S(1)}, u32[]{:S(2)}, u32[]{:S(2)}) %collective-permute-start.12) | collective-permute-done | bytes 122912 | tf_op jit(solution)/shard_map/ppermute | solution.py:275
  60.1 0.9 %collective-permute-done.13.refs_6_ = bf16[4,24,640]{2,1,0:T(8,128)(2,1)S(1)} collective-permute-done((bf16[4,24,640]{2,1,0:T(8,128)(2,1)S(1)}, bf16[4,24,640]{2,1,0:T(8,128)(2,1)S(1)}, u32[]{:S(2)}, u32[]{:S(2)}) %collective-permute-start.13) | collective-permute-done | bytes 122912 | tf_op jit(solution)/shard_map/ppermute | solution.py:275
  61.0 3.3 %collective-permute-done.14.refs_7_ = bf16[4,24,640]{2,1,0:T(8,128)(2,1)S(1)} collective-permute-done((bf16[4,24,640]{2,1,0:T(8,128)(2,1)S(1)}, bf16[4,24,640]{2,1,0:T(8,128)(2,1)S(1)}, u32[]{:S(2)}, u32[]{:S(2)}) %collective-permute-start.14) | collective-permute-done | bytes 122912 | tf_op jit(solution)/shard_map/ppermute | solution.py:275
  64.3 1.4 %finish.1 = bf16[2,4,24,640]{3,2,1,0:T(8,128)(2,1)} custom-call(s32[7]{0:T(128)S(1)} %stack.28.place_ref, bf16[4,24,640]{2,1,0:T(8,128)(2,1)S(1)} %get-tuple-element.23.refs_0_, bf16[4,24,640]{2,1,0:T(8,128)(2,1)S(1)} %collective-permute-done.8.refs_1_, bf16[4,24,640]{2,1,0:T(8,128)(2,1)S(1)} %collective-permute-done.9.refs_2_, ...), custom_call_target="tpu_custom_call" | custom-call | tf_op jit(solution)/shard_map/finish/pallas_call | solution.py:187
Async XLA Ops:
  0.0 23.5 %collective-permute-start = (bf16[5,4,3,3,64,64]{5,4,3,2,1,0:T(8,128)(2,1)}, bf16[5,4,3,3,64,64]{5,4,3,2,1,0:T(8,128)(2,1)S(1)}, u32[]{:S(2)}, u32[]{:S(2)}) collective-permute-start(bf16[5,4,3,3,64,64]{5,4,3,2,1,0:T(8,128)(2,1)} %x_ref), channel_id=1, source_target_pairs={{0,16},{16,0},{1,17},{17,1},{2,18},{18,2},{3,19},{19,3},{4,20},{20... | collective-permute-start | bytes 4423688 | tf_op jit(solution)/shard_map/ppermute | solution.py:33
  0.7 13.4 %collective-permute-start.1 = (bf16[5,40,640]{2,1,0:T(8,128)(2,1)}, bf16[5,40,640]{2,1,0:T(8,128)(2,1)S(1)}, u32[]{:S(2)}, u32[]{:S(2)}) collective-permute-start(bf16[5,40,640]{2,1,0:T(8,128)(2,1)} %refs_6_.1), channel_id=1, source_target_pairs={{0,4},{4,0},{8,12},{12,8},{16,24},{20,28},{24,16},{28,20},{1,5},{5... | collective-permute-start | bytes 768008 | tf_op jit(solution)/shard_map/ppermute | solution.py:229
  3.0 0.9 %copy-start.2 = (bf16[2,4,640,24]{2,3,1,0:T(8,128)(2,1)S(1)}, bf16[2,4,640,24]{2,3,1,0:T(8,128)(2,1)}, u32[]{:S(2)}) copy-start(bf16[2,4,640,24]{2,3,1,0:T(8,128)(2,1)} %param.5) | copy-start | bytes 737284
  14.0 7.5 %collective-permute-start.6 = (bf16[5,40,640]{2,1,0:T(8,128)(2,1)S(1)}, bf16[5,40,640]{2,1,0:T(8,128)(2,1)}, u32[]{:S(2)}, u32[]{:S(2)}) collective-permute-start(bf16[5,40,640]{2,1,0:T(8,128)(2,1)S(1)} %collective-permute-done.1.refs_7_), channel_id=1, source_target_pairs={{16,20},{20,16},{24,28},{28,24},{17,21},{21,17},{25,29},{29,25},{1... | collective-permute-start | bytes 768008 | tf_op jit(solution)/shard_map/ppermute | solution.py:231
  16.1 17.6 %collective-permute-start.5 = (bf16[5,40,640]{2,1,0:T(8,128)(2,1)S(1)}, bf16[5,40,640]{2,1,0:T(8,128)(2,1)}, u32[]{:S(2)}, u32[]{:S(2)}) collective-permute-start(bf16[5,40,640]{2,1,0:T(8,128)(2,1)S(1)} %collective-permute-done.1.refs_7_), channel_id=1, source_target_pairs={{0,16},{16,0},{1,17},{17,1},{2,18},{18,2},{3,19},{19,3},{4,20},{20... | collective-permute-start | bytes 768008 | tf_op jit(solution)/shard_map/ppermute | solution.py:33
  21.5 12.2 %collective-permute-start.7 = (bf16[5,40,640]{2,1,0:T(8,128)(2,1)}, bf16[5,40,640]{2,1,0:T(8,128)(2,1)}, u32[]{:S(2)}, u32[]{:S(2)}) collective-permute-start(bf16[5,40,640]{2,1,0:T(8,128)(2,1)} %collective-permute-done.6.refs_9_), channel_id=1, source_target_pairs={{16,0},{17,1},{18,2},{19,3},{20,4},{21,5},{22,6},{23,7},{24,8},{25... | collective-permute-start | bytes 768008 | tf_op jit(solution)/shard_map/ppermute | solution.py:233
  23.5 10.2 %collective-permute-start.2 = (bf16[2,96,640]{2,1,0:T(8,128)(2,1)S(1)}, bf16[2,96,640]{2,1,0:T(8,128)(2,1)}, u32[]{:S(2)}, u32[]{:S(2)}) collective-permute-start(bf16[2,96,640]{2,1,0:T(8,128)(2,1)S(1)} %bitcast.9), channel_id=1, source_target_pairs={{0,4},{4,0},{8,12},{12,8},{1,5},{5,1},{9,13},{13,9},{2,6},{6,2},{1... | collective-permute-start | bytes 737288 | tf_op jit(solution)/shard_map/ppermute | solution.py:33
  23.5 15.6 %collective-permute-start.3 = (bf16[2,96,640]{2,1,0:T(8,128)(2,1)S(1)}, bf16[2,96,640]{2,1,0:T(8,128)(2,1)}, u32[]{:S(2)}, u32[]{:S(2)}) collective-permute-start(bf16[2,96,640]{2,1,0:T(8,128)(2,1)S(1)} %bitcast.10), channel_id=1, source_target_pairs={{0,8},{4,12},{8,0},{12,4},{1,9},{5,13},{9,1},{13,5},{2,10},{6,14},... | collective-permute-start | bytes 737288 | tf_op jit(solution)/shard_map/ppermute | solution.py:33
  25.2 18.5 %collective-permute-start.4 = (bf16[2,96,640]{2,1,0:T(8,128)(2,1)S(1)}, bf16[2,96,640]{2,1,0:T(8,128)(2,1)}, u32[]{:S(2)}, u32[]{:S(2)}) collective-permute-start(bf16[2,96,640]{2,1,0:T(8,128)(2,1)S(1)} %bitcast.11), channel_id=1, source_target_pairs={{0,12},{4,8},{8,4},{12,0},{1,13},{5,9},{9,5},{13,1},{2,14},{6,10},... | collective-permute-start | bytes 737288 | tf_op jit(solution)/shard_map/ppermute | solution.py:33
  27.0 1.8 %copy-start = (bf16[5,4,3,3,64,64]{5,4,3,2,1,0:T(8,128)(2,1)S(1)}, bf16[5,4,3,3,64,64]{5,4,3,2,1,0:T(8,128)(2,1)}, u32[]{:S(2)}) copy-start(bf16[5,4,3,3,64,64]{5,4,3,2,1,0:T(8,128)(2,1)} %x_ref) | copy-start | bytes 4423684
  31.3 12.4 %copy-start.1 = (bf16[5,40,640]{2,1,0:T(8,128)(2,1)S(1)}, bf16[5,40,640]{2,1,0:T(8,128)(2,1)}, u32[]{:S(2)}) copy-start(bf16[5,40,640]{2,1,0:T(8,128)(2,1)} %refs_6_.1) | copy-start | bytes 768004
  31.3 12.3 %copy-start.3 = (s32[5,8]{1,0:T(8,128)S(1)}, s32[5,8]{1,0:T(8,128)}, u32[]{:S(2)}) copy-start(s32[5,8]{1,0:T(8,128)} %low_ref) | copy-start | bytes 484
  50.6 4.8 %collective-permute-start.8 = (bf16[4,24,640]{2,1,0:T(8,128)(2,1)S(1)}, bf16[4,24,640]{2,1,0:T(8,128)(2,1)S(1)}, u32[]{:S(2)}, u32[]{:S(2)}) collective-permute-start(bf16[4,24,640]{2,1,0:T(8,128)(2,1)S(1)} %get-tuple-element.24), channel_id=1, source_target_pairs={{0,1},{1,0},{2,3},{3,2},{16,17},{17,16},{18,19},{19,18},{4,5},{5,4... | collective-permute-start | bytes 368648 | tf_op jit(solution)/shard_map/ppermute | solution.py:275
  51.2 7.4 %collective-permute-start.9 = (bf16[4,24,640]{2,1,0:T(8,128)(2,1)S(1)}, bf16[4,24,640]{2,1,0:T(8,128)(2,1)S(1)}, u32[]{:S(2)}, u32[]{:S(2)}) collective-permute-start(bf16[4,24,640]{2,1,0:T(8,128)(2,1)S(1)} %get-tuple-element.25), channel_id=1, source_target_pairs={{0,2},{1,3},{2,0},{3,1},{16,18},{17,19},{18,16},{19,17},{4,6},{5,7... | collective-permute-start | bytes 368648 | tf_op jit(solution)/shard_map/ppermute | solution.py:275
  51.3 7.3 %collective-permute-start.10 = (bf16[4,24,640]{2,1,0:T(8,128)(2,1)S(1)}, bf16[4,24,640]{2,1,0:T(8,128)(2,1)S(1)}, u32[]{:S(2)}, u32[]{:S(2)}) collective-permute-start(bf16[4,24,640]{2,1,0:T(8,128)(2,1)S(1)} %get-tuple-element.26), channel_id=1, source_target_pairs={{0,3},{1,2},{2,1},{3,0},{16,19},{17,18},{18,17},{19,16},{4,7},{5,6... | collective-permute-start | bytes 368648 | tf_op jit(solution)/shard_map/ppermute | solution.py:275
  53.3 5.3 %collective-permute-start.11 = (bf16[4,24,640]{2,1,0:T(8,128)(2,1)S(1)}, bf16[4,24,640]{2,1,0:T(8,128)(2,1)S(1)}, u32[]{:S(2)}, u32[]{:S(2)}) collective-permute-start(bf16[4,24,640]{2,1,0:T(8,128)(2,1)S(1)} %get-tuple-element.27), channel_id=1, source_target_pairs={{0,16},{1,17},{2,18},{3,19},{16,0},{17,1},{18,2},{19,3},{4,20},{5,... | collective-permute-start | bytes 368648 | tf_op jit(solution)/shard_map/ppermute | solution.py:275
  53.3 6.8 %collective-permute-start.12 = (bf16[4,24,640]{2,1,0:T(8,128)(2,1)S(1)}, bf16[4,24,640]{2,1,0:T(8,128)(2,1)S(1)}, u32[]{:S(2)}, u32[]{:S(2)}) collective-permute-start(bf16[4,24,640]{2,1,0:T(8,128)(2,1)S(1)} %get-tuple-element.28), channel_id=1, source_target_pairs={{0,17},{1,16},{2,19},{3,18},{16,1},{17,0},{18,3},{19,2},{4,21},{5,... | collective-permute-start | bytes 368648 | tf_op jit(solution)/shard_map/ppermute | solution.py:275
  55.5 5.5 %collective-permute-start.13 = (bf16[4,24,640]{2,1,0:T(8,128)(2,1)S(1)}, bf16[4,24,640]{2,1,0:T(8,128)(2,1)S(1)}, u32[]{:S(2)}, u32[]{:S(2)}) collective-permute-start(bf16[4,24,640]{2,1,0:T(8,128)(2,1)S(1)} %get-tuple-element.29), channel_id=1, source_target_pairs={{0,18},{1,19},{2,16},{3,17},{16,2},{17,3},{18,0},{19,1},{4,22},{5,... | collective-permute-start | bytes 368648 | tf_op jit(solution)/shard_map/ppermute | solution.py:275
  58.6 5.7 %collective-permute-start.14 = (bf16[4,24,640]{2,1,0:T(8,128)(2,1)S(1)}, bf16[4,24,640]{2,1,0:T(8,128)(2,1)S(1)}, u32[]{:S(2)}, u32[]{:S(2)}) collective-permute-start(bf16[4,24,640]{2,1,0:T(8,128)(2,1)S(1)} %get-tuple-element.30), channel_id=1, source_target_pairs={{0,19},{1,18},{2,17},{3,16},{16,3},{17,2},{18,1},{19,0},{4,23},{5,... | collective-permute-start | bytes 368648 | tf_op jit(solution)/shard_map/ppermute | solution.py:275

commit v10 on v9

--- a/solution.py
+++ b/solution.py
@@ -68,13 +68,13 @@
 def conv_mix_kernel(geometry, counts, low_ref, shift_ref, place_ref, *refs):
     bases, taps, slots, halo, sub, groups = geometry
     refs = list(refs)
-    field_refs = [refs.pop(0) for _ in range(counts[0])]
+    field_slots = [[refs.pop(0) for _ in range(n)] for n in counts[0]]
     weight_refs = [refs.pop(0) for _ in range(counts[1])]
     mix_slots = [[refs.pop(0) for _ in range(n)] for n in counts[2]]
     field_rows, total, mix_all, mixed = refs[-4:]
     outs = refs[:-4]
-    late, span, _ = field_refs[0].shape
-    owners = len(field_refs)
+    late, span, _ = field_slots[0][0].shape
+    owners = len(field_slots)
     depth, width = mix_slots[0][0].shape[1:]
     channels = owners * depth
     padded = total.shape[-1]
@@ -87,9 +87,9 @@
     field_rows[...] = jnp.zeros_like(field_rows)
     for s in range(late):
         lat = partner_in_kernel(member, s, late)
-        for d, ref in enumerate(field_refs):
+        for d, slot in enumerate(field_slots):
             at = pl.ds(pl.multiple_of(partner_in_kernel(owner, d, owners) * span, sub), span)
-            value = ref[lat]
+            value = added(slot, lat)
             for r in range(rows):
                 field_rows[r, at, :channels] = value[:, r * channels : (r + 1) * channels]
 
@@ -144,7 +144,7 @@
 def conv_mix(low, shift, place, fields, weights, mix, halo, groups, block):
     bases, all_rows = low.shape
     slots = shift.shape[1]
-    late, span, _ = fields[0].shape
+    late, span, _ = fields[0][0].shape
     owners = len(fields)
     rows = all_rows // late
     depth, width = mix[0][0].shape[1:]
@@ -154,8 +154,8 @@
     shapes = [jax.ShapeDtypeStruct((rows, span // groups, width), jnp.bfloat16)] * (late * groups)
     if halo:
         shapes.append(jax.ShapeDtypeStruct((2, halo, span, width), jnp.bfloat16))
-    operands = fields + weights + [x for slot in mix for x in slot]
-    counts = (len(fields), len(weights), [len(s) for s in mix])
+    operands = [x for slot in fields for x in slot] + weights + [x for slot in mix for x in slot]
+    counts = ([len(s) for s in fields], len(weights), [len(s) for s in mix])
     return pl.pallas_call(
         functools.partial(conv_mix_kernel, (bases, taps, slots, halo, sub, groups), counts),
         out_shape=shapes,
@@ -222,19 +222,35 @@
     )(x)
 
 
-def gather_mix(mix, spread, late, owners):
+def pairs(*cores):
+    return [(4 * c + a, 4 * c + b) for c, planes in enumerate(cores) for a, b in planes]
+
+
+NEAR = [(0, 1), (1, 0), (2, 3), (3, 2)]
+FAR = [(0, 2), (2, 0), (1, 3), (3, 1)]
+MIDDLE = [(1, 2), (2, 1)]
+TO_ENDS = [(1, 0), (2, 3)]
+
+
+def gather(spread, mix, kernels, late, owners):
     core, own = lax.axis_index("late"), lax.axis_index("lonp")
-    if owners == 4 and late == 2:
-        route = [(p, p ^ 1) for p in range(4)] + [(4 + p, 4 + (p ^ 2)) for p in range(4)]
-        first = lax.ppermute(mix, ("late", "lonp"), route)
-        spread, first = lax.optimization_barrier((spread, first))
-        third = lax.ppermute(first, ("late", "lonp"), [(4 + p, 4 + (p ^ 1)) for p in range(4)])
-        other = trade(first, "late", 1, late)
-        copied = lax.ppermute(third, "late", [(1, 0)])
-        slots, origins = [[mix], [first], [other], [third, copied]], [own, own ^ (1 + core), own ^ (2 - core), own ^ 3]
-        return slots, origins, spread
-    slots = [[mix]] + [[trade(mix, "lonp", d, owners)] for d in range(1, owners)]
-    return slots, [partner(own, d, owners) for d in range(owners)], spread
+    if owners != 4 or late != 2:
+        fields = [[spread]] + [[trade(spread, "lonp", d, owners)] for d in range(1, owners)]
+        mixes = [[mix]] + [[trade(mix, "lonp", d, owners)] for d in range(1, owners)]
+        return fields, mixes, [partner(own, d, owners) for d in range(owners)], kernels
+    first = lax.ppermute(mix, ("late", "lonp"), pairs(NEAR, FAR))
+    spread, first, *kernels = lax.optimization_barrier((spread, first, *kernels))
+    two = lax.ppermute(spread, "lonp", FAR)
+    one = lax.ppermute(spread, "lonp", NEAR)
+    spread_late, two, first = lax.optimization_barrier((spread, two, first))
+    passed = lax.ppermute(two, "lonp", TO_ENDS)
+    middle = lax.ppermute(spread_late, "lonp", MIDDLE)
+    third = lax.ppermute(first, ("late", "lonp"), pairs([], NEAR))
+    other = trade(first, "late", 1, late)
+    copied = lax.ppermute(third, "late", [(1, 0)])
+    fields = [[spread], [one], [two], [middle, passed]]
+    mixes = [[mix], [first], [other], [third, copied]]
+    return fields, mixes, [own, own ^ (1 + core), own ^ (2 - core), own ^ 3], kernels
 
 
 def per_device(sizes, fields, kernel, band_low, block_shift, mix_weight):
@@ -248,11 +264,9 @@
     packed = pack(fields.transpose(0, 1, 3, 2), groups, owners)
     packed = packed.reshape((late * groups,) + packed.shape[2:])
     spread = lax.all_to_all(packed, ("late", "lonq"), split_axis=0, concat_axis=0, tiled=True)
-    mix, origins, spread = gather_mix(mix_weight, spread, late, owners)
-    *kernels, spread = lax.optimization_barrier((*kernels, spread))
+    spread = spread.reshape(late, groups * cells, -1)
+    spread, mix, origins, kernels = gather(spread, mix_weight, kernels, late, owners)
     weights = [turn(x) for x in kernels]
-    spread = spread.reshape(late, groups * cells, -1)
-    spread = [spread] + [trade(spread, "lonp", d, owners) for d in range(1, owners)]
 
     start = lax.axis_index("lath") * all_rows
     low = lax.dynamic_slice_in_dim(band_low, start, all_rows, 1)

time: 66 us -> 69.3 us (1.050)
  the two profiles are of different devices: /device:TPU:9 before, /device:TPU:0 now
where the time goes in v10:
time: 69.3 us; the launch traced here: 68.4 us
  waiting for transfers between devices  21.1 us (30%)
  starting transfers between devices  19 us (27%)
  Pallas kernels  13.8 us (20%)
  blocking collectives  10.8 us (16%)
  local copies, waits for them, and re-layouts  3.63 us (5%)
    ppermute x1, waiting for transfers between devices, gather(): two = lax.ppermute(spread, 'lonp', FAR)  12.5 us
    all_to_all x1, blocking collectives, per_device(): lax.all_to_all(packed, ('late', 'lonq'), split_axis=0, concat_axis=0, til...  10.8 us
    ppermute x7, starting transfers between devices, per_device(): lax.ppermute(partial[dl * groups + dq], ('late', 'lonq'), [(l * groups +...  7.21 us
    pallas_call x1, Pallas kernels, conv_mix(): pl.pallas_call(functools.partial(conv_mix_kernel, (bases, taps, slots, ha...  7.06 us
    ppermute x7, waiting for transfers between devices, per_device(): lax.ppermute(partial[dl * groups + dq], ('late', 'lonq'), [(l * groups +...  6.55 us
    pallas_call x2, Pallas kernels, turn(): pl.pallas_call(turn_kernel, out_shape=jax.ShapeDtypeStruct((rows, bases *...  4.86 us
    unnamed x9, local copies, waits for them, and re-layouts  3.55 us
    ppermute x1, starting transfers between devices, gather(): first = lax.ppermute(mix, ('late', 'lonp'), pairs(NEAR, FAR))  2.57 us
  transfers between devices with their start and end apart: 16, of which 5 were waited for; matrix products, arithmetic and copies ran while one was open for 1% of the time, Pallas kernels for 8%

profile of v10, /device:TPU:0, one launch (start us, length us, event | category | flops | bytes accessed | tf_op | source)
XLA Modules:
  0.0 68.4 jit_solution(1284456451206739260)
XLA Ops:
  0.0 0.5 collective-permute-start.1
  0.5 2.6 %collective-permute-start = (bf16[5,40,640]{2,1,0:T(8,128)(2,1)}, bf16[5,40,640]{2,1,0:T(8,128)(2,1)S(1)}, u32[]{:S(2)}, u32[]{:S(2)}) collective-permute-start(bf16[5,40,640]{2,1,0:T(8,128)(2,1)} %refs_7_.1), channel_id=1, source_target_pairs={{0,4},{4,0},{8,12},{12,8},{16,24},{24,16},{20,28},{28,20},{1,5},{5... | collective-permute-start | bytes 768008 | tf_op jit(solution)/shard_map/ppermute | solution.py:241
  3.0 0.0 copy-start.2
  3.0 0.9 %copy-done.2 = bf16[2,4,640,24]{2,3,1,0:T(8,128)(2,1)S(1)} copy-done((bf16[2,4,640,24]{2,3,1,0:T(8,128)(2,1)S(1)}, bf16[2,4,640,24]{2,3,1,0:T(8,128)(2,1)}, u32[]{:S(2)}) %copy-start.2) | copy-done | bytes 245784
  4.0 0.4 pack.1
  4.4 10.8 %all_to_all.5 = bf16[8,24,640]{2,1,0:T(8,128)(2,1)S(1)} all-to-all(bf16[8,24,640]{2,1,0:T(8,128)(2,1)S(1)} %bitcast.13), channel_id=1, replica_groups=mesh['lath'=1,'late'=2,'lonp'=4,'lonq'=4] {'late','lonq'}, dimensions={0} | all-to-all | bytes 491520 | tf_op jit(solution)/shard_map/all_to_all | solution.py:266
  15.2 0.0 collective-permute-done.refs_8_
  15.2 0.0 collective-permute-done.1.x_ref
  15.2 1.7 %collective-permute-start.3 = (bf16[2,96,640]{2,1,0:T(8,128)(2,1)S(1)}, bf16[2,96,640]{2,1,0:T(8,128)(2,1)}, u32[]{:S(2)}, u32[]{:S(2)}) collective-permute-start(bf16[2,96,640]{2,1,0:T(8,128)(2,1)S(1)} %bitcast.9), channel_id=1, source_target_pairs={{0,8},{8,0},{4,12},{12,4},{1,9},{9,1},{5,13},{13,5},{2,10},{10,2},... | collective-permute-start | bytes 737288 | tf_op jit(solution)/shard_map/ppermute | solution.py:243
  16.9 12.5 %collective-permute-done.3.refs_2_ = bf16[2,96,640]{2,1,0:T(8,128)(2,1)} collective-permute-done((bf16[2,96,640]{2,1,0:T(8,128)(2,1)S(1)}, bf16[2,96,640]{2,1,0:T(8,128)(2,1)}, u32[]{:S(2)}, u32[]{:S(2)}) %collective-permute-start.3) | collective-permute-done | bytes 245792 | tf_op jit(solution)/shard_map/ppermute | solution.py:243
  29.4 1.4 %collective-permute-start.7 = (bf16[5,40,640]{2,1,0:T(8,128)(2,1)S(1)}, bf16[5,40,640]{2,1,0:T(8,128)(2,1)}, u32[]{:S(2)}, u32[]{:S(2)}) collective-permute-start(bf16[5,40,640]{2,1,0:T(8,128)(2,1)S(1)} %collective-permute-done.refs_8_), channel_id=1, source_target_pairs={{16,20},{20,16},{24,28},{28,24},{17,21},{21,17},{25,29},{29,25},{1... | collective-permute-start | bytes 768008 | tf_op jit(solution)/shard_map/ppermute | solution.py:248
  30.8 0.0 collective-permute-start.6
  30.8 0.0 collective-permute-done.7.refs_10_
  30.8 1.3 %collective-permute-start.8 = (bf16[5,40,640]{2,1,0:T(8,128)(2,1)}, bf16[5,40,640]{2,1,0:T(8,128)(2,1)}, u32[]{:S(2)}, u32[]{:S(2)}) collective-permute-start(bf16[5,40,640]{2,1,0:T(8,128)(2,1)} %collective-permute-done.7.refs_10_), channel_id=1, source_target_pairs={{16,0},{17,1},{18,2},{19,3},{20,4},{21,5},{22,6},{23,7},{24,8},{25... | collective-permute-start | bytes 768008 | tf_op jit(solution)/shard_map/ppermute | solution.py:250
  32.1 1.7 %collective-permute-start.2 = (bf16[2,96,640]{2,1,0:T(8,128)(2,1)S(1)}, bf16[2,96,640]{2,1,0:T(8,128)(2,1)}, u32[]{:S(2)}, u32[]{:S(2)}) collective-permute-start(bf16[2,96,640]{2,1,0:T(8,128)(2,1)S(1)} %bitcast.10), channel_id=1, source_target_pairs={{0,4},{4,0},{8,12},{12,8},{1,5},{5,1},{9,13},{13,9},{2,6},{6,2},{1... | collective-permute-start | bytes 737288 | tf_op jit(solution)/shard_map/ppermute | solution.py:244
  33.8 1.4 %collective-permute-start.4 = (bf16[2,96,640]{2,1,0:T(8,128)(2,1)S(1)}, bf16[2,96,640]{2,1,0:T(8,128)(2,1)}, u32[]{:S(2)}, u32[]{:S(2)}) collective-permute-start(bf16[2,96,640]{2,1,0:T(8,128)(2,1)S(1)} %bitcast.11), channel_id=1, source_target_pairs={{4,8},{8,4},{5,9},{9,5},{6,10},{10,6},{7,11},{11,7},{20,24},{24,20... | collective-permute-start | bytes 737288 | tf_op jit(solution)/shard_map/ppermute | solution.py:247
  35.2 1.3 %collective-permute-start.5 = (bf16[2,96,640]{2,1,0:T(8,128)(2,1)}, bf16[2,96,640]{2,1,0:T(8,128)(2,1)}, u32[]{:S(2)}, u32[]{:S(2)}) collective-permute-start(bf16[2,96,640]{2,1,0:T(8,128)(2,1)} %collective-permute-done.3.refs_2_), channel_id=1, source_target_pairs={{4,0},{8,12},{5,1},{9,13},{6,2},{10,14},{7,3},{11,15},{20,16},{24,... | collective-permute-start | bytes 737288 | tf_op jit(solution)/shard_map/ppermute | solution.py:246
  36.5 0.8 %copy.6.shift_ref = s32[8,3]{1,0:T(8,128)S(1)} copy(s32[8,3]{0,1:T(4,128)} %param.8) | data formatting | bytes 192 | tf_op args[3]
  37.3 0.1 stack.28.place_ref
  37.3 0.0 copy-start
  37.3 1.8 %copy-done = bf16[5,4,3,3,64,64]{5,4,3,2,1,0:T(8,128)(2,1)S(1)} copy-done((bf16[5,4,3,3,64,64]{5,4,3,2,1,0:T(8,128)(2,1)S(1)}, bf16[5,4,3,3,64,64]{5,4,3,2,1,0:T(8,128)(2,1)}, u32[]{:S(2)}) %copy-start) | copy-done | bytes 1474584
  39.2 2.4 %turn.2.refs_5_ = bf16[4,15,64,192]{3,2,1,0:T(8,128)(2,1)S(1)} custom-call(bf16[5,4,3,3,64,64]{5,4,3,2,1,0:T(8,128)(2,1)S(1)} %copy-done), custom_call_target="tpu_custom_call" | custom-call | tf_op jit(solution)/shard_map/turn/pallas_call | solution.py:215
  41.6 0.0 copy-start.1
  41.6 0.0 copy-start.3
  41.6 2.4 %turn.3.refs_6_ = bf16[4,15,64,192]{3,2,1,0:T(8,128)(2,1)S(1)} custom-call(bf16[5,4,3,3,64,64]{5,4,3,2,1,0:T(8,128)(2,1)S(1)} %collective-permute-done.1.x_ref), custom_call_target="tpu_custom_call" | custom-call | tf_op jit(solution)/shard_map/turn/pallas_call | solution.py:215
  44.1 0.0 collective-permute-done.2.refs_1_
  44.1 0.0 collective-permute-done.4.refs_3_
  44.1 2.0 %collective-permute-done.5.refs_4_ = bf16[2,96,640]{2,1,0:T(8,128)(2,1)} collective-permute-done((bf16[2,96,640]{2,1,0:T(8,128)(2,1)}, bf16[2,96,640]{2,1,0:T(8,128)(2,1)}, u32[]{:S(2)}, u32[]{:S(2)}) %collective-permute-start.5) | collective-permute-done | bytes 245792 | tf_op jit(solution)/shard_map/ppermute | solution.py:246
  46.1 0.0 collective-permute-done.6.refs_9_
  46.1 0.0 collective-permute-done.8.refs_11_
  46.1 0.0 copy-done.1
  46.1 0.0 copy-done.3
  46.1 7.1 %conv_mix.1 = (bf16[4,24,640]{2,1,0:T(8,128)(2,1)S(1)}, bf16[4,24,640]{2,1,0:T(8,128)(2,1)S(1)}, bf16[4,24,640]{2,1,0:T(8,128)(2,1)S(1)}, bf16[4,24,640]{2,1,0:T...) custom-call(s32[5,8]{1,0:T(8,128)S(1)} %copy-done.3, ...), custom_call_target="tpu_custom_call" | custom-call | tf_op jit(solution)/shard_map/conv_mix/pallas_call | solution.py:159
  53.2 0.9 %collective-permute-start.9 = (bf16[4,24,640]{2,1,0:T(8,128)(2,1)S(1)}, bf16[4,24,640]{2,1,0:T(8,128)(2,1)S(1)}, u32[]{:S(2)}, u32[]{:S(2)}) collective-permute-start(bf16[4,24,640]{2,1,0:T(8,128)(2,1)S(1)} %get-tuple-element.28), channel_id=1, source_target_pairs={{0,1},{1,0},{2,3},{3,2},{16,17},{17,16},{18,19},{19,18},{4,5},{5,4... | collective-permute-start | bytes 368648 | tf_op jit(solution)/shard_map/ppermute | solution.py:289
  54.0 0.1 collective-permute-start.10
  54.1 2.6 %collective-permute-start.11 = (bf16[4,24,640]{2,1,0:T(8,128)(2,1)S(1)}, bf16[4,24,640]{2,1,0:T(8,128)(2,1)S(1)}, u32[]{:S(2)}, u32[]{:S(2)}) collective-permute-start(bf16[4,24,640]{2,1,0:T(8,128)(2,1)S(1)} %get-tuple-element.30), channel_id=1, source_target_pairs={{0,3},{1,2},{2,1},{3,0},{16,19},{17,18},{18,17},{19,16},{4,7},{5,6... | collective-permute-start | bytes 368648 | tf_op jit(solution)/shard_map/ppermute | solution.py:289
  56.7 1.8 %collective-permute-start.12 = (bf16[4,24,640]{2,1,0:T(8,128)(2,1)S(1)}, bf16[4,24,640]{2,1,0:T(8,128)(2,1)S(1)}, u32[]{:S(2)}, u32[]{:S(2)}) collective-permute-start(bf16[4,24,640]{2,1,0:T(8,128)(2,1)S(1)} %get-tuple-element.31), channel_id=1, source_target_pairs={{0,16},{1,17},{2,18},{3,19},{16,0},{17,1},{18,2},{19,3},{4,20},{5,... | collective-permute-start | bytes 368648 | tf_op jit(solution)/shard_map/ppermute | solution.py:289
  58.5 0.4 collective-permute-start.13
  58.9 0.0 collective-permute-done.9.refs_1_
  58.9 0.4 collective-permute-start.14
  59.3 2.4 %collective-permute-done.10.refs_2_ = bf16[4,24,640]{2,1,0:T(8,128)(2,1)S(1)} collective-permute-done((bf16[4,24,640]{2,1,0:T(8,128)(2,1)S(1)}, bf16[4,24,640]{2,1,0:T(8,128)(2,1)S(1)}, u32[]{:S(2)}, u32[]{:S(2)}) %collective-permute-start.10) | collective-permute-done | bytes 122912 | tf_op jit(solution)/shard_map/ppermute | solution.py:289
  61.7 1.1 %collective-permute-start.15 = (bf16[4,24,640]{2,1,0:T(8,128)(2,1)S(1)}, bf16[4,24,640]{2,1,0:T(8,128)(2,1)S(1)}, u32[]{:S(2)}, u32[]{:S(2)}) collective-permute-start(bf16[4,24,640]{2,1,0:T(8,128)(2,1)S(1)} %get-tuple-element.34), channel_id=1, source_target_pairs={{0,19},{1,18},{2,17},{3,16},{16,3},{17,2},{18,1},{19,0},{4,23},{5,... | collective-permute-start | bytes 368648 | tf_op jit(solution)/shard_map/ppermute | solution.py:289
  62.8 0.0 collective-permute-done.11.refs_3_
  62.8 0.0 collective-permute-done.12.refs_4_
  62.8 2.2 %collective-permute-done.13.refs_5_ = bf16[4,24,640]{2,1,0:T(8,128)(2,1)S(1)} collective-permute-done((bf16[4,24,640]{2,1,0:T(8,128)(2,1)S(1)}, bf16[4,24,640]{2,1,0:T(8,128)(2,1)S(1)}, u32[]{:S(2)}, u32[]{:S(2)}) %collective-permute-start.13) | collective-permute-done | bytes 122912 | tf_op jit(solution)/shard_map/ppermute | solution.py:289
  65.0 0.0 collective-permute-done.14.refs_6_
  65.0 1.9 %collective-permute-done.15.refs_7_ = bf16[4,24,640]{2,1,0:T(8,128)(2,1)S(1)} collective-permute-done((bf16[4,24,640]{2,1,0:T(8,128)(2,1)S(1)}, bf16[4,24,640]{2,1,0:T(8,128)(2,1)S(1)}, u32[]{:S(2)}, u32[]{:S(2)}) %collective-permute-start.15) | collective-permute-done | bytes 122912 | tf_op jit(solution)/shard_map/ppermute | solution.py:289
  66.9 1.4 %finish.1 = bf16[2,4,24,640]{3,2,1,0:T(8,128)(2,1)} custom-call(s32[7]{0:T(128)S(1)} %stack.28.place_ref, bf16[4,24,640]{2,1,0:T(8,128)(2,1)S(1)} %get-tuple-element.27.refs_0_, bf16[4,24,640]{2,1,0:T(8,128)(2,1)S(1)} %collective-permute-done.9.refs_1_, bf16[4,24,640]{2,1,0:T(8,128)(2,1)S(1)} %collective-permute-done.10.refs_2_, ...), custom_call_target="tpu_custom_call" | custom-call | tf_op jit(solution)/shard_map/finish/pallas_call | solution.py:187
Async XLA Ops:
  0.0 15.2 %collective-permute-start.1 = (bf16[5,4,3,3,64,64]{5,4,3,2,1,0:T(8,128)(2,1)}, bf16[5,4,3,3,64,64]{5,4,3,2,1,0:T(8,128)(2,1)S(1)}, u32[]{:S(2)}, u32[]{:S(2)}) collective-permute-start(bf16[5,4,3,3,64,64]{5,4,3,2,1,0:T(8,128)(2,1)} %x_ref), channel_id=1, source_target_pairs={{0,16},{16,0},{1,17},{17,1},{2,18},{18,2},{3,19},{19,3},{4,20},{20... | collective-permute-start | bytes 4423688 | tf_op jit(solution)/shard_map/ppermute | solution.py:33
  0.5 14.7 %collective-permute-start = (bf16[5,40,640]{2,1,0:T(8,128)(2,1)}, bf16[5,40,640]{2,1,0:T(8,128)(2,1)S(1)}, u32[]{:S(2)}, u32[]{:S(2)}) collective-permute-start(bf16[5,40,640]{2,1,0:T(8,128)(2,1)} %refs_7_.1), channel_id=1, source_target_pairs={{0,4},{4,0},{8,12},{12,8},{16,24},{24,16},{20,28},{28,20},{1,5},{5... | collective-permute-start | bytes 768008 | tf_op jit(solution)/shard_map/ppermute | solution.py:241
  3.0 0.9 %copy-start.2 = (bf16[2,4,640,24]{2,3,1,0:T(8,128)(2,1)S(1)}, bf16[2,4,640,24]{2,3,1,0:T(8,128)(2,1)}, u32[]{:S(2)}) copy-start(bf16[2,4,640,24]{2,3,1,0:T(8,128)(2,1)} %param.5) | copy-start | bytes 737284
  15.2 14.3 %collective-permute-start.3 = (bf16[2,96,640]{2,1,0:T(8,128)(2,1)S(1)}, bf16[2,96,640]{2,1,0:T(8,128)(2,1)}, u32[]{:S(2)}, u32[]{:S(2)}) collective-permute-start(bf16[2,96,640]{2,1,0:T(8,128)(2,1)S(1)} %bitcast.9), channel_id=1, source_target_pairs={{0,8},{8,0},{4,12},{12,4},{1,9},{9,1},{5,13},{13,5},{2,10},{10,2},... | collective-permute-start | bytes 737288 | tf_op jit(solution)/shard_map/ppermute | solution.py:243
  29.4 1.4 %collective-permute-start.7 = (bf16[5,40,640]{2,1,0:T(8,128)(2,1)S(1)}, bf16[5,40,640]{2,1,0:T(8,128)(2,1)}, u32[]{:S(2)}, u32[]{:S(2)}) collective-permute-start(bf16[5,40,640]{2,1,0:T(8,128)(2,1)S(1)} %collective-permute-done.refs_8_), channel_id=1, source_target_pairs={{16,20},{20,16},{24,28},{28,24},{17,21},{21,17},{25,29},{29,25},{1... | collective-permute-start | bytes 768008 | tf_op jit(solution)/shard_map/ppermute | solution.py:248
  30.8 15.3 %collective-permute-start.6 = (bf16[5,40,640]{2,1,0:T(8,128)(2,1)S(1)}, bf16[5,40,640]{2,1,0:T(8,128)(2,1)}, u32[]{:S(2)}, u32[]{:S(2)}) collective-permute-start(bf16[5,40,640]{2,1,0:T(8,128)(2,1)S(1)} %collective-permute-done.refs_8_), channel_id=1, source_target_pairs={{0,16},{16,0},{1,17},{17,1},{2,18},{18,2},{3,19},{19,3},{4,20},{20... | collective-permute-start | bytes 768008 | tf_op jit(solution)/shard_map/ppermute | solution.py:33
  30.8 15.3 %collective-permute-start.8 = (bf16[5,40,640]{2,1,0:T(8,128)(2,1)}, bf16[5,40,640]{2,1,0:T(8,128)(2,1)}, u32[]{:S(2)}, u32[]{:S(2)}) collective-permute-start(bf16[5,40,640]{2,1,0:T(8,128)(2,1)} %collective-permute-done.7.refs_10_), channel_id=1, source_target_pairs={{16,0},{17,1},{18,2},{19,3},{20,4},{21,5},{22,6},{23,7},{24,8},{25... | collective-permute-start | bytes 768008 | tf_op jit(solution)/shard_map/ppermute | solution.py:250
  32.1 12.0 %collective-permute-start.2 = (bf16[2,96,640]{2,1,0:T(8,128)(2,1)S(1)}, bf16[2,96,640]{2,1,0:T(8,128)(2,1)}, u32[]{:S(2)}, u32[]{:S(2)}) collective-permute-start(bf16[2,96,640]{2,1,0:T(8,128)(2,1)S(1)} %bitcast.10), channel_id=1, source_target_pairs={{0,4},{4,0},{8,12},{12,8},{1,5},{5,1},{9,13},{13,9},{2,6},{6,2},{1... | collective-permute-start | bytes 737288 | tf_op jit(solution)/shard_map/ppermute | solution.py:244
  33.8 10.2 %collective-permute-start.4 = (bf16[2,96,640]{2,1,0:T(8,128)(2,1)S(1)}, bf16[2,96,640]{2,1,0:T(8,128)(2,1)}, u32[]{:S(2)}, u32[]{:S(2)}) collective-permute-start(bf16[2,96,640]{2,1,0:T(8,128)(2,1)S(1)} %bitcast.11), channel_id=1, source_target_pairs={{4,8},{8,4},{5,9},{9,5},{6,10},{10,6},{7,11},{11,7},{20,24},{24,20... | collective-permute-start | bytes 737288 | tf_op jit(solution)/shard_map/ppermute | solution.py:247
  35.2 10.9 %collective-permute-start.5 = (bf16[2,96,640]{2,1,0:T(8,128)(2,1)}, bf16[2,96,640]{2,1,0:T(8,128)(2,1)}, u32[]{:S(2)}, u32[]{:S(2)}) collective-permute-start(bf16[2,96,640]{2,1,0:T(8,128)(2,1)} %collective-permute-done.3.refs_2_), channel_id=1, source_target_pairs={{4,0},{8,12},{5,1},{9,13},{6,2},{10,14},{7,3},{11,15},{20,16},{24,... | collective-permute-start | bytes 737288 | tf_op jit(solution)/shard_map/ppermute | solution.py:246
  37.3 1.8 %copy-start = (bf16[5,4,3,3,64,64]{5,4,3,2,1,0:T(8,128)(2,1)S(1)}, bf16[5,4,3,3,64,64]{5,4,3,2,1,0:T(8,128)(2,1)}, u32[]{:S(2)}) copy-start(bf16[5,4,3,3,64,64]{5,4,3,2,1,0:T(8,128)(2,1)} %x_ref) | copy-start | bytes 4423684
  41.6 4.5 %copy-start.1 = (bf16[5,40,640]{2,1,0:T(8,128)(2,1)S(1)}, bf16[5,40,640]{2,1,0:T(8,128)(2,1)}, u32[]{:S(2)}) copy-start(bf16[5,40,640]{2,1,0:T(8,128)(2,1)} %refs_7_.1) | copy-start | bytes 768004
  41.6 4.5 %copy-start.3 = (s32[5,8]{1,0:T(8,128)S(1)}, s32[5,8]{1,0:T(8,128)}, u32[]{:S(2)}) copy-start(s32[5,8]{1,0:T(8,128)} %low_ref) | copy-start | bytes 484
  53.2 5.7 %collective-permute-start.9 = (bf16[4,24,640]{2,1,0:T(8,128)(2,1)S(1)}, bf16[4,24,640]{2,1,0:T(8,128)(2,1)S(1)}, u32[]{:S(2)}, u32[]{:S(2)}) collective-permute-start(bf16[4,24,640]{2,1,0:T(8,128)(2,1)S(1)} %get-tuple-element.28), channel_id=1, source_target_pairs={{0,1},{1,0},{2,3},{3,2},{16,17},{17,16},{18,19},{19,18},{4,5},{5,4... | collective-permute-start | bytes 368648 | tf_op jit(solution)/shard_map/ppermute | solution.py:289
  54.0 7.6 %collective-permute-start.10 = (bf16[4,24,640]{2,1,0:T(8,128)(2,1)S(1)}, bf16[4,24,640]{2,1,0:T(8,128)(2,1)S(1)}, u32[]{:S(2)}, u32[]{:S(2)}) collective-permute-start(bf16[4,24,640]{2,1,0:T(8,128)(2,1)S(1)} %get-tuple-element.29), channel_id=1, source_target_pairs={{0,2},{1,3},{2,0},{3,1},{16,18},{17,19},{18,16},{19,17},{4,6},{5,7... | collective-permute-start | bytes 368648 | tf_op jit(solution)/shard_map/ppermute | solution.py:289
  54.1 8.7 %collective-permute-start.11 = (bf16[4,24,640]{2,1,0:T(8,128)(2,1)S(1)}, bf16[4,24,640]{2,1,0:T(8,128)(2,1)S(1)}, u32[]{:S(2)}, u32[]{:S(2)}) collective-permute-start(bf16[4,24,640]{2,1,0:T(8,128)(2,1)S(1)} %get-tuple-element.30), channel_id=1, source_target_pairs={{0,3},{1,2},{2,1},{3,0},{16,19},{17,18},{18,17},{19,16},{4,7},{5,6... | collective-permute-start | bytes 368648 | tf_op jit(solution)/shard_map/ppermute | solution.py:289
  56.7 6.1 %collective-permute-start.12 = (bf16[4,24,640]{2,1,0:T(8,128)(2,1)S(1)}, bf16[4,24,640]{2,1,0:T(8,128)(2,1)S(1)}, u32[]{:S(2)}, u32[]{:S(2)}) collective-permute-start(bf16[4,24,640]{2,1,0:T(8,128)(2,1)S(1)} %get-tuple-element.31), channel_id=1, source_target_pairs={{0,16},{1,17},{2,18},{3,19},{16,0},{17,1},{18,2},{19,3},{4,20},{5,... | collective-permute-start | bytes 368648 | tf_op jit(solution)/shard_map/ppermute | solution.py:289
  58.5 6.5 %collective-permute-start.13 = (bf16[4,24,640]{2,1,0:T(8,128)(2,1)S(1)}, bf16[4,24,640]{2,1,0:T(8,128)(2,1)S(1)}, u32[]{:S(2)}, u32[]{:S(2)}) collective-permute-start(bf16[4,24,640]{2,1,0:T(8,128)(2,1)S(1)} %get-tuple-element.32), channel_id=1, source_target_pairs={{0,17},{1,16},{2,19},{3,18},{16,1},{17,0},{18,3},{19,2},{4,21},{5,... | collective-permute-start | bytes 368648 | tf_op jit(solution)/shard_map/ppermute | solution.py:289
  58.9 6.1 %collective-permute-start.14 = (bf16[4,24,640]{2,1,0:T(8,128)(2,1)S(1)}, bf16[4,24,640]{2,1,0:T(8,128)(2,1)S(1)}, u32[]{:S(2)}, u32[]{:S(2)}) collective-permute-start(bf16[4,24,640]{2,1,0:T(8,128)(2,1)S(1)} %get-tuple-element.33), channel_id=1, source_target_pairs={{0,18},{1,19},{2,16},{3,17},{16,2},{17,3},{18,0},{19,1},{4,22},{5,... | collective-permute-start | bytes 368648 | tf_op jit(solution)/shard_map/ppermute | solution.py:289
  61.7 5.3 %collective-permute-start.15 = (bf16[4,24,640]{2,1,0:T(8,128)(2,1)S(1)}, bf16[4,24,640]{2,1,0:T(8,128)(2,1)S(1)}, u32[]{:S(2)}, u32[]{:S(2)}) collective-permute-start(bf16[4,24,640]{2,1,0:T(8,128)(2,1)S(1)} %get-tuple-element.34), channel_id=1, source_target_pairs={{0,19},{1,18},{2,17},{3,16},{16,3},{17,2},{18,1},{19,0},{4,23},{5,... | collective-permute-start | bytes 368648 | tf_op jit(solution)/shard_map/ppermute | solution.py:289

commit v11 on v9

--- a/solution.py
+++ b/solution.py
@@ -58,24 +58,15 @@
     )(x)
 
 
-def added(refs, *at):
-    value = refs[0][at]
-    for ref in refs[1:]:
-        value = value + ref[at]
-    return value
-
-
 def conv_mix_kernel(geometry, counts, low_ref, shift_ref, place_ref, *refs):
     bases, taps, slots, halo, sub, groups = geometry
     refs = list(refs)
-    field_refs = [refs.pop(0) for _ in range(counts[0])]
-    weight_refs = [refs.pop(0) for _ in range(counts[1])]
-    mix_slots = [[refs.pop(0) for _ in range(n)] for n in counts[2]]
+    field_refs, weight_refs, mix_refs = [[refs.pop(0) for _ in range(n)] for n in counts]
     field_rows, total, mix_all, mixed = refs[-4:]
     outs = refs[:-4]
     late, span, _ = field_refs[0].shape
     owners = len(field_refs)
-    depth, width = mix_slots[0][0].shape[1:]
+    depth, width = mix_refs[0].shape[1:]
     channels = owners * depth
     padded = total.shape[-1]
     rows, _, block, _ = weight_refs[0].shape
@@ -114,9 +105,8 @@
 
         lax.fori_loop(0, rows, one_row, 0, unroll=2)
 
-    for d, slot in enumerate(mix_slots):
-        for k in range(bases):
-            mix_all[place_ref[3 + d], k] = added(slot, k)
+    for d, ref in enumerate(mix_refs):
+        mix_all[partner_in_kernel(owner, d, owners)] = ref[...]
     fill = jnp.zeros((padded - channels, width), jnp.bfloat16)
     matrix = jnp.concatenate(
         [x for k in range(bases) for x in [mix_all[p, k] for p in range(owners)] + [fill]], axis=0
@@ -147,15 +137,15 @@
     late, span, _ = fields[0].shape
     owners = len(fields)
     rows = all_rows // late
-    depth, width = mix[0][0].shape[1:]
+    depth, width = mix[0].shape[1:]
     padded = -(-owners * depth // LANES) * LANES
     taps = weights[0].shape[1] // bases
     sub = math.gcd(span, block)
     shapes = [jax.ShapeDtypeStruct((rows, span // groups, width), jnp.bfloat16)] * (late * groups)
     if halo:
         shapes.append(jax.ShapeDtypeStruct((2, halo, span, width), jnp.bfloat16))
-    operands = fields + weights + [x for slot in mix for x in slot]
-    counts = (len(fields), len(weights), [len(s) for s in mix])
+    operands = fields + weights + mix
+    counts = (len(fields), len(weights), len(mix))
     return pl.pallas_call(
         functools.partial(conv_mix_kernel, (bases, taps, slots, halo, sub, groups), counts),
         out_shape=shapes,
@@ -222,19 +212,14 @@
     )(x)
 
 
-def gather_mix(mix, spread, late, owners):
-    core, own = lax.axis_index("late"), lax.axis_index("lonp")
-    if owners == 4 and late == 2:
-        route = [(p, p ^ 1) for p in range(4)] + [(4 + p, 4 + (p ^ 2)) for p in range(4)]
-        first = lax.ppermute(mix, ("late", "lonp"), route)
-        spread, first = lax.optimization_barrier((spread, first))
-        third = lax.ppermute(first, ("late", "lonp"), [(4 + p, 4 + (p ^ 1)) for p in range(4)])
-        other = trade(first, "late", 1, late)
-        copied = lax.ppermute(third, "late", [(1, 0)])
-        slots, origins = [[mix], [first], [other], [third, copied]], [own, own ^ (1 + core), own ^ (2 - core), own ^ 3]
-        return slots, origins, spread
-    slots = [[mix]] + [[trade(mix, "lonp", d, owners)] for d in range(1, owners)]
-    return slots, [partner(own, d, owners) for d in range(owners)], spread
+def gather(spread, mix, kernels, late, owners):
+    if owners != 4:
+        return *([x] + [trade(x, "lonp", d, owners) for d in range(1, owners)] for x in (spread, mix)), kernels
+    mixes = [mix, trade(mix, "lonp", 1, owners), trade(mix, "lonp", 2, owners)]
+    spread, *tied = lax.optimization_barrier((spread, *mixes[1:], *kernels))
+    mixes[1:], kernels = tied[:2], tied[2:]
+    fields = [spread] + [trade(spread, "lonp", d, owners) for d in (1, 2, 3)]
+    return fields, mixes + [trade(mixes[2], "lonp", 1, owners)], kernels
 
 
 def per_device(sizes, fields, kernel, band_low, block_shift, mix_weight):
@@ -248,16 +233,14 @@
     packed = pack(fields.transpose(0, 1, 3, 2), groups, owners)
     packed = packed.reshape((late * groups,) + packed.shape[2:])
     spread = lax.all_to_all(packed, ("late", "lonq"), split_axis=0, concat_axis=0, tiled=True)
-    mix, origins, spread = gather_mix(mix_weight, spread, late, owners)
-    *kernels, spread = lax.optimization_barrier((*kernels, spread))
+    spread = spread.reshape(late, groups * cells, -1)
+    spread, mix, kernels = gather(spread, mix_weight, kernels, late, owners)
     weights = [turn(x) for x in kernels]
-    spread = spread.reshape(late, groups * cells, -1)
-    spread = [spread] + [trade(spread, "lonp", d, owners) for d in range(1, owners)]
 
     start = lax.axis_index("lath") * all_rows
     low = lax.dynamic_slice_in_dim(band_low, start, all_rows, 1)
     shift = lax.dynamic_slice_in_dim(block_shift, start, all_rows, 0)
-    place = [lax.axis_index("late"), lax.axis_index("lonp"), lax.axis_index("lonq")] + origins
+    place = [lax.axis_index("late"), lax.axis_index("lonp"), lax.axis_index("lonq")]
     place = jnp.stack(place).astype(jnp.int32)
     partial = conv_mix(low, shift, place, spread, weights, mix, halo, groups, block)
     if halo:

time: 66 us -> 66 us (level)
  the two profiles are of different devices: /device:TPU:9 before, /device:TPU:0 now
where the time goes in v11:
time: 66 us; the launch traced here: 65.7 us
  waiting for transfers between devices  22.2 us (34%)
  starting transfers between devices  16.3 us (25%)
  Pallas kernels  13.5 us (20%)
  blocking collectives  9.95 us (15%)
  local copies, waits for them, and re-layouts  3.54 us (5%)
    ppermute x7, waiting for transfers between devices, trade(): lax.ppermute(x, axis, [(i, partner(i, distance, size)) for i in range(siz...  13.2 us
    ppermute x7, starting transfers between devices, trade(): lax.ppermute(x, axis, [(i, partner(i, distance, size)) for i in range(siz...  10.4 us
    all_to_all x1, blocking collectives, per_device(): lax.all_to_all(packed, ('late', 'lonq'), split_axis=0, concat_axis=0, til...  9.95 us
    ppermute x7, waiting for transfers between devices, per_device(): lax.ppermute(partial[dl * groups + dq], ('late', 'lonq'), [(l * groups +...  8.96 us
    pallas_call x1, Pallas kernels, conv_mix(): pl.pallas_call(functools.partial(conv_mix_kernel, (bases, taps, slots, ha...  6.84 us
    ppermute x7, starting transfers between devices, per_device(): lax.ppermute(partial[dl * groups + dq], ('late', 'lonq'), [(l * groups +...  5.9 us
    pallas_call x2, Pallas kernels, turn(): pl.pallas_call(turn_kernel, out_shape=jax.ShapeDtypeStruct((rows, bases *...  4.86 us
    unnamed x9, local copies, waits for them, and re-layouts  3.54 us
  transfers between devices with their start and end apart: 14, of which 7 were waited for; matrix products, arithmetic and copies ran while one was open for 1% of the time, Pallas kernels for 8%

profile of v11, /device:TPU:0, one launch (start us, length us, event | category | flops | bytes accessed | tf_op | source)
XLA Modules:
  0.0 65.7 jit_solution(15294301764409634852)
XLA Ops:
  0.0 0.5 collective-permute-start.2
  0.5 2.6 %collective-permute-start = (bf16[5,40,640]{2,1,0:T(8,128)(2,1)}, bf16[5,40,640]{2,1,0:T(8,128)(2,1)S(1)}, u32[]{:S(2)}, u32[]{:S(2)}) collective-permute-start(bf16[5,40,640]{2,1,0:T(8,128)(2,1)} %refs_6_.1), channel_id=1, source_target_pairs={{0,4},{4,0},{8,12},{12,8},{1,5},{5,1},{9,13},{13,9},{2,6},{6,2},{1... | collective-permute-start | bytes 768008 | tf_op jit(solution)/shard_map/ppermute | solution.py:33
  3.0 2.6 %collective-permute-start.1 = (bf16[5,40,640]{2,1,0:T(8,128)(2,1)}, bf16[5,40,640]{2,1,0:T(8,128)(2,1)}, u32[]{:S(2)}, u32[]{:S(2)}) collective-permute-start(bf16[5,40,640]{2,1,0:T(8,128)(2,1)} %refs_6_.1), channel_id=1, source_target_pairs={{0,8},{4,12},{8,0},{12,4},{1,9},{5,13},{9,1},{13,5},{2,10},{6,14},... | collective-permute-start | bytes 768008 | tf_op jit(solution)/shard_map/ppermute | solution.py:33
  5.6 0.0 copy-start.2
  5.6 0.9 %copy-done.2 = bf16[2,4,640,24]{2,3,1,0:T(8,128)(2,1)S(1)} copy-done((bf16[2,4,640,24]{2,3,1,0:T(8,128)(2,1)S(1)}, bf16[2,4,640,24]{2,3,1,0:T(8,128)(2,1)}, u32[]{:S(2)}) %copy-start.2) | copy-done | bytes 245784
  6.6 0.4 pack.1
  7.0 9.9 %all_to_all.5 = bf16[8,24,640]{2,1,0:T(8,128)(2,1)S(1)} all-to-all(bf16[8,24,640]{2,1,0:T(8,128)(2,1)S(1)} %bitcast.10), channel_id=1, replica_groups=mesh['lath'=1,'late'=2,'lonp'=4,'lonq'=4] {'late','lonq'}, dimensions={0} | all-to-all | bytes 491520 | tf_op jit(solution)/shard_map/all_to_all | solution.py:235
  16.9 0.0 collective-permute-done.refs_7_
  16.9 1.2 %collective-permute-done.1.refs_8_ = bf16[5,40,640]{2,1,0:T(8,128)(2,1)} collective-permute-done((bf16[5,40,640]{2,1,0:T(8,128)(2,1)}, bf16[5,40,640]{2,1,0:T(8,128)(2,1)}, u32[]{:S(2)}, u32[]{:S(2)}) %collective-permute-start.1) | collective-permute-done | bytes 256032 | tf_op jit(solution)/shard_map/ppermute | solution.py:33
  18.1 0.0 collective-permute-done.2.x_ref
  18.1 0.4 collective-permute-start.6
  18.5 1.6 %collective-permute-start.3 = (bf16[2,96,640]{2,1,0:T(8,128)(2,1)S(1)}, bf16[2,96,640]{2,1,0:T(8,128)(2,1)}, u32[]{:S(2)}, u32[]{:S(2)}) collective-permute-start(bf16[2,96,640]{2,1,0:T(8,128)(2,1)S(1)} %bitcast.6), channel_id=1, source_target_pairs={{0,4},{4,0},{8,12},{12,8},{1,5},{5,1},{9,13},{13,9},{2,6},{6,2},{1... | collective-permute-start | bytes 737288 | tf_op jit(solution)/shard_map/ppermute | solution.py:33
  20.1 1.0 %collective-permute-start.4 = (bf16[2,96,640]{2,1,0:T(8,128)(2,1)S(1)}, bf16[2,96,640]{2,1,0:T(8,128)(2,1)}, u32[]{:S(2)}, u32[]{:S(2)}) collective-permute-start(bf16[2,96,640]{2,1,0:T(8,128)(2,1)S(1)} %bitcast.7), channel_id=1, source_target_pairs={{0,8},{4,12},{8,0},{12,4},{1,9},{5,13},{9,1},{13,5},{2,10},{6,14},... | collective-permute-start | bytes 737288 | tf_op jit(solution)/shard_map/ppermute | solution.py:33
  21.2 1.8 %collective-permute-start.5 = (bf16[2,96,640]{2,1,0:T(8,128)(2,1)S(1)}, bf16[2,96,640]{2,1,0:T(8,128)(2,1)}, u32[]{:S(2)}, u32[]{:S(2)}) collective-permute-start(bf16[2,96,640]{2,1,0:T(8,128)(2,1)S(1)} %bitcast.8), channel_id=1, source_target_pairs={{0,12},{4,8},{8,4},{12,0},{1,13},{5,9},{9,5},{13,1},{2,14},{6,10},... | collective-permute-start | bytes 737288 | tf_op jit(solution)/shard_map/ppermute | solution.py:33
  22.9 0.8 %copy.6.shift_ref = s32[8,3]{1,0:T(8,128)S(1)} copy(s32[8,3]{0,1:T(4,128)} %param.8) | data formatting | bytes 192 | tf_op args[3]
  23.7 0.1 pad_add_fusion.place_ref
  23.8 0.0 copy-start
  23.8 1.8 %copy-done = bf16[5,4,3,3,64,64]{5,4,3,2,1,0:T(8,128)(2,1)S(1)} copy-done((bf16[5,4,3,3,64,64]{5,4,3,2,1,0:T(8,128)(2,1)S(1)}, bf16[5,4,3,3,64,64]{5,4,3,2,1,0:T(8,128)(2,1)}, u32[]{:S(2)}) %copy-start) | copy-done | bytes 1474584
  25.6 2.4 %turn.2.refs_4_ = bf16[4,15,64,192]{3,2,1,0:T(8,128)(2,1)S(1)} custom-call(bf16[5,4,3,3,64,64]{5,4,3,2,1,0:T(8,128)(2,1)S(1)} %copy-done), custom_call_target="tpu_custom_call" | custom-call | tf_op jit(solution)/shard_map/turn/pallas_call | solution.py:205
  28.0 0.0 copy-start.1
  28.0 0.0 copy-start.3
  28.0 2.4 %turn.3.refs_5_ = bf16[4,15,64,192]{3,2,1,0:T(8,128)(2,1)S(1)} custom-call(bf16[5,4,3,3,64,64]{5,4,3,2,1,0:T(8,128)(2,1)S(1)} %collective-permute-done.2.x_ref), custom_call_target="tpu_custom_call" | custom-call | tf_op jit(solution)/shard_map/turn/pallas_call | solution.py:205
  30.5 6.5 %collective-permute-done.3.refs_1_ = bf16[2,96,640]{2,1,0:T(8,128)(2,1)} collective-permute-done((bf16[2,96,640]{2,1,0:T(8,128)(2,1)S(1)}, bf16[2,96,640]{2,1,0:T(8,128)(2,1)}, u32[]{:S(2)}, u32[]{:S(2)}) %collective-permute-start.3) | collective-permute-done | bytes 245792 | tf_op jit(solution)/shard_map/ppermute | solution.py:33
  37.0 0.0 collective-permute-done.4.refs_2_
  37.0 5.5 %collective-permute-done.5.refs_3_ = bf16[2,96,640]{2,1,0:T(8,128)(2,1)} collective-permute-done((bf16[2,96,640]{2,1,0:T(8,128)(2,1)S(1)}, bf16[2,96,640]{2,1,0:T(8,128)(2,1)}, u32[]{:S(2)}, u32[]{:S(2)}) %collective-permute-start.5) | collective-permute-done | bytes 245792 | tf_op jit(solution)/shard_map/ppermute | solution.py:33
  42.5 0.0 collective-permute-done.6.refs_9_
  42.5 0.0 copy-done.1
  42.5 0.0 copy-done.3
  42.5 6.8 %conv_mix.1 = (bf16[4,24,640]{2,1,0:T(8,128)(2,1)S(1)}, bf16[4,24,640]{2,1,0:T(8,128)(2,1)S(1)}, bf16[4,24,640]{2,1,0:T(8,128)(2,1)S(1)}, bf16[4,24,640]{2,1,0:T...) custom-call(s32[5,8]{1,0:T(8,128)S(1)} %copy-done.3, ...), custom_call_target="tpu_custom_call" | custom-call | tf_op jit(solution)/shard_map/conv_mix/pallas_call | solution.py:149
  49.4 1.6 %collective-permute-start.7 = (bf16[4,24,640]{2,1,0:T(8,128)(2,1)S(1)}, bf16[4,24,640]{2,1,0:T(8,128)(2,1)S(1)}, u32[]{:S(2)}, u32[]{:S(2)}) collective-permute-start(bf16[4,24,640]{2,1,0:T(8,128)(2,1)S(1)} %get-tuple-element.24), channel_id=1, source_target_pairs={{0,1},{1,0},{2,3},{3,2},{16,17},{17,16},{18,19},{19,18},{4,5},{5,4... | collective-permute-start | bytes 368648 | tf_op jit(solution)/shard_map/ppermute | solution.py:258
  50.9 1.5 %collective-permute-start.8 = (bf16[4,24,640]{2,1,0:T(8,128)(2,1)S(1)}, bf16[4,24,640]{2,1,0:T(8,128)(2,1)S(1)}, u32[]{:S(2)}, u32[]{:S(2)}) collective-permute-start(bf16[4,24,640]{2,1,0:T(8,128)(2,1)S(1)} %get-tuple-element.25), channel_id=1, source_target_pairs={{0,2},{1,3},{2,0},{3,1},{16,18},{17,19},{18,16},{19,17},{4,6},{5,7... | collective-permute-start | bytes 368648 | tf_op jit(solution)/shard_map/ppermute | solution.py:258
  52.5 0.5 collective-permute-start.9
  52.9 0.0 collective-permute-start.10
  52.9 1.6 %collective-permute-start.11 = (bf16[4,24,640]{2,1,0:T(8,128)(2,1)S(1)}, bf16[4,24,640]{2,1,0:T(8,128)(2,1)S(1)}, u32[]{:S(2)}, u32[]{:S(2)}) collective-permute-start(bf16[4,24,640]{2,1,0:T(8,128)(2,1)S(1)} %get-tuple-element.28), channel_id=1, source_target_pairs={{0,17},{1,16},{2,19},{3,18},{16,1},{17,0},{18,3},{19,2},{4,21},{5,... | collective-permute-start | bytes 368648 | tf_op jit(solution)/shard_map/ppermute | solution.py:258
  54.5 0.9 %collective-permute-done.7.refs_1_ = bf16[4,24,640]{2,1,0:T(8,128)(2,1)S(1)} collective-permute-done((bf16[4,24,640]{2,1,0:T(8,128)(2,1)S(1)}, bf16[4,24,640]{2,1,0:T(8,128)(2,1)S(1)}, u32[]{:S(2)}, u32[]{:S(2)}) %collective-permute-start.7) | collective-permute-done | bytes 122912 | tf_op jit(solution)/shard_map/ppermute | solution.py:258
  55.5 0.2 collective-permute-start.12
  55.7 1.3 %collective-permute-done.8.refs_2_ = bf16[4,24,640]{2,1,0:T(8,128)(2,1)S(1)} collective-permute-done((bf16[4,24,640]{2,1,0:T(8,128)(2,1)S(1)}, bf16[4,24,640]{2,1,0:T(8,128)(2,1)S(1)}, u32[]{:S(2)}, u32[]{:S(2)}) %collective-permute-start.8) | collective-permute-done | bytes 122912 | tf_op jit(solution)/shard_map/ppermute | solution.py:258
  57.0 0.6 collective-permute-start.13
  57.5 2.0 %collective-permute-done.9.refs_3_ = bf16[4,24,640]{2,1,0:T(8,128)(2,1)S(1)} collective-permute-done((bf16[4,24,640]{2,1,0:T(8,128)(2,1)S(1)}, bf16[4,24,640]{2,1,0:T(8,128)(2,1)S(1)}, u32[]{:S(2)}, u32[]{:S(2)}) %collective-permute-start.9) | collective-permute-done | bytes 122912 | tf_op jit(solution)/shard_map/ppermute | solution.py:258
  59.5 0.0 collective-permute-done.10.refs_4_
  59.5 0.0 collective-permute-done.11.refs_5_
  59.5 4.7 %collective-permute-done.12.refs_6_ = bf16[4,24,640]{2,1,0:T(8,128)(2,1)S(1)} collective-permute-done((bf16[4,24,640]{2,1,0:T(8,128)(2,1)S(1)}, bf16[4,24,640]{2,1,0:T(8,128)(2,1)S(1)}, u32[]{:S(2)}, u32[]{:S(2)}) %collective-permute-start.12) | collective-permute-done | bytes 122912 | tf_op jit(solution)/shard_map/ppermute | solution.py:258
  64.3 0.0 collective-permute-done.13.refs_7_
  64.3 1.4 %finish.1 = bf16[2,4,24,640]{3,2,1,0:T(8,128)(2,1)} custom-call(s32[3]{0:T(128)S(1)} %pad_add_fusion.place_ref, bf16[4,24,640]{2,1,0:T(8,128)(2,1)S(1)} %get-tuple-element.23.refs_0_, bf16[4,24,640]{2,1,0:T(8,128)(2,1)S(1)} %collective-permute-done.7.refs_1_, bf16[4,24,640]{2,1,0:T(8,128)(2,1)S(1)} %collective-permute-done.8.refs_2_, ...), custom_call_target="tpu_custom_call" | custom-call | tf_op jit(solution)/shard_map/finish/pallas_call | solution.py:177
Async XLA Ops:
  0.0 18.1 %collective-permute-start.2 = (bf16[5,4,3,3,64,64]{5,4,3,2,1,0:T(8,128)(2,1)}, bf16[5,4,3,3,64,64]{5,4,3,2,1,0:T(8,128)(2,1)S(1)}, u32[]{:S(2)}, u32[]{:S(2)}) collective-permute-start(bf16[5,4,3,3,64,64]{5,4,3,2,1,0:T(8,128)(2,1)} %x_ref), channel_id=1, source_target_pairs={{0,16},{16,0},{1,17},{17,1},{2,18},{18,2},{3,19},{19,3},{4,20},{20... | collective-permute-start | bytes 4423688 | tf_op jit(solution)/shard_map/ppermute | solution.py:33
  0.5 16.5 %collective-permute-start = (bf16[5,40,640]{2,1,0:T(8,128)(2,1)}, bf16[5,40,640]{2,1,0:T(8,128)(2,1)S(1)}, u32[]{:S(2)}, u32[]{:S(2)}) collective-permute-start(bf16[5,40,640]{2,1,0:T(8,128)(2,1)} %refs_6_.1), channel_id=1, source_target_pairs={{0,4},{4,0},{8,12},{12,8},{1,5},{5,1},{9,13},{13,9},{2,6},{6,2},{1... | collective-permute-start | bytes 768008 | tf_op jit(solution)/shard_map/ppermute | solution.py:33
  3.0 15.1 %collective-permute-start.1 = (bf16[5,40,640]{2,1,0:T(8,128)(2,1)}, bf16[5,40,640]{2,1,0:T(8,128)(2,1)}, u32[]{:S(2)}, u32[]{:S(2)}) collective-permute-start(bf16[5,40,640]{2,1,0:T(8,128)(2,1)} %refs_6_.1), channel_id=1, source_target_pairs={{0,8},{4,12},{8,0},{12,4},{1,9},{5,13},{9,1},{13,5},{2,10},{6,14},... | collective-permute-start | bytes 768008 | tf_op jit(solution)/shard_map/ppermute | solution.py:33
  5.6 0.9 %copy-start.2 = (bf16[2,4,640,24]{2,3,1,0:T(8,128)(2,1)S(1)}, bf16[2,4,640,24]{2,3,1,0:T(8,128)(2,1)}, u32[]{:S(2)}) copy-start(bf16[2,4,640,24]{2,3,1,0:T(8,128)(2,1)} %param.5) | copy-start | bytes 737284
  18.1 24.4 %collective-permute-start.6 = (bf16[5,40,640]{2,1,0:T(8,128)(2,1)}, bf16[5,40,640]{2,1,0:T(8,128)(2,1)}, u32[]{:S(2)}, u32[]{:S(2)}) collective-permute-start(bf16[5,40,640]{2,1,0:T(8,128)(2,1)} %collective-permute-done.1.refs_8_), channel_id=1, source_target_pairs={{0,4},{4,0},{8,12},{12,8},{1,5},{5,1},{9,13},{13,9},{2,6},{6,2},{1... | collective-permute-start | bytes 768008 | tf_op jit(solution)/shard_map/ppermute | solution.py:33
  18.5 18.4 %collective-permute-start.3 = (bf16[2,96,640]{2,1,0:T(8,128)(2,1)S(1)}, bf16[2,96,640]{2,1,0:T(8,128)(2,1)}, u32[]{:S(2)}, u32[]{:S(2)}) collective-permute-start(bf16[2,96,640]{2,1,0:T(8,128)(2,1)S(1)} %bitcast.6), channel_id=1, source_target_pairs={{0,4},{4,0},{8,12},{12,8},{1,5},{5,1},{9,13},{13,9},{2,6},{6,2},{1... | collective-permute-start | bytes 737288 | tf_op jit(solution)/shard_map/ppermute | solution.py:33
  20.1 16.9 %collective-permute-start.4 = (bf16[2,96,640]{2,1,0:T(8,128)(2,1)S(1)}, bf16[2,96,640]{2,1,0:T(8,128)(2,1)}, u32[]{:S(2)}, u32[]{:S(2)}) collective-permute-start(bf16[2,96,640]{2,1,0:T(8,128)(2,1)S(1)} %bitcast.7), channel_id=1, source_target_pairs={{0,8},{4,12},{8,0},{12,4},{1,9},{5,13},{9,1},{13,5},{2,10},{6,14},... | collective-permute-start | bytes 737288 | tf_op jit(solution)/shard_map/ppermute | solution.py:33
  21.2 21.4 %collective-permute-start.5 = (bf16[2,96,640]{2,1,0:T(8,128)(2,1)S(1)}, bf16[2,96,640]{2,1,0:T(8,128)(2,1)}, u32[]{:S(2)}, u32[]{:S(2)}) collective-permute-start(bf16[2,96,640]{2,1,0:T(8,128)(2,1)S(1)} %bitcast.8), channel_id=1, source_target_pairs={{0,12},{4,8},{8,4},{12,0},{1,13},{5,9},{9,5},{13,1},{2,14},{6,10},... | collective-permute-start | bytes 737288 | tf_op jit(solution)/shard_map/ppermute | solution.py:33
  23.8 1.8 %copy-start = (bf16[5,4,3,3,64,64]{5,4,3,2,1,0:T(8,128)(2,1)S(1)}, bf16[5,4,3,3,64,64]{5,4,3,2,1,0:T(8,128)(2,1)}, u32[]{:S(2)}) copy-start(bf16[5,4,3,3,64,64]{5,4,3,2,1,0:T(8,128)(2,1)} %x_ref) | copy-start | bytes 4423684
  28.0 14.5 %copy-start.1 = (bf16[5,40,640]{2,1,0:T(8,128)(2,1)S(1)}, bf16[5,40,640]{2,1,0:T(8,128)(2,1)}, u32[]{:S(2)}) copy-start(bf16[5,40,640]{2,1,0:T(8,128)(2,1)} %refs_6_.1) | copy-start | bytes 768004
  28.0 14.5 %copy-start.3 = (s32[5,8]{1,0:T(8,128)S(1)}, s32[5,8]{1,0:T(8,128)}, u32[]{:S(2)}) copy-start(s32[5,8]{1,0:T(8,128)} %low_ref) | copy-start | bytes 484
  49.4 6.1 %collective-permute-start.7 = (bf16[4,24,640]{2,1,0:T(8,128)(2,1)S(1)}, bf16[4,24,640]{2,1,0:T(8,128)(2,1)S(1)}, u32[]{:S(2)}, u32[]{:S(2)}) collective-permute-start(bf16[4,24,640]{2,1,0:T(8,128)(2,1)S(1)} %get-tuple-element.24), channel_id=1, source_target_pairs={{0,1},{1,0},{2,3},{3,2},{16,17},{17,16},{18,19},{19,18},{4,5},{5,4... | collective-permute-start | bytes 368648 | tf_op jit(solution)/shard_map/ppermute | solution.py:258
  50.9 6.0 %collective-permute-start.8 = (bf16[4,24,640]{2,1,0:T(8,128)(2,1)S(1)}, bf16[4,24,640]{2,1,0:T(8,128)(2,1)S(1)}, u32[]{:S(2)}, u32[]{:S(2)}) collective-permute-start(bf16[4,24,640]{2,1,0:T(8,128)(2,1)S(1)} %get-tuple-element.25), channel_id=1, source_target_pairs={{0,2},{1,3},{2,0},{3,1},{16,18},{17,19},{18,16},{19,17},{4,6},{5,7... | collective-permute-start | bytes 368648 | tf_op jit(solution)/shard_map/ppermute | solution.py:258
  52.5 7.1 %collective-permute-start.9 = (bf16[4,24,640]{2,1,0:T(8,128)(2,1)S(1)}, bf16[4,24,640]{2,1,0:T(8,128)(2,1)S(1)}, u32[]{:S(2)}, u32[]{:S(2)}) collective-permute-start(bf16[4,24,640]{2,1,0:T(8,128)(2,1)S(1)} %get-tuple-element.26), channel_id=1, source_target_pairs={{0,3},{1,2},{2,1},{3,0},{16,19},{17,18},{18,17},{19,16},{4,7},{5,6... | collective-permute-start | bytes 368648 | tf_op jit(solution)/shard_map/ppermute | solution.py:258
  52.9 6.6 %collective-permute-start.10 = (bf16[4,24,640]{2,1,0:T(8,128)(2,1)S(1)}, bf16[4,24,640]{2,1,0:T(8,128)(2,1)S(1)}, u32[]{:S(2)}, u32[]{:S(2)}) collective-permute-start(bf16[4,24,640]{2,1,0:T(8,128)(2,1)S(1)} %get-tuple-element.27), channel_id=1, source_target_pairs={{0,16},{1,17},{2,18},{3,19},{16,0},{17,1},{18,2},{19,3},{4,20},{5,... | collective-permute-start | bytes 368648 | tf_op jit(solution)/shard_map/ppermute | solution.py:258
  52.9 6.6 %collective-permute-start.11 = (bf16[4,24,640]{2,1,0:T(8,128)(2,1)S(1)}, bf16[4,24,640]{2,1,0:T(8,128)(2,1)S(1)}, u32[]{:S(2)}, u32[]{:S(2)}) collective-permute-start(bf16[4,24,640]{2,1,0:T(8,128)(2,1)S(1)} %get-tuple-element.28), channel_id=1, source_target_pairs={{0,17},{1,16},{2,19},{3,18},{16,1},{17,0},{18,3},{19,2},{4,21},{5,... | collective-permute-start | bytes 368648 | tf_op jit(solution)/shard_map/ppermute | solution.py:258
  55.5 8.8 %collective-permute-start.12 = (bf16[4,24,640]{2,1,0:T(8,128)(2,1)S(1)}, bf16[4,24,640]{2,1,0:T(8,128)(2,1)S(1)}, u32[]{:S(2)}, u32[]{:S(2)}) collective-permute-start(bf16[4,24,640]{2,1,0:T(8,128)(2,1)S(1)} %get-tuple-element.29), channel_id=1, source_target_pairs={{0,18},{1,19},{2,16},{3,17},{16,2},{17,3},{18,0},{19,1},{4,22},{5,... | collective-permute-start | bytes 368648 | tf_op jit(solution)/shard_map/ppermute | solution.py:258
  57.0 7.3 %collective-permute-start.13 = (bf16[4,24,640]{2,1,0:T(8,128)(2,1)S(1)}, bf16[4,24,640]{2,1,0:T(8,128)(2,1)S(1)}, u32[]{:S(2)}, u32[]{:S(2)}) collective-permute-start(bf16[4,24,640]{2,1,0:T(8,128)(2,1)S(1)} %get-tuple-element.30), channel_id=1, source_target_pairs={{0,19},{1,18},{2,17},{3,16},{16,3},{17,2},{18,1},{19,0},{4,23},{5,... | collective-permute-start | bytes 368648 | tf_op jit(solution)/shard_map/ppermute | solution.py:258

commit v12 on v11

v12 whole, which is shorter than its diff:
```python
import functools
import math

import jax
import jax.numpy as jnp
from jax import lax
from jax.experimental import pallas as pl
from jax.experimental.pallas import tpu as pltpu
from jax.sharding import Mesh
from jax.sharding import PartitionSpec as P

HALO = 2
LANES = 128
VMEM = pltpu.VMEM
LIMIT = 16 * 1024 * 1024
SMEM_SPEC = pl.BlockSpec(memory_space=pltpu.SMEM)
VMEM_SPEC = pl.BlockSpec(memory_space=VMEM)


def partner(index, distance, size):
    if size & (size - 1) == 0:
        return index ^ distance
    return (distance - index) % size


def partner_in_kernel(index, distance, size):
    if size & (size - 1) == 0:
        return lax.bitwise_xor(index, distance)
    return lax.rem(distance - index + size, size)


def trade(x, axis, distance, size):
    return lax.ppermute(x, axis, [(i, partner(i, distance, size)) for i in range(size)])


def pack_kernel(groups, owners, x_ref, out_ref):
    members, rows, cells, channels = x_ref.shape
    width = channels // (groups * owners)
    for e in range(members):
        for q in range(groups):
            parts = [
                x_ref[e, i, :, (p * groups + q) * width : (p * groups + q + 1) * width]
                for i in range(rows)
                for p in range(owners)
            ]
            block = jnp.concatenate(parts, axis=-1)
            for p in range(owners):
                out_ref[e, p, q] = block


def pack(x, groups, owners):
    members, rows, cells, channels = x.shape
    return pl.pallas_call(
        functools.partial(pack_kernel, groups, owners),
        out_shape=jax.ShapeDtypeStruct((members, owners, groups, cells, rows * channels // groups), x.dtype),
        in_specs=[VMEM_SPEC],
        out_specs=VMEM_SPEC,
        compiler_params=pltpu.CompilerParams(vmem_limit_bytes=LIMIT),
        name="pack",
    )(x)


def conv_kernel(geometry, low_ref, shift_ref, place_ref, fields_ref, *refs):
    bases, taps, slots, halo, sub = geometry
    late, owners, span, _ = fields_ref.shape
    weight_refs = refs[:late]
    outs = refs[late:-2]
    field_rows, total = refs[-2:]
    padded = total.shape[-1]
    rows, _, block, _ = weight_refs[0].shape
    channels = fields_ref.shape[-1] // rows
    nblocks = owners * span // block
    member, owner = place_ref[0], place_ref[1]

    total[...] = jnp.zeros_like(total)
    field_rows[...] = jnp.zeros_like(field_rows)
    for s in range(late):
        lat = partner_in_kernel(member, s, late)
        for p in range(owners):
            value = fields_ref[lat, p]
            for r in range(rows):
                field_rows[r, p * span : (p + 1) * span, :channels] = value[:, r * channels : (r + 1) * channels]

        def one_row(r, carry):
            row = lat * rows + r
            for piece in range(span // sub):
                cell = owner * span + piece * sub
                b = lax.div(cell, block)
                q = pl.multiple_of(lax.rem(cell, block), sub)
                chosen = []
                for j in range(slots):
                    source = lax.rem(b + shift_ref[row, j] + nblocks, nblocks)
                    chosen.append(field_rows[r, pl.ds(pl.multiple_of(source * block, block), block)])
                picked = jnp.concatenate(chosen, axis=0)
                lhs = weight_refs[s][r, :, pl.ds(q, sub), :].reshape(bases * taps * sub, slots * block)
                product = jnp.dot(lhs, picked, preferred_element_type=jnp.float32)
                for k in range(bases):
                    at = pl.ds(row + low_ref[k, row] + HALO, taps)
                    slab = product[k * taps * sub : (k + 1) * taps * sub].reshape(taps, sub, padded)
                    total[k, at, piece * sub : (piece + 1) * sub] += slab
            return carry

        lax.fori_loop(0, rows, one_row, 0, unroll=2)

    for dl in range(late):
        at = pl.ds(partner_in_kernel(member, dl, late) * rows + HALO, rows)
        for k in range(bases):
            outs[dl][:, :, k * padded : (k + 1) * padded] = total[k, at].astype(jnp.bfloat16)
    if halo:
        for side, first in enumerate((0, late * rows + HALO)):
            for k in range(bases):
                outs[-1][side * halo : (side + 1) * halo, :, k * padded : (k + 1) * padded] = total[
                    k, first : first + halo
                ].astype(jnp.bfloat16)


def conv(low, shift, place, fields, weights, halo, block):
    bases, all_rows = low.shape
    slots = shift.shape[1]
    late, owners, span, lanes = fields.shape
    rows = all_rows // late
    padded = -(-lanes // rows // LANES) * LANES
    taps = weights[0].shape[1] // bases
    shapes = [jax.ShapeDtypeStruct((rows, span, bases * padded), jnp.bfloat16)] * late
    if halo:
        shapes.append(jax.ShapeDtypeStruct((2 * halo, span, bases * padded), jnp.bfloat16))
    return pl.pallas_call(
        functools.partial(conv_kernel, (bases, taps, slots, halo, math.gcd(span, block))),
        out_shape=shapes,
        in_specs=[SMEM_SPEC] * 3 + [VMEM_SPEC] * (1 + late),
        out_specs=[VMEM_SPEC] * len(shapes),
        scratch_shapes=[
            VMEM((rows, owners * span, padded), jnp.bfloat16),
            VMEM((bases, all_rows + 2 * HALO, span, padded), jnp.float32),
        ],
        compiler_params=pltpu.CompilerParams(vmem_limit_bytes=LIMIT),
        name="conv",
    )(low, shift, place, fields, *weights)


def mix_kernel(groups, counts, place_ref, conv_ref, *refs):
    refs = list(refs)
    slots = [[refs.pop(0) for _ in range(n)] for n in counts]
    ordered, mixed = refs[-2:]
    outs = refs[:-2]
    owners, bases, depth, width = ordered.shape
    rows, span, lanes = conv_ref.shape
    cells = span // groups
    for d, slot in enumerate(slots):
        value = slot[0][...]
        for ref in slot[1:]:
            value = value + ref[...]
        ordered[place_ref[3 + d]] = value
    fill = jnp.zeros((lanes // bases - owners * depth, width), jnp.bfloat16)
    parts = [x for k in range(bases) for x in [ordered[p, k] for p in range(owners)] + [fill]]
    matrix = jnp.concatenate(parts, axis=0)
    lhs = conv_ref[...].reshape(rows * span, lanes)
    mixed[...] = jnp.dot(lhs, matrix, preferred_element_type=jnp.float32).reshape(rows, span, width)
    for dq in range(groups):
        start = pl.multiple_of(partner_in_kernel(place_ref[2], dq, groups) * cells, 8 if cells % 8 == 0 else cells)
        for r in range(rows):
            outs[dq][r] = mixed[r, pl.ds(start, cells)].astype(jnp.bfloat16)


def mix_rows(place, rows, mix, groups):
    count, span, _ = rows.shape
    bases, depth, width = mix[0][0].shape
    operands = [x for slot in mix for x in slot]
    return pl.pallas_call(
        functools.partial(mix_kernel, groups, [len(slot) for slot in mix]),
        out_shape=[jax.ShapeDtypeStruct((count, span // groups, width), jnp.bfloat16)] * groups,
        in_specs=[SMEM_SPEC] + [VMEM_SPEC] * (1 + len(operands)),
        out_specs=[VMEM_SPEC] * groups,
        scratch_shapes=[VMEM((len(mix), bases, depth, width), jnp.bfloat16), VMEM((count, span, width), jnp.float32)],
        compiler_params=pltpu.CompilerParams(vmem_limit_bytes=LIMIT),
        name="mix",
    )(place, rows, *operands)


def finish_kernel(groups, place_ref, *refs):
    out_ref = refs[-1]
    late = out_ref.shape[0]
    for dl in range(late):
        total = refs[dl * groups][...].astype(jnp.float32)
        for dq in range(1, groups):
            total += refs[dl * groups + dq][...].astype(jnp.float32)
        value = total * (1.0 + lax.erf(total * (0.5**0.5))) * 0.5
        out_ref[partner_in_kernel(place_ref[0], dl, late)] = value.astype(jnp.bfloat16)


def finish(place, parts, groups):
    return pl.pallas_call(
        functools.partial(finish_kernel, groups),
        out_shape=jax.ShapeDtypeStruct((len(parts) // groups,) + parts[0].shape, jnp.bfloat16),
        in_specs=[SMEM_SPEC] + [VMEM_SPEC] * len(parts),
        out_specs=VMEM_SPEC,
        compiler_params=pltpu.CompilerParams(vmem_limit_bytes=LIMIT),
        name="finish",
    )(place, *parts)


def turn_kernel(x_ref, out_ref):
    bases, rows, taps, slots, block, _ = x_ref.shape
    unit = (lax.broadcasted_iota(jnp.int32, (block, block), 0) == lax.broadcasted_iota(jnp.int32, (block, block), 1))
    unit = unit.astype(jnp.float32).astype(x_ref.dtype)

    def one_row(r, carry):
        for k in range(bases):
            for t in range(taps):
                cells = x_ref[k, r, t].reshape(slots * block, block)
                turned = lax.dot_general(unit, cells, (((1,), (1,)), ((), ())), preferred_element_type=jnp.float32)
                out_ref[r, k * taps + t] = turned.astype(out_ref.dtype)
        return carry

    lax.fori_loop(0, rows, one_row, 0)


def turn(x):
    bases, rows, taps, slots, block, _ = x.shape
    return pl.pallas_call(
        turn_kernel,
        out_shape=jax.ShapeDtypeStruct((rows, bases * taps, block, slots * block), x.dtype),
        in_specs=[VMEM_SPEC],
        out_specs=VMEM_SPEC,
        compiler_params=pltpu.CompilerParams(vmem_limit_bytes=LIMIT),
        name="turn",
    )(x)


def fetch_mix(mix, late, owners):
    if owners == 4 and late == 2:
        first = lax.ppermute(mix, ("late", "lonp"), [(4 * c + p, 4 * c + (p ^ (1 + c))) for c in range(2) for p in range(4)])
        far = [(0, 3), (3, 0)], [(1, 2), (2, 1)]
        third = lax.ppermute(mix, ("late", "lonp"), [(4 * c + a, 4 * c + b) for c in range(2) for a, b in far[c]])
        return [first, third]
    return [trade(mix, "lonp", d, owners) for d in range(1, owners)]


def gather_mix(mix, fetched, late, owners):
    core, own = lax.axis_index("late"), lax.axis_index("lonp")
    if owners == 4 and late == 2:
        first, third = fetched
        slots = [[mix], [first], [trade(first, "late", 1, late)], [third, trade(third, "late", 1, late)]]
        return slots, [own, own ^ (1 + core), own ^ (2 - core), own ^ 3]
    return [[mix]] + [[x] for x in fetched], [partner(own, d, owners) for d in range(owners)]


def per_device(sizes, fields, kernel, band_low, block_shift, mix_weight):
    halves, late, owners, groups = sizes
    members, rows, channels, cells = fields.shape
    block = kernel.shape[-1]
    all_rows = late * rows
    halo = HALO if halves > 1 else 0

    packed = pack(fields.transpose(0, 1, 3, 2), groups, owners)
    packed = packed.reshape((-1,) + packed.shape[3:])
    spread = lax.all_to_all(packed, ("late", "lonp", "lonq"), split_axis=0, concat_axis=0, tiled=True)
    spread = spread.reshape(late, owners, groups * cells, -1)
    weights = [turn(x) for x in [kernel] + [trade(kernel, "late", s, late) for s in range(1, late)]]
    fetched = fetch_mix(mix_weight, late, owners)

    start = lax.axis_index("lath") * all_rows
    low = lax.dynamic_slice_in_dim(band_low, start, all_rows, 1)
    shift = lax.dynamic_slice_in_dim(block_shift, start, all_rows, 0)
    place = [lax.axis_index("late"), lax.axis_index("lonp"), lax.axis_index("lonq")]
    convolved = conv(low, shift, jnp.stack(place).astype(jnp.int32), spread, weights, halo, block)
    fetched, convolved = lax.optimization_barrier((fetched, convolved))
    mix, origins = gather_mix(mix_weight, fetched, late, owners)
    place = jnp.stack(place + origins).astype(jnp.int32)
    partial = [None] * late
    for dl in reversed(range(late)):
        partial[dl] = list(mix_rows(place, convolved[dl], mix, groups))
    if halo:
        beyond = mix_rows(place, convolved[-1], mix, groups)
        below = [lax.ppermute(x[halo:], "lath", [(i, i + 1) for i in range(halves - 1)]) for x in beyond]
        above = [lax.ppermute(x[:halo], "lath", [(i + 1, i) for i in range(halves - 1)]) for x in beyond]
        for dq in range(groups):
            filler = jnp.zeros((all_rows - 2 * halo,) + below[dq].shape[1:], below[dq].dtype)
            extra = jnp.concatenate([below[dq], filler, above[dq]], axis=0).reshape((late,) + partial[0][dq].shape)
            for dl in range(late):
                partial[dl][dq] += extra[partner(lax.axis_index("late"), dl, late)]
    parts = [
        lax.ppermute(
            partial[dl][dq],
            ("late", "lonq"),
            [
                (l * groups + q, partner(l, dl, late) * groups + partner(q, dq, groups))
                for l in range(late)
                for q in range(groups)
            ],
        )
        if dl or dq
        else partial[0][0]
        for dl in range(late)
        for dq in range(groups)
    ]
    return finish(place, parts, groups)


def solution(mesh):
    lat, lon = mesh.shape["lat"], mesh.shape["lon"]
    groups = max(g for g in range(1, lon + 1) if lon % g == 0 and g * g <= lon)

    def whole(fields, kernel, band_low, block_shift, mix_weight):
        late = fields.shape[0]
        sizes = (lat // late, late, lon // groups, groups)
        split = Mesh(mesh.devices.reshape(sizes), ("lath", "late", "lonp", "lonq"))
        rows, cells = ("lath", "late"), ("lonp", "lonq")
        return jax.shard_map(
            functools.partial(per_device, sizes),
            mesh=split,
            in_specs=(
                P(None, rows, None, cells),
                P(None, rows, None, None, None, None),
                P(),
                P(),
                P(None, cells, None),
            ),
            out_specs=P(None, rows, cells, None),
            check_vma=False,
        )(fields, kernel, band_low, block_shift, mix_weight)

    return whole
```

time: 66 us -> 73.7 us (1.12)
  blocking collectives: 9.95 us -> 0 us
  local copies, waits for them, and re-layouts: 3.54 us -> 8.98 us
  waiting for transfers between devices: 22.2 us -> 27.6 us
  Pallas kernels: 13.5 us -> 17.8 us
  starting transfers between devices: 16.3 us -> 18.6 us
    all_to_all x0 -> x1, waiting for transfers between devices: none -> 16.3 us  [per_device(): lax.all_to_all(packed, ('late', 'lonp', 'lonq'), split_axis=0, concat_axi...]
    ppermute x7 -> x3, waiting for transfers between devices: 13.2 us -> 1.51 us  [trade(): lax.ppermute(x, axis, [(i, partner(i, distance, size)) for i in range(siz...]
    all_to_all x1 -> x0, blocking collectives: 9.95 us -> none  [per_device(): lax.all_to_all(packed, ('late', 'lonq'), split_axis=0, concat_axis=0, til...]
    ppermute x7 -> x3, starting transfers between devices: 10.4 us -> 0.88 us  [trade(): lax.ppermute(x, axis, [(i, partner(i, distance, size)) for i in range(siz...]
    all_to_all x0 -> x1, starting transfers between devices: none -> 7.3 us  [per_device(): lax.all_to_all(packed, ('late', 'lonp', 'lonq'), split_axis=0, concat_axi...]
    unnamed x9 -> x23, local copies, waits for them, and re-layouts: 3.54 us -> 8.89 us
    ppermute x7 -> x9, starting transfers between devices: 5.9 us -> 10.4 us  [the longest x7 4.48 us: per_device(): lax.ppermute(partial[dl][dq], ('late', 'lonq'), [(l * groups + q, partner...]
    pallas_call x2, Pallas kernels: 4.86 us -> 6.7 us  [turn(): pl.pallas_call(turn_kernel, out_shape=jax.ShapeDtypeStruct((rows, bases *...]
  transfers between devices with their start and end apart: 14 -> 13, of which waited for: 7 -> 7; matrix products, arithmetic and copies ran while one was open for 1% -> 0% of each run, Pallas kernels for 8% -> 18%
where the time goes in v12:
time: 73.7 us; the launch traced here: 73.2 us
  waiting for transfers between devices  27.6 us (37%)
  starting transfers between devices  18.6 us (25%)
  Pallas kernels  17.8 us (24%)
  local copies, waits for them, and re-layouts  8.98 us (12%)
    all_to_all x1, waiting for transfers between devices, per_device(): lax.all_to_all(packed, ('late', 'lonp', 'lonq'), split_axis=0, concat_axi...  16.3 us
    ppermute x7, waiting for transfers between devices, per_device(): lax.ppermute(partial[dl][dq], ('late', 'lonq'), [(l * groups + q, partner...  9.78 us
    unnamed x23, local copies, waits for them, and re-layouts  8.89 us
    all_to_all x1, starting transfers between devices, per_device(): lax.all_to_all(packed, ('late', 'lonp', 'lonq'), split_axis=0, concat_axi...  7.3 us
    pallas_call x2, Pallas kernels, turn(): pl.pallas_call(turn_kernel, out_shape=jax.ShapeDtypeStruct((rows, bases *...  6.7 us
    ppermute x7, starting transfers between devices, per_device(): lax.ppermute(partial[dl][dq], ('late', 'lonq'), [(l * groups + q, partner...  4.48 us
    pallas_call x1, Pallas kernels, conv(): pl.pallas_call(functools.partial(conv_kernel, (bases, taps, slots, halo,...  4.3 us
    ppermute x1, starting transfers between devices, fetch_mix(): lax.ppermute(mix, ('late', 'lonp'), [(4 * c + a, 4 * c + b) for c in rang...  4.26 us
  transfers between devices with their start and end apart: 13, of which 7 were waited for; matrix products, arithmetic and copies ran while one was open for 0% of the time, Pallas kernels for 18%

profile of v12, /device:TPU:0, one launch (start us, length us, event | category | flops | bytes accessed | tf_op | source)
XLA Modules:
  0.0 73.2 jit_solution(17320513228499281304)
XLA Ops:
  0.0 1.0 %copy-done.8 = bf16[2,4,640,24]{2,3,1,0:T(8,128)(2,1)S(1)} copy-done((bf16[2,4,640,24]{2,3,1,0:T(8,128)(2,1)S(1)}, bf16[2,4,640,24]{2,3,1,0:T(8,128)(2,1)}, u32[]{:S(2)}) %copy-start.8) | copy-done | bytes 245784
  1.0 1.4 %pack.1 = bf16[2,4,4,24,640]{4,3,2,1,0:T(8,128)(2,1)} custom-call(bf16[2,4,24,640]{3,2,1,0:T(8,128)(2,1)S(1)} %bitcast.10), custom_call_target="tpu_custom_call" | custom-call | tf_op jit(solution)/shard_map/pack/pallas_call | solution.py:53
  2.4 7.3 %all-to-all-start = ((bf16[32,24,640]{2,1,0:T(8,128)(2,1)}), bf16[32,24,640]{2,1,0:T(8,128)(2,1)S(1)}, u32[]{:S(2)}, u32[]{:S(2)}) async-start(bf16[32,24,640]{2,1,0:T(8,128)(2,1)} %bitcast.7), calls=%async_computation | async-start | bytes 1966080 | tf_op jit(solution)/shard_map/all_to_all | solution.py:257
  9.7 0.3 collective-permute-start.2
  10.0 0.0 copy-done.3
  10.0 1.7 %collective-permute-start = (bf16[5,40,640]{2,1,0:T(8,128)(2,1)S(1)}, bf16[5,40,640]{2,1,0:T(8,128)(2,1)S(1)}, u32[]{:S(2)}, u32[]{:S(2)}) collective-permute-start(bf16[5,40,640]{2,1,0:T(8,128)(2,1)S(1)} %copy-done.3), channel_id=1, source_target_pairs={{0,4},{4,0},{8,12},{12,8},{16,24},{20,28},{24,16},{28,20},{1,5},{5... | collective-permute-start | bytes 768008 | tf_op jit(solution)/shard_map/ppermute | solution.py:232
  11.7 4.3 %collective-permute-start.1 = (bf16[5,40,640]{2,1,0:T(8,128)(2,1)S(1)}, bf16[5,40,640]{2,1,0:T(8,128)(2,1)}, u32[]{:S(2)}, u32[]{:S(2)}) collective-permute-start(bf16[5,40,640]{2,1,0:T(8,128)(2,1)S(1)} %copy-done.3), channel_id=1, source_target_pairs={{0,12},{12,0},{20,24},{24,20},{1,13},{13,1},{21,25},{25,21},{2,14}... | collective-permute-start | bytes 768008 | tf_op jit(solution)/shard_map/ppermute | solution.py:234
  15.9 0.0 copy-start.2
  15.9 1.8 %copy-done.2 = bf16[5,4,3,3,64,64]{5,4,3,2,1,0:T(8,128)(2,1)S(1)} copy-done((bf16[5,4,3,3,64,64]{5,4,3,2,1,0:T(8,128)(2,1)S(1)}, bf16[5,4,3,3,64,64]{5,4,3,2,1,0:T(8,128)(2,1)}, u32[]{:S(2)}) %copy-start.2) | copy-done | bytes 1474584
  17.8 2.4 %turn.2.refs_0_ = bf16[4,15,64,192]{3,2,1,0:T(8,128)(2,1)S(1)} custom-call(bf16[5,4,3,3,64,64]{5,4,3,2,1,0:T(8,128)(2,1)S(1)} %copy-done.2), custom_call_target="tpu_custom_call" | custom-call | tf_op jit(solution)/shard_map/turn/pallas_call | solution.py:220
  20.2 0.0 copy-start.9
  20.2 0.1 copy.6.shift_ref
  20.3 0.1 pad_add_fusion.place_ref
  20.4 0.0 collective-permute-done.2.x_ref
  20.4 4.3 %turn.3.refs_1_ = bf16[4,15,64,192]{3,2,1,0:T(8,128)(2,1)S(1)} custom-call(bf16[5,4,3,3,64,64]{5,4,3,2,1,0:T(8,128)(2,1)} %collective-permute-done.2.x_ref), custom_call_target="tpu_custom_call" | custom-call | tf_op jit(solution)/shard_map/turn/pallas_call | solution.py:220
  24.7 0.0 copy-start
  24.7 1.3 %copy-done = bf16[4,15,64,192]{3,2,1,0:T(8,128)(2,1)} copy-done((bf16[4,15,64,192]{3,2,1,0:T(8,128)(2,1)}, bf16[4,15,64,192]{3,2,1,0:T(8,128)(2,1)S(1)}, u32[]{:S(2)}) %copy-start) | copy-done | bytes 1474584
  26.0 16.3 %all-to-all-done = bf16[32,24,640]{2,1,0:T(8,128)(2,1)S(1)} async-done(((bf16[32,24,640]{2,1,0:T(8,128)(2,1)}), bf16[32,24,640]{2,1,0:T(8,128)(2,1)S(1)}, u32[]{:S(2)}, u32[]{:S(2)}) %all-to-all-start) | async-done | bytes 983072 | tf_op jit(solution)/shard_map/all_to_all | solution.py:257
  42.3 1.5 %copy-done.1 = bf16[4,15,64,192]{3,2,1,0:T(8,128)(2,1)S(1)} copy-done((bf16[4,15,64,192]{3,2,1,0:T(8,128)(2,1)S(1)}, bf16[4,15,64,192]{3,2,1,0:T(8,128)(2,1)}, u32[]{:S(2)}) %copy-start.1) | copy-done | bytes 1474584
  43.8 4.3 %conv.1 = (bf16[4,96,1280]{2,1,0:T(8,128)(2,1)S(1)}, bf16[4,96,1280]{2,1,0:T(8,128)(2,1)S(1)}) custom-call(s32[5,8]{1,0:T(8,128)S(1)} %copy-done.9, s32[8,3]{1,0:T(8,128)S(1)} %copy.6.shift_ref, s32[3]{0:T(128)S(1)} %pad_add_fusion.place_ref, bf16[2,4,96,640]{3,2,1,0:T(8,128)(2,1)S(1)} %bitcast.9, bf16[4,15,64,192]{3,2,1,0:T(8,128)(2,1)S(1)} %turn.2.refs_0_, ...), custom_call_target="tpu_custom_call" | custom-call | tf_op jit(solution)/shard_map/conv/pallas_call | solution.py:127
  48.2 1.0 %copy-done.4 = bf16[4,96,1280]{2,1,0:T(8,128)(2,1)} copy-done((bf16[4,96,1280]{2,1,0:T(8,128)(2,1)}, bf16[4,96,1280]{2,1,0:T(8,128)(2,1)S(1)}, u32[]{:S(2)}) %copy-start.4) | copy-done | bytes 983064
  49.1 1.0 %copy-done.6 = bf16[4,96,1280]{2,1,0:T(8,128)(2,1)} copy-done((bf16[4,96,1280]{2,1,0:T(8,128)(2,1)}, bf16[4,96,1280]{2,1,0:T(8,128)(2,1)S(1)}, u32[]{:S(2)}) %copy-start.6) | copy-done | bytes 983064
  50.1 0.0 collective-permute-done.refs_1_
  50.1 0.0 collective-permute-done.1.refs_3_
  50.1 0.1 collective-permute-start.3
  50.2 0.5 collective-permute-start.4
  50.7 0.1 stack.34.place_ref
  50.8 0.9 %collective-permute-done.3.refs_2_ = bf16[5,40,640]{2,1,0:T(8,128)(2,1)S(1)} collective-permute-done((bf16[5,40,640]{2,1,0:T(8,128)(2,1)S(1)}, bf16[5,40,640]{2,1,0:T(8,128)(2,1)S(1)}, u32[]{:S(2)}, u32[]{:S(2)}) %collective-permute-start.3) | collective-permute-done | bytes 256032 | tf_op jit(solution)/shard_map/ppermute | solution.py:33
  51.7 0.6 collective-permute-done.4.refs_4_
  52.3 1.2 %copy-done.7 = bf16[4,96,1280]{2,1,0:T(8,128)(2,1)S(1)} copy-done((bf16[4,96,1280]{2,1,0:T(8,128)(2,1)S(1)}, bf16[4,96,1280]{2,1,0:T(8,128)(2,1)}, u32[]{:S(2)}) %copy-start.7) | copy-done | bytes 983064
  53.5 2.0 %mix.3 = (bf16[4,24,640]{2,1,0:T(8,128)(2,1)S(1)}, bf16[4,24,640]{2,1,0:T(8,128)(2,1)S(1)}, bf16[4,24,640]{2,1,0:T(8,128)(2,1)S(1)}, bf16[4,24,640]{2,1,0:T(8,128)(2,1)S(1)}) custom-call(s32[7]{0:T(128)S(1)} %stack.34.place_ref, bf16[4,96,1280]{2,1,0:T(8,128)(2,1)S(1)} %copy-done.7, bf16[5,40,640]{2,1,0:T(8,128)(2,1)S(1)} %copy-done.3, ...), custom_call_target="tpu_custom_call" | custom-call | tf_op jit(solution)/shard_map/mix/pallas_call | solution.py:169
  55.5 0.1 collective-permute-start.10
  55.6 0.3 collective-permute-start.11
  55.8 0.4 collective-permute-start.8
  56.2 2.7 %collective-permute-start.9 = (bf16[4,24,640]{2,1,0:T(8,128)(2,1)S(1)}, bf16[4,24,640]{2,1,0:T(8,128)(2,1)S(1)}, u32[]{:S(2)}, u32[]{:S(2)}) collective-permute-start(bf16[4,24,640]{2,1,0:T(8,128)(2,1)S(1)} %get-tuple-element.30), channel_id=1, source_target_pairs={{0,17},{1,16},{2,19},{3,18},{16,1},{17,0},{18,3},{19,2},{4,21},{5,... | collective-permute-start | bytes 368648 | tf_op jit(solution)/shard_map/ppermute | solution.py:283
  58.9 0.0 copy-done.5
  58.9 2.0 %mix.2 = (bf16[4,24,640]{2,1,0:T(8,128)(2,1)S(1)}, bf16[4,24,640]{2,1,0:T(8,128)(2,1)S(1)}, bf16[4,24,640]{2,1,0:T(8,128)(2,1)S(1)}, bf16[4,24,640]{2,1,0:T(8,128)(2,1)S(1)}) custom-call(s32[7]{0:T(128)S(1)} %stack.34.place_ref, bf16[4,96,1280]{2,1,0:T(8,128)(2,1)S(1)} %copy-done.5, bf16[5,40,640]{2,1,0:T(8,128)(2,1)S(1)} %copy-done.3, ...), custom_call_target="tpu_custom_call" | custom-call | tf_op jit(solution)/shard_map/mix/pallas_call | solution.py:169
  60.9 0.1 collective-permute-start.5
  61.0 2.5 %collective-permute-done.10.refs_6_ = bf16[4,24,640]{2,1,0:T(8,128)(2,1)S(1)} collective-permute-done((bf16[4,24,640]{2,1,0:T(8,128)(2,1)S(1)}, bf16[4,24,640]{2,1,0:T(8,128)(2,1)S(1)}, u32[]{:S(2)}, u32[]{:S(2)}) %collective-permute-start.10) | collective-permute-done | bytes 122912 | tf_op jit(solution)/shard_map/ppermute | solution.py:283
  63.5 0.0 collective-permute-start.6
  63.5 0.0 collective-permute-done.11.refs_7_
  63.5 1.0 %collective-permute-start.7 = (bf16[4,24,640]{2,1,0:T(8,128)(2,1)S(1)}, bf16[4,24,640]{2,1,0:T(8,128)(2,1)S(1)}, u32[]{:S(2)}, u32[]{:S(2)}) collective-permute-start(bf16[4,24,640]{2,1,0:T(8,128)(2,1)S(1)} %get-tuple-element.27), channel_id=1, source_target_pairs={{0,3},{1,2},{2,1},{3,0},{16,19},{17,18},{18,17},{19,16},{4,7},{5,6... | collective-permute-start | bytes 368648 | tf_op jit(solution)/shard_map/ppermute | solution.py:283
  64.5 0.0 collective-permute-done.8.refs_4_
  64.5 0.1 collective-permute-done.9.refs_5_
  64.6 3.1 %collective-permute-done.5.refs_1_ = bf16[4,24,640]{2,1,0:T(8,128)(2,1)S(1)} collective-permute-done((bf16[4,24,640]{2,1,0:T(8,128)(2,1)S(1)}, bf16[4,24,640]{2,1,0:T(8,128)(2,1)S(1)}, u32[]{:S(2)}, u32[]{:S(2)}) %collective-permute-start.5) | collective-permute-done | bytes 122912 | tf_op jit(solution)/shard_map/ppermute | solution.py:283
  67.7 4.1 %collective-permute-done.6.refs_2_ = bf16[4,24,640]{2,1,0:T(8,128)(2,1)S(1)} collective-permute-done((bf16[4,24,640]{2,1,0:T(8,128)(2,1)S(1)}, bf16[4,24,640]{2,1,0:T(8,128)(2,1)S(1)}, u32[]{:S(2)}, u32[]{:S(2)}) %collective-permute-start.6) | collective-permute-done | bytes 122912 | tf_op jit(solution)/shard_map/ppermute | solution.py:283
  71.8 0.0 collective-permute-done.7.refs_3_
  71.8 1.4 %finish.1 = bf16[2,4,24,640]{3,2,1,0:T(8,128)(2,1)} custom-call(s32[7]{0:T(128)S(1)} %stack.34.place_ref, bf16[4,24,640]{2,1,0:T(8,128)(2,1)S(1)} %get-tuple-element.24.refs_0_, bf16[4,24,640]{2,1,0:T(8,128)(2,1)S(1)} %collective-permute-done.5.refs_1_, bf16[4,24,640]{2,1,0:T(8,128)(2,1)S(1)} %collective-permute-done.6.refs_2_, ...), custom_call_target="tpu_custom_call" | custom-call | tf_op jit(solution)/shard_map/finish/pallas_call | solution.py:192
  (10 shorter events, 0.0 us)
Async XLA Ops:
  0.0 10.0 %copy-start.3 = (bf16[5,40,640]{2,1,0:T(8,128)(2,1)S(1)}, bf16[5,40,640]{2,1,0:T(8,128)(2,1)}, u32[]{:S(2)}) copy-start(bf16[5,40,640]{2,1,0:T(8,128)(2,1)} %refs_0_.3) | copy-start | bytes 768004
  0.0 1.0 %copy-start.8 = (bf16[2,4,640,24]{2,3,1,0:T(8,128)(2,1)S(1)}, bf16[2,4,640,24]{2,3,1,0:T(8,128)(2,1)}, u32[]{:S(2)}) copy-start(bf16[2,4,640,24]{2,3,1,0:T(8,128)(2,1)} %param.5) | copy-start | bytes 737284
  2.4 17.9 %copy-start.10 = (s32[8,3]{0,1:T(4,128)S(1)}, s32[8,3]{0,1:T(4,128)}, u32[]{:S(2)}) copy-start(s32[8,3]{0,1:T(4,128)} %param.8) | copy-start | bytes 292
  2.4 39.9 %all-to-all-start = ((bf16[32,24,640]{2,1,0:T(8,128)(2,1)}), bf16[32,24,640]{2,1,0:T(8,128)(2,1)S(1)}, u32[]{:S(2)}, u32[]{:S(2)}) async-start(bf16[32,24,640]{2,1,0:T(8,128)(2,1)} %bitcast.7), calls=%async_computation | async-start | bytes 1966080 | tf_op jit(solution)/shard_map/all_to_all | solution.py:257
  9.7 10.7 %collective-permute-start.2 = (bf16[5,4,3,3,64,64]{5,4,3,2,1,0:T(8,128)(2,1)}, bf16[5,4,3,3,64,64]{5,4,3,2,1,0:T(8,128)(2,1)}, u32[]{:S(2)}, u32[]{:S(2)}) collective-permute-start(bf16[5,4,3,3,64,64]{5,4,3,2,1,0:T(8,128)(2,1)} %x_ref.1), channel_id=1, source_target_pairs={{0,16},{16,0},{1,17},{17,1},{2,18},{18,2},{3,19},{19,3},{4,20},{20... | collective-permute-start | bytes 4423688 | tf_op jit(solution)/shard_map/ppermute | solution.py:33
  10.0 40.1 %collective-permute-start = (bf16[5,40,640]{2,1,0:T(8,128)(2,1)S(1)}, bf16[5,40,640]{2,1,0:T(8,128)(2,1)S(1)}, u32[]{:S(2)}, u32[]{:S(2)}) collective-permute-start(bf16[5,40,640]{2,1,0:T(8,128)(2,1)S(1)} %copy-done.3), channel_id=1, source_target_pairs={{0,4},{4,0},{8,12},{12,8},{16,24},{20,28},{24,16},{28,20},{1,5},{5... | collective-permute-start | bytes 768008 | tf_op jit(solution)/shard_map/ppermute | solution.py:232
  11.7 38.4 %collective-permute-start.1 = (bf16[5,40,640]{2,1,0:T(8,128)(2,1)S(1)}, bf16[5,40,640]{2,1,0:T(8,128)(2,1)}, u32[]{:S(2)}, u32[]{:S(2)}) collective-permute-start(bf16[5,40,640]{2,1,0:T(8,128)(2,1)S(1)} %copy-done.3), channel_id=1, source_target_pairs={{0,12},{12,0},{20,24},{24,20},{1,13},{13,1},{21,25},{25,21},{2,14}... | collective-permute-start | bytes 768008 | tf_op jit(solution)/shard_map/ppermute | solution.py:234
  15.9 1.8 %copy-start.2 = (bf16[5,4,3,3,64,64]{5,4,3,2,1,0:T(8,128)(2,1)S(1)}, bf16[5,4,3,3,64,64]{5,4,3,2,1,0:T(8,128)(2,1)}, u32[]{:S(2)}) copy-start(bf16[5,4,3,3,64,64]{5,4,3,2,1,0:T(8,128)(2,1)} %x_ref.1) | copy-start | bytes 4423684
  20.2 22.1 %copy-start.9 = (s32[5,8]{1,0:T(8,128)S(1)}, s32[5,8]{1,0:T(8,128)}, u32[]{:S(2)}) copy-start(s32[5,8]{1,0:T(8,128)} %low_ref) | copy-start | bytes 484
  24.7 1.3 %copy-start = (bf16[4,15,64,192]{3,2,1,0:T(8,128)(2,1)}, bf16[4,15,64,192]{3,2,1,0:T(8,128)(2,1)S(1)}, u32[]{:S(2)}) copy-start(bf16[4,15,64,192]{3,2,1,0:T(8,128)(2,1)S(1)} %turn.3.refs_1_) | copy-start | bytes 4423684
  42.3 1.5 %copy-start.1 = (bf16[4,15,64,192]{3,2,1,0:T(8,128)(2,1)S(1)}, bf16[4,15,64,192]{3,2,1,0:T(8,128)(2,1)}, u32[]{:S(2)}) copy-start(bf16[4,15,64,192]{3,2,1,0:T(8,128)(2,1)} %copy-done) | copy-start | bytes 4423684
  48.1 1.0 %copy-start.4 = (bf16[4,96,1280]{2,1,0:T(8,128)(2,1)}, bf16[4,96,1280]{2,1,0:T(8,128)(2,1)S(1)}, u32[]{:S(2)}) copy-start(bf16[4,96,1280]{2,1,0:T(8,128)(2,1)S(1)} %get-tuple-element.21.conv_ref) | copy-start | bytes 2949124
  49.1 1.0 %copy-start.6 = (bf16[4,96,1280]{2,1,0:T(8,128)(2,1)}, bf16[4,96,1280]{2,1,0:T(8,128)(2,1)S(1)}, u32[]{:S(2)}) copy-start(bf16[4,96,1280]{2,1,0:T(8,128)(2,1)S(1)} %get-tuple-element.28.conv_ref) | copy-start | bytes 2949124
  50.1 8.8 %copy-start.5 = (bf16[4,96,1280]{2,1,0:T(8,128)(2,1)S(1)}, bf16[4,96,1280]{2,1,0:T(8,128)(2,1)}, u32[]{:S(2)}) copy-start(bf16[4,96,1280]{2,1,0:T(8,128)(2,1)} %copy-done.4) | copy-start | bytes 2949124
  50.1 1.6 %collective-permute-start.3 = (bf16[5,40,640]{2,1,0:T(8,128)(2,1)S(1)}, bf16[5,40,640]{2,1,0:T(8,128)(2,1)S(1)}, u32[]{:S(2)}, u32[]{:S(2)}) collective-permute-start(bf16[5,40,640]{2,1,0:T(8,128)(2,1)S(1)} %collective-permute-done.refs_1_), channel_id=1, source_target_pairs={{0,16},{16,0},{1,17},{17,1},{2,18},{18,2},{3,19},{19,3},{4,20},{20... | collective-permute-start | bytes 768008 | tf_op jit(solution)/shard_map/ppermute | solution.py:33
  50.2 2.1 %collective-permute-start.4 = (bf16[5,40,640]{2,1,0:T(8,128)(2,1)}, bf16[5,40,640]{2,1,0:T(8,128)(2,1)S(1)}, u32[]{:S(2)}, u32[]{:S(2)}) collective-permute-start(bf16[5,40,640]{2,1,0:T(8,128)(2,1)} %collective-permute-done.1.refs_3_), channel_id=1, source_target_pairs={{0,16},{16,0},{1,17},{17,1},{2,18},{18,2},{3,19},{19,3},{4,20},{20... | collective-permute-start | bytes 768008 | tf_op jit(solution)/shard_map/ppermute | solution.py:33
  52.3 1.2 %copy-start.7 = (bf16[4,96,1280]{2,1,0:T(8,128)(2,1)S(1)}, bf16[4,96,1280]{2,1,0:T(8,128)(2,1)}, u32[]{:S(2)}) copy-start(bf16[4,96,1280]{2,1,0:T(8,128)(2,1)} %copy-done.6) | copy-start | bytes 2949124
  55.5 8.0 %collective-permute-start.10 = (bf16[4,24,640]{2,1,0:T(8,128)(2,1)S(1)}, bf16[4,24,640]{2,1,0:T(8,128)(2,1)S(1)}, u32[]{:S(2)}, u32[]{:S(2)}) collective-permute-start(bf16[4,24,640]{2,1,0:T(8,128)(2,1)S(1)} %get-tuple-element.31), channel_id=1, source_target_pairs={{0,18},{1,19},{2,16},{3,17},{16,2},{17,3},{18,0},{19,1},{4,22},{5,... | collective-permute-start | bytes 368648 | tf_op jit(solution)/shard_map/ppermute | solution.py:283
  55.6 7.9 %collective-permute-start.11 = (bf16[4,24,640]{2,1,0:T(8,128)(2,1)S(1)}, bf16[4,24,640]{2,1,0:T(8,128)(2,1)S(1)}, u32[]{:S(2)}, u32[]{:S(2)}) collective-permute-start(bf16[4,24,640]{2,1,0:T(8,128)(2,1)S(1)} %get-tuple-element.32), channel_id=1, source_target_pairs={{0,19},{1,18},{2,17},{3,16},{16,3},{17,2},{18,1},{19,0},{4,23},{5,... | collective-permute-start | bytes 368648 | tf_op jit(solution)/shard_map/ppermute | solution.py:283
  55.8 8.6 %collective-permute-start.8 = (bf16[4,24,640]{2,1,0:T(8,128)(2,1)S(1)}, bf16[4,24,640]{2,1,0:T(8,128)(2,1)S(1)}, u32[]{:S(2)}, u32[]{:S(2)}) collective-permute-start(bf16[4,24,640]{2,1,0:T(8,128)(2,1)S(1)} %get-tuple-element.29), channel_id=1, source_target_pairs={{0,16},{1,17},{2,18},{3,19},{16,0},{17,1},{18,2},{19,3},{4,20},{5,... | collective-permute-start | bytes 368648 | tf_op jit(solution)/shard_map/ppermute | solution.py:283
  56.2 8.4 %collective-permute-start.9 = (bf16[4,24,640]{2,1,0:T(8,128)(2,1)S(1)}, bf16[4,24,640]{2,1,0:T(8,128)(2,1)S(1)}, u32[]{:S(2)}, u32[]{:S(2)}) collective-permute-start(bf16[4,24,640]{2,1,0:T(8,128)(2,1)S(1)} %get-tuple-element.30), channel_id=1, source_target_pairs={{0,17},{1,16},{2,19},{3,18},{16,1},{17,0},{18,3},{19,2},{4,21},{5,... | collective-permute-start | bytes 368648 | tf_op jit(solution)/shard_map/ppermute | solution.py:283
  60.9 6.8 %collective-permute-start.5 = (bf16[4,24,640]{2,1,0:T(8,128)(2,1)S(1)}, bf16[4,24,640]{2,1,0:T(8,128)(2,1)S(1)}, u32[]{:S(2)}, u32[]{:S(2)}) collective-permute-start(bf16[4,24,640]{2,1,0:T(8,128)(2,1)S(1)} %get-tuple-element.25), channel_id=1, source_target_pairs={{0,1},{1,0},{2,3},{3,2},{16,17},{17,16},{18,19},{19,18},{4,5},{5,4... | collective-permute-start | bytes 368648 | tf_op jit(solution)/shard_map/ppermute | solution.py:283
  63.5 8.3 %collective-permute-start.6 = (bf16[4,24,640]{2,1,0:T(8,128)(2,1)S(1)}, bf16[4,24,640]{2,1,0:T(8,128)(2,1)S(1)}, u32[]{:S(2)}, u32[]{:S(2)}) collective-permute-start(bf16[4,24,640]{2,1,0:T(8,128)(2,1)S(1)} %get-tuple-element.26), channel_id=1, source_target_pairs={{0,2},{1,3},{2,0},{3,1},{16,18},{17,19},{18,16},{19,17},{4,6},{5,7... | collective-permute-start | bytes 368648 | tf_op jit(solution)/shard_map/ppermute | solution.py:283
  63.5 8.3 %collective-permute-start.7 = (bf16[4,24,640]{2,1,0:T(8,128)(2,1)S(1)}, bf16[4,24,640]{2,1,0:T(8,128)(2,1)S(1)}, u32[]{:S(2)}, u32[]{:S(2)}) collective-permute-start(bf16[4,24,640]{2,1,0:T(8,128)(2,1)S(1)} %get-tuple-element.27), channel_id=1, source_target_pairs={{0,3},{1,2},{2,1},{3,0},{16,19},{17,18},{18,17},{19,16},{4,7},{5,6... | collective-permute-start | bytes 368648 | tf_op jit(solution)/shard_map/ppermute | solution.py:283

commit v13 on v11

--- a/solution.py
+++ b/solution.py
@@ -215,11 +215,16 @@
 def gather(spread, mix, kernels, late, owners):
     if owners != 4:
         return *([x] + [trade(x, "lonp", d, owners) for d in range(1, owners)] for x in (spread, mix)), kernels
-    mixes = [mix, trade(mix, "lonp", 1, owners), trade(mix, "lonp", 2, owners)]
-    spread, *tied = lax.optimization_barrier((spread, *mixes[1:], *kernels))
-    mixes[1:], kernels = tied[:2], tied[2:]
-    fields = [spread] + [trade(spread, "lonp", d, owners) for d in (1, 2, 3)]
-    return fields, mixes + [trade(mixes[2], "lonp", 1, owners)], kernels
+    two = trade(mix, "lonp", 2, owners)
+    one = trade(mix, "lonp", 1, owners)
+    spread, two, one, *kernels = lax.optimization_barrier((spread, two, one, *kernels))
+    fields = [trade(spread, "lonp", d, owners) for d in (3, 2, 1)] + [spread]
+    return fields[::-1], [mix, one, two, trade(two, "lonp", 1, owners)], kernels
+
+
+def send_rank(dl, dq):
+    first = [(0, 0), (1, 0), (0, 1), (0, 3), (1, 3), (1, 1), (0, 2), (1, 2)]
+    return first.index((dl, dq)) if (dl, dq) in first else len(first) + dl + dq
 
 
 def per_device(sizes, fields, kernel, band_low, block_shift, mix_weight):
@@ -254,21 +259,17 @@
             for dq in range(groups):
                 group = partner(lax.axis_index("lonq"), dq, groups)
                 partial[dl * groups + dq] += extra[lat, :, group]
-    parts = [
-        lax.ppermute(
-            partial[dl * groups + dq],
-            ("late", "lonq"),
-            [
-                (l * groups + q, partner(l, dl, late) * groups + partner(q, dq, groups))
-                for l in range(late)
-                for q in range(groups)
-            ],
-        )
-        if dl or dq
-        else partial[0]
-        for dl in range(late)
-        for dq in range(groups)
-    ]
+    order = sorted(((dl, dq) for dl in range(late) for dq in range(groups)), key=lambda at: send_rank(*at))
+    parts = [[None] * groups for _ in range(late)]
+    for dl, dq in order:
+        route = [
+            (l * groups + q, partner(l, dl, late) * groups + partner(q, dq, groups))
+            for l in range(late)
+            for q in range(groups)
+        ]
+        block = partial[dl * groups + dq]
+        parts[dl][dq] = lax.ppermute(block, ("late", "lonq"), route) if dl or dq else block
+    parts = [x for row in parts for x in row]
     return finish(place, parts, groups)
 
 

time: 66 us -> 66.2 us (level)
  waiting for transfers between devices: 22.2 us -> 19.7 us
  starting transfers between devices: 16.3 us -> 18.5 us
  local copies, waits for them, and re-layouts: 3.54 us -> 4.25 us
    ppermute x7, waiting for transfers between devices: 8.96 us -> 7.45 us  [per_device(): lax.ppermute(block, ('late', 'lonq'), route)]
    ppermute x7, starting transfers between devices: 5.9 us -> 7.03 us  [per_device(): lax.ppermute(block, ('late', 'lonq'), route)]
    ppermute x7, starting transfers between devices: 10.4 us -> 11.5 us  [trade(): lax.ppermute(x, axis, [(i, partner(i, distance, size)) for i in range(siz...]
    ppermute x7, waiting for transfers between devices: 13.2 us -> 12.2 us  [trade(): lax.ppermute(x, axis, [(i, partner(i, distance, size)) for i in range(siz...]
    unnamed x9 -> x13, local copies, waits for them, and re-layouts: 3.54 us -> 4.25 us
  transfers between devices with their start and end apart: 14 -> 14, of which waited for: 7 -> 6; matrix products, arithmetic and copies ran while one was open for 1% -> 1% of each run, Pallas kernels for 8% -> 8%
where the time goes in v13:
time: 66.2 us; the launch traced here: 66 us
  waiting for transfers between devices  19.7 us (30%)
  starting transfers between devices  18.5 us (28%)
  Pallas kernels  13.5 us (20%)
  blocking collectives  9.95 us (15%)
  local copies, waits for them, and re-layouts  4.25 us (6%)
    ppermute x7, waiting for transfers between devices, trade(): lax.ppermute(x, axis, [(i, partner(i, distance, size)) for i in range(siz...  12.2 us
    ppermute x7, starting transfers between devices, trade(): lax.ppermute(x, axis, [(i, partner(i, distance, size)) for i in range(siz...  11.5 us
    all_to_all x1, blocking collectives, per_device(): lax.all_to_all(packed, ('late', 'lonq'), split_axis=0, concat_axis=0, til...  9.95 us
    ppermute x7, waiting for transfers between devices, per_device(): lax.ppermute(block, ('late', 'lonq'), route)  7.45 us
    ppermute x7, starting transfers between devices, per_device(): lax.ppermute(block, ('late', 'lonq'), route)  7.03 us
    pallas_call x1, Pallas kernels, conv_mix(): pl.pallas_call(functools.partial(conv_mix_kernel, (bases, taps, slots, ha...  6.76 us
    pallas_call x2, Pallas kernels, turn(): pl.pallas_call(turn_kernel, out_shape=jax.ShapeDtypeStruct((rows, bases *...  4.86 us
    unnamed x13, local copies, waits for them, and re-layouts  4.25 us
  transfers between devices with their start and end apart: 14, of which 6 were waited for; matrix products, arithmetic and copies ran while one was open for 1% of the time, Pallas kernels for 8%

profile of v13, /device:TPU:0, one launch (start us, length us, event | category | flops | bytes accessed | tf_op | source)
XLA Modules:
  0.0 66.0 jit_solution(10609032626296109302)
XLA Ops:
  0.0 0.5 collective-permute-start.2
  0.5 3.6 %collective-permute-start = (bf16[5,40,640]{2,1,0:T(8,128)(2,1)}, bf16[5,40,640]{2,1,0:T(8,128)(2,1)S(1)}, u32[]{:S(2)}, u32[]{:S(2)}) collective-permute-start(bf16[5,40,640]{2,1,0:T(8,128)(2,1)} %refs_6_.1), channel_id=1, source_target_pairs={{0,8},{4,12},{8,0},{12,4},{1,9},{5,13},{9,1},{13,5},{2,10},{6,14},... | collective-permute-start | bytes 768008 | tf_op jit(solution)/shard_map/ppermute | solution.py:33
  4.0 1.6 %collective-permute-start.1 = (bf16[5,40,640]{2,1,0:T(8,128)(2,1)}, bf16[5,40,640]{2,1,0:T(8,128)(2,1)S(1)}, u32[]{:S(2)}, u32[]{:S(2)}) collective-permute-start(bf16[5,40,640]{2,1,0:T(8,128)(2,1)} %refs_6_.1), channel_id=1, source_target_pairs={{0,4},{4,0},{8,12},{12,8},{1,5},{5,1},{9,13},{13,9},{2,6},{6,2},{1... | collective-permute-start | bytes 768008 | tf_op jit(solution)/shard_map/ppermute | solution.py:33
  5.6 0.0 copy-start.4
  5.6 0.9 %copy-done.4 = bf16[2,4,640,24]{2,3,1,0:T(8,128)(2,1)S(1)} copy-done((bf16[2,4,640,24]{2,3,1,0:T(8,128)(2,1)S(1)}, bf16[2,4,640,24]{2,3,1,0:T(8,128)(2,1)}, u32[]{:S(2)}) %copy-start.4) | copy-done | bytes 245784
  6.6 0.4 pack.1
  7.0 9.9 %all_to_all.5 = bf16[8,24,640]{2,1,0:T(8,128)(2,1)S(1)} all-to-all(bf16[8,24,640]{2,1,0:T(8,128)(2,1)S(1)} %bitcast.10), channel_id=1, replica_groups=mesh['lath'=1,'late'=2,'lonp'=4,'lonq'=4] {'late','lonq'}, dimensions={0} | all-to-all | bytes 491520 | tf_op jit(solution)/shard_map/all_to_all | solution.py:240
  16.9 0.0 collective-permute-done.refs_8_
  16.9 0.0 collective-permute-done.1.refs_7_
  16.9 0.0 copy-start.2
  16.9 0.7 %copy-done.2 = bf16[5,40,640]{2,1,0:T(8,128)(2,1)} copy-done((bf16[5,40,640]{2,1,0:T(8,128)(2,1)}, bf16[5,40,640]{2,1,0:T(8,128)(2,1)S(1)}, u32[]{:S(2)}) %copy-start.2) | copy-done | bytes 256024
  17.6 0.0 collective-permute-done.2.x_ref
  17.6 1.5 %collective-permute-start.6 = (bf16[5,40,640]{2,1,0:T(8,128)(2,1)S(1)}, bf16[5,40,640]{2,1,0:T(8,128)(2,1)}, u32[]{:S(2)}, u32[]{:S(2)}) collective-permute-start(bf16[5,40,640]{2,1,0:T(8,128)(2,1)S(1)} %collective-permute-done.refs_8_), channel_id=1, source_target_pairs={{0,4},{4,0},{8,12},{12,8},{1,5},{5,1},{9,13},{13,9},{2,6},{6,2},{1... | collective-permute-start | bytes 768008 | tf_op jit(solution)/shard_map/ppermute | solution.py:33
  19.1 0.6 collective-permute-start.3
  19.6 1.8 %collective-permute-start.4 = (bf16[2,96,640]{2,1,0:T(8,128)(2,1)S(1)}, bf16[2,96,640]{2,1,0:T(8,128)(2,1)}, u32[]{:S(2)}, u32[]{:S(2)}) collective-permute-start(bf16[2,96,640]{2,1,0:T(8,128)(2,1)S(1)} %bitcast.7), channel_id=1, source_target_pairs={{0,8},{4,12},{8,0},{12,4},{1,9},{5,13},{9,1},{13,5},{2,10},{6,14},... | collective-permute-start | bytes 737288 | tf_op jit(solution)/shard_map/ppermute | solution.py:33
  21.4 2.0 %collective-permute-start.5 = (bf16[2,96,640]{2,1,0:T(8,128)(2,1)S(1)}, bf16[2,96,640]{2,1,0:T(8,128)(2,1)}, u32[]{:S(2)}, u32[]{:S(2)}) collective-permute-start(bf16[2,96,640]{2,1,0:T(8,128)(2,1)S(1)} %bitcast.8), channel_id=1, source_target_pairs={{0,12},{4,8},{8,4},{12,0},{1,13},{5,9},{9,5},{13,1},{2,14},{6,10},... | collective-permute-start | bytes 737288 | tf_op jit(solution)/shard_map/ppermute | solution.py:33
  23.5 0.8 %copy.6.shift_ref = s32[8,3]{1,0:T(8,128)S(1)} copy(s32[8,3]{0,1:T(4,128)} %param.8) | data formatting | bytes 192 | tf_op args[3]
  24.2 0.1 pad_add_fusion.place_ref
  24.3 0.0 copy-start
  24.3 1.8 %copy-done = bf16[5,4,3,3,64,64]{5,4,3,2,1,0:T(8,128)(2,1)S(1)} copy-done((bf16[5,4,3,3,64,64]{5,4,3,2,1,0:T(8,128)(2,1)S(1)}, bf16[5,4,3,3,64,64]{5,4,3,2,1,0:T(8,128)(2,1)}, u32[]{:S(2)}) %copy-start) | copy-done | bytes 1474584
  26.1 2.4 %turn.2.refs_4_ = bf16[4,15,64,192]{3,2,1,0:T(8,128)(2,1)S(1)} custom-call(bf16[5,4,3,3,64,64]{5,4,3,2,1,0:T(8,128)(2,1)S(1)} %copy-done), custom_call_target="tpu_custom_call" | custom-call | tf_op jit(solution)/shard_map/turn/pallas_call | solution.py:205
  28.6 0.0 copy-start.1
  28.6 0.0 copy-start.3
  28.6 0.0 copy-start.5
  28.6 2.4 %turn.3.refs_5_ = bf16[4,15,64,192]{3,2,1,0:T(8,128)(2,1)S(1)} custom-call(bf16[5,4,3,3,64,64]{5,4,3,2,1,0:T(8,128)(2,1)S(1)} %collective-permute-done.2.x_ref), custom_call_target="tpu_custom_call" | custom-call | tf_op jit(solution)/shard_map/turn/pallas_call | solution.py:205
  31.0 5.5 %collective-permute-done.3.refs_1_ = bf16[2,96,640]{2,1,0:T(8,128)(2,1)} collective-permute-done((bf16[2,96,640]{2,1,0:T(8,128)(2,1)S(1)}, bf16[2,96,640]{2,1,0:T(8,128)(2,1)}, u32[]{:S(2)}, u32[]{:S(2)}) %collective-permute-start.3) | collective-permute-done | bytes 245792 | tf_op jit(solution)/shard_map/ppermute | solution.py:33
  36.5 0.0 collective-permute-done.4.refs_2_
  36.5 6.8 %collective-permute-done.5.refs_3_ = bf16[2,96,640]{2,1,0:T(8,128)(2,1)} collective-permute-done((bf16[2,96,640]{2,1,0:T(8,128)(2,1)S(1)}, bf16[2,96,640]{2,1,0:T(8,128)(2,1)}, u32[]{:S(2)}, u32[]{:S(2)}) %collective-permute-start.5) | collective-permute-done | bytes 245792 | tf_op jit(solution)/shard_map/ppermute | solution.py:33
  43.3 0.0 collective-permute-done.6.refs_9_
  43.3 0.0 copy-done.1
  43.3 0.0 copy-done.3
  43.3 0.0 copy-done.5
  43.3 6.8 %conv_mix.1 = (bf16[4,24,640]{2,1,0:T(8,128)(2,1)S(1)}, bf16[4,24,640]{2,1,0:T(8,128)(2,1)S(1)}, bf16[4,24,640]{2,1,0:T(8,128)(2,1)S(1)}, bf16[4,24,640]{2,1,0:T...) custom-call(s32[5,8]{1,0:T(8,128)S(1)} %copy-done.5, ...), custom_call_target="tpu_custom_call" | custom-call | tf_op jit(solution)/shard_map/conv_mix/pallas_call | solution.py:149
  50.0 1.6 %collective-permute-start.7 = (bf16[4,24,640]{2,1,0:T(8,128)(2,1)S(1)}, bf16[4,24,640]{2,1,0:T(8,128)(2,1)S(1)}, u32[]{:S(2)}, u32[]{:S(2)}) collective-permute-start(bf16[4,24,640]{2,1,0:T(8,128)(2,1)S(1)} %get-tuple-element.24), channel_id=1, source_target_pairs={{0,1},{1,0},{2,3},{3,2},{16,17},{17,16},{18,19},{19,18},{4,5},{5,4... | collective-permute-start | bytes 368648 | tf_op jit(solution)/shard_map/ppermute | solution.py:271
  51.6 1.5 %collective-permute-start.8 = (bf16[4,24,640]{2,1,0:T(8,128)(2,1)S(1)}, bf16[4,24,640]{2,1,0:T(8,128)(2,1)S(1)}, u32[]{:S(2)}, u32[]{:S(2)}) collective-permute-start(bf16[4,24,640]{2,1,0:T(8,128)(2,1)S(1)} %get-tuple-element.25), channel_id=1, source_target_pairs={{0,2},{1,3},{2,0},{3,1},{16,18},{17,19},{18,16},{19,17},{4,6},{5,7... | collective-permute-start | bytes 368648 | tf_op jit(solution)/shard_map/ppermute | solution.py:271
  53.1 0.5 collective-permute-start.9
  53.6 0.0 collective-permute-start.10
  53.6 1.6 %collective-permute-start.11 = (bf16[4,24,640]{2,1,0:T(8,128)(2,1)S(1)}, bf16[4,24,640]{2,1,0:T(8,128)(2,1)S(1)}, u32[]{:S(2)}, u32[]{:S(2)}) collective-permute-start(bf16[4,24,640]{2,1,0:T(8,128)(2,1)S(1)} %get-tuple-element.28), channel_id=1, source_target_pairs={{0,17},{1,16},{2,19},{3,18},{16,1},{17,0},{18,3},{19,2},{4,21},{5,... | collective-permute-start | bytes 368648 | tf_op jit(solution)/shard_map/ppermute | solution.py:271
  55.2 0.2 collective-permute-done.7.refs_1_
  55.4 0.9 %collective-permute-start.12 = (bf16[4,24,640]{2,1,0:T(8,128)(2,1)S(1)}, bf16[4,24,640]{2,1,0:T(8,128)(2,1)S(1)}, u32[]{:S(2)}, u32[]{:S(2)}) collective-permute-start(bf16[4,24,640]{2,1,0:T(8,128)(2,1)S(1)} %get-tuple-element.29), channel_id=1, source_target_pairs={{0,18},{1,19},{2,16},{3,17},{16,2},{17,3},{18,0},{19,1},{4,22},{5,... | collective-permute-start | bytes 368648 | tf_op jit(solution)/shard_map/ppermute | solution.py:271
  56.3 1.7 %collective-permute-done.8.refs_2_ = bf16[4,24,640]{2,1,0:T(8,128)(2,1)S(1)} collective-permute-done((bf16[4,24,640]{2,1,0:T(8,128)(2,1)S(1)}, bf16[4,24,640]{2,1,0:T(8,128)(2,1)S(1)}, u32[]{:S(2)}, u32[]{:S(2)}) %collective-permute-start.8) | collective-permute-done | bytes 122912 | tf_op jit(solution)/shard_map/ppermute | solution.py:271
  58.0 0.9 %collective-permute-start.13 = (bf16[4,24,640]{2,1,0:T(8,128)(2,1)S(1)}, bf16[4,24,640]{2,1,0:T(8,128)(2,1)S(1)}, u32[]{:S(2)}, u32[]{:S(2)}) collective-permute-start(bf16[4,24,640]{2,1,0:T(8,128)(2,1)S(1)} %get-tuple-element.30), channel_id=1, source_target_pairs={{0,19},{1,18},{2,17},{3,16},{16,3},{17,2},{18,1},{19,0},{4,23},{5,... | collective-permute-start | bytes 368648 | tf_op jit(solution)/shard_map/ppermute | solution.py:271
  58.9 1.2 %collective-permute-done.9.refs_3_ = bf16[4,24,640]{2,1,0:T(8,128)(2,1)S(1)} collective-permute-done((bf16[4,24,640]{2,1,0:T(8,128)(2,1)S(1)}, bf16[4,24,640]{2,1,0:T(8,128)(2,1)S(1)}, u32[]{:S(2)}, u32[]{:S(2)}) %collective-permute-start.9) | collective-permute-done | bytes 122912 | tf_op jit(solution)/shard_map/ppermute | solution.py:271
  60.2 0.0 collective-permute-done.10.refs_4_
  60.2 0.0 collective-permute-done.11.refs_5_
  60.2 4.3 %collective-permute-done.12.refs_6_ = bf16[4,24,640]{2,1,0:T(8,128)(2,1)S(1)} collective-permute-done((bf16[4,24,640]{2,1,0:T(8,128)(2,1)S(1)}, bf16[4,24,640]{2,1,0:T(8,128)(2,1)S(1)}, u32[]{:S(2)}, u32[]{:S(2)}) %collective-permute-start.12) | collective-permute-done | bytes 122912 | tf_op jit(solution)/shard_map/ppermute | solution.py:271
  64.5 0.0 collective-permute-done.13.refs_7_
  64.5 1.4 %finish.1 = bf16[2,4,24,640]{3,2,1,0:T(8,128)(2,1)} custom-call(s32[3]{0:T(128)S(1)} %pad_add_fusion.place_ref, bf16[4,24,640]{2,1,0:T(8,128)(2,1)S(1)} %get-tuple-element.23.refs_0_, bf16[4,24,640]{2,1,0:T(8,128)(2,1)S(1)} %collective-permute-done.7.refs_1_, bf16[4,24,640]{2,1,0:T(8,128)(2,1)S(1)} %collective-permute-done.8.refs_2_, ...), custom_call_target="tpu_custom_call" | custom-call | tf_op jit(solution)/shard_map/finish/pallas_call | solution.py:177
Async XLA Ops:
  0.0 17.6 %collective-permute-start.2 = (bf16[5,4,3,3,64,64]{5,4,3,2,1,0:T(8,128)(2,1)}, bf16[5,4,3,3,64,64]{5,4,3,2,1,0:T(8,128)(2,1)S(1)}, u32[]{:S(2)}, u32[]{:S(2)}) collective-permute-start(bf16[5,4,3,3,64,64]{5,4,3,2,1,0:T(8,128)(2,1)} %x_ref), channel_id=1, source_target_pairs={{0,16},{16,0},{1,17},{17,1},{2,18},{18,2},{3,19},{19,3},{4,20},{20... | collective-permute-start | bytes 4423688 | tf_op jit(solution)/shard_map/ppermute | solution.py:33
  0.5 16.5 %collective-permute-start = (bf16[5,40,640]{2,1,0:T(8,128)(2,1)}, bf16[5,40,640]{2,1,0:T(8,128)(2,1)S(1)}, u32[]{:S(2)}, u32[]{:S(2)}) collective-permute-start(bf16[5,40,640]{2,1,0:T(8,128)(2,1)} %refs_6_.1), channel_id=1, source_target_pairs={{0,8},{4,12},{8,0},{12,4},{1,9},{5,13},{9,1},{13,5},{2,10},{6,14},... | collective-permute-start | bytes 768008 | tf_op jit(solution)/shard_map/ppermute | solution.py:33
  4.0 12.9 %collective-permute-start.1 = (bf16[5,40,640]{2,1,0:T(8,128)(2,1)}, bf16[5,40,640]{2,1,0:T(8,128)(2,1)S(1)}, u32[]{:S(2)}, u32[]{:S(2)}) collective-permute-start(bf16[5,40,640]{2,1,0:T(8,128)(2,1)} %refs_6_.1), channel_id=1, source_target_pairs={{0,4},{4,0},{8,12},{12,8},{1,5},{5,1},{9,13},{13,9},{2,6},{6,2},{1... | collective-permute-start | bytes 768008 | tf_op jit(solution)/shard_map/ppermute | solution.py:33
  5.6 0.9 %copy-start.4 = (bf16[2,4,640,24]{2,3,1,0:T(8,128)(2,1)S(1)}, bf16[2,4,640,24]{2,3,1,0:T(8,128)(2,1)}, u32[]{:S(2)}) copy-start(bf16[2,4,640,24]{2,3,1,0:T(8,128)(2,1)} %param.5) | copy-start | bytes 737284
  16.9 0.7 %copy-start.2 = (bf16[5,40,640]{2,1,0:T(8,128)(2,1)}, bf16[5,40,640]{2,1,0:T(8,128)(2,1)S(1)}, u32[]{:S(2)}) copy-start(bf16[5,40,640]{2,1,0:T(8,128)(2,1)S(1)} %collective-permute-done.1.refs_7_) | copy-start | bytes 768004
  17.6 25.6 %collective-permute-start.6 = (bf16[5,40,640]{2,1,0:T(8,128)(2,1)S(1)}, bf16[5,40,640]{2,1,0:T(8,128)(2,1)}, u32[]{:S(2)}, u32[]{:S(2)}) collective-permute-start(bf16[5,40,640]{2,1,0:T(8,128)(2,1)S(1)} %collective-permute-done.refs_8_), channel_id=1, source_target_pairs={{0,4},{4,0},{8,12},{12,8},{1,5},{5,1},{9,13},{13,9},{2,6},{6,2},{1... | collective-permute-start | bytes 768008 | tf_op jit(solution)/shard_map/ppermute | solution.py:33
  19.1 17.4 %collective-permute-start.3 = (bf16[2,96,640]{2,1,0:T(8,128)(2,1)S(1)}, bf16[2,96,640]{2,1,0:T(8,128)(2,1)}, u32[]{:S(2)}, u32[]{:S(2)}) collective-permute-start(bf16[2,96,640]{2,1,0:T(8,128)(2,1)S(1)} %bitcast.6), channel_id=1, source_target_pairs={{0,4},{4,0},{8,12},{12,8},{1,5},{5,1},{9,13},{13,9},{2,6},{6,2},{1... | collective-permute-start | bytes 737288 | tf_op jit(solution)/shard_map/ppermute | solution.py:33
  19.6 16.8 %collective-permute-start.4 = (bf16[2,96,640]{2,1,0:T(8,128)(2,1)S(1)}, bf16[2,96,640]{2,1,0:T(8,128)(2,1)}, u32[]{:S(2)}, u32[]{:S(2)}) collective-permute-start(bf16[2,96,640]{2,1,0:T(8,128)(2,1)S(1)} %bitcast.7), channel_id=1, source_target_pairs={{0,8},{4,12},{8,0},{12,4},{1,9},{5,13},{9,1},{13,5},{2,10},{6,14},... | collective-permute-start | bytes 737288 | tf_op jit(solution)/shard_map/ppermute | solution.py:33
  21.4 21.8 %collective-permute-start.5 = (bf16[2,96,640]{2,1,0:T(8,128)(2,1)S(1)}, bf16[2,96,640]{2,1,0:T(8,128)(2,1)}, u32[]{:S(2)}, u32[]{:S(2)}) collective-permute-start(bf16[2,96,640]{2,1,0:T(8,128)(2,1)S(1)} %bitcast.8), channel_id=1, source_target_pairs={{0,12},{4,8},{8,4},{12,0},{1,13},{5,9},{9,5},{13,1},{2,14},{6,10},... | collective-permute-start | bytes 737288 | tf_op jit(solution)/shard_map/ppermute | solution.py:33
  24.3 1.8 %copy-start = (bf16[5,4,3,3,64,64]{5,4,3,2,1,0:T(8,128)(2,1)S(1)}, bf16[5,4,3,3,64,64]{5,4,3,2,1,0:T(8,128)(2,1)}, u32[]{:S(2)}) copy-start(bf16[5,4,3,3,64,64]{5,4,3,2,1,0:T(8,128)(2,1)} %x_ref) | copy-start | bytes 4423684
  28.6 14.7 %copy-start.1 = (bf16[5,40,640]{2,1,0:T(8,128)(2,1)S(1)}, bf16[5,40,640]{2,1,0:T(8,128)(2,1)}, u32[]{:S(2)}) copy-start(bf16[5,40,640]{2,1,0:T(8,128)(2,1)} %refs_6_.1) | copy-start | bytes 768004
  28.6 14.7 %copy-start.3 = (bf16[5,40,640]{2,1,0:T(8,128)(2,1)S(1)}, bf16[5,40,640]{2,1,0:T(8,128)(2,1)}, u32[]{:S(2)}) copy-start(bf16[5,40,640]{2,1,0:T(8,128)(2,1)} %copy-done.2) | copy-start | bytes 768004
  28.6 14.7 %copy-start.5 = (s32[5,8]{1,0:T(8,128)S(1)}, s32[5,8]{1,0:T(8,128)}, u32[]{:S(2)}) copy-start(s32[5,8]{1,0:T(8,128)} %low_ref) | copy-start | bytes 484
  50.0 5.4 %collective-permute-start.7 = (bf16[4,24,640]{2,1,0:T(8,128)(2,1)S(1)}, bf16[4,24,640]{2,1,0:T(8,128)(2,1)S(1)}, u32[]{:S(2)}, u32[]{:S(2)}) collective-permute-start(bf16[4,24,640]{2,1,0:T(8,128)(2,1)S(1)} %get-tuple-element.24), channel_id=1, source_target_pairs={{0,1},{1,0},{2,3},{3,2},{16,17},{17,16},{18,19},{19,18},{4,5},{5,4... | collective-permute-start | bytes 368648 | tf_op jit(solution)/shard_map/ppermute | solution.py:271
  51.6 6.4 %collective-permute-start.8 = (bf16[4,24,640]{2,1,0:T(8,128)(2,1)S(1)}, bf16[4,24,640]{2,1,0:T(8,128)(2,1)S(1)}, u32[]{:S(2)}, u32[]{:S(2)}) collective-permute-start(bf16[4,24,640]{2,1,0:T(8,128)(2,1)S(1)} %get-tuple-element.25), channel_id=1, source_target_pairs={{0,2},{1,3},{2,0},{3,1},{16,18},{17,19},{18,16},{19,17},{4,6},{5,7... | collective-permute-start | bytes 368648 | tf_op jit(solution)/shard_map/ppermute | solution.py:271
  53.1 7.1 %collective-permute-start.9 = (bf16[4,24,640]{2,1,0:T(8,128)(2,1)S(1)}, bf16[4,24,640]{2,1,0:T(8,128)(2,1)S(1)}, u32[]{:S(2)}, u32[]{:S(2)}) collective-permute-start(bf16[4,24,640]{2,1,0:T(8,128)(2,1)S(1)} %get-tuple-element.26), channel_id=1, source_target_pairs={{0,3},{1,2},{2,1},{3,0},{16,19},{17,18},{18,17},{19,16},{4,7},{5,6... | collective-permute-start | bytes 368648 | tf_op jit(solution)/shard_map/ppermute | solution.py:271
  53.6 6.6 %collective-permute-start.10 = (bf16[4,24,640]{2,1,0:T(8,128)(2,1)S(1)}, bf16[4,24,640]{2,1,0:T(8,128)(2,1)S(1)}, u32[]{:S(2)}, u32[]{:S(2)}) collective-permute-start(bf16[4,24,640]{2,1,0:T(8,128)(2,1)S(1)} %get-tuple-element.27), channel_id=1, source_target_pairs={{0,16},{1,17},{2,18},{3,19},{16,0},{17,1},{18,2},{19,3},{4,20},{5,... | collective-permute-start | bytes 368648 | tf_op jit(solution)/shard_map/ppermute | solution.py:271
  53.6 6.6 %collective-permute-start.11 = (bf16[4,24,640]{2,1,0:T(8,128)(2,1)S(1)}, bf16[4,24,640]{2,1,0:T(8,128)(2,1)S(1)}, u32[]{:S(2)}, u32[]{:S(2)}) collective-permute-start(bf16[4,24,640]{2,1,0:T(8,128)(2,1)S(1)} %get-tuple-element.28), channel_id=1, source_target_pairs={{0,17},{1,16},{2,19},{3,18},{16,1},{17,0},{18,3},{19,2},{4,21},{5,... | collective-permute-start | bytes 368648 | tf_op jit(solution)/shard_map/ppermute | solution.py:271
  55.4 9.1 %collective-permute-start.12 = (bf16[4,24,640]{2,1,0:T(8,128)(2,1)S(1)}, bf16[4,24,640]{2,1,0:T(8,128)(2,1)S(1)}, u32[]{:S(2)}, u32[]{:S(2)}) collective-permute-start(bf16[4,24,640]{2,1,0:T(8,128)(2,1)S(1)} %get-tuple-element.29), channel_id=1, source_target_pairs={{0,18},{1,19},{2,16},{3,17},{16,2},{17,3},{18,0},{19,1},{4,22},{5,... | collective-permute-start | bytes 368648 | tf_op jit(solution)/shard_map/ppermute | solution.py:271
  58.0 6.5 %collective-permute-start.13 = (bf16[4,24,640]{2,1,0:T(8,128)(2,1)S(1)}, bf16[4,24,640]{2,1,0:T(8,128)(2,1)S(1)}, u32[]{:S(2)}, u32[]{:S(2)}) collective-permute-start(bf16[4,24,640]{2,1,0:T(8,128)(2,1)S(1)} %get-tuple-element.30), channel_id=1, source_target_pairs={{0,19},{1,18},{2,17},{3,16},{16,3},{17,2},{18,1},{19,0},{4,23},{5,... | collective-permute-start | bytes 368648 | tf_op jit(solution)/shard_map/ppermute | solution.py:271

commit v14 on v13

--- a/solution.py
+++ b/solution.py
@@ -62,6 +62,7 @@
     bases, taps, slots, halo, sub, groups = geometry
     refs = list(refs)
     field_refs, weight_refs, mix_refs = [[refs.pop(0) for _ in range(n)] for n in counts]
+    field_refs = field_refs[::-1]
     field_rows, total, mix_all, mixed = refs[-4:]
     outs = refs[:-4]
     late, span, _ = field_refs[0].shape
@@ -144,7 +145,7 @@
     shapes = [jax.ShapeDtypeStruct((rows, span // groups, width), jnp.bfloat16)] * (late * groups)
     if halo:
         shapes.append(jax.ShapeDtypeStruct((2, halo, span, width), jnp.bfloat16))
-    operands = fields + weights + mix
+    operands = fields[::-1] + weights + mix
     counts = (len(fields), len(weights), len(mix))
     return pl.pallas_call(
         functools.partial(conv_mix_kernel, (bases, taps, slots, halo, sub, groups), counts),
@@ -162,21 +163,22 @@
     )(low, shift, place, *operands)
 
 
-def finish_kernel(groups, place_ref, *refs):
+def finish_kernel(owners, place_ref, *refs):
     out_ref = refs[-1]
     late = out_ref.shape[0]
     for dl in range(late):
-        total = refs[dl * groups][...].astype(jnp.float32)
-        for dq in range(1, groups):
-            total += refs[dl * groups + dq][...].astype(jnp.float32)
+        mine = [ref for ref, owner in zip(refs, owners) if owner == dl]
+        total = mine[0][...].astype(jnp.float32)
+        for ref in mine[1:]:
+            total += ref[...].astype(jnp.float32)
         value = total * (1.0 + lax.erf(total * (0.5**0.5))) * 0.5
         out_ref[partner_in_kernel(place_ref[0], dl, late)] = value.astype(jnp.bfloat16)
 
 
-def finish(place, parts, groups):
+def finish(place, parts, owners):
     return pl.pallas_call(
-        functools.partial(finish_kernel, groups),
-        out_shape=jax.ShapeDtypeStruct((len(parts) // groups,) + parts[0].shape, jnp.bfloat16),
+        functools.partial(finish_kernel, owners),
+        out_shape=jax.ShapeDtypeStruct((len(set(owners)),) + parts[0].shape, jnp.bfloat16),
         in_specs=[SMEM_SPEC] + [VMEM_SPEC] * len(parts),
         out_specs=VMEM_SPEC,
         compiler_params=pltpu.CompilerParams(vmem_limit_bytes=LIMIT),
@@ -260,7 +262,7 @@
                 group = partner(lax.axis_index("lonq"), dq, groups)
                 partial[dl * groups + dq] += extra[lat, :, group]
     order = sorted(((dl, dq) for dl in range(late) for dq in range(groups)), key=lambda at: send_rank(*at))
-    parts = [[None] * groups for _ in range(late)]
+    parts = []
     for dl, dq in order:
         route = [
             (l * groups + q, partner(l, dl, late) * groups + partner(q, dq, groups))
@@ -268,9 +270,8 @@
             for q in range(groups)
         ]
         block = partial[dl * groups + dq]
-        parts[dl][dq] = lax.ppermute(block, ("late", "lonq"), route) if dl or dq else block
-    parts = [x for row in parts for x in row]
-    return finish(place, parts, groups)
+        parts.append(lax.ppermute(block, ("late", "lonq"), route) if dl or dq else block)
+    return finish(place, parts, [dl for dl, _ in order])
 
 
 def solution(mesh):

time: 66.2 us -> 68.9 us (1.041)
  waiting for transfers between devices: 19.7 us -> 22.8 us
    ppermute x7, waiting for transfers between devices: 7.45 us -> 10.6 us  [per_device(): lax.ppermute(block, ('late', 'lonq'), route)]
  transfers between devices with their start and end apart: 14 -> 14, of which waited for: 6 -> 7; matrix products, arithmetic and copies ran while one was open for 1% -> 1% of each run, Pallas kernels for 8% -> 8%
where the time goes in v14:
time: 68.9 us; the launch traced here: 68.7 us
  waiting for transfers between devices  22.8 us (33%)
  starting transfers between devices  18 us (26%)
  Pallas kernels  13.5 us (20%)
  blocking collectives  9.95 us (14%)
  local copies, waits for them, and re-layouts  4.25 us (6%)
    ppermute x7, waiting for transfers between devices, trade(): lax.ppermute(x, axis, [(i, partner(i, distance, size)) for i in range(siz...  12.2 us
    ppermute x7, starting transfers between devices, trade(): lax.ppermute(x, axis, [(i, partner(i, distance, size)) for i in range(siz...  11.5 us
    ppermute x7, waiting for transfers between devices, per_device(): lax.ppermute(block, ('late', 'lonq'), route)  10.6 us
    all_to_all x1, blocking collectives, per_device(): lax.all_to_all(packed, ('late', 'lonq'), split_axis=0, concat_axis=0, til...  9.95 us
    pallas_call x1, Pallas kernels, conv_mix(): pl.pallas_call(functools.partial(conv_mix_kernel, (bases, taps, slots, ha...  6.76 us
    ppermute x7, starting transfers between devices, per_device(): lax.ppermute(block, ('late', 'lonq'), route)  6.58 us
    pallas_call x2, Pallas kernels, turn(): pl.pallas_call(turn_kernel, out_shape=jax.ShapeDtypeStruct((rows, bases *...  4.86 us
    unnamed x13, local copies, waits for them, and re-layouts  4.25 us
  transfers between devices with their start and end apart: 14, of which 7 were waited for; matrix products, arithmetic and copies ran while one was open for 1% of the time, Pallas kernels for 8%

profile of v14, /device:TPU:0, one launch (start us, length us, event | category | flops | bytes accessed | tf_op | source)
XLA Modules:
  0.0 68.7 jit_solution(1585974156437731111)
XLA Ops:
  0.0 0.5 collective-permute-start.2
  0.5 3.6 %collective-permute-start = (bf16[5,40,640]{2,1,0:T(8,128)(2,1)}, bf16[5,40,640]{2,1,0:T(8,128)(2,1)S(1)}, u32[]{:S(2)}, u32[]{:S(2)}) collective-permute-start(bf16[5,40,640]{2,1,0:T(8,128)(2,1)} %refs_6_.1), channel_id=1, source_target_pairs={{0,8},{4,12},{8,0},{12,4},{1,9},{5,13},{9,1},{13,5},{2,10},{6,14},... | collective-permute-start | bytes 768008 | tf_op jit(solution)/shard_map/ppermute | solution.py:33
  4.0 1.6 %collective-permute-start.1 = (bf16[5,40,640]{2,1,0:T(8,128)(2,1)}, bf16[5,40,640]{2,1,0:T(8,128)(2,1)S(1)}, u32[]{:S(2)}, u32[]{:S(2)}) collective-permute-start(bf16[5,40,640]{2,1,0:T(8,128)(2,1)} %refs_6_.1), channel_id=1, source_target_pairs={{0,4},{4,0},{8,12},{12,8},{1,5},{5,1},{9,13},{13,9},{2,6},{6,2},{1... | collective-permute-start | bytes 768008 | tf_op jit(solution)/shard_map/ppermute | solution.py:33
  5.6 0.0 copy-start.4
  5.6 0.9 %copy-done.4 = bf16[2,4,640,24]{2,3,1,0:T(8,128)(2,1)S(1)} copy-done((bf16[2,4,640,24]{2,3,1,0:T(8,128)(2,1)S(1)}, bf16[2,4,640,24]{2,3,1,0:T(8,128)(2,1)}, u32[]{:S(2)}) %copy-start.4) | copy-done | bytes 245784
  6.6 0.4 pack.1
  7.0 9.9 %all_to_all.5 = bf16[8,24,640]{2,1,0:T(8,128)(2,1)S(1)} all-to-all(bf16[8,24,640]{2,1,0:T(8,128)(2,1)S(1)} %bitcast.10), channel_id=1, replica_groups=mesh['lath'=1,'late'=2,'lonp'=4,'lonq'=4] {'late','lonq'}, dimensions={0} | all-to-all | bytes 491520 | tf_op jit(solution)/shard_map/all_to_all | solution.py:242
  16.9 0.0 collective-permute-done.refs_8_
  16.9 0.0 collective-permute-done.1.refs_7_
  16.9 0.0 copy-start.2
  16.9 0.7 %copy-done.2 = bf16[5,40,640]{2,1,0:T(8,128)(2,1)} copy-done((bf16[5,40,640]{2,1,0:T(8,128)(2,1)}, bf16[5,40,640]{2,1,0:T(8,128)(2,1)S(1)}, u32[]{:S(2)}) %copy-start.2) | copy-done | bytes 256024
  17.6 0.0 collective-permute-done.2.x_ref
  17.6 1.5 %collective-permute-start.6 = (bf16[5,40,640]{2,1,0:T(8,128)(2,1)S(1)}, bf16[5,40,640]{2,1,0:T(8,128)(2,1)}, u32[]{:S(2)}, u32[]{:S(2)}) collective-permute-start(bf16[5,40,640]{2,1,0:T(8,128)(2,1)S(1)} %collective-permute-done.refs_8_), channel_id=1, source_target_pairs={{0,4},{4,0},{8,12},{12,8},{1,5},{5,1},{9,13},{13,9},{2,6},{6,2},{1... | collective-permute-start | bytes 768008 | tf_op jit(solution)/shard_map/ppermute | solution.py:33
  19.1 1.8 %collective-permute-start.3 = (bf16[2,96,640]{2,1,0:T(8,128)(2,1)S(1)}, bf16[2,96,640]{2,1,0:T(8,128)(2,1)}, u32[]{:S(2)}, u32[]{:S(2)}) collective-permute-start(bf16[2,96,640]{2,1,0:T(8,128)(2,1)S(1)} %bitcast.6), channel_id=1, source_target_pairs={{0,12},{4,8},{8,4},{12,0},{1,13},{5,9},{9,5},{13,1},{2,14},{6,10},... | collective-permute-start | bytes 737288 | tf_op jit(solution)/shard_map/ppermute | solution.py:33
  20.8 0.6 collective-permute-start.4
  21.4 2.1 %collective-permute-start.5 = (bf16[2,96,640]{2,1,0:T(8,128)(2,1)S(1)}, bf16[2,96,640]{2,1,0:T(8,128)(2,1)}, u32[]{:S(2)}, u32[]{:S(2)}) collective-permute-start(bf16[2,96,640]{2,1,0:T(8,128)(2,1)S(1)} %bitcast.8), channel_id=1, source_target_pairs={{0,4},{4,0},{8,12},{12,8},{1,5},{5,1},{9,13},{13,9},{2,6},{6,2},{1... | collective-permute-start | bytes 737288 | tf_op jit(solution)/shard_map/ppermute | solution.py:33
  23.5 0.8 %copy.6.shift_ref = s32[8,3]{1,0:T(8,128)S(1)} copy(s32[8,3]{0,1:T(4,128)} %param.8) | data formatting | bytes 192 | tf_op args[3]
  24.2 0.1 pad_add_fusion.place_ref
  24.3 0.0 copy-start
  24.3 1.8 %copy-done = bf16[5,4,3,3,64,64]{5,4,3,2,1,0:T(8,128)(2,1)S(1)} copy-done((bf16[5,4,3,3,64,64]{5,4,3,2,1,0:T(8,128)(2,1)S(1)}, bf16[5,4,3,3,64,64]{5,4,3,2,1,0:T(8,128)(2,1)}, u32[]{:S(2)}) %copy-start) | copy-done | bytes 1474584
  26.1 2.4 %turn.2.refs_4_ = bf16[4,15,64,192]{3,2,1,0:T(8,128)(2,1)S(1)} custom-call(bf16[5,4,3,3,64,64]{5,4,3,2,1,0:T(8,128)(2,1)S(1)} %copy-done), custom_call_target="tpu_custom_call" | custom-call | tf_op jit(solution)/shard_map/turn/pallas_call | solution.py:207
  28.6 0.0 copy-start.1
  28.6 0.0 copy-start.3
  28.6 0.0 copy-start.5
  28.6 2.4 %turn.3.refs_5_ = bf16[4,15,64,192]{3,2,1,0:T(8,128)(2,1)S(1)} custom-call(bf16[5,4,3,3,64,64]{5,4,3,2,1,0:T(8,128)(2,1)S(1)} %collective-permute-done.2.x_ref), custom_call_target="tpu_custom_call" | custom-call | tf_op jit(solution)/shard_map/turn/pallas_call | solution.py:207
  31.0 2.2 %collective-permute-done.3.refs_0_ = bf16[2,96,640]{2,1,0:T(8,128)(2,1)} collective-permute-done((bf16[2,96,640]{2,1,0:T(8,128)(2,1)S(1)}, bf16[2,96,640]{2,1,0:T(8,128)(2,1)}, u32[]{:S(2)}, u32[]{:S(2)}) %collective-permute-start.3) | collective-permute-done | bytes 245792 | tf_op jit(solution)/shard_map/ppermute | solution.py:33
  33.3 9.9 %collective-permute-done.4.refs_1_ = bf16[2,96,640]{2,1,0:T(8,128)(2,1)} collective-permute-done((bf16[2,96,640]{2,1,0:T(8,128)(2,1)S(1)}, bf16[2,96,640]{2,1,0:T(8,128)(2,1)}, u32[]{:S(2)}, u32[]{:S(2)}) %collective-permute-start.4) | collective-permute-done | bytes 245792 | tf_op jit(solution)/shard_map/ppermute | solution.py:33
  43.2 0.0 collective-permute-done.5.refs_2_
  43.2 0.0 collective-permute-done.6.refs_9_
  43.2 0.0 copy-done.1
  43.2 0.0 copy-done.3
  43.2 0.0 copy-done.5
  43.2 6.8 %conv_mix.1 = (bf16[4,24,640]{2,1,0:T(8,128)(2,1)S(1)}, bf16[4,24,640]{2,1,0:T(8,128)(2,1)S(1)}, bf16[4,24,640]{2,1,0:T(8,128)(2,1)S(1)}, bf16[4,24,640]{2,1,0:T...) custom-call(s32[5,8]{1,0:T(8,128)S(1)} %copy-done.5, ...), custom_call_target="tpu_custom_call" | custom-call | tf_op jit(solution)/shard_map/conv_mix/pallas_call | solution.py:150
  50.0 0.1 collective-permute-start.7
  50.1 1.6 %collective-permute-start.8 = (bf16[4,24,640]{2,1,0:T(8,128)(2,1)S(1)}, bf16[4,24,640]{2,1,0:T(8,128)(2,1)S(1)}, u32[]{:S(2)}, u32[]{:S(2)}) collective-permute-start(bf16[4,24,640]{2,1,0:T(8,128)(2,1)S(1)} %get-tuple-element.25), channel_id=1, source_target_pairs={{0,1},{1,0},{2,3},{3,2},{16,17},{17,16},{18,19},{19,18},{4,5},{5,4... | collective-permute-start | bytes 368648 | tf_op jit(solution)/shard_map/ppermute | solution.py:273
  51.6 1.5 %collective-permute-start.9 = (bf16[4,24,640]{2,1,0:T(8,128)(2,1)S(1)}, bf16[4,24,640]{2,1,0:T(8,128)(2,1)S(1)}, u32[]{:S(2)}, u32[]{:S(2)}) collective-permute-start(bf16[4,24,640]{2,1,0:T(8,128)(2,1)S(1)} %get-tuple-element.26), channel_id=1, source_target_pairs={{0,3},{1,2},{2,1},{3,0},{16,19},{17,18},{18,17},{19,16},{4,7},{5,6... | collective-permute-start | bytes 368648 | tf_op jit(solution)/shard_map/ppermute | solution.py:273
  53.1 0.9 %collective-permute-start.10 = (bf16[4,24,640]{2,1,0:T(8,128)(2,1)S(1)}, bf16[4,24,640]{2,1,0:T(8,128)(2,1)S(1)}, u32[]{:S(2)}, u32[]{:S(2)}) collective-permute-start(bf16[4,24,640]{2,1,0:T(8,128)(2,1)S(1)} %get-tuple-element.27), channel_id=1, source_target_pairs={{0,19},{1,18},{2,17},{3,16},{16,3},{17,2},{18,1},{19,0},{4,23},{5,... | collective-permute-start | bytes 368648 | tf_op jit(solution)/shard_map/ppermute | solution.py:273
  54.1 0.8 %collective-permute-start.11 = (bf16[4,24,640]{2,1,0:T(8,128)(2,1)S(1)}, bf16[4,24,640]{2,1,0:T(8,128)(2,1)S(1)}, u32[]{:S(2)}, u32[]{:S(2)}) collective-permute-start(bf16[4,24,640]{2,1,0:T(8,128)(2,1)S(1)} %get-tuple-element.28), channel_id=1, source_target_pairs={{0,17},{1,16},{2,19},{3,18},{16,1},{17,0},{18,3},{19,2},{4,21},{5,... | collective-permute-start | bytes 368648 | tf_op jit(solution)/shard_map/ppermute | solution.py:273
  54.8 0.0 collective-permute-done.7.refs_1_
  54.8 1.5 %collective-permute-start.12 = (bf16[4,24,640]{2,1,0:T(8,128)(2,1)S(1)}, bf16[4,24,640]{2,1,0:T(8,128)(2,1)S(1)}, u32[]{:S(2)}, u32[]{:S(2)}) collective-permute-start(bf16[4,24,640]{2,1,0:T(8,128)(2,1)S(1)} %get-tuple-element.29), channel_id=1, source_target_pairs={{0,2},{1,3},{2,0},{3,1},{16,18},{17,19},{18,16},{19,17},{4,6},{5,7... | collective-permute-start | bytes 368648 | tf_op jit(solution)/shard_map/ppermute | solution.py:273
  56.4 0.0 collective-permute-done.8.refs_2_
  56.4 0.3 collective-permute-start.13
  56.6 3.4 %collective-permute-done.9.refs_3_ = bf16[4,24,640]{2,1,0:T(8,128)(2,1)S(1)} collective-permute-done((bf16[4,24,640]{2,1,0:T(8,128)(2,1)S(1)}, bf16[4,24,640]{2,1,0:T(8,128)(2,1)S(1)}, u32[]{:S(2)}, u32[]{:S(2)}) %collective-permute-start.9) | collective-permute-done | bytes 122912 | tf_op jit(solution)/shard_map/ppermute | solution.py:273
  60.0 1.7 %collective-permute-done.10.refs_4_ = bf16[4,24,640]{2,1,0:T(8,128)(2,1)S(1)} collective-permute-done((bf16[4,24,640]{2,1,0:T(8,128)(2,1)S(1)}, bf16[4,24,640]{2,1,0:T(8,128)(2,1)S(1)}, u32[]{:S(2)}, u32[]{:S(2)}) %collective-permute-start.10) | collective-permute-done | bytes 122912 | tf_op jit(solution)/shard_map/ppermute | solution.py:273
  61.7 1.6 %collective-permute-done.11.refs_5_ = bf16[4,24,640]{2,1,0:T(8,128)(2,1)S(1)} collective-permute-done((bf16[4,24,640]{2,1,0:T(8,128)(2,1)S(1)}, bf16[4,24,640]{2,1,0:T(8,128)(2,1)S(1)}, u32[]{:S(2)}, u32[]{:S(2)}) %collective-permute-start.11) | collective-permute-done | bytes 122912 | tf_op jit(solution)/shard_map/ppermute | solution.py:273
  63.3 1.5 %collective-permute-done.12.refs_6_ = bf16[4,24,640]{2,1,0:T(8,128)(2,1)S(1)} collective-permute-done((bf16[4,24,640]{2,1,0:T(8,128)(2,1)S(1)}, bf16[4,24,640]{2,1,0:T(8,128)(2,1)S(1)}, u32[]{:S(2)}, u32[]{:S(2)}) %collective-permute-start.12) | collective-permute-done | bytes 122912 | tf_op jit(solution)/shard_map/ppermute | solution.py:273
  64.8 2.4 %collective-permute-done.13.refs_7_ = bf16[4,24,640]{2,1,0:T(8,128)(2,1)S(1)} collective-permute-done((bf16[4,24,640]{2,1,0:T(8,128)(2,1)S(1)}, bf16[4,24,640]{2,1,0:T(8,128)(2,1)S(1)}, u32[]{:S(2)}, u32[]{:S(2)}) %collective-permute-start.13) | collective-permute-done | bytes 122912 | tf_op jit(solution)/shard_map/ppermute | solution.py:273
  67.2 1.4 %finish.1 = bf16[2,4,24,640]{3,2,1,0:T(8,128)(2,1)} custom-call(s32[3]{0:T(128)S(1)} %pad_add_fusion.place_ref, bf16[4,24,640]{2,1,0:T(8,128)(2,1)S(1)} %get-tuple-element.23.refs_0_, bf16[4,24,640]{2,1,0:T(8,128)(2,1)S(1)} %collective-permute-done.7.refs_1_, bf16[4,24,640]{2,1,0:T(8,128)(2,1)S(1)} %collective-permute-done.8.refs_2_, ...), custom_call_target="tpu_custom_call" | custom-call | tf_op jit(solution)/shard_map/finish/pallas_call | solution.py:179
Async XLA Ops:
  0.0 17.6 %collective-permute-start.2 = (bf16[5,4,3,3,64,64]{5,4,3,2,1,0:T(8,128)(2,1)}, bf16[5,4,3,3,64,64]{5,4,3,2,1,0:T(8,128)(2,1)S(1)}, u32[]{:S(2)}, u32[]{:S(2)}) collective-permute-start(bf16[5,4,3,3,64,64]{5,4,3,2,1,0:T(8,128)(2,1)} %x_ref), channel_id=1, source_target_pairs={{0,16},{16,0},{1,17},{17,1},{2,18},{18,2},{3,19},{19,3},{4,20},{20... | collective-permute-start | bytes 4423688 | tf_op jit(solution)/shard_map/ppermute | solution.py:33
  0.5 16.5 %collective-permute-start = (bf16[5,40,640]{2,1,0:T(8,128)(2,1)}, bf16[5,40,640]{2,1,0:T(8,128)(2,1)S(1)}, u32[]{:S(2)}, u32[]{:S(2)}) collective-permute-start(bf16[5,40,640]{2,1,0:T(8,128)(2,1)} %refs_6_.1), channel_id=1, source_target_pairs={{0,8},{4,12},{8,0},{12,4},{1,9},{5,13},{9,1},{13,5},{2,10},{6,14},... | collective-permute-start | bytes 768008 | tf_op jit(solution)/shard_map/ppermute | solution.py:33
  4.0 12.9 %collective-permute-start.1 = (bf16[5,40,640]{2,1,0:T(8,128)(2,1)}, bf16[5,40,640]{2,1,0:T(8,128)(2,1)S(1)}, u32[]{:S(2)}, u32[]{:S(2)}) collective-permute-start(bf16[5,40,640]{2,1,0:T(8,128)(2,1)} %refs_6_.1), channel_id=1, source_target_pairs={{0,4},{4,0},{8,12},{12,8},{1,5},{5,1},{9,13},{13,9},{2,6},{6,2},{1... | collective-permute-start | bytes 768008 | tf_op jit(solution)/shard_map/ppermute | solution.py:33
  5.6 0.9 %copy-start.4 = (bf16[2,4,640,24]{2,3,1,0:T(8,128)(2,1)S(1)}, bf16[2,4,640,24]{2,3,1,0:T(8,128)(2,1)}, u32[]{:S(2)}) copy-start(bf16[2,4,640,24]{2,3,1,0:T(8,128)(2,1)} %param.5) | copy-start | bytes 737284
  16.9 0.7 %copy-start.2 = (bf16[5,40,640]{2,1,0:T(8,128)(2,1)}, bf16[5,40,640]{2,1,0:T(8,128)(2,1)S(1)}, u32[]{:S(2)}) copy-start(bf16[5,40,640]{2,1,0:T(8,128)(2,1)S(1)} %collective-permute-done.1.refs_7_) | copy-start | bytes 768004
  17.6 25.6 %collective-permute-start.6 = (bf16[5,40,640]{2,1,0:T(8,128)(2,1)S(1)}, bf16[5,40,640]{2,1,0:T(8,128)(2,1)}, u32[]{:S(2)}, u32[]{:S(2)}) collective-permute-start(bf16[5,40,640]{2,1,0:T(8,128)(2,1)S(1)} %collective-permute-done.refs_8_), channel_id=1, source_target_pairs={{0,4},{4,0},{8,12},{12,8},{1,5},{5,1},{9,13},{13,9},{2,6},{6,2},{1... | collective-permute-start | bytes 768008 | tf_op jit(solution)/shard_map/ppermute | solution.py:33
  19.1 14.2 %collective-permute-start.3 = (bf16[2,96,640]{2,1,0:T(8,128)(2,1)S(1)}, bf16[2,96,640]{2,1,0:T(8,128)(2,1)}, u32[]{:S(2)}, u32[]{:S(2)}) collective-permute-start(bf16[2,96,640]{2,1,0:T(8,128)(2,1)S(1)} %bitcast.6), channel_id=1, source_target_pairs={{0,12},{4,8},{8,4},{12,0},{1,13},{5,9},{9,5},{13,1},{2,14},{6,10},... | collective-permute-start | bytes 737288 | tf_op jit(solution)/shard_map/ppermute | solution.py:33
  20.8 22.4 %collective-permute-start.4 = (bf16[2,96,640]{2,1,0:T(8,128)(2,1)S(1)}, bf16[2,96,640]{2,1,0:T(8,128)(2,1)}, u32[]{:S(2)}, u32[]{:S(2)}) collective-permute-start(bf16[2,96,640]{2,1,0:T(8,128)(2,1)S(1)} %bitcast.7), channel_id=1, source_target_pairs={{0,8},{4,12},{8,0},{12,4},{1,9},{5,13},{9,1},{13,5},{2,10},{6,14},... | collective-permute-start | bytes 737288 | tf_op jit(solution)/shard_map/ppermute | solution.py:33
  21.4 21.8 %collective-permute-start.5 = (bf16[2,96,640]{2,1,0:T(8,128)(2,1)S(1)}, bf16[2,96,640]{2,1,0:T(8,128)(2,1)}, u32[]{:S(2)}, u32[]{:S(2)}) collective-permute-start(bf16[2,96,640]{2,1,0:T(8,128)(2,1)S(1)} %bitcast.8), channel_id=1, source_target_pairs={{0,4},{4,0},{8,12},{12,8},{1,5},{5,1},{9,13},{13,9},{2,6},{6,2},{1... | collective-permute-start | bytes 737288 | tf_op jit(solution)/shard_map/ppermute | solution.py:33
  24.3 1.8 %copy-start = (bf16[5,4,3,3,64,64]{5,4,3,2,1,0:T(8,128)(2,1)S(1)}, bf16[5,4,3,3,64,64]{5,4,3,2,1,0:T(8,128)(2,1)}, u32[]{:S(2)}) copy-start(bf16[5,4,3,3,64,64]{5,4,3,2,1,0:T(8,128)(2,1)} %x_ref) | copy-start | bytes 4423684
  28.6 14.7 %copy-start.1 = (bf16[5,40,640]{2,1,0:T(8,128)(2,1)S(1)}, bf16[5,40,640]{2,1,0:T(8,128)(2,1)}, u32[]{:S(2)}) copy-start(bf16[5,40,640]{2,1,0:T(8,128)(2,1)} %refs_6_.1) | copy-start | bytes 768004
  28.6 14.7 %copy-start.3 = (bf16[5,40,640]{2,1,0:T(8,128)(2,1)S(1)}, bf16[5,40,640]{2,1,0:T(8,128)(2,1)}, u32[]{:S(2)}) copy-start(bf16[5,40,640]{2,1,0:T(8,128)(2,1)} %copy-done.2) | copy-start | bytes 768004
  28.6 14.7 %copy-start.5 = (s32[5,8]{1,0:T(8,128)S(1)}, s32[5,8]{1,0:T(8,128)}, u32[]{:S(2)}) copy-start(s32[5,8]{1,0:T(8,128)} %low_ref) | copy-start | bytes 484
  50.0 4.8 %collective-permute-start.7 = (bf16[4,24,640]{2,1,0:T(8,128)(2,1)S(1)}, bf16[4,24,640]{2,1,0:T(8,128)(2,1)S(1)}, u32[]{:S(2)}, u32[]{:S(2)}) collective-permute-start(bf16[4,24,640]{2,1,0:T(8,128)(2,1)S(1)} %get-tuple-element.24), channel_id=1, source_target_pairs={{0,16},{1,17},{2,18},{3,19},{16,0},{17,1},{18,2},{19,3},{4,20},{5,... | collective-permute-start | bytes 368648 | tf_op jit(solution)/shard_map/ppermute | solution.py:273
  50.1 6.3 %collective-permute-start.8 = (bf16[4,24,640]{2,1,0:T(8,128)(2,1)S(1)}, bf16[4,24,640]{2,1,0:T(8,128)(2,1)S(1)}, u32[]{:S(2)}, u32[]{:S(2)}) collective-permute-start(bf16[4,24,640]{2,1,0:T(8,128)(2,1)S(1)} %get-tuple-element.25), channel_id=1, source_target_pairs={{0,1},{1,0},{2,3},{3,2},{16,17},{17,16},{18,19},{19,18},{4,5},{5,4... | collective-permute-start | bytes 368648 | tf_op jit(solution)/shard_map/ppermute | solution.py:273
  51.6 8.3 %collective-permute-start.9 = (bf16[4,24,640]{2,1,0:T(8,128)(2,1)S(1)}, bf16[4,24,640]{2,1,0:T(8,128)(2,1)S(1)}, u32[]{:S(2)}, u32[]{:S(2)}) collective-permute-start(bf16[4,24,640]{2,1,0:T(8,128)(2,1)S(1)} %get-tuple-element.26), channel_id=1, source_target_pairs={{0,3},{1,2},{2,1},{3,0},{16,19},{17,18},{18,17},{19,16},{4,7},{5,6... | collective-permute-start | bytes 368648 | tf_op jit(solution)/shard_map/ppermute | solution.py:273
  53.1 8.6 %collective-permute-start.10 = (bf16[4,24,640]{2,1,0:T(8,128)(2,1)S(1)}, bf16[4,24,640]{2,1,0:T(8,128)(2,1)S(1)}, u32[]{:S(2)}, u32[]{:S(2)}) collective-permute-start(bf16[4,24,640]{2,1,0:T(8,128)(2,1)S(1)} %get-tuple-element.27), channel_id=1, source_target_pairs={{0,19},{1,18},{2,17},{3,16},{16,3},{17,2},{18,1},{19,0},{4,23},{5,... | collective-permute-start | bytes 368648 | tf_op jit(solution)/shard_map/ppermute | solution.py:273
  54.1 9.3 %collective-permute-start.11 = (bf16[4,24,640]{2,1,0:T(8,128)(2,1)S(1)}, bf16[4,24,640]{2,1,0:T(8,128)(2,1)S(1)}, u32[]{:S(2)}, u32[]{:S(2)}) collective-permute-start(bf16[4,24,640]{2,1,0:T(8,128)(2,1)S(1)} %get-tuple-element.28), channel_id=1, source_target_pairs={{0,17},{1,16},{2,19},{3,18},{16,1},{17,0},{18,3},{19,2},{4,21},{5,... | collective-permute-start | bytes 368648 | tf_op jit(solution)/shard_map/ppermute | solution.py:273
  54.8 9.9 %collective-permute-start.12 = (bf16[4,24,640]{2,1,0:T(8,128)(2,1)S(1)}, bf16[4,24,640]{2,1,0:T(8,128)(2,1)S(1)}, u32[]{:S(2)}, u32[]{:S(2)}) collective-permute-start(bf16[4,24,640]{2,1,0:T(8,128)(2,1)S(1)} %get-tuple-element.29), channel_id=1, source_target_pairs={{0,2},{1,3},{2,0},{3,1},{16,18},{17,19},{18,16},{19,17},{4,6},{5,7... | collective-permute-start | bytes 368648 | tf_op jit(solution)/shard_map/ppermute | solution.py:273
  56.4 10.9 %collective-permute-start.13 = (bf16[4,24,640]{2,1,0:T(8,128)(2,1)S(1)}, bf16[4,24,640]{2,1,0:T(8,128)(2,1)S(1)}, u32[]{:S(2)}, u32[]{:S(2)}) collective-permute-start(bf16[4,24,640]{2,1,0:T(8,128)(2,1)S(1)} %get-tuple-element.30), channel_id=1, source_target_pairs={{0,18},{1,19},{2,16},{3,17},{16,2},{17,3},{18,0},{19,1},{4,22},{5,... | collective-permute-start | bytes 368648 | tf_op jit(solution)/shard_map/ppermute | solution.py:273

commit v15 on v14

--- a/solution.py
+++ b/solution.py
@@ -107,7 +107,7 @@
         lax.fori_loop(0, rows, one_row, 0, unroll=2)
 
     for d, ref in enumerate(mix_refs):
-        mix_all[partner_in_kernel(owner, d, owners)] = ref[...]
+        mix_all[place_ref[3 + d]] = ref[...]
     fill = jnp.zeros((padded - channels, width), jnp.bfloat16)
     matrix = jnp.concatenate(
         [x for k in range(bases) for x in [mix_all[p, k] for p in range(owners)] + [fill]], axis=0
@@ -215,17 +215,21 @@
 
 
 def gather(spread, mix, kernels, late, owners):
-    if owners != 4:
-        return *([x] + [trade(x, "lonp", d, owners) for d in range(1, owners)] for x in (spread, mix)), kernels
-    two = trade(mix, "lonp", 2, owners)
-    one = trade(mix, "lonp", 1, owners)
-    spread, two, one, *kernels = lax.optimization_barrier((spread, two, one, *kernels))
+    core, own = lax.axis_index("late"), lax.axis_index("lonp")
+    if owners != 4 or late != 2:
+        fields, mixes = [[x] + [trade(x, "lonp", d, owners) for d in range(1, owners)] for x in (spread, mix)]
+        return fields, mixes, [partner(own, d, owners) for d in range(owners)], kernels
+    route = [(4 * c + p, 4 * c + (p ^ (3 - c))) for c in range(2) for p in range(4)]
+    far = lax.ppermute(mix, ("late", "lonp"), route)
+    near = trade(mix, "lonp", 1, owners)
+    spread, far, near, *kernels = lax.optimization_barrier((spread, far, near, *kernels))
     fields = [trade(spread, "lonp", d, owners) for d in (3, 2, 1)] + [spread]
-    return fields[::-1], [mix, one, two, trade(two, "lonp", 1, owners)], kernels
+    mixes = [mix, near, far, trade(far, "late", 1, late)]
+    return fields[::-1], mixes, [own, own ^ 1, own ^ (3 - core), own ^ (2 + core)], kernels
 
 
 def send_rank(dl, dq):
-    first = [(0, 0), (1, 0), (0, 1), (0, 3), (1, 3), (1, 1), (0, 2), (1, 2)]
+    first = [(0, 0), (1, 0), (0, 1), (0, 2), (1, 1), (1, 2), (0, 3), (1, 3)]
     return first.index((dl, dq)) if (dl, dq) in first else len(first) + dl + dq
 
 
@@ -241,13 +245,13 @@
     packed = packed.reshape((late * groups,) + packed.shape[2:])
     spread = lax.all_to_all(packed, ("late", "lonq"), split_axis=0, concat_axis=0, tiled=True)
     spread = spread.reshape(late, groups * cells, -1)
-    spread, mix, kernels = gather(spread, mix_weight, kernels, late, owners)
+    spread, mix, origins, kernels = gather(spread, mix_weight, kernels, late, owners)
     weights = [turn(x) for x in kernels]
 
     start = lax.axis_index("lath") * all_rows
     low = lax.dynamic_slice_in_dim(band_low, start, all_rows, 1)
     shift = lax.dynamic_slice_in_dim(block_shift, start, all_rows, 0)
-    place = [lax.axis_index("late"), lax.axis_index("lonp"), lax.axis_index("lonq")]
+    place = [lax.axis_index("late"), lax.axis_index("lonp"), lax.axis_index("lonq")] + origins
     place = jnp.stack(place).astype(jnp.int32)
     partial = conv_mix(low, shift, place, spread, weights, mix, halo, groups, block)
     if halo:

time: 68.9 us -> 65.6 us (0.952)
  waiting for transfers between devices: 22.8 us -> 20.5 us
  starting transfers between devices: 18 us -> 17 us
    ppermute x7 -> x6, starting transfers between devices: 11.5 us -> 4.85 us  [trade(): lax.ppermute(x, axis, [(i, partner(i, distance, size)) for i in range(siz...]
    ppermute x0 -> x1, starting transfers between devices: none -> 4.6 us  [gather(): far = lax.ppermute(mix, ('late', 'lonp'), route)]
    ppermute x7, waiting for transfers between devices: 10.6 us -> 6.79 us  [per_device(): lax.ppermute(block, ('late', 'lonq'), route)]
    ppermute x7 -> x6, waiting for transfers between devices: 12.2 us -> 13.7 us  [trade(): lax.ppermute(x, axis, [(i, partner(i, distance, size)) for i in range(siz...]
    ppermute x7, starting transfers between devices: 6.58 us -> 7.51 us  [per_device(): lax.ppermute(block, ('late', 'lonq'), route)]
  transfers between devices with their start and end apart: 14 -> 14, of which waited for: 7 -> 6; matrix products, arithmetic and copies ran while one was open for 1% -> 1% of each run, Pallas kernels for 8% -> 8%
where the time goes in v15:
time: 65.6 us; the launch traced here: 65.4 us
  waiting for transfers between devices  20.5 us (31%)
  starting transfers between devices  17 us (26%)
  Pallas kernels  13.5 us (21%)
  blocking collectives  10.1 us (15%)
  local copies, waits for them, and re-layouts  4.33 us (7%)
    ppermute x6, waiting for transfers between devices, trade(): lax.ppermute(x, axis, [(i, partner(i, distance, size)) for i in range(siz...  13.7 us
    all_to_all x1, blocking collectives, per_device(): lax.all_to_all(packed, ('late', 'lonq'), split_axis=0, concat_axis=0, til...  10.1 us
    ppermute x7, starting transfers between devices, per_device(): lax.ppermute(block, ('late', 'lonq'), route)  7.51 us
    ppermute x7, waiting for transfers between devices, per_device(): lax.ppermute(block, ('late', 'lonq'), route)  6.79 us
    pallas_call x1, Pallas kernels, conv_mix(): pl.pallas_call(functools.partial(conv_mix_kernel, (bases, taps, slots, ha...  6.76 us
    pallas_call x2, Pallas kernels, turn(): pl.pallas_call(turn_kernel, out_shape=jax.ShapeDtypeStruct((rows, bases *...  4.86 us
    ppermute x6, starting transfers between devices, trade(): lax.ppermute(x, axis, [(i, partner(i, distance, size)) for i in range(siz...  4.85 us
    ppermute x1, starting transfers between devices, gather(): far = lax.ppermute(mix, ('late', 'lonp'), route)  4.6 us
  transfers between devices with their start and end apart: 14, of which 6 were waited for; matrix products, arithmetic and copies ran while one was open for 1% of the time, Pallas kernels for 8%

profile of v15, /device:TPU:0, one launch (start us, length us, event | category | flops | bytes accessed | tf_op | source)
XLA Modules:
  0.0 65.4 jit_solution(3268517524270153757)
XLA Ops:
  0.0 0.5 collective-permute-start.2
  0.5 4.6 %collective-permute-start = (bf16[5,40,640]{2,1,0:T(8,128)(2,1)}, bf16[5,40,640]{2,1,0:T(8,128)(2,1)S(1)}, u32[]{:S(2)}, u32[]{:S(2)}) collective-permute-start(bf16[5,40,640]{2,1,0:T(8,128)(2,1)} %refs_6_.1), channel_id=1, source_target_pairs={{0,12},{4,8},{8,4},{12,0},{16,24},{20,28},{24,16},{28,20},{1,13},{... | collective-permute-start | bytes 768008 | tf_op jit(solution)/shard_map/ppermute | solution.py:223
  5.1 0.0 collective-permute-start.1
  5.1 0.0 copy-start.4
  5.1 0.9 %copy-done.4 = bf16[2,4,640,24]{2,3,1,0:T(8,128)(2,1)S(1)} copy-done((bf16[2,4,640,24]{2,3,1,0:T(8,128)(2,1)S(1)}, bf16[2,4,640,24]{2,3,1,0:T(8,128)(2,1)}, u32[]{:S(2)}) %copy-start.4) | copy-done | bytes 245784
  6.0 0.4 pack.1
  6.4 10.1 %all_to_all.5 = bf16[8,24,640]{2,1,0:T(8,128)(2,1)S(1)} all-to-all(bf16[8,24,640]{2,1,0:T(8,128)(2,1)S(1)} %bitcast.13), channel_id=1, replica_groups=mesh['lath'=1,'late'=2,'lonp'=4,'lonq'=4] {'late','lonq'}, dimensions={0} | all-to-all | bytes 491520 | tf_op jit(solution)/shard_map/all_to_all | solution.py:246
  16.5 0.0 collective-permute-done.refs_8_
  16.5 0.6 collective-permute-done.1.refs_7_
  17.1 0.0 copy-start.2
  17.1 0.7 %copy-done.2 = bf16[5,40,640]{2,1,0:T(8,128)(2,1)} copy-done((bf16[5,40,640]{2,1,0:T(8,128)(2,1)}, bf16[5,40,640]{2,1,0:T(8,128)(2,1)S(1)}, u32[]{:S(2)}) %copy-start.2) | copy-done | bytes 256024
  17.8 0.0 collective-permute-done.2.x_ref
  17.8 0.0 collective-permute-start.6
  17.8 2.4 %collective-permute-start.3 = (bf16[2,96,640]{2,1,0:T(8,128)(2,1)S(1)}, bf16[2,96,640]{2,1,0:T(8,128)(2,1)}, u32[]{:S(2)}, u32[]{:S(2)}) collective-permute-start(bf16[2,96,640]{2,1,0:T(8,128)(2,1)S(1)} %bitcast.9), channel_id=1, source_target_pairs={{0,12},{4,8},{8,4},{12,0},{1,13},{5,9},{9,5},{13,1},{2,14},{6,10},... | collective-permute-start | bytes 737288 | tf_op jit(solution)/shard_map/ppermute | solution.py:33
  20.2 0.5 collective-permute-start.4
  20.7 1.5 %collective-permute-start.5 = (bf16[2,96,640]{2,1,0:T(8,128)(2,1)S(1)}, bf16[2,96,640]{2,1,0:T(8,128)(2,1)}, u32[]{:S(2)}, u32[]{:S(2)}) collective-permute-start(bf16[2,96,640]{2,1,0:T(8,128)(2,1)S(1)} %bitcast.11), channel_id=1, source_target_pairs={{0,4},{4,0},{8,12},{12,8},{1,5},{5,1},{9,13},{13,9},{2,6},{6,2},{1... | collective-permute-start | bytes 737288 | tf_op jit(solution)/shard_map/ppermute | solution.py:33
  22.2 0.8 %copy.6.shift_ref = s32[8,3]{1,0:T(8,128)S(1)} copy(s32[8,3]{0,1:T(4,128)} %param.8) | data formatting | bytes 192 | tf_op args[3]
  22.9 0.1 stack.28.place_ref
  23.0 0.0 copy-start
  23.0 1.8 %copy-done = bf16[5,4,3,3,64,64]{5,4,3,2,1,0:T(8,128)(2,1)S(1)} copy-done((bf16[5,4,3,3,64,64]{5,4,3,2,1,0:T(8,128)(2,1)S(1)}, bf16[5,4,3,3,64,64]{5,4,3,2,1,0:T(8,128)(2,1)}, u32[]{:S(2)}) %copy-start) | copy-done | bytes 1474584
  24.9 2.4 %turn.2.refs_4_ = bf16[4,15,64,192]{3,2,1,0:T(8,128)(2,1)S(1)} custom-call(bf16[5,4,3,3,64,64]{5,4,3,2,1,0:T(8,128)(2,1)S(1)} %copy-done), custom_call_target="tpu_custom_call" | custom-call | tf_op jit(solution)/shard_map/turn/pallas_call | solution.py:207
  27.3 0.0 copy-start.1
  27.3 0.0 copy-start.3
  27.3 0.0 copy-start.5
  27.3 2.4 %turn.3.refs_5_ = bf16[4,15,64,192]{3,2,1,0:T(8,128)(2,1)S(1)} custom-call(bf16[5,4,3,3,64,64]{5,4,3,2,1,0:T(8,128)(2,1)S(1)} %collective-permute-done.2.x_ref), custom_call_target="tpu_custom_call" | custom-call | tf_op jit(solution)/shard_map/turn/pallas_call | solution.py:207
  29.8 0.0 collective-permute-done.3.refs_0_
  29.8 13.0 %collective-permute-done.4.refs_1_ = bf16[2,96,640]{2,1,0:T(8,128)(2,1)} collective-permute-done((bf16[2,96,640]{2,1,0:T(8,128)(2,1)S(1)}, bf16[2,96,640]{2,1,0:T(8,128)(2,1)}, u32[]{:S(2)}, u32[]{:S(2)}) %collective-permute-start.4) | collective-permute-done | bytes 245792 | tf_op jit(solution)/shard_map/ppermute | solution.py:33
  42.8 0.0 collective-permute-done.5.refs_2_
  42.8 0.0 collective-permute-done.6.refs_9_
  42.8 0.0 copy-done.1
  42.8 0.0 copy-done.3
  42.8 0.0 copy-done.5
  42.8 6.8 %conv_mix.1 = (bf16[4,24,640]{2,1,0:T(8,128)(2,1)S(1)}, bf16[4,24,640]{2,1,0:T(8,128)(2,1)S(1)}, bf16[4,24,640]{2,1,0:T(8,128)(2,1)S(1)}, bf16[4,24,640]{2,1,0:T...) custom-call(s32[5,8]{1,0:T(8,128)S(1)} %copy-done.5, ...), custom_call_target="tpu_custom_call" | custom-call | tf_op jit(solution)/shard_map/conv_mix/pallas_call | solution.py:150
  49.6 0.1 collective-permute-start.7
  49.7 1.6 %collective-permute-start.8 = (bf16[4,24,640]{2,1,0:T(8,128)(2,1)S(1)}, bf16[4,24,640]{2,1,0:T(8,128)(2,1)S(1)}, u32[]{:S(2)}, u32[]{:S(2)}) collective-permute-start(bf16[4,24,640]{2,1,0:T(8,128)(2,1)S(1)} %get-tuple-element.25), channel_id=1, source_target_pairs={{0,1},{1,0},{2,3},{3,2},{16,17},{17,16},{18,19},{19,18},{4,5},{5,4... | collective-permute-start | bytes 368648 | tf_op jit(solution)/shard_map/ppermute | solution.py:277
  51.2 1.5 %collective-permute-start.9 = (bf16[4,24,640]{2,1,0:T(8,128)(2,1)S(1)}, bf16[4,24,640]{2,1,0:T(8,128)(2,1)S(1)}, u32[]{:S(2)}, u32[]{:S(2)}) collective-permute-start(bf16[4,24,640]{2,1,0:T(8,128)(2,1)S(1)} %get-tuple-element.26), channel_id=1, source_target_pairs={{0,2},{1,3},{2,0},{3,1},{16,18},{17,19},{18,16},{19,17},{4,6},{5,7... | collective-permute-start | bytes 368648 | tf_op jit(solution)/shard_map/ppermute | solution.py:277
  52.7 0.0 collective-permute-start.10
  52.8 0.7 %collective-permute-start.11 = (bf16[4,24,640]{2,1,0:T(8,128)(2,1)S(1)}, bf16[4,24,640]{2,1,0:T(8,128)(2,1)S(1)}, u32[]{:S(2)}, u32[]{:S(2)}) collective-permute-start(bf16[4,24,640]{2,1,0:T(8,128)(2,1)S(1)} %get-tuple-element.28), channel_id=1, source_target_pairs={{0,18},{1,19},{2,16},{3,17},{16,2},{17,3},{18,0},{19,1},{4,22},{5,... | collective-permute-start | bytes 368648 | tf_op jit(solution)/shard_map/ppermute | solution.py:277
  53.5 0.0 collective-permute-done.7.refs_1_
  53.5 2.4 %collective-permute-start.12 = (bf16[4,24,640]{2,1,0:T(8,128)(2,1)S(1)}, bf16[4,24,640]{2,1,0:T(8,128)(2,1)S(1)}, u32[]{:S(2)}, u32[]{:S(2)}) collective-permute-start(bf16[4,24,640]{2,1,0:T(8,128)(2,1)S(1)} %get-tuple-element.29), channel_id=1, source_target_pairs={{0,3},{1,2},{2,1},{3,0},{16,19},{17,18},{18,17},{19,16},{4,7},{5,6... | collective-permute-start | bytes 368648 | tf_op jit(solution)/shard_map/ppermute | solution.py:277
  56.0 0.0 collective-permute-done.8.refs_2_
  56.0 1.2 %collective-permute-start.13 = (bf16[4,24,640]{2,1,0:T(8,128)(2,1)S(1)}, bf16[4,24,640]{2,1,0:T(8,128)(2,1)S(1)}, u32[]{:S(2)}, u32[]{:S(2)}) collective-permute-start(bf16[4,24,640]{2,1,0:T(8,128)(2,1)S(1)} %get-tuple-element.30), channel_id=1, source_target_pairs={{0,19},{1,18},{2,17},{3,16},{16,3},{17,2},{18,1},{19,0},{4,23},{5,... | collective-permute-start | bytes 368648 | tf_op jit(solution)/shard_map/ppermute | solution.py:277
  57.1 0.3 collective-permute-done.9.refs_3_
  57.4 0.9 %collective-permute-done.10.refs_4_ = bf16[4,24,640]{2,1,0:T(8,128)(2,1)S(1)} collective-permute-done((bf16[4,24,640]{2,1,0:T(8,128)(2,1)S(1)}, bf16[4,24,640]{2,1,0:T(8,128)(2,1)S(1)}, u32[]{:S(2)}, u32[]{:S(2)}) %collective-permute-start.10) | collective-permute-done | bytes 122912 | tf_op jit(solution)/shard_map/ppermute | solution.py:277
  58.3 5.3 %collective-permute-done.11.refs_5_ = bf16[4,24,640]{2,1,0:T(8,128)(2,1)S(1)} collective-permute-done((bf16[4,24,640]{2,1,0:T(8,128)(2,1)S(1)}, bf16[4,24,640]{2,1,0:T(8,128)(2,1)S(1)}, u32[]{:S(2)}, u32[]{:S(2)}) %collective-permute-start.11) | collective-permute-done | bytes 122912 | tf_op jit(solution)/shard_map/ppermute | solution.py:277
  63.6 0.0 collective-permute-done.12.refs_6_
  63.6 0.3 collective-permute-done.13.refs_7_
  63.9 1.4 %finish.1 = bf16[2,4,24,640]{3,2,1,0:T(8,128)(2,1)} custom-call(s32[7]{0:T(128)S(1)} %stack.28.place_ref, bf16[4,24,640]{2,1,0:T(8,128)(2,1)S(1)} %get-tuple-element.23.refs_0_, bf16[4,24,640]{2,1,0:T(8,128)(2,1)S(1)} %collective-permute-done.7.refs_1_, bf16[4,24,640]{2,1,0:T(8,128)(2,1)S(1)} %collective-permute-done.8.refs_2_, ...), custom_call_target="tpu_custom_call" | custom-call | tf_op jit(solution)/shard_map/finish/pallas_call | solution.py:179
Async XLA Ops:
  0.0 17.8 %collective-permute-start.2 = (bf16[5,4,3,3,64,64]{5,4,3,2,1,0:T(8,128)(2,1)}, bf16[5,4,3,3,64,64]{5,4,3,2,1,0:T(8,128)(2,1)S(1)}, u32[]{:S(2)}, u32[]{:S(2)}) collective-permute-start(bf16[5,4,3,3,64,64]{5,4,3,2,1,0:T(8,128)(2,1)} %x_ref), channel_id=1, source_target_pairs={{0,16},{16,0},{1,17},{17,1},{2,18},{18,2},{3,19},{19,3},{4,20},{20... | collective-permute-start | bytes 4423688 | tf_op jit(solution)/shard_map/ppermute | solution.py:33
  0.5 16.0 %collective-permute-start = (bf16[5,40,640]{2,1,0:T(8,128)(2,1)}, bf16[5,40,640]{2,1,0:T(8,128)(2,1)S(1)}, u32[]{:S(2)}, u32[]{:S(2)}) collective-permute-start(bf16[5,40,640]{2,1,0:T(8,128)(2,1)} %refs_6_.1), channel_id=1, source_target_pairs={{0,12},{4,8},{8,4},{12,0},{16,24},{20,28},{24,16},{28,20},{1,13},{... | collective-permute-start | bytes 768008 | tf_op jit(solution)/shard_map/ppermute | solution.py:223
  5.1 12.0 %collective-permute-start.1 = (bf16[5,40,640]{2,1,0:T(8,128)(2,1)}, bf16[5,40,640]{2,1,0:T(8,128)(2,1)S(1)}, u32[]{:S(2)}, u32[]{:S(2)}) collective-permute-start(bf16[5,40,640]{2,1,0:T(8,128)(2,1)} %refs_6_.1), channel_id=1, source_target_pairs={{0,4},{4,0},{8,12},{12,8},{1,5},{5,1},{9,13},{13,9},{2,6},{6,2},{1... | collective-permute-start | bytes 768008 | tf_op jit(solution)/shard_map/ppermute | solution.py:33
  5.1 0.9 %copy-start.4 = (bf16[2,4,640,24]{2,3,1,0:T(8,128)(2,1)S(1)}, bf16[2,4,640,24]{2,3,1,0:T(8,128)(2,1)}, u32[]{:S(2)}) copy-start(bf16[2,4,640,24]{2,3,1,0:T(8,128)(2,1)} %param.5) | copy-start | bytes 737284
  17.1 0.7 %copy-start.2 = (bf16[5,40,640]{2,1,0:T(8,128)(2,1)}, bf16[5,40,640]{2,1,0:T(8,128)(2,1)S(1)}, u32[]{:S(2)}) copy-start(bf16[5,40,640]{2,1,0:T(8,128)(2,1)S(1)} %collective-permute-done.1.refs_7_) | copy-start | bytes 768004
  17.8 25.0 %collective-permute-start.6 = (bf16[5,40,640]{2,1,0:T(8,128)(2,1)S(1)}, bf16[5,40,640]{2,1,0:T(8,128)(2,1)}, u32[]{:S(2)}, u32[]{:S(2)}) collective-permute-start(bf16[5,40,640]{2,1,0:T(8,128)(2,1)S(1)} %collective-permute-done.refs_8_), channel_id=1, source_target_pairs={{0,16},{16,0},{1,17},{17,1},{2,18},{18,2},{3,19},{19,3},{4,20},{20... | collective-permute-start | bytes 768008 | tf_op jit(solution)/shard_map/ppermute | solution.py:33
  17.8 12.0 %collective-permute-start.3 = (bf16[2,96,640]{2,1,0:T(8,128)(2,1)S(1)}, bf16[2,96,640]{2,1,0:T(8,128)(2,1)}, u32[]{:S(2)}, u32[]{:S(2)}) collective-permute-start(bf16[2,96,640]{2,1,0:T(8,128)(2,1)S(1)} %bitcast.9), channel_id=1, source_target_pairs={{0,12},{4,8},{8,4},{12,0},{1,13},{5,9},{9,5},{13,1},{2,14},{6,10},... | collective-permute-start | bytes 737288 | tf_op jit(solution)/shard_map/ppermute | solution.py:33
  20.2 22.6 %collective-permute-start.4 = (bf16[2,96,640]{2,1,0:T(8,128)(2,1)S(1)}, bf16[2,96,640]{2,1,0:T(8,128)(2,1)}, u32[]{:S(2)}, u32[]{:S(2)}) collective-permute-start(bf16[2,96,640]{2,1,0:T(8,128)(2,1)S(1)} %bitcast.10), channel_id=1, source_target_pairs={{0,8},{4,12},{8,0},{12,4},{1,9},{5,13},{9,1},{13,5},{2,10},{6,14},... | collective-permute-start | bytes 737288 | tf_op jit(solution)/shard_map/ppermute | solution.py:33
  20.7 22.1 %collective-permute-start.5 = (bf16[2,96,640]{2,1,0:T(8,128)(2,1)S(1)}, bf16[2,96,640]{2,1,0:T(8,128)(2,1)}, u32[]{:S(2)}, u32[]{:S(2)}) collective-permute-start(bf16[2,96,640]{2,1,0:T(8,128)(2,1)S(1)} %bitcast.11), channel_id=1, source_target_pairs={{0,4},{4,0},{8,12},{12,8},{1,5},{5,1},{9,13},{13,9},{2,6},{6,2},{1... | collective-permute-start | bytes 737288 | tf_op jit(solution)/shard_map/ppermute | solution.py:33
  23.0 1.8 %copy-start = (bf16[5,4,3,3,64,64]{5,4,3,2,1,0:T(8,128)(2,1)S(1)}, bf16[5,4,3,3,64,64]{5,4,3,2,1,0:T(8,128)(2,1)}, u32[]{:S(2)}) copy-start(bf16[5,4,3,3,64,64]{5,4,3,2,1,0:T(8,128)(2,1)} %x_ref) | copy-start | bytes 4423684
  27.3 15.5 %copy-start.1 = (bf16[5,40,640]{2,1,0:T(8,128)(2,1)S(1)}, bf16[5,40,640]{2,1,0:T(8,128)(2,1)}, u32[]{:S(2)}) copy-start(bf16[5,40,640]{2,1,0:T(8,128)(2,1)} %refs_6_.1) | copy-start | bytes 768004
  27.3 15.5 %copy-start.3 = (bf16[5,40,640]{2,1,0:T(8,128)(2,1)S(1)}, bf16[5,40,640]{2,1,0:T(8,128)(2,1)}, u32[]{:S(2)}) copy-start(bf16[5,40,640]{2,1,0:T(8,128)(2,1)} %copy-done.2) | copy-start | bytes 768004
  27.3 15.5 %copy-start.5 = (s32[5,8]{1,0:T(8,128)S(1)}, s32[5,8]{1,0:T(8,128)}, u32[]{:S(2)}) copy-start(s32[5,8]{1,0:T(8,128)} %low_ref) | copy-start | bytes 484
  49.6 3.9 %collective-permute-start.7 = (bf16[4,24,640]{2,1,0:T(8,128)(2,1)S(1)}, bf16[4,24,640]{2,1,0:T(8,128)(2,1)S(1)}, u32[]{:S(2)}, u32[]{:S(2)}) collective-permute-start(bf16[4,24,640]{2,1,0:T(8,128)(2,1)S(1)} %get-tuple-element.24), channel_id=1, source_target_pairs={{0,16},{1,17},{2,18},{3,19},{16,0},{17,1},{18,2},{19,3},{4,20},{5,... | collective-permute-start | bytes 368648 | tf_op jit(solution)/shard_map/ppermute | solution.py:277
  49.7 6.3 %collective-permute-start.8 = (bf16[4,24,640]{2,1,0:T(8,128)(2,1)S(1)}, bf16[4,24,640]{2,1,0:T(8,128)(2,1)S(1)}, u32[]{:S(2)}, u32[]{:S(2)}) collective-permute-start(bf16[4,24,640]{2,1,0:T(8,128)(2,1)S(1)} %get-tuple-element.25), channel_id=1, source_target_pairs={{0,1},{1,0},{2,3},{3,2},{16,17},{17,16},{18,19},{19,18},{4,5},{5,4... | collective-permute-start | bytes 368648 | tf_op jit(solution)/shard_map/ppermute | solution.py:277
  51.2 6.2 %collective-permute-start.9 = (bf16[4,24,640]{2,1,0:T(8,128)(2,1)S(1)}, bf16[4,24,640]{2,1,0:T(8,128)(2,1)S(1)}, u32[]{:S(2)}, u32[]{:S(2)}) collective-permute-start(bf16[4,24,640]{2,1,0:T(8,128)(2,1)S(1)} %get-tuple-element.26), channel_id=1, source_target_pairs={{0,2},{1,3},{2,0},{3,1},{16,18},{17,19},{18,16},{19,17},{4,6},{5,7... | collective-permute-start | bytes 368648 | tf_op jit(solution)/shard_map/ppermute | solution.py:277
  52.7 5.6 %collective-permute-start.10 = (bf16[4,24,640]{2,1,0:T(8,128)(2,1)S(1)}, bf16[4,24,640]{2,1,0:T(8,128)(2,1)S(1)}, u32[]{:S(2)}, u32[]{:S(2)}) collective-permute-start(bf16[4,24,640]{2,1,0:T(8,128)(2,1)S(1)} %get-tuple-element.27), channel_id=1, source_target_pairs={{0,17},{1,16},{2,19},{3,18},{16,1},{17,0},{18,3},{19,2},{4,21},{5,... | collective-permute-start | bytes 368648 | tf_op jit(solution)/shard_map/ppermute | solution.py:277
  52.8 10.8 %collective-permute-start.11 = (bf16[4,24,640]{2,1,0:T(8,128)(2,1)S(1)}, bf16[4,24,640]{2,1,0:T(8,128)(2,1)S(1)}, u32[]{:S(2)}, u32[]{:S(2)}) collective-permute-start(bf16[4,24,640]{2,1,0:T(8,128)(2,1)S(1)} %get-tuple-element.28), channel_id=1, source_target_pairs={{0,18},{1,19},{2,16},{3,17},{16,2},{17,3},{18,0},{19,1},{4,22},{5,... | collective-permute-start | bytes 368648 | tf_op jit(solution)/shard_map/ppermute | solution.py:277
  53.5 10.0 %collective-permute-start.12 = (bf16[4,24,640]{2,1,0:T(8,128)(2,1)S(1)}, bf16[4,24,640]{2,1,0:T(8,128)(2,1)S(1)}, u32[]{:S(2)}, u32[]{:S(2)}) collective-permute-start(bf16[4,24,640]{2,1,0:T(8,128)(2,1)S(1)} %get-tuple-element.29), channel_id=1, source_target_pairs={{0,3},{1,2},{2,1},{3,0},{16,19},{17,18},{18,17},{19,16},{4,7},{5,6... | collective-permute-start | bytes 368648 | tf_op jit(solution)/shard_map/ppermute | solution.py:277
  56.0 7.9 %collective-permute-start.13 = (bf16[4,24,640]{2,1,0:T(8,128)(2,1)S(1)}, bf16[4,24,640]{2,1,0:T(8,128)(2,1)S(1)}, u32[]{:S(2)}, u32[]{:S(2)}) collective-permute-start(bf16[4,24,640]{2,1,0:T(8,128)(2,1)S(1)} %get-tuple-element.30), channel_id=1, source_target_pairs={{0,19},{1,18},{2,17},{3,16},{16,3},{17,2},{18,1},{19,0},{4,23},{5,... | collective-permute-start | bytes 368648 | tf_op jit(solution)/shard_map/ppermute | solution.py:277

commit v16 on v15

--- a/solution.py
+++ b/solution.py
@@ -66,7 +66,7 @@
     field_rows, total, mix_all, mixed = refs[-4:]
     outs = refs[:-4]
     late, span, _ = field_refs[0].shape
-    owners = len(field_refs)
+    owners = len(mix_refs)
     depth, width = mix_refs[0].shape[1:]
     channels = owners * depth
     padded = total.shape[-1]
@@ -79,9 +79,11 @@
     field_rows[...] = jnp.zeros_like(field_rows)
     for s in range(late):
         lat = partner_in_kernel(member, s, late)
-        for d, ref in enumerate(field_refs):
+        for d in range(owners):
             at = pl.ds(pl.multiple_of(partner_in_kernel(owner, d, owners) * span, sub), span)
-            value = ref[lat]
+            value = field_refs[d][lat]
+            if d == owners - 1 and len(field_refs) > owners:
+                value = value + field_refs[owners][lat]
             for r in range(rows):
                 field_rows[r, at, :channels] = value[:, r * channels : (r + 1) * channels]
 
@@ -136,7 +138,7 @@
     bases, all_rows = low.shape
     slots = shift.shape[1]
     late, span, _ = fields[0].shape
-    owners = len(fields)
+    owners = len(mix)
     rows = all_rows // late
     depth, width = mix[0].shape[1:]
     padded = -(-owners * depth // LANES) * LANES
@@ -218,14 +220,18 @@
     core, own = lax.axis_index("late"), lax.axis_index("lonp")
     if owners != 4 or late != 2:
         fields, mixes = [[x] + [trade(x, "lonp", d, owners) for d in range(1, owners)] for x in (spread, mix)]
-        return fields, mixes, [partner(own, d, owners) for d in range(owners)], kernels
+        return fields, mixes, [partner(own, d, owners) for d in range(owners)], [turn(x) for x in kernels]
     route = [(4 * c + p, 4 * c + (p ^ (3 - c))) for c in range(2) for p in range(4)]
     far = lax.ppermute(mix, ("late", "lonp"), route)
     near = trade(mix, "lonp", 1, owners)
     spread, far, near, *kernels = lax.optimization_barrier((spread, far, near, *kernels))
-    fields = [trade(spread, "lonp", d, owners) for d in (3, 2, 1)] + [spread]
-    mixes = [mix, near, far, trade(far, "late", 1, late)]
-    return fields[::-1], mixes, [own, own ^ 1, own ^ (3 - core), own ^ (2 + core)], kernels
+    two, one, swapped = trade(spread, "lonp", 2, owners), trade(spread, "lonp", 1, owners), trade(far, "late", 1, late)
+    weights = [turn(x) for x in kernels]
+    middle, two, one, swapped, *weights = lax.optimization_barrier((spread, two, one, swapped, *weights))
+    passed = lax.ppermute(two, "lonp", [(1, 0), (2, 3)])
+    middle = lax.ppermute(middle, "lonp", [(1, 2), (2, 1)])
+    origins = [own, own ^ 1, own ^ (3 - core), own ^ (2 + core)]
+    return [spread, one, two, middle, passed], [mix, near, far, swapped], origins, weights
 
 
 def send_rank(dl, dq):
@@ -245,8 +251,7 @@
     packed = packed.reshape((late * groups,) + packed.shape[2:])
     spread = lax.all_to_all(packed, ("late", "lonq"), split_axis=0, concat_axis=0, tiled=True)
     spread = spread.reshape(late, groups * cells, -1)
-    spread, mix, origins, kernels = gather(spread, mix_weight, kernels, late, owners)
-    weights = [turn(x) for x in kernels]
+    spread, mix, origins, weights = gather(spread, mix_weight, kernels, late, owners)
 
     start = lax.axis_index("lath") * all_rows
     low = lax.dynamic_slice_in_dim(band_low, start, all_rows, 1)

time: 65.6 us -> 69.2 us (1.055)
  the two profiles are of different devices: /device:TPU:0 before, /device:TPU:8 now
where the time goes in v16:
time: 69.2 us; the launch traced here: 68.9 us
  starting transfers between devices  20.7 us (30%)
  waiting for transfers between devices  17.6 us (25%)
  Pallas kernels  13.1 us (19%)
  blocking collectives  9.95 us (14%)
  local copies, waits for them, and re-layouts  7.43 us (11%)
    all_to_all x1, blocking collectives, per_device(): lax.all_to_all(packed, ('late', 'lonq'), split_axis=0, concat_axis=0, til...  9.95 us
    ppermute x7, waiting for transfers between devices, per_device(): lax.ppermute(block, ('late', 'lonq'), route)  8.18 us
    unnamed x19, local copies, waits for them, and re-layouts  7.35 us
    ppermute x7, starting transfers between devices, per_device(): lax.ppermute(block, ('late', 'lonq'), route)  7.09 us
    pallas_call x1, Pallas kernels, conv_mix(): pl.pallas_call(functools.partial(conv_mix_kernel, (bases, taps, slots, ha...  6.41 us
    ppermute x1, waiting for transfers between devices, gather(): middle = lax.ppermute(middle, 'lonp', [(1, 2), (2, 1)])  4.9 us
    pallas_call x2, Pallas kernels, turn(): pl.pallas_call(turn_kernel, out_shape=jax.ShapeDtypeStruct((rows, bases *...  4.86 us
    ppermute x5, starting transfers between devices, trade(): lax.ppermute(x, axis, [(i, partner(i, distance, size)) for i in range(siz...  4.52 us
  transfers between devices with their start and end apart: 15, of which 8 were waited for; matrix products, arithmetic and copies ran while one was open for 0% of the time, Pallas kernels for 8%

profile of v16, /device:TPU:8, one launch (start us, length us, event | category | flops | bytes accessed | tf_op | source)
XLA Modules:
  0.0 68.9 jit_solution(10981490745135336768)
XLA Ops:
  0.0 0.0 collective-permute-start.2
  0.0 1.6 %collective-permute-start = (bf16[5,40,640]{2,1,0:T(8,128)(2,1)}, bf16[5,40,640]{2,1,0:T(8,128)(2,1)S(1)}, u32[]{:S(2)}, u32[]{:S(2)}) collective-permute-start(bf16[5,40,640]{2,1,0:T(8,128)(2,1)} %refs_7_.1), channel_id=1, source_target_pairs={{0,12},{4,8},{8,4},{12,0},{16,24},{20,28},{24,16},{28,20},{1,13},{... | collective-permute-start | bytes 768008 | tf_op jit(solution)/shard_map/ppermute | solution.py:225
  1.6 2.5 %collective-permute-start.1 = (bf16[5,40,640]{2,1,0:T(8,128)(2,1)}, bf16[5,40,640]{2,1,0:T(8,128)(2,1)S(1)}, u32[]{:S(2)}, u32[]{:S(2)}) collective-permute-start(bf16[5,40,640]{2,1,0:T(8,128)(2,1)} %refs_7_.1), channel_id=1, source_target_pairs={{0,4},{4,0},{8,12},{12,8},{1,5},{5,1},{9,13},{13,9},{2,6},{6,2},{1... | collective-permute-start | bytes 768008 | tf_op jit(solution)/shard_map/ppermute | solution.py:33
  4.1 0.9 %copy-done.4 = bf16[2,4,640,24]{2,3,1,0:T(8,128)(2,1)S(1)} copy-done((bf16[2,4,640,24]{2,3,1,0:T(8,128)(2,1)S(1)}, bf16[2,4,640,24]{2,3,1,0:T(8,128)(2,1)}, u32[]{:S(2)}) %copy-start.4) | copy-done | bytes 245784
  5.0 0.4 pack.1
  5.4 9.9 %all_to_all.5 = bf16[8,24,640]{2,1,0:T(8,128)(2,1)S(1)} all-to-all(bf16[8,24,640]{2,1,0:T(8,128)(2,1)S(1)} %bitcast.13), channel_id=1, replica_groups=mesh['lath'=1,'late'=2,'lonp'=4,'lonq'=4] {'late','lonq'}, dimensions={0} | all-to-all | bytes 491520 | tf_op jit(solution)/shard_map/all_to_all | solution.py:252
  15.3 0.0 collective-permute-done.refs_9_
  15.3 0.0 collective-permute-done.1.refs_8_
  15.3 0.0 collective-permute-done.2.x_ref
  15.4 0.2 collective-permute-start.5
  15.6 1.5 %collective-permute-start.3 = (bf16[2,96,640]{2,1,0:T(8,128)(2,1)S(1)}, bf16[2,96,640]{2,1,0:T(8,128)(2,1)S(1)}, u32[]{:S(2)}, u32[]{:S(2)}) collective-permute-start(bf16[2,96,640]{2,1,0:T(8,128)(2,1)S(1)} %bitcast.9), channel_id=1, source_target_pairs={{0,8},{4,12},{8,0},{12,4},{1,9},{5,13},{9,1},{13,5},{2,10},{6,14},... | collective-permute-start | bytes 737288 | tf_op jit(solution)/shard_map/ppermute | solution.py:33
  17.1 0.3 collective-permute-start.4
  17.4 1.8 %copy-done.2 = bf16[5,4,3,3,64,64]{5,4,3,2,1,0:T(8,128)(2,1)S(1)} copy-done((bf16[5,4,3,3,64,64]{5,4,3,2,1,0:T(8,128)(2,1)S(1)}, bf16[5,4,3,3,64,64]{5,4,3,2,1,0:T(8,128)(2,1)}, u32[]{:S(2)}) %copy-start.2) | copy-done | bytes 1474584
  19.2 2.4 %turn.2.refs_5_ = bf16[4,15,64,192]{3,2,1,0:T(8,128)(2,1)S(1)} custom-call(bf16[5,4,3,3,64,64]{5,4,3,2,1,0:T(8,128)(2,1)S(1)} %copy-done.2), custom_call_target="tpu_custom_call" | custom-call | tf_op jit(solution)/shard_map/turn/pallas_call | solution.py:209
  21.7 0.0 copy-start.8
  21.7 0.0 copy-start.3
  21.7 0.0 copy-start.7
  21.7 2.4 %turn.3.refs_6_ = bf16[4,15,64,192]{3,2,1,0:T(8,128)(2,1)S(1)} custom-call(bf16[5,4,3,3,64,64]{5,4,3,2,1,0:T(8,128)(2,1)S(1)} %collective-permute-done.2.x_ref), custom_call_target="tpu_custom_call" | custom-call | tf_op jit(solution)/shard_map/turn/pallas_call | solution.py:209
  24.1 0.0 copy-start
  24.1 1.3 %copy-done = bf16[4,15,64,192]{3,2,1,0:T(8,128)(2,1)} copy-done((bf16[4,15,64,192]{3,2,1,0:T(8,128)(2,1)}, bf16[4,15,64,192]{3,2,1,0:T(8,128)(2,1)S(1)}, u32[]{:S(2)}) %copy-start) | copy-done | bytes 1474584
  25.4 2.4 %collective-permute-done.3.refs_2_ = bf16[2,96,640]{2,1,0:T(8,128)(2,1)S(1)} collective-permute-done((bf16[2,96,640]{2,1,0:T(8,128)(2,1)S(1)}, bf16[2,96,640]{2,1,0:T(8,128)(2,1)S(1)}, u32[]{:S(2)}, u32[]{:S(2)}) %collective-permute-start.3) | collective-permute-done | bytes 245792 | tf_op jit(solution)/shard_map/ppermute | solution.py:33
  27.8 1.2 %collective-permute-done.4.refs_3_ = bf16[2,96,640]{2,1,0:T(8,128)(2,1)S(1)} collective-permute-done((bf16[2,96,640]{2,1,0:T(8,128)(2,1)S(1)}, bf16[2,96,640]{2,1,0:T(8,128)(2,1)S(1)}, u32[]{:S(2)}, u32[]{:S(2)}) %collective-permute-start.4) | collective-permute-done | bytes 245792 | tf_op jit(solution)/shard_map/ppermute | solution.py:33
  29.0 0.7 %copy-done.5 = bf16[2,96,640]{2,1,0:T(8,128)(2,1)} copy-done((bf16[2,96,640]{2,1,0:T(8,128)(2,1)}, bf16[2,96,640]{2,1,0:T(8,128)(2,1)S(1)}, u32[]{:S(2)}) %copy-start.5) | copy-done | bytes 245784
  29.7 0.0 collective-permute-done.5.refs_10_
  29.7 4.3 %collective-permute-start.6 = (bf16[2,96,640]{2,1,0:T(8,128)(2,1)S(1)}, bf16[2,96,640]{2,1,0:T(8,128)(2,1)}, u32[]{:S(2)}, u32[]{:S(2)}) collective-permute-start(bf16[2,96,640]{2,1,0:T(8,128)(2,1)S(1)} %collective-permute-done.3.refs_2_), channel_id=1, source_target_pairs={{4,0},{8,12},{5,1},{9,13},{6,2},{10,14},{7,3},{11,15},{20,16},{24,... | collective-permute-start | bytes 737288 | tf_op jit(solution)/shard_map/ppermute | solution.py:231
  33.9 3.3 %collective-permute-start.7 = (bf16[2,96,640]{2,1,0:T(8,128)(2,1)S(1)}, bf16[2,96,640]{2,1,0:T(8,128)(2,1)}, u32[]{:S(2)}, u32[]{:S(2)}) collective-permute-start(bf16[2,96,640]{2,1,0:T(8,128)(2,1)S(1)} %bitcast.11), channel_id=1, source_target_pairs={{4,8},{8,4},{5,9},{9,5},{6,10},{10,6},{7,11},{11,7},{20,24},{24,20... | collective-permute-start | bytes 737288 | tf_op jit(solution)/shard_map/ppermute | solution.py:232
  37.2 0.1 copy.6.shift_ref
  37.3 0.1 stack.28.place_ref
  37.4 0.9 %collective-permute-done.6.refs_0_ = bf16[2,96,640]{2,1,0:T(8,128)(2,1)} collective-permute-done((bf16[2,96,640]{2,1,0:T(8,128)(2,1)S(1)}, bf16[2,96,640]{2,1,0:T(8,128)(2,1)}, u32[]{:S(2)}, u32[]{:S(2)}) %collective-permute-start.6) | collective-permute-done | bytes 245792 | tf_op jit(solution)/shard_map/ppermute | solution.py:231
  38.3 4.9 %collective-permute-done.7.refs_1_ = bf16[2,96,640]{2,1,0:T(8,128)(2,1)} collective-permute-done((bf16[2,96,640]{2,1,0:T(8,128)(2,1)S(1)}, bf16[2,96,640]{2,1,0:T(8,128)(2,1)}, u32[]{:S(2)}, u32[]{:S(2)}) %collective-permute-start.7) | collective-permute-done | bytes 245792 | tf_op jit(solution)/shard_map/ppermute | solution.py:232
  43.2 1.5 %copy-done.1 = bf16[4,15,64,192]{3,2,1,0:T(8,128)(2,1)S(1)} copy-done((bf16[4,15,64,192]{3,2,1,0:T(8,128)(2,1)S(1)}, bf16[4,15,64,192]{3,2,1,0:T(8,128)(2,1)}, u32[]{:S(2)}) %copy-start.1) | copy-done | bytes 1474584
  44.8 0.9 %copy-done.6 = bf16[2,96,640]{2,1,0:T(8,128)(2,1)S(1)} copy-done((bf16[2,96,640]{2,1,0:T(8,128)(2,1)S(1)}, bf16[2,96,640]{2,1,0:T(8,128)(2,1)}, u32[]{:S(2)}) %copy-start.6) | copy-done | bytes 245784
  45.7 6.4 %conv_mix.1 = (bf16[4,24,640]{2,1,0:T(8,128)(2,1)S(1)}, bf16[4,24,640]{2,1,0:T(8,128)(2,1)S(1)}, bf16[4,24,640]{2,1,0:T(8,128)(2,1)S(1)}, bf16[4,24,640]{2,1,0:T...) custom-call(s32[5,8]{1,0:T(8,128)S(1)} %copy-done.7, ...), custom_call_target="tpu_custom_call" | custom-call | tf_op jit(solution)/shard_map/conv_mix/pallas_call | solution.py:152
  52.1 1.7 %collective-permute-start.10 = (bf16[4,24,640]{2,1,0:T(8,128)(2,1)S(1)}, bf16[4,24,640]{2,1,0:T(8,128)(2,1)S(1)}, u32[]{:S(2)}, u32[]{:S(2)}) collective-permute-start(bf16[4,24,640]{2,1,0:T(8,128)(2,1)S(1)} %get-tuple-element.38), channel_id=1, source_target_pairs={{0,2},{1,3},{2,0},{3,1},{16,18},{17,19},{18,16},{19,17},{4,6},{5,7... | collective-permute-start | bytes 368648 | tf_op jit(solution)/shard_map/ppermute | solution.py:282
  53.9 0.0 collective-permute-start.11
  53.9 1.7 %collective-permute-start.12 = (bf16[4,24,640]{2,1,0:T(8,128)(2,1)S(1)}, bf16[4,24,640]{2,1,0:T(8,128)(2,1)S(1)}, u32[]{:S(2)}, u32[]{:S(2)}) collective-permute-start(bf16[4,24,640]{2,1,0:T(8,128)(2,1)S(1)} %get-tuple-element.40), channel_id=1, source_target_pairs={{0,18},{1,19},{2,16},{3,17},{16,2},{17,3},{18,0},{19,1},{4,22},{5,... | collective-permute-start | bytes 368648 | tf_op jit(solution)/shard_map/ppermute | solution.py:282
  55.6 1.5 %collective-permute-start.13 = (bf16[4,24,640]{2,1,0:T(8,128)(2,1)S(1)}, bf16[4,24,640]{2,1,0:T(8,128)(2,1)S(1)}, u32[]{:S(2)}, u32[]{:S(2)}) collective-permute-start(bf16[4,24,640]{2,1,0:T(8,128)(2,1)S(1)} %get-tuple-element.41), channel_id=1, source_target_pairs={{0,3},{1,2},{2,1},{3,0},{16,19},{17,18},{18,17},{19,16},{4,7},{5,6... | collective-permute-start | bytes 368648 | tf_op jit(solution)/shard_map/ppermute | solution.py:282
  57.1 0.6 collective-permute-start.14
  57.7 0.0 collective-permute-done.10.refs_3_
  57.7 0.9 %collective-permute-start.8 = (bf16[4,24,640]{2,1,0:T(8,128)(2,1)S(1)}, bf16[4,24,640]{2,1,0:T(8,128)(2,1)S(1)}, u32[]{:S(2)}, u32[]{:S(2)}) collective-permute-start(bf16[4,24,640]{2,1,0:T(8,128)(2,1)S(1)} %get-tuple-element.36), channel_id=1, source_target_pairs={{0,16},{1,17},{2,18},{3,19},{16,0},{17,1},{18,2},{19,3},{4,20},{5,... | collective-permute-start | bytes 368648 | tf_op jit(solution)/shard_map/ppermute | solution.py:282
  58.6 0.8 %collective-permute-done.11.refs_4_ = bf16[4,24,640]{2,1,0:T(8,128)(2,1)S(1)} collective-permute-done((bf16[4,24,640]{2,1,0:T(8,128)(2,1)S(1)}, bf16[4,24,640]{2,1,0:T(8,128)(2,1)S(1)}, u32[]{:S(2)}, u32[]{:S(2)}) %collective-permute-start.11) | collective-permute-done | bytes 122912 | tf_op jit(solution)/shard_map/ppermute | solution.py:282
  59.4 0.6 collective-permute-start.9
  60.1 3.7 %collective-permute-done.12.refs_5_ = bf16[4,24,640]{2,1,0:T(8,128)(2,1)S(1)} collective-permute-done((bf16[4,24,640]{2,1,0:T(8,128)(2,1)S(1)}, bf16[4,24,640]{2,1,0:T(8,128)(2,1)S(1)}, u32[]{:S(2)}, u32[]{:S(2)}) %collective-permute-start.12) | collective-permute-done | bytes 122912 | tf_op jit(solution)/shard_map/ppermute | solution.py:282
  63.7 0.0 collective-permute-done.13.refs_6_
  63.7 0.1 collective-permute-done.14.refs_7_
  63.8 0.0 collective-permute-done.8.refs_1_
  63.8 3.6 %collective-permute-done.9.refs_2_ = bf16[4,24,640]{2,1,0:T(8,128)(2,1)S(1)} collective-permute-done((bf16[4,24,640]{2,1,0:T(8,128)(2,1)S(1)}, bf16[4,24,640]{2,1,0:T(8,128)(2,1)S(1)}, u32[]{:S(2)}, u32[]{:S(2)}) %collective-permute-start.9) | collective-permute-done | bytes 122912 | tf_op jit(solution)/shard_map/ppermute | solution.py:282
  67.4 1.4 %finish.1 = bf16[2,4,24,640]{3,2,1,0:T(8,128)(2,1)} custom-call(s32[7]{0:T(128)S(1)} %stack.28.place_ref, bf16[4,24,640]{2,1,0:T(8,128)(2,1)S(1)} %get-tuple-element.35.refs_0_, bf16[4,24,640]{2,1,0:T(8,128)(2,1)S(1)} %collective-permute-done.8.refs_1_, bf16[4,24,640]{2,1,0:T(8,128)(2,1)S(1)} %collective-permute-done.9.refs_2_, ...), custom_call_target="tpu_custom_call" | custom-call | tf_op jit(solution)/shard_map/finish/pallas_call | solution.py:181
  (8 shorter events, 0.0 us)
Async XLA Ops:
  0.0 15.3 %collective-permute-start.2 = (bf16[5,4,3,3,64,64]{5,4,3,2,1,0:T(8,128)(2,1)}, bf16[5,4,3,3,64,64]{5,4,3,2,1,0:T(8,128)(2,1)S(1)}, u32[]{:S(2)}, u32[]{:S(2)}) collective-permute-start(bf16[5,4,3,3,64,64]{5,4,3,2,1,0:T(8,128)(2,1)} %x_ref), channel_id=1, source_target_pairs={{0,16},{16,0},{1,17},{17,1},{2,18},{18,2},{3,19},{19,3},{4,20},{20... | collective-permute-start | bytes 4423688 | tf_op jit(solution)/shard_map/ppermute | solution.py:33
  0.0 15.3 %collective-permute-start = (bf16[5,40,640]{2,1,0:T(8,128)(2,1)}, bf16[5,40,640]{2,1,0:T(8,128)(2,1)S(1)}, u32[]{:S(2)}, u32[]{:S(2)}) collective-permute-start(bf16[5,40,640]{2,1,0:T(8,128)(2,1)} %refs_7_.1), channel_id=1, source_target_pairs={{0,12},{4,8},{8,4},{12,0},{16,24},{20,28},{24,16},{28,20},{1,13},{... | collective-permute-start | bytes 768008 | tf_op jit(solution)/shard_map/ppermute | solution.py:225
  1.6 13.8 %collective-permute-start.1 = (bf16[5,40,640]{2,1,0:T(8,128)(2,1)}, bf16[5,40,640]{2,1,0:T(8,128)(2,1)S(1)}, u32[]{:S(2)}, u32[]{:S(2)}) collective-permute-start(bf16[5,40,640]{2,1,0:T(8,128)(2,1)} %refs_7_.1), channel_id=1, source_target_pairs={{0,4},{4,0},{8,12},{12,8},{1,5},{5,1},{9,13},{13,9},{2,6},{6,2},{1... | collective-permute-start | bytes 768008 | tf_op jit(solution)/shard_map/ppermute | solution.py:33
  4.1 0.9 %copy-start.4 = (bf16[2,4,640,24]{2,3,1,0:T(8,128)(2,1)S(1)}, bf16[2,4,640,24]{2,3,1,0:T(8,128)(2,1)}, u32[]{:S(2)}) copy-start(bf16[2,4,640,24]{2,3,1,0:T(8,128)(2,1)} %param.5) | copy-start | bytes 737284
  15.4 14.3 %collective-permute-start.5 = (bf16[5,40,640]{2,1,0:T(8,128)(2,1)S(1)}, bf16[5,40,640]{2,1,0:T(8,128)(2,1)S(1)}, u32[]{:S(2)}, u32[]{:S(2)}) collective-permute-start(bf16[5,40,640]{2,1,0:T(8,128)(2,1)S(1)} %collective-permute-done.refs_9_), channel_id=1, source_target_pairs={{0,16},{16,0},{1,17},{17,1},{2,18},{18,2},{3,19},{19,3},{4,20},{20... | collective-permute-start | bytes 768008 | tf_op jit(solution)/shard_map/ppermute | solution.py:33
  15.6 12.2 %collective-permute-start.3 = (bf16[2,96,640]{2,1,0:T(8,128)(2,1)S(1)}, bf16[2,96,640]{2,1,0:T(8,128)(2,1)S(1)}, u32[]{:S(2)}, u32[]{:S(2)}) collective-permute-start(bf16[2,96,640]{2,1,0:T(8,128)(2,1)S(1)} %bitcast.9), channel_id=1, source_target_pairs={{0,8},{4,12},{8,0},{12,4},{1,9},{5,13},{9,1},{13,5},{2,10},{6,14},... | collective-permute-start | bytes 737288 | tf_op jit(solution)/shard_map/ppermute | solution.py:33
  17.1 11.9 %collective-permute-start.4 = (bf16[2,96,640]{2,1,0:T(8,128)(2,1)S(1)}, bf16[2,96,640]{2,1,0:T(8,128)(2,1)S(1)}, u32[]{:S(2)}, u32[]{:S(2)}) collective-permute-start(bf16[2,96,640]{2,1,0:T(8,128)(2,1)S(1)} %bitcast.10), channel_id=1, source_target_pairs={{0,4},{4,0},{8,12},{12,8},{1,5},{5,1},{9,13},{13,9},{2,6},{6,2},{1... | collective-permute-start | bytes 737288 | tf_op jit(solution)/shard_map/ppermute | solution.py:33
  17.4 1.8 %copy-start.2 = (bf16[5,4,3,3,64,64]{5,4,3,2,1,0:T(8,128)(2,1)S(1)}, bf16[5,4,3,3,64,64]{5,4,3,2,1,0:T(8,128)(2,1)}, u32[]{:S(2)}) copy-start(bf16[5,4,3,3,64,64]{5,4,3,2,1,0:T(8,128)(2,1)} %x_ref) | copy-start | bytes 4423684
  21.7 15.6 %copy-start.8 = (s32[8,3]{0,1:T(4,128)S(1)}, s32[8,3]{0,1:T(4,128)}, u32[]{:S(2)}) copy-start(s32[8,3]{0,1:T(4,128)} %param.8) | copy-start | bytes 292
  21.7 21.6 %copy-start.3 = (bf16[5,40,640]{2,1,0:T(8,128)(2,1)S(1)}, bf16[5,40,640]{2,1,0:T(8,128)(2,1)}, u32[]{:S(2)}) copy-start(bf16[5,40,640]{2,1,0:T(8,128)(2,1)} %refs_7_.1) | copy-start | bytes 768004
  21.7 21.5 %copy-start.7 = (s32[5,8]{1,0:T(8,128)S(1)}, s32[5,8]{1,0:T(8,128)}, u32[]{:S(2)}) copy-start(s32[5,8]{1,0:T(8,128)} %low_ref) | copy-start | bytes 484
  24.1 1.3 %copy-start = (bf16[4,15,64,192]{3,2,1,0:T(8,128)(2,1)}, bf16[4,15,64,192]{3,2,1,0:T(8,128)(2,1)S(1)}, u32[]{:S(2)}) copy-start(bf16[4,15,64,192]{3,2,1,0:T(8,128)(2,1)S(1)} %turn.3.refs_6_) | copy-start | bytes 4423684
  29.0 0.7 %copy-start.5 = (bf16[2,96,640]{2,1,0:T(8,128)(2,1)}, bf16[2,96,640]{2,1,0:T(8,128)(2,1)S(1)}, u32[]{:S(2)}) copy-start(bf16[2,96,640]{2,1,0:T(8,128)(2,1)S(1)} %collective-permute-done.4.refs_3_) | copy-start | bytes 737284
  29.7 8.6 %collective-permute-start.6 = (bf16[2,96,640]{2,1,0:T(8,128)(2,1)S(1)}, bf16[2,96,640]{2,1,0:T(8,128)(2,1)}, u32[]{:S(2)}, u32[]{:S(2)}) collective-permute-start(bf16[2,96,640]{2,1,0:T(8,128)(2,1)S(1)} %collective-permute-done.3.refs_2_), channel_id=1, source_target_pairs={{4,0},{8,12},{5,1},{9,13},{6,2},{10,14},{7,3},{11,15},{20,16},{24,... | collective-permute-start | bytes 737288 | tf_op jit(solution)/shard_map/ppermute | solution.py:231
  33.9 9.3 %collective-permute-start.7 = (bf16[2,96,640]{2,1,0:T(8,128)(2,1)S(1)}, bf16[2,96,640]{2,1,0:T(8,128)(2,1)}, u32[]{:S(2)}, u32[]{:S(2)}) collective-permute-start(bf16[2,96,640]{2,1,0:T(8,128)(2,1)S(1)} %bitcast.11), channel_id=1, source_target_pairs={{4,8},{8,4},{5,9},{9,5},{6,10},{10,6},{7,11},{11,7},{20,24},{24,20... | collective-permute-start | bytes 737288 | tf_op jit(solution)/shard_map/ppermute | solution.py:232
  43.2 1.5 %copy-start.1 = (bf16[4,15,64,192]{3,2,1,0:T(8,128)(2,1)S(1)}, bf16[4,15,64,192]{3,2,1,0:T(8,128)(2,1)}, u32[]{:S(2)}) copy-start(bf16[4,15,64,192]{3,2,1,0:T(8,128)(2,1)} %copy-done) | copy-start | bytes 4423684
  44.8 0.9 %copy-start.6 = (bf16[2,96,640]{2,1,0:T(8,128)(2,1)S(1)}, bf16[2,96,640]{2,1,0:T(8,128)(2,1)}, u32[]{:S(2)}) copy-start(bf16[2,96,640]{2,1,0:T(8,128)(2,1)} %copy-done.5) | copy-start | bytes 737284
  52.1 5.6 %collective-permute-start.10 = (bf16[4,24,640]{2,1,0:T(8,128)(2,1)S(1)}, bf16[4,24,640]{2,1,0:T(8,128)(2,1)S(1)}, u32[]{:S(2)}, u32[]{:S(2)}) collective-permute-start(bf16[4,24,640]{2,1,0:T(8,128)(2,1)S(1)} %get-tuple-element.38), channel_id=1, source_target_pairs={{0,2},{1,3},{2,0},{3,1},{16,18},{17,19},{18,16},{19,17},{4,6},{5,7... | collective-permute-start | bytes 368648 | tf_op jit(solution)/shard_map/ppermute | solution.py:282
  53.9 5.6 %collective-permute-start.11 = (bf16[4,24,640]{2,1,0:T(8,128)(2,1)S(1)}, bf16[4,24,640]{2,1,0:T(8,128)(2,1)S(1)}, u32[]{:S(2)}, u32[]{:S(2)}) collective-permute-start(bf16[4,24,640]{2,1,0:T(8,128)(2,1)S(1)} %get-tuple-element.39), channel_id=1, source_target_pairs={{0,17},{1,16},{2,19},{3,18},{16,1},{17,0},{18,3},{19,2},{4,21},{5,... | collective-permute-start | bytes 368648 | tf_op jit(solution)/shard_map/ppermute | solution.py:282
  53.9 9.9 %collective-permute-start.12 = (bf16[4,24,640]{2,1,0:T(8,128)(2,1)S(1)}, bf16[4,24,640]{2,1,0:T(8,128)(2,1)S(1)}, u32[]{:S(2)}, u32[]{:S(2)}) collective-permute-start(bf16[4,24,640]{2,1,0:T(8,128)(2,1)S(1)} %get-tuple-element.40), channel_id=1, source_target_pairs={{0,18},{1,19},{2,16},{3,17},{16,2},{17,3},{18,0},{19,1},{4,22},{5,... | collective-permute-start | bytes 368648 | tf_op jit(solution)/shard_map/ppermute | solution.py:282
  55.6 8.1 %collective-permute-start.13 = (bf16[4,24,640]{2,1,0:T(8,128)(2,1)S(1)}, bf16[4,24,640]{2,1,0:T(8,128)(2,1)S(1)}, u32[]{:S(2)}, u32[]{:S(2)}) collective-permute-start(bf16[4,24,640]{2,1,0:T(8,128)(2,1)S(1)} %get-tuple-element.41), channel_id=1, source_target_pairs={{0,3},{1,2},{2,1},{3,0},{16,19},{17,18},{18,17},{19,16},{4,7},{5,6... | collective-permute-start | bytes 368648 | tf_op jit(solution)/shard_map/ppermute | solution.py:282
  57.1 6.8 %collective-permute-start.14 = (bf16[4,24,640]{2,1,0:T(8,128)(2,1)S(1)}, bf16[4,24,640]{2,1,0:T(8,128)(2,1)S(1)}, u32[]{:S(2)}, u32[]{:S(2)}) collective-permute-start(bf16[4,24,640]{2,1,0:T(8,128)(2,1)S(1)} %get-tuple-element.42), channel_id=1, source_target_pairs={{0,19},{1,18},{2,17},{3,16},{16,3},{17,2},{18,1},{19,0},{4,23},{5,... | collective-permute-start | bytes 368648 | tf_op jit(solution)/shard_map/ppermute | solution.py:282
  57.7 6.1 %collective-permute-start.8 = (bf16[4,24,640]{2,1,0:T(8,128)(2,1)S(1)}, bf16[4,24,640]{2,1,0:T(8,128)(2,1)S(1)}, u32[]{:S(2)}, u32[]{:S(2)}) collective-permute-start(bf16[4,24,640]{2,1,0:T(8,128)(2,1)S(1)} %get-tuple-element.36), channel_id=1, source_target_pairs={{0,16},{1,17},{2,18},{3,19},{16,0},{17,1},{18,2},{19,3},{4,20},{5,... | collective-permute-start | bytes 368648 | tf_op jit(solution)/shard_map/ppermute | solution.py:282
  59.4 8.0 %collective-permute-start.9 = (bf16[4,24,640]{2,1,0:T(8,128)(2,1)S(1)}, bf16[4,24,640]{2,1,0:T(8,128)(2,1)S(1)}, u32[]{:S(2)}, u32[]{:S(2)}) collective-permute-start(bf16[4,24,640]{2,1,0:T(8,128)(2,1)S(1)} %get-tuple-element.37), channel_id=1, source_target_pairs={{0,1},{1,0},{2,3},{3,2},{16,17},{17,16},{18,19},{19,18},{4,5},{5,4... | collective-permute-start | bytes 368648 | tf_op jit(solution)/shard_map/ppermute | solution.py:282

commit v17 on v15

--- a/solution.py
+++ b/solution.py
@@ -75,8 +75,10 @@
     cells = span // groups
     member, owner, group = place_ref[0], place_ref[1], place_ref[2]
 
-    total[...] = jnp.zeros_like(total)
-    field_rows[...] = jnp.zeros_like(field_rows)
+    read = pl.ds(HALO - halo, late * rows + 2 * halo)
+    total[:, read] = jnp.zeros((bases, late * rows + 2 * halo) + total.shape[2:], total.dtype)
+    upper = pl.ds(padded - LANES, LANES)
+    field_rows[:, :, upper] = jnp.zeros(field_rows.shape[:2] + (LANES,), field_rows.dtype)
     for s in range(late):
         lat = partner_in_kernel(member, s, late)
         for d, ref in enumerate(field_refs):
@@ -119,8 +121,7 @@
         product = jnp.dot(jnp.concatenate(lhs, axis=-1), matrix, preferred_element_type=jnp.float32)
         return product.reshape(count, span, width)
 
-    for lat in range(late):
-        mixed[lat * rows : (lat + 1) * rows] = one_out(lat * rows, rows)
+    mixed[...] = one_out(0, late * rows)
     for dl in range(late):
         lat = partner_in_kernel(member, dl, late)
         for dq in range(groups):
@@ -228,11 +229,6 @@
     return fields[::-1], mixes, [own, own ^ 1, own ^ (3 - core), own ^ (2 + core)], kernels
 
 
-def send_rank(dl, dq):
-    first = [(0, 0), (1, 0), (0, 1), (0, 2), (1, 1), (1, 2), (0, 3), (1, 3)]
-    return first.index((dl, dq)) if (dl, dq) in first else len(first) + dl + dq
-
-
 def per_device(sizes, fields, kernel, band_low, block_shift, mix_weight):
     halves, late, owners, groups = sizes
     members, rows, channels, cells = fields.shape
@@ -265,7 +261,7 @@
             for dq in range(groups):
                 group = partner(lax.axis_index("lonq"), dq, groups)
                 partial[dl * groups + dq] += extra[lat, :, group]
-    order = sorted(((dl, dq) for dl in range(late) for dq in range(groups)), key=lambda at: send_rank(*at))
+    order = [(dl, dq) for dl in range(late) for dq in range(groups)]
     parts = []
     for dl, dq in order:
         route = [

time: 65.6 us -> 65.7 us (level)
  no operation moved by 1% of the time
where the time goes in v17:
time: 65.7 us; the launch traced here: 65.4 us
  waiting for transfers between devices  21 us (32%)
  starting transfers between devices  16.6 us (25%)
  Pallas kernels  13.3 us (20%)
  blocking collectives  10.1 us (15%)
  local copies, waits for them, and re-layouts  4.33 us (7%)
    ppermute x6, waiting for transfers between devices, trade(): lax.ppermute(x, axis, [(i, partner(i, distance, size)) for i in range(siz...  13.7 us
    all_to_all x1, blocking collectives, per_device(): lax.all_to_all(packed, ('late', 'lonq'), split_axis=0, concat_axis=0, til...  10.1 us
    ppermute x7, waiting for transfers between devices, per_device(): lax.ppermute(block, ('late', 'lonq'), route)  7.32 us
    ppermute x7, starting transfers between devices, per_device(): lax.ppermute(block, ('late', 'lonq'), route)  7.15 us
    pallas_call x1, Pallas kernels, conv_mix(): pl.pallas_call(functools.partial(conv_mix_kernel, (bases, taps, slots, ha...  6.64 us
    pallas_call x2, Pallas kernels, turn(): pl.pallas_call(turn_kernel, out_shape=jax.ShapeDtypeStruct((rows, bases *...  4.86 us
    ppermute x6, starting transfers between devices, trade(): lax.ppermute(x, axis, [(i, partner(i, distance, size)) for i in range(siz...  4.85 us
    ppermute x1, starting transfers between devices, gather(): far = lax.ppermute(mix, ('late', 'lonp'), route)  4.6 us
  transfers between devices with their start and end apart: 14, of which 6 were waited for; matrix products, arithmetic and copies ran while one was open for 1% of the time, Pallas kernels for 8%

profile of v17, /device:TPU:0, one launch (start us, length us, event | category | flops | bytes accessed | tf_op | source)
XLA Modules:
  0.0 65.4 jit_solution(2156878942568923849)
XLA Ops:
  0.0 0.5 collective-permute-start.2
  0.5 4.6 %collective-permute-start = (bf16[5,40,640]{2,1,0:T(8,128)(2,1)}, bf16[5,40,640]{2,1,0:T(8,128)(2,1)S(1)}, u32[]{:S(2)}, u32[]{:S(2)}) collective-permute-start(bf16[5,40,640]{2,1,0:T(8,128)(2,1)} %refs_6_.1), channel_id=1, source_target_pairs={{0,12},{4,8},{8,4},{12,0},{16,24},{20,28},{24,16},{28,20},{1,13},{... | collective-permute-start | bytes 768008 | tf_op jit(solution)/shard_map/ppermute | solution.py:224
  5.1 0.0 collective-permute-start.1
  5.1 0.0 copy-start.4
  5.1 0.9 %copy-done.4 = bf16[2,4,640,24]{2,3,1,0:T(8,128)(2,1)S(1)} copy-done((bf16[2,4,640,24]{2,3,1,0:T(8,128)(2,1)S(1)}, bf16[2,4,640,24]{2,3,1,0:T(8,128)(2,1)}, u32[]{:S(2)}) %copy-start.4) | copy-done | bytes 245784
  6.0 0.4 pack.1
  6.4 10.1 %all_to_all.5 = bf16[8,24,640]{2,1,0:T(8,128)(2,1)S(1)} all-to-all(bf16[8,24,640]{2,1,0:T(8,128)(2,1)S(1)} %bitcast.13), channel_id=1, replica_groups=mesh['lath'=1,'late'=2,'lonp'=4,'lonq'=4] {'late','lonq'}, dimensions={0} | all-to-all | bytes 491520 | tf_op jit(solution)/shard_map/all_to_all | solution.py:242
  16.5 0.0 collective-permute-done.refs_8_
  16.5 0.6 collective-permute-done.1.refs_7_
  17.1 0.0 copy-start.2
  17.1 0.7 %copy-done.2 = bf16[5,40,640]{2,1,0:T(8,128)(2,1)} copy-done((bf16[5,40,640]{2,1,0:T(8,128)(2,1)}, bf16[5,40,640]{2,1,0:T(8,128)(2,1)S(1)}, u32[]{:S(2)}) %copy-start.2) | copy-done | bytes 256024
  17.8 0.0 collective-permute-done.2.x_ref
  17.8 0.0 collective-permute-start.6
  17.8 2.4 %collective-permute-start.3 = (bf16[2,96,640]{2,1,0:T(8,128)(2,1)S(1)}, bf16[2,96,640]{2,1,0:T(8,128)(2,1)}, u32[]{:S(2)}, u32[]{:S(2)}) collective-permute-start(bf16[2,96,640]{2,1,0:T(8,128)(2,1)S(1)} %bitcast.9), channel_id=1, source_target_pairs={{0,12},{4,8},{8,4},{12,0},{1,13},{5,9},{9,5},{13,1},{2,14},{6,10},... | collective-permute-start | bytes 737288 | tf_op jit(solution)/shard_map/ppermute | solution.py:33
  20.2 0.5 collective-permute-start.4
  20.7 1.5 %collective-permute-start.5 = (bf16[2,96,640]{2,1,0:T(8,128)(2,1)S(1)}, bf16[2,96,640]{2,1,0:T(8,128)(2,1)}, u32[]{:S(2)}, u32[]{:S(2)}) collective-permute-start(bf16[2,96,640]{2,1,0:T(8,128)(2,1)S(1)} %bitcast.11), channel_id=1, source_target_pairs={{0,4},{4,0},{8,12},{12,8},{1,5},{5,1},{9,13},{13,9},{2,6},{6,2},{1... | collective-permute-start | bytes 737288 | tf_op jit(solution)/shard_map/ppermute | solution.py:33
  22.2 0.8 %copy.6.shift_ref = s32[8,3]{1,0:T(8,128)S(1)} copy(s32[8,3]{0,1:T(4,128)} %param.8) | data formatting | bytes 192 | tf_op args[3]
  22.9 0.1 stack.28.place_ref
  23.0 0.0 copy-start
  23.0 1.8 %copy-done = bf16[5,4,3,3,64,64]{5,4,3,2,1,0:T(8,128)(2,1)S(1)} copy-done((bf16[5,4,3,3,64,64]{5,4,3,2,1,0:T(8,128)(2,1)S(1)}, bf16[5,4,3,3,64,64]{5,4,3,2,1,0:T(8,128)(2,1)}, u32[]{:S(2)}) %copy-start) | copy-done | bytes 1474584
  24.9 2.4 %turn.2.refs_4_ = bf16[4,15,64,192]{3,2,1,0:T(8,128)(2,1)S(1)} custom-call(bf16[5,4,3,3,64,64]{5,4,3,2,1,0:T(8,128)(2,1)S(1)} %copy-done), custom_call_target="tpu_custom_call" | custom-call | tf_op jit(solution)/shard_map/turn/pallas_call | solution.py:208
  27.3 0.0 copy-start.1
  27.3 0.0 copy-start.3
  27.3 0.0 copy-start.5
  27.3 2.4 %turn.3.refs_5_ = bf16[4,15,64,192]{3,2,1,0:T(8,128)(2,1)S(1)} custom-call(bf16[5,4,3,3,64,64]{5,4,3,2,1,0:T(8,128)(2,1)S(1)} %collective-permute-done.2.x_ref), custom_call_target="tpu_custom_call" | custom-call | tf_op jit(solution)/shard_map/turn/pallas_call | solution.py:208
  29.8 0.0 collective-permute-done.3.refs_0_
  29.8 13.0 %collective-permute-done.4.refs_1_ = bf16[2,96,640]{2,1,0:T(8,128)(2,1)} collective-permute-done((bf16[2,96,640]{2,1,0:T(8,128)(2,1)S(1)}, bf16[2,96,640]{2,1,0:T(8,128)(2,1)}, u32[]{:S(2)}, u32[]{:S(2)}) %collective-permute-start.4) | collective-permute-done | bytes 245792 | tf_op jit(solution)/shard_map/ppermute | solution.py:33
  42.8 0.0 collective-permute-done.5.refs_2_
  42.8 0.0 collective-permute-done.6.refs_9_
  42.8 0.0 copy-done.1
  42.8 0.0 copy-done.3
  42.8 0.0 copy-done.5
  42.8 6.6 %conv_mix.1 = (bf16[4,24,640]{2,1,0:T(8,128)(2,1)S(1)}, bf16[4,24,640]{2,1,0:T(8,128)(2,1)S(1)}, bf16[4,24,640]{2,1,0:T(8,128)(2,1)S(1)}, bf16[4,24,640]{2,1,0:T...) custom-call(s32[5,8]{1,0:T(8,128)S(1)} %copy-done.5, ...), custom_call_target="tpu_custom_call" | custom-call | tf_op jit(solution)/shard_map/conv_mix/pallas_call | solution.py:151
  49.5 1.6 %collective-permute-start.7 = (bf16[4,24,640]{2,1,0:T(8,128)(2,1)S(1)}, bf16[4,24,640]{2,1,0:T(8,128)(2,1)S(1)}, u32[]{:S(2)}, u32[]{:S(2)}) collective-permute-start(bf16[4,24,640]{2,1,0:T(8,128)(2,1)S(1)} %get-tuple-element.24), channel_id=1, source_target_pairs={{0,1},{1,0},{2,3},{3,2},{16,17},{17,16},{18,19},{19,18},{4,5},{5,4... | collective-permute-start | bytes 368648 | tf_op jit(solution)/shard_map/ppermute | solution.py:273
  51.0 1.5 %collective-permute-start.8 = (bf16[4,24,640]{2,1,0:T(8,128)(2,1)S(1)}, bf16[4,24,640]{2,1,0:T(8,128)(2,1)S(1)}, u32[]{:S(2)}, u32[]{:S(2)}) collective-permute-start(bf16[4,24,640]{2,1,0:T(8,128)(2,1)S(1)} %get-tuple-element.25), channel_id=1, source_target_pairs={{0,2},{1,3},{2,0},{3,1},{16,18},{17,19},{18,16},{19,17},{4,6},{5,7... | collective-permute-start | bytes 368648 | tf_op jit(solution)/shard_map/ppermute | solution.py:273
  52.5 0.5 collective-permute-start.9
  53.0 0.0 collective-permute-start.10
  53.0 1.6 %collective-permute-start.11 = (bf16[4,24,640]{2,1,0:T(8,128)(2,1)S(1)}, bf16[4,24,640]{2,1,0:T(8,128)(2,1)S(1)}, u32[]{:S(2)}, u32[]{:S(2)}) collective-permute-start(bf16[4,24,640]{2,1,0:T(8,128)(2,1)S(1)} %get-tuple-element.28), channel_id=1, source_target_pairs={{0,17},{1,16},{2,19},{3,18},{16,1},{17,0},{18,3},{19,2},{4,21},{5,... | collective-permute-start | bytes 368648 | tf_op jit(solution)/shard_map/ppermute | solution.py:273
  54.6 0.1 collective-permute-done.7.refs_1_
  54.8 1.0 %collective-permute-start.12 = (bf16[4,24,640]{2,1,0:T(8,128)(2,1)S(1)}, bf16[4,24,640]{2,1,0:T(8,128)(2,1)S(1)}, u32[]{:S(2)}, u32[]{:S(2)}) collective-permute-start(bf16[4,24,640]{2,1,0:T(8,128)(2,1)S(1)} %get-tuple-element.29), channel_id=1, source_target_pairs={{0,18},{1,19},{2,16},{3,17},{16,2},{17,3},{18,0},{19,1},{4,22},{5,... | collective-permute-start | bytes 368648 | tf_op jit(solution)/shard_map/ppermute | solution.py:273
  55.8 1.7 %collective-permute-done.8.refs_2_ = bf16[4,24,640]{2,1,0:T(8,128)(2,1)S(1)} collective-permute-done((bf16[4,24,640]{2,1,0:T(8,128)(2,1)S(1)}, bf16[4,24,640]{2,1,0:T(8,128)(2,1)S(1)}, u32[]{:S(2)}, u32[]{:S(2)}) %collective-permute-start.8) | collective-permute-done | bytes 122912 | tf_op jit(solution)/shard_map/ppermute | solution.py:273
  57.4 1.0 %collective-permute-start.13 = (bf16[4,24,640]{2,1,0:T(8,128)(2,1)S(1)}, bf16[4,24,640]{2,1,0:T(8,128)(2,1)S(1)}, u32[]{:S(2)}, u32[]{:S(2)}) collective-permute-start(bf16[4,24,640]{2,1,0:T(8,128)(2,1)S(1)} %get-tuple-element.30), channel_id=1, source_target_pairs={{0,19},{1,18},{2,17},{3,16},{16,3},{17,2},{18,1},{19,0},{4,23},{5,... | collective-permute-start | bytes 368648 | tf_op jit(solution)/shard_map/ppermute | solution.py:273
  58.4 1.2 %collective-permute-done.9.refs_3_ = bf16[4,24,640]{2,1,0:T(8,128)(2,1)S(1)} collective-permute-done((bf16[4,24,640]{2,1,0:T(8,128)(2,1)S(1)}, bf16[4,24,640]{2,1,0:T(8,128)(2,1)S(1)}, u32[]{:S(2)}, u32[]{:S(2)}) %collective-permute-start.9) | collective-permute-done | bytes 122912 | tf_op jit(solution)/shard_map/ppermute | solution.py:273
  59.6 0.0 collective-permute-done.10.refs_4_
  59.6 0.0 collective-permute-done.11.refs_5_
  59.6 4.3 %collective-permute-done.12.refs_6_ = bf16[4,24,640]{2,1,0:T(8,128)(2,1)S(1)} collective-permute-done((bf16[4,24,640]{2,1,0:T(8,128)(2,1)S(1)}, bf16[4,24,640]{2,1,0:T(8,128)(2,1)S(1)}, u32[]{:S(2)}, u32[]{:S(2)}) %collective-permute-start.12) | collective-permute-done | bytes 122912 | tf_op jit(solution)/shard_map/ppermute | solution.py:273
  63.9 0.0 collective-permute-done.13.refs_7_
  63.9 1.4 %finish.1 = bf16[2,4,24,640]{3,2,1,0:T(8,128)(2,1)} custom-call(s32[7]{0:T(128)S(1)} %stack.28.place_ref, bf16[4,24,640]{2,1,0:T(8,128)(2,1)S(1)} %get-tuple-element.23.refs_0_, bf16[4,24,640]{2,1,0:T(8,128)(2,1)S(1)} %collective-permute-done.7.refs_1_, bf16[4,24,640]{2,1,0:T(8,128)(2,1)S(1)} %collective-permute-done.8.refs_2_, ...), custom_call_target="tpu_custom_call" | custom-call | tf_op jit(solution)/shard_map/finish/pallas_call | solution.py:180
Async XLA Ops:
  0.0 17.8 %collective-permute-start.2 = (bf16[5,4,3,3,64,64]{5,4,3,2,1,0:T(8,128)(2,1)}, bf16[5,4,3,3,64,64]{5,4,3,2,1,0:T(8,128)(2,1)S(1)}, u32[]{:S(2)}, u32[]{:S(2)}) collective-permute-start(bf16[5,4,3,3,64,64]{5,4,3,2,1,0:T(8,128)(2,1)} %x_ref), channel_id=1, source_target_pairs={{0,16},{16,0},{1,17},{17,1},{2,18},{18,2},{3,19},{19,3},{4,20},{20... | collective-permute-start | bytes 4423688 | tf_op jit(solution)/shard_map/ppermute | solution.py:33
  0.5 16.0 %collective-permute-start = (bf16[5,40,640]{2,1,0:T(8,128)(2,1)}, bf16[5,40,640]{2,1,0:T(8,128)(2,1)S(1)}, u32[]{:S(2)}, u32[]{:S(2)}) collective-permute-start(bf16[5,40,640]{2,1,0:T(8,128)(2,1)} %refs_6_.1), channel_id=1, source_target_pairs={{0,12},{4,8},{8,4},{12,0},{16,24},{20,28},{24,16},{28,20},{1,13},{... | collective-permute-start | bytes 768008 | tf_op jit(solution)/shard_map/ppermute | solution.py:224
  5.1 12.0 %collective-permute-start.1 = (bf16[5,40,640]{2,1,0:T(8,128)(2,1)}, bf16[5,40,640]{2,1,0:T(8,128)(2,1)S(1)}, u32[]{:S(2)}, u32[]{:S(2)}) collective-permute-start(bf16[5,40,640]{2,1,0:T(8,128)(2,1)} %refs_6_.1), channel_id=1, source_target_pairs={{0,4},{4,0},{8,12},{12,8},{1,5},{5,1},{9,13},{13,9},{2,6},{6,2},{1... | collective-permute-start | bytes 768008 | tf_op jit(solution)/shard_map/ppermute | solution.py:33
  5.1 0.9 %copy-start.4 = (bf16[2,4,640,24]{2,3,1,0:T(8,128)(2,1)S(1)}, bf16[2,4,640,24]{2,3,1,0:T(8,128)(2,1)}, u32[]{:S(2)}) copy-start(bf16[2,4,640,24]{2,3,1,0:T(8,128)(2,1)} %param.5) | copy-start | bytes 737284
  17.1 0.7 %copy-start.2 = (bf16[5,40,640]{2,1,0:T(8,128)(2,1)}, bf16[5,40,640]{2,1,0:T(8,128)(2,1)S(1)}, u32[]{:S(2)}) copy-start(bf16[5,40,640]{2,1,0:T(8,128)(2,1)S(1)} %collective-permute-done.1.refs_7_) | copy-start | bytes 768004
  17.8 25.0 %collective-permute-start.6 = (bf16[5,40,640]{2,1,0:T(8,128)(2,1)S(1)}, bf16[5,40,640]{2,1,0:T(8,128)(2,1)}, u32[]{:S(2)}, u32[]{:S(2)}) collective-permute-start(bf16[5,40,640]{2,1,0:T(8,128)(2,1)S(1)} %collective-permute-done.refs_8_), channel_id=1, source_target_pairs={{0,16},{16,0},{1,17},{17,1},{2,18},{18,2},{3,19},{19,3},{4,20},{20... | collective-permute-start | bytes 768008 | tf_op jit(solution)/shard_map/ppermute | solution.py:33
  17.8 12.0 %collective-permute-start.3 = (bf16[2,96,640]{2,1,0:T(8,128)(2,1)S(1)}, bf16[2,96,640]{2,1,0:T(8,128)(2,1)}, u32[]{:S(2)}, u32[]{:S(2)}) collective-permute-start(bf16[2,96,640]{2,1,0:T(8,128)(2,1)S(1)} %bitcast.9), channel_id=1, source_target_pairs={{0,12},{4,8},{8,4},{12,0},{1,13},{5,9},{9,5},{13,1},{2,14},{6,10},... | collective-permute-start | bytes 737288 | tf_op jit(solution)/shard_map/ppermute | solution.py:33
  20.2 22.6 %collective-permute-start.4 = (bf16[2,96,640]{2,1,0:T(8,128)(2,1)S(1)}, bf16[2,96,640]{2,1,0:T(8,128)(2,1)}, u32[]{:S(2)}, u32[]{:S(2)}) collective-permute-start(bf16[2,96,640]{2,1,0:T(8,128)(2,1)S(1)} %bitcast.10), channel_id=1, source_target_pairs={{0,8},{4,12},{8,0},{12,4},{1,9},{5,13},{9,1},{13,5},{2,10},{6,14},... | collective-permute-start | bytes 737288 | tf_op jit(solution)/shard_map/ppermute | solution.py:33
  20.7 22.1 %collective-permute-start.5 = (bf16[2,96,640]{2,1,0:T(8,128)(2,1)S(1)}, bf16[2,96,640]{2,1,0:T(8,128)(2,1)}, u32[]{:S(2)}, u32[]{:S(2)}) collective-permute-start(bf16[2,96,640]{2,1,0:T(8,128)(2,1)S(1)} %bitcast.11), channel_id=1, source_target_pairs={{0,4},{4,0},{8,12},{12,8},{1,5},{5,1},{9,13},{13,9},{2,6},{6,2},{1... | collective-permute-start | bytes 737288 | tf_op jit(solution)/shard_map/ppermute | solution.py:33
  23.0 1.8 %copy-start = (bf16[5,4,3,3,64,64]{5,4,3,2,1,0:T(8,128)(2,1)S(1)}, bf16[5,4,3,3,64,64]{5,4,3,2,1,0:T(8,128)(2,1)}, u32[]{:S(2)}) copy-start(bf16[5,4,3,3,64,64]{5,4,3,2,1,0:T(8,128)(2,1)} %x_ref) | copy-start | bytes 4423684
  27.3 15.5 %copy-start.1 = (bf16[5,40,640]{2,1,0:T(8,128)(2,1)S(1)}, bf16[5,40,640]{2,1,0:T(8,128)(2,1)}, u32[]{:S(2)}) copy-start(bf16[5,40,640]{2,1,0:T(8,128)(2,1)} %refs_6_.1) | copy-start | bytes 768004
  27.3 15.5 %copy-start.3 = (bf16[5,40,640]{2,1,0:T(8,128)(2,1)S(1)}, bf16[5,40,640]{2,1,0:T(8,128)(2,1)}, u32[]{:S(2)}) copy-start(bf16[5,40,640]{2,1,0:T(8,128)(2,1)} %copy-done.2) | copy-start | bytes 768004
  27.3 15.5 %copy-start.5 = (s32[5,8]{1,0:T(8,128)S(1)}, s32[5,8]{1,0:T(8,128)}, u32[]{:S(2)}) copy-start(s32[5,8]{1,0:T(8,128)} %low_ref) | copy-start | bytes 484
  49.5 5.3 %collective-permute-start.7 = (bf16[4,24,640]{2,1,0:T(8,128)(2,1)S(1)}, bf16[4,24,640]{2,1,0:T(8,128)(2,1)S(1)}, u32[]{:S(2)}, u32[]{:S(2)}) collective-permute-start(bf16[4,24,640]{2,1,0:T(8,128)(2,1)S(1)} %get-tuple-element.24), channel_id=1, source_target_pairs={{0,1},{1,0},{2,3},{3,2},{16,17},{17,16},{18,19},{19,18},{4,5},{5,4... | collective-permute-start | bytes 368648 | tf_op jit(solution)/shard_map/ppermute | solution.py:273
  51.0 6.4 %collective-permute-start.8 = (bf16[4,24,640]{2,1,0:T(8,128)(2,1)S(1)}, bf16[4,24,640]{2,1,0:T(8,128)(2,1)S(1)}, u32[]{:S(2)}, u32[]{:S(2)}) collective-permute-start(bf16[4,24,640]{2,1,0:T(8,128)(2,1)S(1)} %get-tuple-element.25), channel_id=1, source_target_pairs={{0,2},{1,3},{2,0},{3,1},{16,18},{17,19},{18,16},{19,17},{4,6},{5,7... | collective-permute-start | bytes 368648 | tf_op jit(solution)/shard_map/ppermute | solution.py:273
  52.5 7.1 %collective-permute-start.9 = (bf16[4,24,640]{2,1,0:T(8,128)(2,1)S(1)}, bf16[4,24,640]{2,1,0:T(8,128)(2,1)S(1)}, u32[]{:S(2)}, u32[]{:S(2)}) collective-permute-start(bf16[4,24,640]{2,1,0:T(8,128)(2,1)S(1)} %get-tuple-element.26), channel_id=1, source_target_pairs={{0,3},{1,2},{2,1},{3,0},{16,19},{17,18},{18,17},{19,16},{4,7},{5,6... | collective-permute-start | bytes 368648 | tf_op jit(solution)/shard_map/ppermute | solution.py:273
  53.0 6.6 %collective-permute-start.10 = (bf16[4,24,640]{2,1,0:T(8,128)(2,1)S(1)}, bf16[4,24,640]{2,1,0:T(8,128)(2,1)S(1)}, u32[]{:S(2)}, u32[]{:S(2)}) collective-permute-start(bf16[4,24,640]{2,1,0:T(8,128)(2,1)S(1)} %get-tuple-element.27), channel_id=1, source_target_pairs={{0,16},{1,17},{2,18},{3,19},{16,0},{17,1},{18,2},{19,3},{4,20},{5,... | collective-permute-start | bytes 368648 | tf_op jit(solution)/shard_map/ppermute | solution.py:273
  53.0 6.6 %collective-permute-start.11 = (bf16[4,24,640]{2,1,0:T(8,128)(2,1)S(1)}, bf16[4,24,640]{2,1,0:T(8,128)(2,1)S(1)}, u32[]{:S(2)}, u32[]{:S(2)}) collective-permute-start(bf16[4,24,640]{2,1,0:T(8,128)(2,1)S(1)} %get-tuple-element.28), channel_id=1, source_target_pairs={{0,17},{1,16},{2,19},{3,18},{16,1},{17,0},{18,3},{19,2},{4,21},{5,... | collective-permute-start | bytes 368648 | tf_op jit(solution)/shard_map/ppermute | solution.py:273
  54.8 9.2 %collective-permute-start.12 = (bf16[4,24,640]{2,1,0:T(8,128)(2,1)S(1)}, bf16[4,24,640]{2,1,0:T(8,128)(2,1)S(1)}, u32[]{:S(2)}, u32[]{:S(2)}) collective-permute-start(bf16[4,24,640]{2,1,0:T(8,128)(2,1)S(1)} %get-tuple-element.29), channel_id=1, source_target_pairs={{0,18},{1,19},{2,16},{3,17},{16,2},{17,3},{18,0},{19,1},{4,22},{5,... | collective-permute-start | bytes 368648 | tf_op jit(solution)/shard_map/ppermute | solution.py:273
  57.4 6.5 %collective-permute-start.13 = (bf16[4,24,640]{2,1,0:T(8,128)(2,1)S(1)}, bf16[4,24,640]{2,1,0:T(8,128)(2,1)S(1)}, u32[]{:S(2)}, u32[]{:S(2)}) collective-permute-start(bf16[4,24,640]{2,1,0:T(8,128)(2,1)S(1)} %get-tuple-element.30), channel_id=1, source_target_pairs={{0,19},{1,18},{2,17},{3,16},{16,3},{17,2},{18,1},{19,0},{4,23},{5,... | collective-permute-start | bytes 368648 | tf_op jit(solution)/shard_map/ppermute | solution.py:273

commit v18 on v17

--- a/solution.py
+++ b/solution.py
@@ -43,14 +43,16 @@
                 for i in range(rows)
                 for p in range(owners)
             ]
-            out_ref[e, q] = jnp.concatenate(parts, axis=-1)
+            block = jnp.concatenate(parts, axis=-1)
+            for p in range(owners):
+                out_ref[e, p, q] = block
 
 
 def pack(x, groups, owners):
     members, rows, cells, channels = x.shape
     return pl.pallas_call(
         functools.partial(pack_kernel, groups, owners),
-        out_shape=jax.ShapeDtypeStruct((members, groups, cells, rows * channels // groups), x.dtype),
+        out_shape=jax.ShapeDtypeStruct((members, owners, groups, cells, rows * channels // groups), x.dtype),
         in_specs=[VMEM_SPEC],
         out_specs=VMEM_SPEC,
         compiler_params=pltpu.CompilerParams(vmem_limit_bytes=LIMIT),
@@ -58,21 +60,18 @@
     )(x)
 
 
-def conv_mix_kernel(geometry, counts, low_ref, shift_ref, place_ref, *refs):
+def conv_mix_kernel(geometry, counts, low_ref, shift_ref, place_ref, fields_ref, *refs):
     bases, taps, slots, halo, sub, groups = geometry
     refs = list(refs)
-    field_refs, weight_refs, mix_refs = [[refs.pop(0) for _ in range(n)] for n in counts]
-    field_refs = field_refs[::-1]
+    weight_refs, mix_refs = [[refs.pop(0) for _ in range(n)] for n in counts]
     field_rows, total, mix_all, mixed = refs[-4:]
     outs = refs[:-4]
-    late, span, _ = field_refs[0].shape
-    owners = len(field_refs)
+    late, owners, span, _ = fields_ref.shape
     depth, width = mix_refs[0].shape[1:]
     channels = owners * depth
     padded = total.shape[-1]
     rows, _, block, _ = weight_refs[0].shape
     nblocks = owners * span // block
-    cells = span // groups
     member, owner, group = place_ref[0], place_ref[1], place_ref[2]
 
     read = pl.ds(HALO - halo, late * rows + 2 * halo)
@@ -81,11 +80,10 @@
     field_rows[:, :, upper] = jnp.zeros(field_rows.shape[:2] + (LANES,), field_rows.dtype)
     for s in range(late):
         lat = partner_in_kernel(member, s, late)
-        for d, ref in enumerate(field_refs):
-            at = pl.ds(pl.multiple_of(partner_in_kernel(owner, d, owners) * span, sub), span)
-            value = ref[lat]
+        for p in range(owners):
+            value = fields_ref[lat, p]
             for r in range(rows):
-                field_rows[r, at, :channels] = value[:, r * channels : (r + 1) * channels]
+                field_rows[r, p * span : (p + 1) * span, :channels] = value[:, r * channels : (r + 1) * channels]
 
         def one_row(r, carry):
             row = lat * rows + r
@@ -108,46 +106,80 @@
 
         lax.fori_loop(0, rows, one_row, 0, unroll=2)
 
-    for d, ref in enumerate(mix_refs):
-        mix_all[place_ref[3 + d]] = ref[...]
+    for d in range(owners):
+        value = mix_refs[d][...]
+        if d == owners - 1 and len(mix_refs) > owners:
+            value = value + mix_refs[owners][...]
+        mix_all[place_ref[3 + d]] = value
     fill = jnp.zeros((padded - channels, width), jnp.bfloat16)
     matrix = jnp.concatenate(
         [x for k in range(bases) for x in [mix_all[p, k] for p in range(owners)] + [fill]], axis=0
     )
-
-    def one_out(first, count):
+    own_ref, matrix_ref = outs[:2]
+    matrix_ref[...] = matrix
+
+    def rounded(first, count):
         at = pl.ds(first + HALO, count)
-        lhs = [total[k, at].astype(jnp.bfloat16).reshape(count * span, padded) for k in range(bases)]
-        product = jnp.dot(jnp.concatenate(lhs, axis=-1), matrix, preferred_element_type=jnp.float32)
-        return product.reshape(count, span, width)
-
-    mixed[...] = one_out(0, late * rows)
-    for dl in range(late):
-        lat = partner_in_kernel(member, dl, late)
-        for dq in range(groups):
-            start = pl.multiple_of(partner_in_kernel(group, dq, groups) * cells, 8 if cells % 8 == 0 else cells)
-            for r in range(rows):
-                outs[dl * groups + dq][r] = mixed[lat * rows + r, pl.ds(start, cells)].astype(jnp.bfloat16)
+        return jnp.concatenate([total[k, at].astype(jnp.bfloat16) for k in range(bases)], axis=-1)
+
+    own_ref[...] = rounded(member * rows, rows)
+    for dl in range(1, late):
+        first = partner_in_kernel(member, dl, late) * rows
+        mix_into(mixed, outs[2 + (dl - 1) * groups :], rounded(first, rows), matrix, group, groups)
     if halo:
         for side, first in enumerate((-halo, late * rows)):
-            outs[-1][side] = one_out(first, halo).astype(jnp.bfloat16)
+            lhs = rounded(first, halo).reshape(halo * span, -1)
+            product = jnp.dot(lhs, matrix, preferred_element_type=jnp.float32)
+            outs[-1][side] = product.reshape(halo, span, width).astype(jnp.bfloat16)
+
+
+def mix_into(mixed, outs, rounded, matrix, group, groups):
+    rows, span, lanes = rounded.shape
+    cells = span // groups
+    product = jnp.dot(rounded.reshape(rows * span, lanes), matrix, preferred_element_type=jnp.float32)
+    mixed[...] = product.reshape(mixed.shape)
+    for dq in range(groups):
+        start = pl.multiple_of(partner_in_kernel(group, dq, groups) * cells, 8 if cells % 8 == 0 else cells)
+        for r in range(rows):
+            outs[dq][r] = mixed[r, pl.ds(start, cells)].astype(jnp.bfloat16)
+
+
+def mix_own_kernel(groups, place_ref, rounded_ref, matrix_ref, *refs):
+    mix_into(refs[-1], refs[:-1], rounded_ref[...], matrix_ref[...], place_ref[2], groups)
+
+
+def mix_own(place, rounded, matrix, groups):
+    rows, span, _ = rounded.shape
+    width = matrix.shape[-1]
+    return pl.pallas_call(
+        functools.partial(mix_own_kernel, groups),
+        out_shape=[jax.ShapeDtypeStruct((rows, span // groups, width), jnp.bfloat16)] * groups,
+        in_specs=[SMEM_SPEC] + [VMEM_SPEC] * 2,
+        out_specs=[VMEM_SPEC] * groups,
+        scratch_shapes=[VMEM((rows, span, width), jnp.float32)],
+        compiler_params=pltpu.CompilerParams(vmem_limit_bytes=LIMIT),
+        name="mix_own",
+    )(place, rounded, matrix)
 
 
 def conv_mix(low, shift, place, fields, weights, mix, halo, groups, block):
     bases, all_rows = low.shape
     slots = shift.shape[1]
-    late, span, _ = fields[0].shape
-    owners = len(fields)
+    late, owners, span, _ = fields.shape
     rows = all_rows // late
     depth, width = mix[0].shape[1:]
     padded = -(-owners * depth // LANES) * LANES
     taps = weights[0].shape[1] // bases
     sub = math.gcd(span, block)
-    shapes = [jax.ShapeDtypeStruct((rows, span // groups, width), jnp.bfloat16)] * (late * groups)
+    shapes = [
+        jax.ShapeDtypeStruct((rows, span, bases * padded), jnp.bfloat16),
+        jax.ShapeDtypeStruct((bases * padded, width), jnp.bfloat16),
+    ]
+    shapes += [jax.ShapeDtypeStruct((rows, span // groups, width), jnp.bfloat16)] * ((late - 1) * groups)
     if halo:
         shapes.append(jax.ShapeDtypeStruct((2, halo, span, width), jnp.bfloat16))
-    operands = fields[::-1] + weights + mix
-    counts = (len(fields), len(weights), len(mix))
+    operands = [fields] + weights + mix
+    counts = (len(weights), len(mix))
     return pl.pallas_call(
         functools.partial(conv_mix_kernel, (bases, taps, slots, halo, sub, groups), counts),
         out_shape=shapes,
@@ -157,7 +189,7 @@
             VMEM((rows, owners * span, padded), jnp.bfloat16),
             VMEM((bases, all_rows + 2 * HALO, span, padded), jnp.float32),
             VMEM((owners, bases, depth, width), jnp.bfloat16),
-            VMEM((all_rows, span, width), jnp.float32),
+            VMEM((rows, span, width), jnp.float32),
         ],
         compiler_params=pltpu.CompilerParams(vmem_limit_bytes=LIMIT),
         name="conv_mix",
@@ -215,18 +247,18 @@
     )(x)
 
 
-def gather(spread, mix, kernels, late, owners):
+def gather_mix(mix, packed, late, owners):
     core, own = lax.axis_index("late"), lax.axis_index("lonp")
     if owners != 4 or late != 2:
-        fields, mixes = [[x] + [trade(x, "lonp", d, owners) for d in range(1, owners)] for x in (spread, mix)]
-        return fields, mixes, [partner(own, d, owners) for d in range(owners)], kernels
-    route = [(4 * c + p, 4 * c + (p ^ (3 - c))) for c in range(2) for p in range(4)]
-    far = lax.ppermute(mix, ("late", "lonp"), route)
-    near = trade(mix, "lonp", 1, owners)
-    spread, far, near, *kernels = lax.optimization_barrier((spread, far, near, *kernels))
-    fields = [trade(spread, "lonp", d, owners) for d in (3, 2, 1)] + [spread]
-    mixes = [mix, near, far, trade(far, "late", 1, late)]
-    return fields[::-1], mixes, [own, own ^ 1, own ^ (3 - core), own ^ (2 + core)], kernels
+        mixes = [mix] + [trade(mix, "lonp", d, owners) for d in range(1, owners)]
+        return mixes, [partner(own, d, owners) for d in range(owners)], packed
+    route = [(4 * c + p, 4 * c + (p ^ (1 + c))) for c in range(2) for p in range(4)]
+    first = lax.ppermute(mix, ("late", "lonp"), route)
+    packed, first = lax.optimization_barrier((packed, first))
+    third = lax.ppermute(first, ("late", "lonp"), [(4 + p, 4 + (p ^ 1)) for p in range(4)])
+    other = trade(first, "late", 1, late)
+    copied = lax.ppermute(third, "late", [(1, 0)])
+    return [mix, first, other, third, copied], [own, own ^ (1 + core), own ^ (2 - core), own ^ 3], packed
 
 
 def per_device(sizes, fields, kernel, band_low, block_shift, mix_weight):
@@ -238,10 +270,10 @@
 
     kernels = [kernel] + [trade(kernel, "late", s, late) for s in range(1, late)]
     packed = pack(fields.transpose(0, 1, 3, 2), groups, owners)
-    packed = packed.reshape((late * groups,) + packed.shape[2:])
-    spread = lax.all_to_all(packed, ("late", "lonq"), split_axis=0, concat_axis=0, tiled=True)
-    spread = spread.reshape(late, groups * cells, -1)
-    spread, mix, origins, kernels = gather(spread, mix_weight, kernels, late, owners)
+    packed = packed.reshape((-1,) + packed.shape[3:])
+    mix, origins, packed = gather_mix(mix_weight, packed, late, owners)
+    spread = lax.all_to_all(packed, ("late", "lonp", "lonq"), split_axis=0, concat_axis=0, tiled=True)
+    spread = spread.reshape(late, owners, groups * cells, -1)
     weights = [turn(x) for x in kernels]
 
     start = lax.axis_index("lath") * all_rows
@@ -249,7 +281,8 @@
     shift = lax.dynamic_slice_in_dim(block_shift, start, all_rows, 0)
     place = [lax.axis_index("late"), lax.axis_index("lonp"), lax.axis_index("lonq")] + origins
     place = jnp.stack(place).astype(jnp.int32)
-    partial = conv_mix(low, shift, place, spread, weights, mix, halo, groups, block)
+    rounded, matrix, *partial = conv_mix(low, shift, place, spread, weights, mix, halo, groups, block)
+    partial = list(mix_own(place, rounded, matrix, groups)) + partial
     if halo:
         *partial, beyond = partial
         below = lax.ppermute(beyond[1], "lath", [(i, i + 1) for i in range(halves - 1)])
@@ -261,7 +294,7 @@
             for dq in range(groups):
                 group = partner(lax.axis_index("lonq"), dq, groups)
                 partial[dl * groups + dq] += extra[lat, :, group]
-    order = [(dl, dq) for dl in range(late) for dq in range(groups)]
+    order = [(dl, dq) for dl in reversed(range(late)) for dq in range(groups)]
     parts = []
     for dl, dq in order:
         route = [

time: 65.7 us -> 72.4 us (1.10)
  blocking collectives: 10.1 us -> 0 us
  starting transfers between devices: 16.6 us -> 26.4 us
  Pallas kernels: 13.3 us -> 16.8 us
  waiting for transfers between devices: 21 us -> 22.6 us
  local copies, waits for them, and re-layouts: 4.33 us -> 5.8 us
    ppermute x6 -> x2, waiting for transfers between devices: 13.7 us -> 0.01 us  [trade(): lax.ppermute(x, axis, [(i, partner(i, distance, size)) for i in range(siz...]
    ppermute x1 -> x3, waiting for transfers between devices: 0.01 us -> 11.3 us  [the longest x1 6.74 us: gather_mix(): copied = lax.ppermute(third, 'late', [(1, 0)])]
    all_to_all x1 -> x0, blocking collectives: 10.1 us -> none  [per_device(): lax.all_to_all(packed, ('late', 'lonq'), split_axis=0, concat_axis=0, til...]
    all_to_all x0 -> x1, starting transfers between devices: none -> 6.55 us  [per_device(): lax.all_to_all(packed, ('late', 'lonp', 'lonq'), split_axis=0, concat_axi...]
    all_to_all x0 -> x1, waiting for transfers between devices: none -> 4.5 us  [per_device(): lax.all_to_all(packed, ('late', 'lonp', 'lonq'), split_axis=0, concat_axi...]
    ppermute x7, starting transfers between devices: 7.15 us -> 11.5 us  [per_device(): lax.ppermute(block, ('late', 'lonq'), route)]
    ppermute x6 -> x2, starting transfers between devices: 4.85 us -> 2.66 us  [trade(): lax.ppermute(x, axis, [(i, partner(i, distance, size)) for i in range(siz...]
    pallas_call x2, Pallas kernels: 4.86 us -> 6.74 us  [turn(): pl.pallas_call(turn_kernel, out_shape=jax.ShapeDtypeStruct((rows, bases *...]
  transfers between devices with their start and end apart: 14 -> 13, of which waited for: 6 -> 7; matrix products, arithmetic and copies ran while one was open for 1% -> 0% of each run, Pallas kernels for 8% -> 13%
where the time goes in v18:
time: 72.4 us; the launch traced here: 71.6 us
  starting transfers between devices  26.4 us (36%)
  waiting for transfers between devices  22.6 us (31%)
  Pallas kernels  16.8 us (23%)
  local copies, waits for them, and re-layouts  5.8 us (8%)
    ppermute x7, starting transfers between devices, per_device(): lax.ppermute(block, ('late', 'lonq'), route)  11.5 us
    ppermute x7, waiting for transfers between devices, per_device(): lax.ppermute(block, ('late', 'lonq'), route)  6.76 us
    ppermute x1, waiting for transfers between devices, gather_mix(): copied = lax.ppermute(third, 'late', [(1, 0)])  6.74 us
    pallas_call x2, Pallas kernels, turn(): pl.pallas_call(turn_kernel, out_shape=jax.ShapeDtypeStruct((rows, bases *...  6.74 us
    all_to_all x1, starting transfers between devices, per_device(): lax.all_to_all(packed, ('late', 'lonp', 'lonq'), split_axis=0, concat_axi...  6.55 us
    pallas_call x1, Pallas kernels, conv_mix(): pl.pallas_call(functools.partial(conv_mix_kernel, (bases, taps, slots, ha...  5.73 us
    unnamed x15, local copies, waits for them, and re-layouts  5.71 us
    ppermute x1, waiting for transfers between devices, gather_mix(): first = lax.ppermute(mix, ('late', 'lonp'), route)  4.56 us
  transfers between devices with their start and end apart: 13, of which 7 were waited for; matrix products, arithmetic and copies ran while one was open for 0% of the time, Pallas kernels for 13%

profile of v18, /device:TPU:0, one launch (start us, length us, event | category | flops | bytes accessed | tf_op | source)
XLA Modules:
  0.0 71.6 jit_solution(13082782962198211955)
XLA Ops:
  0.0 3.0 %collective-permute-start = (bf16[5,40,640]{2,1,0:T(8,128)(2,1)}, bf16[5,40,640]{2,1,0:T(8,128)(2,1)S(1)}, u32[]{:S(2)}, u32[]{:S(2)}) collective-permute-start(bf16[5,40,640]{2,1,0:T(8,128)(2,1)} %refs_2_.1), channel_id=1, source_target_pairs={{0,4},{4,0},{8,12},{12,8},{16,24},{20,28},{24,16},{28,20},{1,5},{5... | collective-permute-start | bytes 768008 | tf_op jit(solution)/shard_map/ppermute | solution.py:256
  3.0 0.0 copy-start.4
  3.0 0.9 %copy-done.4 = bf16[2,4,640,24]{2,3,1,0:T(8,128)(2,1)S(1)} copy-done((bf16[2,4,640,24]{2,3,1,0:T(8,128)(2,1)S(1)}, bf16[2,4,640,24]{2,3,1,0:T(8,128)(2,1)}, u32[]{:S(2)}) %copy-start.4) | copy-done | bytes 245784
  4.0 1.4 %pack.1 = bf16[2,4,4,24,640]{4,3,2,1,0:T(8,128)(2,1)} custom-call(bf16[2,4,24,640]{3,2,1,0:T(8,128)(2,1)S(1)} %bitcast.10), custom_call_target="tpu_custom_call" | custom-call | tf_op jit(solution)/shard_map/pack/pallas_call | solution.py:53
  5.3 4.6 %collective-permute-done.refs_3_ = bf16[5,40,640]{2,1,0:T(8,128)(2,1)S(1)} collective-permute-done((bf16[5,40,640]{2,1,0:T(8,128)(2,1)}, bf16[5,40,640]{2,1,0:T(8,128)(2,1)S(1)}, u32[]{:S(2)}, u32[]{:S(2)}) %collective-permute-start) | collective-permute-done | bytes 256032 | tf_op jit(solution)/shard_map/ppermute | solution.py:256
  9.9 6.5 %all-to-all-start = ((bf16[32,24,640]{2,1,0:T(8,128)(2,1)}), bf16[32,24,640]{2,1,0:T(8,128)(2,1)S(1)}, u32[]{:S(2)}, u32[]{:S(2)}) async-start(bf16[32,24,640]{2,1,0:T(8,128)(2,1)} %bitcast.7), calls=%async_computation | async-start | bytes 1966080 | tf_op jit(solution)/shard_map/all_to_all | solution.py:275
  16.5 0.3 collective-permute-start.1
  16.8 1.4 %collective-permute-start.3 = (bf16[5,40,640]{2,1,0:T(8,128)(2,1)S(1)}, bf16[5,40,640]{2,1,0:T(8,128)(2,1)}, u32[]{:S(2)}, u32[]{:S(2)}) collective-permute-start(bf16[5,40,640]{2,1,0:T(8,128)(2,1)S(1)} %collective-permute-done.refs_3_), channel_id=1, source_target_pairs={{16,20},{20,16},{24,28},{28,24},{17,21},{21,17},{25,29},{29,25},{1... | collective-permute-start | bytes 768008 | tf_op jit(solution)/shard_map/ppermute | solution.py:258
  18.1 2.3 %collective-permute-start.2 = (bf16[5,40,640]{2,1,0:T(8,128)(2,1)S(1)}, bf16[5,40,640]{2,1,0:T(8,128)(2,1)}, u32[]{:S(2)}, u32[]{:S(2)}) collective-permute-start(bf16[5,40,640]{2,1,0:T(8,128)(2,1)S(1)} %collective-permute-done.refs_3_), channel_id=1, source_target_pairs={{0,16},{16,0},{1,17},{17,1},{2,18},{18,2},{3,19},{19,3},{4,20},{20... | collective-permute-start | bytes 768008 | tf_op jit(solution)/shard_map/ppermute | solution.py:33
  20.5 0.0 collective-permute-done.3.refs_5_
  20.5 1.3 %collective-permute-start.4 = (bf16[5,40,640]{2,1,0:T(8,128)(2,1)}, bf16[5,40,640]{2,1,0:T(8,128)(2,1)}, u32[]{:S(2)}, u32[]{:S(2)}) collective-permute-start(bf16[5,40,640]{2,1,0:T(8,128)(2,1)} %collective-permute-done.3.refs_5_), channel_id=1, source_target_pairs={{16,0},{17,1},{18,2},{19,3},{20,4},{21,5},{22,6},{23,7},{24,8},{25... | collective-permute-start | bytes 768008 | tf_op jit(solution)/shard_map/ppermute | solution.py:260
  21.8 0.0 copy-start.2
  21.8 1.8 %copy-done.2 = bf16[5,4,3,3,64,64]{5,4,3,2,1,0:T(8,128)(2,1)S(1)} copy-done((bf16[5,4,3,3,64,64]{5,4,3,2,1,0:T(8,128)(2,1)S(1)}, bf16[5,4,3,3,64,64]{5,4,3,2,1,0:T(8,128)(2,1)}, u32[]{:S(2)}) %copy-start.2) | copy-done | bytes 1474584
  23.6 0.0 copy-start.6
  23.6 2.4 %turn.2.refs_0_ = bf16[4,15,64,192]{3,2,1,0:T(8,128)(2,1)S(1)} custom-call(bf16[5,4,3,3,64,64]{5,4,3,2,1,0:T(8,128)(2,1)S(1)} %copy-done.2), custom_call_target="tpu_custom_call" | custom-call | tf_op jit(solution)/shard_map/turn/pallas_call | solution.py:240
  26.1 0.0 copy-done.6
  26.1 0.1 copy.6.shift_ref
  26.1 0.1 stack.28.place_ref
  26.2 0.0 copy-start.3
  26.2 0.0 copy-start.5
  26.2 0.0 collective-permute-done.1.x_ref
  26.2 4.3 %turn.3.refs_1_ = bf16[4,15,64,192]{3,2,1,0:T(8,128)(2,1)S(1)} custom-call(bf16[5,4,3,3,64,64]{5,4,3,2,1,0:T(8,128)(2,1)} %collective-permute-done.1.x_ref), custom_call_target="tpu_custom_call" | custom-call | tf_op jit(solution)/shard_map/turn/pallas_call | solution.py:240
  30.6 0.0 copy-start
  30.6 1.3 %copy-done = bf16[4,15,64,192]{3,2,1,0:T(8,128)(2,1)} copy-done((bf16[4,15,64,192]{3,2,1,0:T(8,128)(2,1)}, bf16[4,15,64,192]{3,2,1,0:T(8,128)(2,1)S(1)}, u32[]{:S(2)}) %copy-start) | copy-done | bytes 1474584
  31.9 0.0 collective-permute-done.2.refs_4_
  31.9 6.7 %collective-permute-done.4.refs_6_ = bf16[5,40,640]{2,1,0:T(8,128)(2,1)} collective-permute-done((bf16[5,40,640]{2,1,0:T(8,128)(2,1)}, bf16[5,40,640]{2,1,0:T(8,128)(2,1)}, u32[]{:S(2)}, u32[]{:S(2)}) %collective-permute-start.4) | collective-permute-done | bytes 256032 | tf_op jit(solution)/shard_map/ppermute | solution.py:260
  38.6 4.5 %all-to-all-done = bf16[32,24,640]{2,1,0:T(8,128)(2,1)S(1)} async-done(((bf16[32,24,640]{2,1,0:T(8,128)(2,1)}), bf16[32,24,640]{2,1,0:T(8,128)(2,1)S(1)}, u32[]{:S(2)}, u32[]{:S(2)}) %all-to-all-start) | async-done | bytes 983072 | tf_op jit(solution)/shard_map/all_to_all | solution.py:275
  43.1 0.0 copy-done.3
  43.1 0.0 copy-done.5
  43.1 0.0 copy-start.1
  43.1 1.5 %copy-done.1 = bf16[4,15,64,192]{3,2,1,0:T(8,128)(2,1)S(1)} copy-done((bf16[4,15,64,192]{3,2,1,0:T(8,128)(2,1)S(1)}, bf16[4,15,64,192]{3,2,1,0:T(8,128)(2,1)}, u32[]{:S(2)}) %copy-start.1) | copy-done | bytes 1474584
  44.7 5.7 %conv_mix.1 = (bf16[4,96,1280]{2,1,0:T(8,128)(2,1)S(1)}, bf16[1280,640]{1,0:T(8,128)(2,1)S(1)}, bf16[4,24,640]{2,1,0:T(8,128)(2,1)S(1)}, bf16[4,24,640]{2,1,0:T(...) custom-call(s32[5,8]{1,0:T(8,128)S(1)} %copy-done.5, s32[8,3]{1,0:T(8,128)S(1)} %copy.6.shift_ref, ...), custom_call_target="tpu_custom_call" | custom-call | tf_op jit(solution)/shard_map/conv_mix/pallas_call | solution.py:183
  50.4 5.0 %collective-permute-start.5 = (bf16[4,24,640]{2,1,0:T(8,128)(2,1)S(1)}, bf16[4,24,640]{2,1,0:T(8,128)(2,1)S(1)}, u32[]{:S(2)}, u32[]{:S(2)}) collective-permute-start(bf16[4,24,640]{2,1,0:T(8,128)(2,1)S(1)} %get-tuple-element.19), channel_id=1, source_target_pairs={{0,16},{1,17},{2,18},{3,19},{16,0},{17,1},{18,2},{19,3},{4,20},{5,... | collective-permute-start | bytes 368648 | tf_op jit(solution)/shard_map/ppermute | solution.py:306
  55.4 1.2 %collective-permute-start.6 = (bf16[4,24,640]{2,1,0:T(8,128)(2,1)S(1)}, bf16[4,24,640]{2,1,0:T(8,128)(2,1)S(1)}, u32[]{:S(2)}, u32[]{:S(2)}) collective-permute-start(bf16[4,24,640]{2,1,0:T(8,128)(2,1)S(1)} %get-tuple-element.20), channel_id=1, source_target_pairs={{0,17},{1,16},{2,19},{3,18},{16,1},{17,0},{18,3},{19,2},{4,21},{5,... | collective-permute-start | bytes 368648 | tf_op jit(solution)/shard_map/ppermute | solution.py:306
  56.6 1.5 %collective-permute-start.7 = (bf16[4,24,640]{2,1,0:T(8,128)(2,1)S(1)}, bf16[4,24,640]{2,1,0:T(8,128)(2,1)S(1)}, u32[]{:S(2)}, u32[]{:S(2)}) collective-permute-start(bf16[4,24,640]{2,1,0:T(8,128)(2,1)S(1)} %get-tuple-element.21), channel_id=1, source_target_pairs={{0,18},{1,19},{2,16},{3,17},{16,2},{17,3},{18,0},{19,1},{4,22},{5,... | collective-permute-start | bytes 368648 | tf_op jit(solution)/shard_map/ppermute | solution.py:306
  58.2 0.2 collective-permute-start.8
  58.3 1.5 %mix_own.1 = (bf16[4,24,640]{2,1,0:T(8,128)(2,1)S(1)}, bf16[4,24,640]{2,1,0:T(8,128)(2,1)S(1)}, bf16[4,24,640]{2,1,0:T(8,128)(2,1)S(1)}, bf16[4,24,640]{2,1,0:T(8,128)(2,1)S(1)}) custom-call(s32[7]{0:T(128)S(1)} %stack.28.place_ref, bf16[4,96,1280]{2,1,0:T(8,128)(2,1)S(1)} %get-tuple-element.23.rounded_ref, bf16[1280,640]{1,0:T(8,128)(2,1)S(1)} %get-tuple-element.24.matrix_ref), custom_call_target="tpu_custom_call" | custom-call | tf_op jit(solution)/shard_map/mix_own/pallas_call | solution.py:154
  59.9 1.6 %collective-permute-start.9 = (bf16[4,24,640]{2,1,0:T(8,128)(2,1)S(1)}, bf16[4,24,640]{2,1,0:T(8,128)(2,1)S(1)}, u32[]{:S(2)}, u32[]{:S(2)}) collective-permute-start(bf16[4,24,640]{2,1,0:T(8,128)(2,1)S(1)} %get-tuple-element.26), channel_id=1, source_target_pairs={{0,1},{1,0},{2,3},{3,2},{16,17},{17,16},{18,19},{19,18},{4,5},{5,4... | collective-permute-start | bytes 368648 | tf_op jit(solution)/shard_map/ppermute | solution.py:306
  61.5 0.0 collective-permute-done.5.refs_0_
  61.5 1.5 %collective-permute-start.10 = (bf16[4,24,640]{2,1,0:T(8,128)(2,1)S(1)}, bf16[4,24,640]{2,1,0:T(8,128)(2,1)S(1)}, u32[]{:S(2)}, u32[]{:S(2)}) collective-permute-start(bf16[4,24,640]{2,1,0:T(8,128)(2,1)S(1)} %get-tuple-element.27), channel_id=1, source_target_pairs={{0,2},{1,3},{2,0},{3,1},{16,18},{17,19},{18,16},{19,17},{4,6},{5,7... | collective-permute-start | bytes 368648 | tf_op jit(solution)/shard_map/ppermute | solution.py:306
  62.9 0.0 collective-permute-done.6.refs_1_
  62.9 0.5 collective-permute-start.11
  63.4 1.0 %collective-permute-done.7.refs_2_ = bf16[4,24,640]{2,1,0:T(8,128)(2,1)S(1)} collective-permute-done((bf16[4,24,640]{2,1,0:T(8,128)(2,1)S(1)}, bf16[4,24,640]{2,1,0:T(8,128)(2,1)S(1)}, u32[]{:S(2)}, u32[]{:S(2)}) %collective-permute-start.7) | collective-permute-done | bytes 122912 | tf_op jit(solution)/shard_map/ppermute | solution.py:306
  64.5 0.1 collective-permute-done.8.refs_3_
  64.6 2.1 %collective-permute-done.9.refs_5_ = bf16[4,24,640]{2,1,0:T(8,128)(2,1)S(1)} collective-permute-done((bf16[4,24,640]{2,1,0:T(8,128)(2,1)S(1)}, bf16[4,24,640]{2,1,0:T(8,128)(2,1)S(1)}, u32[]{:S(2)}, u32[]{:S(2)}) %collective-permute-start.9) | collective-permute-done | bytes 122912 | tf_op jit(solution)/shard_map/ppermute | solution.py:306
  66.7 3.5 %collective-permute-done.10.refs_6_ = bf16[4,24,640]{2,1,0:T(8,128)(2,1)S(1)} collective-permute-done((bf16[4,24,640]{2,1,0:T(8,128)(2,1)S(1)}, bf16[4,24,640]{2,1,0:T(8,128)(2,1)S(1)}, u32[]{:S(2)}, u32[]{:S(2)}) %collective-permute-start.10) | collective-permute-done | bytes 122912 | tf_op jit(solution)/shard_map/ppermute | solution.py:306
  70.2 0.0 collective-permute-done.11.refs_7_
  70.2 1.4 %finish.1 = bf16[2,4,24,640]{3,2,1,0:T(8,128)(2,1)} custom-call(s32[7]{0:T(128)S(1)} %stack.28.place_ref, bf16[4,24,640]{2,1,0:T(8,128)(2,1)S(1)} %collective-permute-done.5.refs_0_, bf16[4,24,640]{2,1,0:T(8,128)(2,1)S(1)} %collective-permute-done.6.refs_1_, bf16[4,24,640]{2,1,0:T(8,128)(2,1)S(1)} %collective-permute-done.7.refs_2_, ...), custom_call_target="tpu_custom_call" | custom-call | tf_op jit(solution)/shard_map/finish/pallas_call | solution.py:212
Async XLA Ops:
  0.0 9.9 %collective-permute-start = (bf16[5,40,640]{2,1,0:T(8,128)(2,1)}, bf16[5,40,640]{2,1,0:T(8,128)(2,1)S(1)}, u32[]{:S(2)}, u32[]{:S(2)}) collective-permute-start(bf16[5,40,640]{2,1,0:T(8,128)(2,1)} %refs_2_.1), channel_id=1, source_target_pairs={{0,4},{4,0},{8,12},{12,8},{16,24},{20,28},{24,16},{28,20},{1,5},{5... | collective-permute-start | bytes 768008 | tf_op jit(solution)/shard_map/ppermute | solution.py:256
  3.0 0.9 %copy-start.4 = (bf16[2,4,640,24]{2,3,1,0:T(8,128)(2,1)S(1)}, bf16[2,4,640,24]{2,3,1,0:T(8,128)(2,1)}, u32[]{:S(2)}) copy-start(bf16[2,4,640,24]{2,3,1,0:T(8,128)(2,1)} %param.5) | copy-start | bytes 737284
  9.9 33.2 %all-to-all-start = ((bf16[32,24,640]{2,1,0:T(8,128)(2,1)}), bf16[32,24,640]{2,1,0:T(8,128)(2,1)S(1)}, u32[]{:S(2)}, u32[]{:S(2)}) async-start(bf16[32,24,640]{2,1,0:T(8,128)(2,1)} %bitcast.7), calls=%async_computation | async-start | bytes 1966080 | tf_op jit(solution)/shard_map/all_to_all | solution.py:275
  16.5 9.8 %collective-permute-start.1 = (bf16[5,4,3,3,64,64]{5,4,3,2,1,0:T(8,128)(2,1)}, bf16[5,4,3,3,64,64]{5,4,3,2,1,0:T(8,128)(2,1)}, u32[]{:S(2)}, u32[]{:S(2)}) collective-permute-start(bf16[5,4,3,3,64,64]{5,4,3,2,1,0:T(8,128)(2,1)} %x_ref.1), channel_id=1, source_target_pairs={{0,16},{16,0},{1,17},{17,1},{2,18},{18,2},{3,19},{19,3},{4,20},{20... | collective-permute-start | bytes 4423688 | tf_op jit(solution)/shard_map/ppermute | solution.py:33
  16.8 3.7 %collective-permute-start.3 = (bf16[5,40,640]{2,1,0:T(8,128)(2,1)S(1)}, bf16[5,40,640]{2,1,0:T(8,128)(2,1)}, u32[]{:S(2)}, u32[]{:S(2)}) collective-permute-start(bf16[5,40,640]{2,1,0:T(8,128)(2,1)S(1)} %collective-permute-done.refs_3_), channel_id=1, source_target_pairs={{16,20},{20,16},{24,28},{28,24},{17,21},{21,17},{25,29},{29,25},{1... | collective-permute-start | bytes 768008 | tf_op jit(solution)/shard_map/ppermute | solution.py:258
  18.1 13.7 %collective-permute-start.2 = (bf16[5,40,640]{2,1,0:T(8,128)(2,1)S(1)}, bf16[5,40,640]{2,1,0:T(8,128)(2,1)}, u32[]{:S(2)}, u32[]{:S(2)}) collective-permute-start(bf16[5,40,640]{2,1,0:T(8,128)(2,1)S(1)} %collective-permute-done.refs_3_), channel_id=1, source_target_pairs={{0,16},{16,0},{1,17},{17,1},{2,18},{18,2},{3,19},{19,3},{4,20},{20... | collective-permute-start | bytes 768008 | tf_op jit(solution)/shard_map/ppermute | solution.py:33
  20.5 18.1 %collective-permute-start.4 = (bf16[5,40,640]{2,1,0:T(8,128)(2,1)}, bf16[5,40,640]{2,1,0:T(8,128)(2,1)}, u32[]{:S(2)}, u32[]{:S(2)}) collective-permute-start(bf16[5,40,640]{2,1,0:T(8,128)(2,1)} %collective-permute-done.3.refs_5_), channel_id=1, source_target_pairs={{16,0},{17,1},{18,2},{19,3},{20,4},{21,5},{22,6},{23,7},{24,8},{25... | collective-permute-start | bytes 768008 | tf_op jit(solution)/shard_map/ppermute | solution.py:260
  21.8 1.8 %copy-start.2 = (bf16[5,4,3,3,64,64]{5,4,3,2,1,0:T(8,128)(2,1)S(1)}, bf16[5,4,3,3,64,64]{5,4,3,2,1,0:T(8,128)(2,1)}, u32[]{:S(2)}) copy-start(bf16[5,4,3,3,64,64]{5,4,3,2,1,0:T(8,128)(2,1)} %x_ref.1) | copy-start | bytes 4423684
  23.6 2.4 %copy-start.6 = (s32[8,3]{0,1:T(4,128)S(1)}, s32[8,3]{0,1:T(4,128)}, u32[]{:S(2)}) copy-start(s32[8,3]{0,1:T(4,128)} %param.8) | copy-start | bytes 292
  26.2 16.9 %copy-start.3 = (bf16[5,40,640]{2,1,0:T(8,128)(2,1)S(1)}, bf16[5,40,640]{2,1,0:T(8,128)(2,1)}, u32[]{:S(2)}) copy-start(bf16[5,40,640]{2,1,0:T(8,128)(2,1)} %refs_2_.1) | copy-start | bytes 768004
  26.2 16.9 %copy-start.5 = (s32[5,8]{1,0:T(8,128)S(1)}, s32[5,8]{1,0:T(8,128)}, u32[]{:S(2)}) copy-start(s32[5,8]{1,0:T(8,128)} %low_ref) | copy-start | bytes 484
  30.6 1.3 %copy-start = (bf16[4,15,64,192]{3,2,1,0:T(8,128)(2,1)}, bf16[4,15,64,192]{3,2,1,0:T(8,128)(2,1)S(1)}, u32[]{:S(2)}) copy-start(bf16[4,15,64,192]{3,2,1,0:T(8,128)(2,1)S(1)} %turn.3.refs_1_) | copy-start | bytes 4423684
  43.1 1.5 %copy-start.1 = (bf16[4,15,64,192]{3,2,1,0:T(8,128)(2,1)S(1)}, bf16[4,15,64,192]{3,2,1,0:T(8,128)(2,1)}, u32[]{:S(2)}) copy-start(bf16[4,15,64,192]{3,2,1,0:T(8,128)(2,1)} %copy-done) | copy-start | bytes 4423684
  50.4 11.1 %collective-permute-start.5 = (bf16[4,24,640]{2,1,0:T(8,128)(2,1)S(1)}, bf16[4,24,640]{2,1,0:T(8,128)(2,1)S(1)}, u32[]{:S(2)}, u32[]{:S(2)}) collective-permute-start(bf16[4,24,640]{2,1,0:T(8,128)(2,1)S(1)} %get-tuple-element.19), channel_id=1, source_target_pairs={{0,16},{1,17},{2,18},{3,19},{16,0},{17,1},{18,2},{19,3},{4,20},{5,... | collective-permute-start | bytes 368648 | tf_op jit(solution)/shard_map/ppermute | solution.py:306
  55.4 7.5 %collective-permute-start.6 = (bf16[4,24,640]{2,1,0:T(8,128)(2,1)S(1)}, bf16[4,24,640]{2,1,0:T(8,128)(2,1)S(1)}, u32[]{:S(2)}, u32[]{:S(2)}) collective-permute-start(bf16[4,24,640]{2,1,0:T(8,128)(2,1)S(1)} %get-tuple-element.20), channel_id=1, source_target_pairs={{0,17},{1,16},{2,19},{3,18},{16,1},{17,0},{18,3},{19,2},{4,21},{5,... | collective-permute-start | bytes 368648 | tf_op jit(solution)/shard_map/ppermute | solution.py:306
  56.6 7.8 %collective-permute-start.7 = (bf16[4,24,640]{2,1,0:T(8,128)(2,1)S(1)}, bf16[4,24,640]{2,1,0:T(8,128)(2,1)S(1)}, u32[]{:S(2)}, u32[]{:S(2)}) collective-permute-start(bf16[4,24,640]{2,1,0:T(8,128)(2,1)S(1)} %get-tuple-element.21), channel_id=1, source_target_pairs={{0,18},{1,19},{2,16},{3,17},{16,2},{17,3},{18,0},{19,1},{4,22},{5,... | collective-permute-start | bytes 368648 | tf_op jit(solution)/shard_map/ppermute | solution.py:306
  58.2 6.4 %collective-permute-start.8 = (bf16[4,24,640]{2,1,0:T(8,128)(2,1)S(1)}, bf16[4,24,640]{2,1,0:T(8,128)(2,1)S(1)}, u32[]{:S(2)}, u32[]{:S(2)}) collective-permute-start(bf16[4,24,640]{2,1,0:T(8,128)(2,1)S(1)} %get-tuple-element.22), channel_id=1, source_target_pairs={{0,19},{1,18},{2,17},{3,16},{16,3},{17,2},{18,1},{19,0},{4,23},{5,... | collective-permute-start | bytes 368648 | tf_op jit(solution)/shard_map/ppermute | solution.py:306
  59.9 6.8 %collective-permute-start.9 = (bf16[4,24,640]{2,1,0:T(8,128)(2,1)S(1)}, bf16[4,24,640]{2,1,0:T(8,128)(2,1)S(1)}, u32[]{:S(2)}, u32[]{:S(2)}) collective-permute-start(bf16[4,24,640]{2,1,0:T(8,128)(2,1)S(1)} %get-tuple-element.26), channel_id=1, source_target_pairs={{0,1},{1,0},{2,3},{3,2},{16,17},{17,16},{18,19},{19,18},{4,5},{5,4... | collective-permute-start | bytes 368648 | tf_op jit(solution)/shard_map/ppermute | solution.py:306
  61.5 8.7 %collective-permute-start.10 = (bf16[4,24,640]{2,1,0:T(8,128)(2,1)S(1)}, bf16[4,24,640]{2,1,0:T(8,128)(2,1)S(1)}, u32[]{:S(2)}, u32[]{:S(2)}) collective-permute-start(bf16[4,24,640]{2,1,0:T(8,128)(2,1)S(1)} %get-tuple-element.27), channel_id=1, source_target_pairs={{0,2},{1,3},{2,0},{3,1},{16,18},{17,19},{18,16},{19,17},{4,6},{5,7... | collective-permute-start | bytes 368648 | tf_op jit(solution)/shard_map/ppermute | solution.py:306
  62.9 7.2 %collective-permute-start.11 = (bf16[4,24,640]{2,1,0:T(8,128)(2,1)S(1)}, bf16[4,24,640]{2,1,0:T(8,128)(2,1)S(1)}, u32[]{:S(2)}, u32[]{:S(2)}) collective-permute-start(bf16[4,24,640]{2,1,0:T(8,128)(2,1)S(1)} %get-tuple-element.28), channel_id=1, source_target_pairs={{0,3},{1,2},{2,1},{3,0},{16,19},{17,18},{18,17},{19,16},{4,7},{5,6... | collective-permute-start | bytes 368648 | tf_op jit(solution)/shard_map/ppermute | solution.py:306

commit v19 on v8

--- a/solution.py
+++ b/solution.py
@@ -12,7 +12,7 @@
 HALO = 2
 LANES = 128
 VMEM = pltpu.VMEM
-LIMIT = 24 * 1024 * 1024
+LIMIT = 16 * 1024 * 1024
 SMEM_SPEC = pl.BlockSpec(memory_space=pltpu.SMEM)
 VMEM_SPEC = pl.BlockSpec(memory_space=VMEM)
 
@@ -84,8 +84,10 @@
     cells = span // groups
     member, owner, group = place_ref[0], place_ref[1], place_ref[2]
 
-    total[...] = jnp.zeros_like(total)
-    field_rows[...] = jnp.zeros_like(field_rows)
+    read = pl.ds(HALO - halo, late * rows + 2 * halo)
+    total[:, read] = jnp.zeros((bases, late * rows + 2 * halo) + total.shape[2:], total.dtype)
+    upper = pl.ds(padded - LANES, LANES)
+    field_rows[:, :, upper] = jnp.zeros(field_rows.shape[:2] + (LANES,), field_rows.dtype)
     for s in range(late):
         lat = partner_in_kernel(member, s, late)
         for p in range(owners):
@@ -128,8 +130,7 @@
         product = jnp.dot(jnp.concatenate(lhs, axis=-1), matrix, preferred_element_type=jnp.float32)
         return product.reshape(count, span, width)
 
-    for lat in range(late):
-        mixed[lat * rows : (lat + 1) * rows] = one_out(lat * rows, rows)
+    mixed[...] = one_out(0, late * rows)
     for dl in range(late):
         lat = partner_in_kernel(member, dl, late)
         for dq in range(groups):

time: 65.1 us -> 65 us (level)
  no operation moved by 1% of the time
where the time goes in v19:
time: 65 us; the launch traced here: 64.6 us
  waiting for transfers between devices  27.4 us (42%)
  starting transfers between devices  18.6 us (29%)
  Pallas kernels  9.88 us (15%)
  local copies, waits for them, and re-layouts  8.62 us (13%)
    ppermute x7, waiting for transfers between devices, per_device(): lax.ppermute(partial[dl * groups + dq], ('late', 'lonq'), [(l * groups +...  9.17 us
    ppermute x1, waiting for transfers between devices, gather_mix(): copied = lax.ppermute(third, 'late', [(1, 0)])  9.13 us
    pallas_call x1, Pallas kernels, conv_mix(): pl.pallas_call(functools.partial(conv_mix_kernel, (bases, taps, slots, ha...  7.08 us
    all_to_all x1, starting transfers between devices, per_device(): lax.all_to_all(packed, ('late', 'lonp', 'lonq'), split_axis=0, concat_axi...  6.55 us
    ppermute x1, waiting for transfers between devices, gather_mix(): first = lax.ppermute(mix, ('late', 'lonp'), route)  4.58 us
    all_to_all x1, waiting for transfers between devices, per_device(): lax.all_to_all(packed, ('late', 'lonp', 'lonq'), split_axis=0, concat_axi...  4.5 us
    transpose x1, local copies, waits for them, and re-layouts, both_kernels(): kernel.transpose(1, 0, 2, 5, 3, 4)  4.18 us
    ppermute x7, starting transfers between devices, per_device(): lax.ppermute(partial[dl * groups + dq], ('late', 'lonq'), [(l * groups +...  3.74 us
  transfers between devices with their start and end apart: 13, of which 8 were waited for; matrix products, arithmetic and copies ran while one was open for 12% of the time, Pallas kernels for 2%

profile of v19, /device:TPU:0, one launch (start us, length us, event | category | flops | bytes accessed | tf_op | source)
XLA Modules:
  0.0 64.6 jit_solution(15563788113130532122)
XLA Ops:
  0.0 3.0 %collective-permute-start = (bf16[5,40,640]{2,1,0:T(8,128)(2,1)}, bf16[5,40,640]{2,1,0:T(8,128)(2,1)S(1)}, u32[]{:S(2)}, u32[]{:S(2)}) collective-permute-start(bf16[5,40,640]{2,1,0:T(8,128)(2,1)} %refs_3_.1), channel_id=1, source_target_pairs={{0,4},{4,0},{8,12},{12,8},{16,24},{20,28},{24,16},{28,20},{1,5},{5... | collective-permute-start | bytes 768008 | tf_op jit(solution)/shard_map/ppermute | solution.py:207
  3.0 0.0 copy-start.1
  3.0 0.9 %copy-done.1 = bf16[2,4,640,24]{2,3,1,0:T(8,128)(2,1)S(1)} copy-done((bf16[2,4,640,24]{2,3,1,0:T(8,128)(2,1)S(1)}, bf16[2,4,640,24]{2,3,1,0:T(8,128)(2,1)}, u32[]{:S(2)}) %copy-start.1) | copy-done | bytes 245784
  4.0 1.3 %pack.1 = bf16[2,4,4,24,640]{4,3,2,1,0:T(8,128)(2,1)} custom-call(bf16[2,4,24,640]{3,2,1,0:T(8,128)(2,1)S(1)} %bitcast.12), custom_call_target="tpu_custom_call" | custom-call | tf_op jit(solution)/shard_map/pack/pallas_call | solution.py:53
  5.3 4.6 %collective-permute-done.refs_4_ = bf16[5,40,640]{2,1,0:T(8,128)(2,1)S(1)} collective-permute-done((bf16[5,40,640]{2,1,0:T(8,128)(2,1)}, bf16[5,40,640]{2,1,0:T(8,128)(2,1)S(1)}, u32[]{:S(2)}, u32[]{:S(2)}) %collective-permute-start) | collective-permute-done | bytes 256032 | tf_op jit(solution)/shard_map/ppermute | solution.py:207
  9.9 6.5 %all-to-all-start = ((bf16[32,24,640]{2,1,0:T(8,128)(2,1)}), bf16[32,24,640]{2,1,0:T(8,128)(2,1)S(1)}, u32[]{:S(2)}, u32[]{:S(2)}) async-start(bf16[32,24,640]{2,1,0:T(8,128)(2,1)} %bitcast.7), calls=%async_computation | async-start | bytes 1966080 | tf_op jit(solution)/shard_map/all_to_all | solution.py:228
  16.5 4.2 %copy.8 = bf16[4,5,3,64,3,64]{3,5,4,2,1,0:T(8,128)(2,1)} copy(bf16[4,5,3,64,3,64]{3,5,4,2,0,1:T(8,128)(2,1)} %bitcast.14) | data formatting | bytes 2949120 | tf_op jit(solution)/shard_map/transpose | solution.py:199
  20.6 0.0 copy-start.3
  20.6 0.0 copy-start
  20.6 0.0 copy-start.2
  20.6 3.3 %copy.11.refs_1_ = bf16[4,15,64,192]{3,2,1,0:T(8,128)(2,1)S(1)} copy(bf16[4,15,64,192]{2,3,1,0:T(8,128)(2,1)} %bitcast.13) | data formatting | bytes 2949120 | tf_op jit(solution)/shard_map/reshape | solution.py:199
  24.0 0.3 collective-permute-start.1
  24.3 1.4 %collective-permute-start.3 = (bf16[5,40,640]{2,1,0:T(8,128)(2,1)S(1)}, bf16[5,40,640]{2,1,0:T(8,128)(2,1)}, u32[]{:S(2)}, u32[]{:S(2)}) collective-permute-start(bf16[5,40,640]{2,1,0:T(8,128)(2,1)S(1)} %collective-permute-done.refs_4_), channel_id=1, source_target_pairs={{16,20},{20,16},{24,28},{28,24},{17,21},{21,17},{25,29},{29,25},{1... | collective-permute-start | bytes 768008 | tf_op jit(solution)/shard_map/ppermute | solution.py:209
  25.6 2.4 %collective-permute-start.2 = (bf16[5,40,640]{2,1,0:T(8,128)(2,1)S(1)}, bf16[5,40,640]{2,1,0:T(8,128)(2,1)}, u32[]{:S(2)}, u32[]{:S(2)}) collective-permute-start(bf16[5,40,640]{2,1,0:T(8,128)(2,1)S(1)} %collective-permute-done.refs_4_), channel_id=1, source_target_pairs={{0,16},{16,0},{1,17},{17,1},{2,18},{18,2},{3,19},{19,3},{4,20},{20... | collective-permute-start | bytes 768008 | tf_op jit(solution)/shard_map/ppermute | solution.py:33
  28.0 0.0 collective-permute-done.3.refs_6_
  28.0 1.3 %collective-permute-start.4 = (bf16[5,40,640]{2,1,0:T(8,128)(2,1)}, bf16[5,40,640]{2,1,0:T(8,128)(2,1)}, u32[]{:S(2)}, u32[]{:S(2)}) collective-permute-start(bf16[5,40,640]{2,1,0:T(8,128)(2,1)} %collective-permute-done.3.refs_6_), channel_id=1, source_target_pairs={{16,0},{17,1},{18,2},{19,3},{20,4},{21,5},{22,6},{23,7},{24,8},{25... | collective-permute-start | bytes 768008 | tf_op jit(solution)/shard_map/ppermute | solution.py:211
  29.3 0.0 copy-done.3
  29.3 0.1 copy.10.shift_ref
  29.4 0.1 stack.28.place_ref
  29.5 0.0 collective-permute-done.2.refs_5_
  29.5 9.1 %collective-permute-done.4.refs_7_ = bf16[5,40,640]{2,1,0:T(8,128)(2,1)} collective-permute-done((bf16[5,40,640]{2,1,0:T(8,128)(2,1)}, bf16[5,40,640]{2,1,0:T(8,128)(2,1)}, u32[]{:S(2)}, u32[]{:S(2)}) %collective-permute-start.4) | collective-permute-done | bytes 256032 | tf_op jit(solution)/shard_map/ppermute | solution.py:211
  38.6 0.0 collective-permute-done.1.refs_2_
  38.6 4.5 %all-to-all-done = bf16[32,24,640]{2,1,0:T(8,128)(2,1)S(1)} async-done(((bf16[32,24,640]{2,1,0:T(8,128)(2,1)}), bf16[32,24,640]{2,1,0:T(8,128)(2,1)S(1)}, u32[]{:S(2)}, u32[]{:S(2)}) %all-to-all-start) | async-done | bytes 983072 | tf_op jit(solution)/shard_map/all_to_all | solution.py:228
  43.1 0.0 copy-done
  43.1 0.0 copy-done.2
  43.1 7.1 %conv_mix.1 = (bf16[4,24,640]{2,1,0:T(8,128)(2,1)S(1)}, bf16[4,24,640]{2,1,0:T(8,128)(2,1)S(1)}, bf16[4,24,640]{2,1,0:T(8,128)(2,1)S(1)}, bf16[4,24,640]{2,1,0:T...) custom-call(s32[5,8]{1,0:T(8,128)S(1)} %copy-done.2, ...), custom_call_target="tpu_custom_call" | custom-call | tf_op jit(solution)/shard_map/conv_mix/pallas_call | solution.py:159
  50.2 0.1 collective-permute-start.5
  50.3 0.8 %collective-permute-start.6 = (bf16[4,24,640]{2,1,0:T(8,128)(2,1)S(1)}, bf16[4,24,640]{2,1,0:T(8,128)(2,1)S(1)}, u32[]{:S(2)}, u32[]{:S(2)}) collective-permute-start(bf16[4,24,640]{2,1,0:T(8,128)(2,1)S(1)} %get-tuple-element.19), channel_id=1, source_target_pairs={{0,2},{1,3},{2,0},{3,1},{16,18},{17,19},{18,16},{19,17},{4,6},{5,7... | collective-permute-start | bytes 368648 | tf_op jit(solution)/shard_map/ppermute | solution.py:250
  51.0 2.7 %collective-permute-start.7 = (bf16[4,24,640]{2,1,0:T(8,128)(2,1)S(1)}, bf16[4,24,640]{2,1,0:T(8,128)(2,1)S(1)}, u32[]{:S(2)}, u32[]{:S(2)}) collective-permute-start(bf16[4,24,640]{2,1,0:T(8,128)(2,1)S(1)} %get-tuple-element.20), channel_id=1, source_target_pairs={{0,3},{1,2},{2,1},{3,0},{16,19},{17,18},{18,17},{19,16},{4,7},{5,6... | collective-permute-start | bytes 368648 | tf_op jit(solution)/shard_map/ppermute | solution.py:250
  53.8 0.0 collective-permute-start.8
  53.8 0.2 collective-permute-start.9
  54.0 2.2 %collective-permute-done.5.refs_1_ = bf16[4,24,640]{2,1,0:T(8,128)(2,1)S(1)} collective-permute-done((bf16[4,24,640]{2,1,0:T(8,128)(2,1)S(1)}, bf16[4,24,640]{2,1,0:T(8,128)(2,1)S(1)}, u32[]{:S(2)}, u32[]{:S(2)}) %collective-permute-start.5) | collective-permute-done | bytes 122912 | tf_op jit(solution)/shard_map/ppermute | solution.py:250
  56.2 0.0 collective-permute-start.10
  56.2 1.5 %collective-permute-done.6.refs_2_ = bf16[4,24,640]{2,1,0:T(8,128)(2,1)S(1)} collective-permute-done((bf16[4,24,640]{2,1,0:T(8,128)(2,1)S(1)}, bf16[4,24,640]{2,1,0:T(8,128)(2,1)S(1)}, u32[]{:S(2)}, u32[]{:S(2)}) %collective-permute-start.6) | collective-permute-done | bytes 122912 | tf_op jit(solution)/shard_map/ppermute | solution.py:250
  57.7 0.0 collective-permute-start.11
  57.7 0.3 collective-permute-done.7.refs_3_
  58.0 0.0 collective-permute-done.8.refs_4_
  58.0 1.4 %collective-permute-done.9.refs_5_ = bf16[4,24,640]{2,1,0:T(8,128)(2,1)S(1)} collective-permute-done((bf16[4,24,640]{2,1,0:T(8,128)(2,1)S(1)}, bf16[4,24,640]{2,1,0:T(8,128)(2,1)S(1)}, u32[]{:S(2)}, u32[]{:S(2)}) %collective-permute-start.9) | collective-permute-done | bytes 122912 | tf_op jit(solution)/shard_map/ppermute | solution.py:250
  59.5 3.7 %collective-permute-done.10.refs_6_ = bf16[4,24,640]{2,1,0:T(8,128)(2,1)S(1)} collective-permute-done((bf16[4,24,640]{2,1,0:T(8,128)(2,1)S(1)}, bf16[4,24,640]{2,1,0:T(8,128)(2,1)S(1)}, u32[]{:S(2)}, u32[]{:S(2)}) %collective-permute-start.10) | collective-permute-done | bytes 122912 | tf_op jit(solution)/shard_map/ppermute | solution.py:250
  63.1 0.0 collective-permute-done.11.refs_7_
  63.1 1.4 %finish.1 = bf16[2,4,24,640]{3,2,1,0:T(8,128)(2,1)} custom-call(s32[7]{0:T(128)S(1)} %stack.28.place_ref, bf16[4,24,640]{2,1,0:T(8,128)(2,1)S(1)} %get-tuple-element.17.refs_0_, bf16[4,24,640]{2,1,0:T(8,128)(2,1)S(1)} %collective-permute-done.5.refs_1_, bf16[4,24,640]{2,1,0:T(8,128)(2,1)S(1)} %collective-permute-done.6.refs_2_, ...), custom_call_target="tpu_custom_call" | custom-call | tf_op jit(solution)/shard_map/finish/pallas_call | solution.py:187
Async XLA Ops:
  0.0 9.9 %collective-permute-start = (bf16[5,40,640]{2,1,0:T(8,128)(2,1)}, bf16[5,40,640]{2,1,0:T(8,128)(2,1)S(1)}, u32[]{:S(2)}, u32[]{:S(2)}) collective-permute-start(bf16[5,40,640]{2,1,0:T(8,128)(2,1)} %refs_3_.1), channel_id=1, source_target_pairs={{0,4},{4,0},{8,12},{12,8},{16,24},{20,28},{24,16},{28,20},{1,5},{5... | collective-permute-start | bytes 768008 | tf_op jit(solution)/shard_map/ppermute | solution.py:207
  3.0 0.9 %copy-start.1 = (bf16[2,4,640,24]{2,3,1,0:T(8,128)(2,1)S(1)}, bf16[2,4,640,24]{2,3,1,0:T(8,128)(2,1)}, u32[]{:S(2)}) copy-start(bf16[2,4,640,24]{2,3,1,0:T(8,128)(2,1)} %param.5) | copy-start | bytes 737284
  9.9 33.2 %all-to-all-start = ((bf16[32,24,640]{2,1,0:T(8,128)(2,1)}), bf16[32,24,640]{2,1,0:T(8,128)(2,1)S(1)}, u32[]{:S(2)}, u32[]{:S(2)}) async-start(bf16[32,24,640]{2,1,0:T(8,128)(2,1)} %bitcast.7), calls=%async_computation | async-start | bytes 1966080 | tf_op jit(solution)/shard_map/all_to_all | solution.py:228
  20.6 8.7 %copy-start.3 = (s32[8,3]{0,1:T(4,128)S(1)}, s32[8,3]{0,1:T(4,128)}, u32[]{:S(2)}) copy-start(s32[8,3]{0,1:T(4,128)} %param.8) | copy-start | bytes 292
  20.6 22.5 %copy-start = (bf16[5,40,640]{2,1,0:T(8,128)(2,1)S(1)}, bf16[5,40,640]{2,1,0:T(8,128)(2,1)}, u32[]{:S(2)}) copy-start(bf16[5,40,640]{2,1,0:T(8,128)(2,1)} %refs_3_.1) | copy-start | bytes 768004
  20.6 22.5 %copy-start.2 = (s32[5,8]{1,0:T(8,128)S(1)}, s32[5,8]{1,0:T(8,128)}, u32[]{:S(2)}) copy-start(s32[5,8]{1,0:T(8,128)} %low_ref) | copy-start | bytes 484
  24.0 14.6 %collective-permute-start.1 = (bf16[4,15,64,192]{3,2,1,0:T(8,128)(2,1)S(1)}, bf16[4,15,64,192]{3,2,1,0:T(8,128)(2,1)}, u32[]{:S(2)}, u32[]{:S(2)}) collective-permute-start(bf16[4,15,64,192]{3,2,1,0:T(8,128)(2,1)S(1)} %copy.11.refs_1_), channel_id=1, source_target_pairs={{0,16},{16,0},{1,17},{17,1},{2,18},{18,2},{3,19},{19,3},{4,20},{20... | collective-permute-start | bytes 4423688 | tf_op jit(solution)/shard_map/ppermute | solution.py:33
  24.3 3.7 %collective-permute-start.3 = (bf16[5,40,640]{2,1,0:T(8,128)(2,1)S(1)}, bf16[5,40,640]{2,1,0:T(8,128)(2,1)}, u32[]{:S(2)}, u32[]{:S(2)}) collective-permute-start(bf16[5,40,640]{2,1,0:T(8,128)(2,1)S(1)} %collective-permute-done.refs_4_), channel_id=1, source_target_pairs={{16,20},{20,16},{24,28},{28,24},{17,21},{21,17},{25,29},{29,25},{1... | collective-permute-start | bytes 768008 | tf_op jit(solution)/shard_map/ppermute | solution.py:209
  25.6 3.8 %collective-permute-start.2 = (bf16[5,40,640]{2,1,0:T(8,128)(2,1)S(1)}, bf16[5,40,640]{2,1,0:T(8,128)(2,1)}, u32[]{:S(2)}, u32[]{:S(2)}) collective-permute-start(bf16[5,40,640]{2,1,0:T(8,128)(2,1)S(1)} %collective-permute-done.refs_4_), channel_id=1, source_target_pairs={{0,16},{16,0},{1,17},{17,1},{2,18},{18,2},{3,19},{19,3},{4,20},{20... | collective-permute-start | bytes 768008 | tf_op jit(solution)/shard_map/ppermute | solution.py:33
  28.0 10.6 %collective-permute-start.4 = (bf16[5,40,640]{2,1,0:T(8,128)(2,1)}, bf16[5,40,640]{2,1,0:T(8,128)(2,1)}, u32[]{:S(2)}, u32[]{:S(2)}) collective-permute-start(bf16[5,40,640]{2,1,0:T(8,128)(2,1)} %collective-permute-done.3.refs_6_), channel_id=1, source_target_pairs={{16,0},{17,1},{18,2},{19,3},{20,4},{21,5},{22,6},{23,7},{24,8},{25... | collective-permute-start | bytes 768008 | tf_op jit(solution)/shard_map/ppermute | solution.py:211
  50.2 6.0 %collective-permute-start.5 = (bf16[4,24,640]{2,1,0:T(8,128)(2,1)S(1)}, bf16[4,24,640]{2,1,0:T(8,128)(2,1)S(1)}, u32[]{:S(2)}, u32[]{:S(2)}) collective-permute-start(bf16[4,24,640]{2,1,0:T(8,128)(2,1)S(1)} %get-tuple-element.18), channel_id=1, source_target_pairs={{0,1},{1,0},{2,3},{3,2},{16,17},{17,16},{18,19},{19,18},{4,5},{5,4... | collective-permute-start | bytes 368648 | tf_op jit(solution)/shard_map/ppermute | solution.py:250
  50.3 7.4 %collective-permute-start.6 = (bf16[4,24,640]{2,1,0:T(8,128)(2,1)S(1)}, bf16[4,24,640]{2,1,0:T(8,128)(2,1)S(1)}, u32[]{:S(2)}, u32[]{:S(2)}) collective-permute-start(bf16[4,24,640]{2,1,0:T(8,128)(2,1)S(1)} %get-tuple-element.19), channel_id=1, source_target_pairs={{0,2},{1,3},{2,0},{3,1},{16,18},{17,19},{18,16},{19,17},{4,6},{5,7... | collective-permute-start | bytes 368648 | tf_op jit(solution)/shard_map/ppermute | solution.py:250
  51.0 7.0 %collective-permute-start.7 = (bf16[4,24,640]{2,1,0:T(8,128)(2,1)S(1)}, bf16[4,24,640]{2,1,0:T(8,128)(2,1)S(1)}, u32[]{:S(2)}, u32[]{:S(2)}) collective-permute-start(bf16[4,24,640]{2,1,0:T(8,128)(2,1)S(1)} %get-tuple-element.20), channel_id=1, source_target_pairs={{0,3},{1,2},{2,1},{3,0},{16,19},{17,18},{18,17},{19,16},{4,7},{5,6... | collective-permute-start | bytes 368648 | tf_op jit(solution)/shard_map/ppermute | solution.py:250
  53.8 4.3 %collective-permute-start.8 = (bf16[4,24,640]{2,1,0:T(8,128)(2,1)S(1)}, bf16[4,24,640]{2,1,0:T(8,128)(2,1)S(1)}, u32[]{:S(2)}, u32[]{:S(2)}) collective-permute-start(bf16[4,24,640]{2,1,0:T(8,128)(2,1)S(1)} %get-tuple-element.21), channel_id=1, source_target_pairs={{0,16},{1,17},{2,18},{3,19},{16,0},{17,1},{18,2},{19,3},{4,20},{5,... | collective-permute-start | bytes 368648 | tf_op jit(solution)/shard_map/ppermute | solution.py:250
  53.8 5.7 %collective-permute-start.9 = (bf16[4,24,640]{2,1,0:T(8,128)(2,1)S(1)}, bf16[4,24,640]{2,1,0:T(8,128)(2,1)S(1)}, u32[]{:S(2)}, u32[]{:S(2)}) collective-permute-start(bf16[4,24,640]{2,1,0:T(8,128)(2,1)S(1)} %get-tuple-element.22), channel_id=1, source_target_pairs={{0,17},{1,16},{2,19},{3,18},{16,1},{17,0},{18,3},{19,2},{4,21},{5,... | collective-permute-start | bytes 368648 | tf_op jit(solution)/shard_map/ppermute | solution.py:250
  56.2 7.0 %collective-permute-start.10 = (bf16[4,24,640]{2,1,0:T(8,128)(2,1)S(1)}, bf16[4,24,640]{2,1,0:T(8,128)(2,1)S(1)}, u32[]{:S(2)}, u32[]{:S(2)}) collective-permute-start(bf16[4,24,640]{2,1,0:T(8,128)(2,1)S(1)} %get-tuple-element.23), channel_id=1, source_target_pairs={{0,18},{1,19},{2,16},{3,17},{16,2},{17,3},{18,0},{19,1},{4,22},{5,... | collective-permute-start | bytes 368648 | tf_op jit(solution)/shard_map/ppermute | solution.py:250
  57.7 5.4 %collective-permute-start.11 = (bf16[4,24,640]{2,1,0:T(8,128)(2,1)S(1)}, bf16[4,24,640]{2,1,0:T(8,128)(2,1)S(1)}, u32[]{:S(2)}, u32[]{:S(2)}) collective-permute-start(bf16[4,24,640]{2,1,0:T(8,128)(2,1)S(1)} %get-tuple-element.24), channel_id=1, source_target_pairs={{0,19},{1,18},{2,17},{3,16},{16,3},{17,2},{18,1},{19,0},{4,23},{5,... | collective-permute-start | bytes 368648 | tf_op jit(solution)/shard_map/ppermute | solution.py:250

commit v20 on v19

--- a/solution.py
+++ b/solution.py
@@ -172,21 +172,22 @@
     )(low, shift, place, *operands)
 
 
-def finish_kernel(groups, place_ref, *refs):
+def finish_kernel(owners, place_ref, *refs):
     out_ref = refs[-1]
     late = out_ref.shape[0]
     for dl in range(late):
-        total = refs[dl * groups][...].astype(jnp.float32)
-        for dq in range(1, groups):
-            total += refs[dl * groups + dq][...].astype(jnp.float32)
+        mine = [ref for ref, owner in zip(refs, owners) if owner == dl]
+        total = mine[0][...].astype(jnp.float32)
+        for ref in mine[1:]:
+            total += ref[...].astype(jnp.float32)
         value = total * (1.0 + lax.erf(total * (0.5**0.5))) * 0.5
         out_ref[partner_in_kernel(place_ref[0], dl, late)] = value.astype(jnp.bfloat16)
 
 
-def finish(place, parts, groups):
+def finish(place, parts, owners):
     return pl.pallas_call(
-        functools.partial(finish_kernel, groups),
-        out_shape=jax.ShapeDtypeStruct((len(parts) // groups,) + parts[0].shape, jnp.bfloat16),
+        functools.partial(finish_kernel, owners),
+        out_shape=jax.ShapeDtypeStruct((len(set(owners)),) + parts[0].shape, jnp.bfloat16),
         in_specs=[SMEM_SPEC] + [VMEM_SPEC] * len(parts),
         out_specs=VMEM_SPEC,
         compiler_params=pltpu.CompilerParams(vmem_limit_bytes=LIMIT),
@@ -246,22 +247,18 @@
             for dq in range(groups):
                 group = partner(lax.axis_index("lonq"), dq, groups)
                 partial[dl * groups + dq] += extra[lat, :, group]
-    parts = [
-        lax.ppermute(
-            partial[dl * groups + dq],
-            ("late", "lonq"),
-            [
-                (l * groups + q, partner(l, dl, late) * groups + partner(q, dq, groups))
-                for l in range(late)
-                for q in range(groups)
-            ],
-        )
-        if dl or dq
-        else partial[0]
-        for dl in range(late)
-        for dq in range(groups)
-    ]
-    return finish(place, parts, groups)
+    order = [(dl, dq) for dl in range(late) for dq in range(groups)]
+    order.sort(key=lambda at: (at[1] == 0, bin(at[1]).count("1"), at))
+    parts = []
+    for dl, dq in order:
+        route = [
+            (l * groups + q, partner(l, dl, late) * groups + partner(q, dq, groups))
+            for l in range(late)
+            for q in range(groups)
+        ]
+        block = partial[dl * groups + dq]
+        parts.append(lax.ppermute(block, ("late", "lonq"), route) if dl or dq else block)
+    return finish(place, parts, [dl for dl, _ in order])
 
 
 def solution(mesh):

time: 65 us -> 64.7 us (level)
  waiting for transfers between devices: 27.4 us -> 26 us
  starting transfers between devices: 18.6 us -> 19.8 us
    ppermute x7, waiting for transfers between devices: 9.17 us -> 7.82 us  [per_device(): lax.ppermute(block, ('late', 'lonq'), route)]
    ppermute x7, starting transfers between devices: 3.74 us -> 4.86 us  [per_device(): lax.ppermute(block, ('late', 'lonq'), route)]
  transfers between devices with their start and end apart: 13 -> 13, of which waited for: 8 -> 5; matrix products, arithmetic and copies ran while one was open for 12% -> 12% of each run, Pallas kernels for 2% -> 2%
where the time goes in v20:
time: 64.7 us; the launch traced here: 64.4 us
  waiting for transfers between devices  26 us (40%)
  starting transfers between devices  19.8 us (31%)
  Pallas kernels  9.88 us (15%)
  local copies, waits for them, and re-layouts  8.62 us (13%)
    ppermute x1, waiting for transfers between devices, gather_mix(): copied = lax.ppermute(third, 'late', [(1, 0)])  9.13 us
    ppermute x7, waiting for transfers between devices, per_device(): lax.ppermute(block, ('late', 'lonq'), route)  7.82 us
    pallas_call x1, Pallas kernels, conv_mix(): pl.pallas_call(functools.partial(conv_mix_kernel, (bases, taps, slots, ha...  7.08 us
    all_to_all x1, starting transfers between devices, per_device(): lax.all_to_all(packed, ('late', 'lonp', 'lonq'), split_axis=0, concat_axi...  6.55 us
    ppermute x7, starting transfers between devices, per_device(): lax.ppermute(block, ('late', 'lonq'), route)  4.86 us
    ppermute x1, waiting for transfers between devices, gather_mix(): first = lax.ppermute(mix, ('late', 'lonp'), route)  4.58 us
    all_to_all x1, waiting for transfers between devices, per_device(): lax.all_to_all(packed, ('late', 'lonp', 'lonq'), split_axis=0, concat_axi...  4.5 us
    transpose x1, local copies, waits for them, and re-layouts, both_kernels(): kernel.transpose(1, 0, 2, 5, 3, 4)  4.18 us
  transfers between devices with their start and end apart: 13, of which 5 were waited for; matrix products, arithmetic and copies ran while one was open for 12% of the time, Pallas kernels for 2%

profile of v20, /device:TPU:0, one launch (start us, length us, event | category | flops | bytes accessed | tf_op | source)
XLA Modules:
  0.0 64.4 jit_solution(7335669582631915798)
XLA Ops:
  0.0 3.0 %collective-permute-start = (bf16[5,40,640]{2,1,0:T(8,128)(2,1)}, bf16[5,40,640]{2,1,0:T(8,128)(2,1)S(1)}, u32[]{:S(2)}, u32[]{:S(2)}) collective-permute-start(bf16[5,40,640]{2,1,0:T(8,128)(2,1)} %refs_3_.1), channel_id=1, source_target_pairs={{0,4},{4,0},{8,12},{12,8},{16,24},{20,28},{24,16},{28,20},{1,5},{5... | collective-permute-start | bytes 768008 | tf_op jit(solution)/shard_map/ppermute | solution.py:208
  3.0 0.0 copy-start.1
  3.0 0.9 %copy-done.1 = bf16[2,4,640,24]{2,3,1,0:T(8,128)(2,1)S(1)} copy-done((bf16[2,4,640,24]{2,3,1,0:T(8,128)(2,1)S(1)}, bf16[2,4,640,24]{2,3,1,0:T(8,128)(2,1)}, u32[]{:S(2)}) %copy-start.1) | copy-done | bytes 245784
  4.0 1.3 %pack.1 = bf16[2,4,4,24,640]{4,3,2,1,0:T(8,128)(2,1)} custom-call(bf16[2,4,24,640]{3,2,1,0:T(8,128)(2,1)S(1)} %bitcast.12), custom_call_target="tpu_custom_call" | custom-call | tf_op jit(solution)/shard_map/pack/pallas_call | solution.py:53
  5.3 4.6 %collective-permute-done.refs_4_ = bf16[5,40,640]{2,1,0:T(8,128)(2,1)S(1)} collective-permute-done((bf16[5,40,640]{2,1,0:T(8,128)(2,1)}, bf16[5,40,640]{2,1,0:T(8,128)(2,1)S(1)}, u32[]{:S(2)}, u32[]{:S(2)}) %collective-permute-start) | collective-permute-done | bytes 256032 | tf_op jit(solution)/shard_map/ppermute | solution.py:208
  9.9 6.5 %all-to-all-start = ((bf16[32,24,640]{2,1,0:T(8,128)(2,1)}), bf16[32,24,640]{2,1,0:T(8,128)(2,1)S(1)}, u32[]{:S(2)}, u32[]{:S(2)}) async-start(bf16[32,24,640]{2,1,0:T(8,128)(2,1)} %bitcast.7), calls=%async_computation | async-start | bytes 1966080 | tf_op jit(solution)/shard_map/all_to_all | solution.py:229
  16.5 4.2 %copy.8 = bf16[4,5,3,64,3,64]{3,5,4,2,1,0:T(8,128)(2,1)} copy(bf16[4,5,3,64,3,64]{3,5,4,2,0,1:T(8,128)(2,1)} %bitcast.14) | data formatting | bytes 2949120 | tf_op jit(solution)/shard_map/transpose | solution.py:200
  20.6 0.0 copy-start.3
  20.6 0.0 copy-start
  20.6 0.0 copy-start.2
  20.6 3.3 %copy.11.refs_1_ = bf16[4,15,64,192]{3,2,1,0:T(8,128)(2,1)S(1)} copy(bf16[4,15,64,192]{2,3,1,0:T(8,128)(2,1)} %bitcast.13) | data formatting | bytes 2949120 | tf_op jit(solution)/shard_map/reshape | solution.py:200
  24.0 0.3 collective-permute-start.1
  24.3 1.4 %collective-permute-start.3 = (bf16[5,40,640]{2,1,0:T(8,128)(2,1)S(1)}, bf16[5,40,640]{2,1,0:T(8,128)(2,1)}, u32[]{:S(2)}, u32[]{:S(2)}) collective-permute-start(bf16[5,40,640]{2,1,0:T(8,128)(2,1)S(1)} %collective-permute-done.refs_4_), channel_id=1, source_target_pairs={{16,20},{20,16},{24,28},{28,24},{17,21},{21,17},{25,29},{29,25},{1... | collective-permute-start | bytes 768008 | tf_op jit(solution)/shard_map/ppermute | solution.py:210
  25.6 2.4 %collective-permute-start.2 = (bf16[5,40,640]{2,1,0:T(8,128)(2,1)S(1)}, bf16[5,40,640]{2,1,0:T(8,128)(2,1)}, u32[]{:S(2)}, u32[]{:S(2)}) collective-permute-start(bf16[5,40,640]{2,1,0:T(8,128)(2,1)S(1)} %collective-permute-done.refs_4_), channel_id=1, source_target_pairs={{0,16},{16,0},{1,17},{17,1},{2,18},{18,2},{3,19},{19,3},{4,20},{20... | collective-permute-start | bytes 768008 | tf_op jit(solution)/shard_map/ppermute | solution.py:33
  28.0 0.0 collective-permute-done.3.refs_6_
  28.0 1.3 %collective-permute-start.4 = (bf16[5,40,640]{2,1,0:T(8,128)(2,1)}, bf16[5,40,640]{2,1,0:T(8,128)(2,1)}, u32[]{:S(2)}, u32[]{:S(2)}) collective-permute-start(bf16[5,40,640]{2,1,0:T(8,128)(2,1)} %collective-permute-done.3.refs_6_), channel_id=1, source_target_pairs={{16,0},{17,1},{18,2},{19,3},{20,4},{21,5},{22,6},{23,7},{24,8},{25... | collective-permute-start | bytes 768008 | tf_op jit(solution)/shard_map/ppermute | solution.py:212
  29.3 0.0 copy-done.3
  29.3 0.1 copy.10.shift_ref
  29.4 0.1 stack.28.place_ref
  29.5 0.0 collective-permute-done.2.refs_5_
  29.5 9.1 %collective-permute-done.4.refs_7_ = bf16[5,40,640]{2,1,0:T(8,128)(2,1)} collective-permute-done((bf16[5,40,640]{2,1,0:T(8,128)(2,1)}, bf16[5,40,640]{2,1,0:T(8,128)(2,1)}, u32[]{:S(2)}, u32[]{:S(2)}) %collective-permute-start.4) | collective-permute-done | bytes 256032 | tf_op jit(solution)/shard_map/ppermute | solution.py:212
  38.6 0.0 collective-permute-done.1.refs_2_
  38.6 4.5 %all-to-all-done = bf16[32,24,640]{2,1,0:T(8,128)(2,1)S(1)} async-done(((bf16[32,24,640]{2,1,0:T(8,128)(2,1)}), bf16[32,24,640]{2,1,0:T(8,128)(2,1)S(1)}, u32[]{:S(2)}, u32[]{:S(2)}) %all-to-all-start) | async-done | bytes 983072 | tf_op jit(solution)/shard_map/all_to_all | solution.py:229
  43.1 0.0 copy-done
  43.1 0.0 copy-done.2
  43.1 7.1 %conv_mix.1 = (bf16[4,24,640]{2,1,0:T(8,128)(2,1)S(1)}, bf16[4,24,640]{2,1,0:T(8,128)(2,1)S(1)}, bf16[4,24,640]{2,1,0:T(8,128)(2,1)S(1)}, bf16[4,24,640]{2,1,0:T...) custom-call(s32[5,8]{1,0:T(8,128)S(1)} %copy-done.2, ...), custom_call_target="tpu_custom_call" | custom-call | tf_op jit(solution)/shard_map/conv_mix/pallas_call | solution.py:159
  50.2 0.1 collective-permute-start.5
  50.3 0.8 %collective-permute-start.6 = (bf16[4,24,640]{2,1,0:T(8,128)(2,1)S(1)}, bf16[4,24,640]{2,1,0:T(8,128)(2,1)S(1)}, u32[]{:S(2)}, u32[]{:S(2)}) collective-permute-start(bf16[4,24,640]{2,1,0:T(8,128)(2,1)S(1)} %get-tuple-element.18), channel_id=1, source_target_pairs={{0,2},{1,3},{2,0},{3,1},{16,18},{17,19},{18,16},{19,17},{4,6},{5,7... | collective-permute-start | bytes 368648 | tf_op jit(solution)/shard_map/ppermute | solution.py:260
  51.0 0.0 collective-permute-start.7
  51.1 3.0 %collective-permute-start.8 = (bf16[4,24,640]{2,1,0:T(8,128)(2,1)S(1)}, bf16[4,24,640]{2,1,0:T(8,128)(2,1)S(1)}, u32[]{:S(2)}, u32[]{:S(2)}) collective-permute-start(bf16[4,24,640]{2,1,0:T(8,128)(2,1)S(1)} %get-tuple-element.20), channel_id=1, source_target_pairs={{0,18},{1,19},{2,16},{3,17},{16,2},{17,3},{18,0},{19,1},{4,22},{5,... | collective-permute-start | bytes 368648 | tf_op jit(solution)/shard_map/ppermute | solution.py:260
  54.0 0.2 collective-permute-start.9
  54.3 2.0 %collective-permute-done.5.refs_0_ = bf16[4,24,640]{2,1,0:T(8,128)(2,1)S(1)} collective-permute-done((bf16[4,24,640]{2,1,0:T(8,128)(2,1)S(1)}, bf16[4,24,640]{2,1,0:T(8,128)(2,1)S(1)}, u32[]{:S(2)}, u32[]{:S(2)}) %collective-permute-start.5) | collective-permute-done | bytes 122912 | tf_op jit(solution)/shard_map/ppermute | solution.py:260
  56.3 0.0 collective-permute-start.10
  56.3 0.0 collective-permute-done.6.refs_1_
  56.3 0.8 %collective-permute-start.11 = (bf16[4,24,640]{2,1,0:T(8,128)(2,1)S(1)}, bf16[4,24,640]{2,1,0:T(8,128)(2,1)S(1)}, u32[]{:S(2)}, u32[]{:S(2)}) collective-permute-start(bf16[4,24,640]{2,1,0:T(8,128)(2,1)S(1)} %get-tuple-element.24), channel_id=1, source_target_pairs={{0,16},{1,17},{2,18},{3,19},{16,0},{17,1},{18,2},{19,3},{4,20},{5,... | collective-permute-start | bytes 368648 | tf_op jit(solution)/shard_map/ppermute | solution.py:260
  57.1 0.0 collective-permute-done.7.refs_2_
  57.1 5.8 %collective-permute-done.8.refs_3_ = bf16[4,24,640]{2,1,0:T(8,128)(2,1)S(1)} collective-permute-done((bf16[4,24,640]{2,1,0:T(8,128)(2,1)S(1)}, bf16[4,24,640]{2,1,0:T(8,128)(2,1)S(1)}, u32[]{:S(2)}, u32[]{:S(2)}) %collective-permute-start.8) | collective-permute-done | bytes 122912 | tf_op jit(solution)/shard_map/ppermute | solution.py:260
  62.9 0.0 collective-permute-done.9.refs_4_
  62.9 0.0 collective-permute-done.10.refs_5_
  62.9 0.0 collective-permute-done.11.refs_7_
  62.9 1.5 %finish.1 = bf16[2,4,24,640]{3,2,1,0:T(8,128)(2,1)} custom-call(s32[7]{0:T(128)S(1)} %stack.28.place_ref, bf16[4,24,640]{2,1,0:T(8,128)(2,1)S(1)} %collective-permute-done.5.refs_0_, bf16[4,24,640]{2,1,0:T(8,128)(2,1)S(1)} %collective-permute-done.6.refs_1_, bf16[4,24,640]{2,1,0:T(8,128)(2,1)S(1)} %collective-permute-done.7.refs_2_, ...), custom_call_target="tpu_custom_call" | custom-call | tf_op jit(solution)/shard_map/finish/pallas_call | solution.py:188
Async XLA Ops:
  0.0 9.9 %collective-permute-start = (bf16[5,40,640]{2,1,0:T(8,128)(2,1)}, bf16[5,40,640]{2,1,0:T(8,128)(2,1)S(1)}, u32[]{:S(2)}, u32[]{:S(2)}) collective-permute-start(bf16[5,40,640]{2,1,0:T(8,128)(2,1)} %refs_3_.1), channel_id=1, source_target_pairs={{0,4},{4,0},{8,12},{12,8},{16,24},{20,28},{24,16},{28,20},{1,5},{5... | collective-permute-start | bytes 768008 | tf_op jit(solution)/shard_map/ppermute | solution.py:208
  3.0 0.9 %copy-start.1 = (bf16[2,4,640,24]{2,3,1,0:T(8,128)(2,1)S(1)}, bf16[2,4,640,24]{2,3,1,0:T(8,128)(2,1)}, u32[]{:S(2)}) copy-start(bf16[2,4,640,24]{2,3,1,0:T(8,128)(2,1)} %param.5) | copy-start | bytes 737284
  9.9 33.2 %all-to-all-start = ((bf16[32,24,640]{2,1,0:T(8,128)(2,1)}), bf16[32,24,640]{2,1,0:T(8,128)(2,1)S(1)}, u32[]{:S(2)}, u32[]{:S(2)}) async-start(bf16[32,24,640]{2,1,0:T(8,128)(2,1)} %bitcast.7), calls=%async_computation | async-start | bytes 1966080 | tf_op jit(solution)/shard_map/all_to_all | solution.py:229
  20.6 8.7 %copy-start.3 = (s32[8,3]{0,1:T(4,128)S(1)}, s32[8,3]{0,1:T(4,128)}, u32[]{:S(2)}) copy-start(s32[8,3]{0,1:T(4,128)} %param.8) | copy-start | bytes 292
  20.6 22.5 %copy-start = (bf16[5,40,640]{2,1,0:T(8,128)(2,1)S(1)}, bf16[5,40,640]{2,1,0:T(8,128)(2,1)}, u32[]{:S(2)}) copy-start(bf16[5,40,640]{2,1,0:T(8,128)(2,1)} %refs_3_.1) | copy-start | bytes 768004
  20.6 22.5 %copy-start.2 = (s32[5,8]{1,0:T(8,128)S(1)}, s32[5,8]{1,0:T(8,128)}, u32[]{:S(2)}) copy-start(s32[5,8]{1,0:T(8,128)} %low_ref) | copy-start | bytes 484
  24.0 14.6 %collective-permute-start.1 = (bf16[4,15,64,192]{3,2,1,0:T(8,128)(2,1)S(1)}, bf16[4,15,64,192]{3,2,1,0:T(8,128)(2,1)}, u32[]{:S(2)}, u32[]{:S(2)}) collective-permute-start(bf16[4,15,64,192]{3,2,1,0:T(8,128)(2,1)S(1)} %copy.11.refs_1_), channel_id=1, source_target_pairs={{0,16},{16,0},{1,17},{17,1},{2,18},{18,2},{3,19},{19,3},{4,20},{20... | collective-permute-start | bytes 4423688 | tf_op jit(solution)/shard_map/ppermute | solution.py:33
  24.3 3.7 %collective-permute-start.3 = (bf16[5,40,640]{2,1,0:T(8,128)(2,1)S(1)}, bf16[5,40,640]{2,1,0:T(8,128)(2,1)}, u32[]{:S(2)}, u32[]{:S(2)}) collective-permute-start(bf16[5,40,640]{2,1,0:T(8,128)(2,1)S(1)} %collective-permute-done.refs_4_), channel_id=1, source_target_pairs={{16,20},{20,16},{24,28},{28,24},{17,21},{21,17},{25,29},{29,25},{1... | collective-permute-start | bytes 768008 | tf_op jit(solution)/shard_map/ppermute | solution.py:210
  25.6 3.8 %collective-permute-start.2 = (bf16[5,40,640]{2,1,0:T(8,128)(2,1)S(1)}, bf16[5,40,640]{2,1,0:T(8,128)(2,1)}, u32[]{:S(2)}, u32[]{:S(2)}) collective-permute-start(bf16[5,40,640]{2,1,0:T(8,128)(2,1)S(1)} %collective-permute-done.refs_4_), channel_id=1, source_target_pairs={{0,16},{16,0},{1,17},{17,1},{2,18},{18,2},{3,19},{19,3},{4,20},{20... | collective-permute-start | bytes 768008 | tf_op jit(solution)/shard_map/ppermute | solution.py:33
  28.0 10.6 %collective-permute-start.4 = (bf16[5,40,640]{2,1,0:T(8,128)(2,1)}, bf16[5,40,640]{2,1,0:T(8,128)(2,1)}, u32[]{:S(2)}, u32[]{:S(2)}) collective-permute-start(bf16[5,40,640]{2,1,0:T(8,128)(2,1)} %collective-permute-done.3.refs_6_), channel_id=1, source_target_pairs={{16,0},{17,1},{18,2},{19,3},{20,4},{21,5},{22,6},{23,7},{24,8},{25... | collective-permute-start | bytes 768008 | tf_op jit(solution)/shard_map/ppermute | solution.py:212
  50.2 6.1 %collective-permute-start.5 = (bf16[4,24,640]{2,1,0:T(8,128)(2,1)S(1)}, bf16[4,24,640]{2,1,0:T(8,128)(2,1)S(1)}, u32[]{:S(2)}, u32[]{:S(2)}) collective-permute-start(bf16[4,24,640]{2,1,0:T(8,128)(2,1)S(1)} %get-tuple-element.17), channel_id=1, source_target_pairs={{0,1},{1,0},{2,3},{3,2},{16,17},{17,16},{18,19},{19,18},{4,5},{5,4... | collective-permute-start | bytes 368648 | tf_op jit(solution)/shard_map/ppermute | solution.py:260
  50.3 6.0 %collective-permute-start.6 = (bf16[4,24,640]{2,1,0:T(8,128)(2,1)S(1)}, bf16[4,24,640]{2,1,0:T(8,128)(2,1)S(1)}, u32[]{:S(2)}, u32[]{:S(2)}) collective-permute-start(bf16[4,24,640]{2,1,0:T(8,128)(2,1)S(1)} %get-tuple-element.18), channel_id=1, source_target_pairs={{0,2},{1,3},{2,0},{3,1},{16,18},{17,19},{18,16},{19,17},{4,6},{5,7... | collective-permute-start | bytes 368648 | tf_op jit(solution)/shard_map/ppermute | solution.py:260
  51.0 6.1 %collective-permute-start.7 = (bf16[4,24,640]{2,1,0:T(8,128)(2,1)S(1)}, bf16[4,24,640]{2,1,0:T(8,128)(2,1)S(1)}, u32[]{:S(2)}, u32[]{:S(2)}) collective-permute-start(bf16[4,24,640]{2,1,0:T(8,128)(2,1)S(1)} %get-tuple-element.19), channel_id=1, source_target_pairs={{0,17},{1,16},{2,19},{3,18},{16,1},{17,0},{18,3},{19,2},{4,21},{5,... | collective-permute-start | bytes 368648 | tf_op jit(solution)/shard_map/ppermute | solution.py:260
  51.1 11.8 %collective-permute-start.8 = (bf16[4,24,640]{2,1,0:T(8,128)(2,1)S(1)}, bf16[4,24,640]{2,1,0:T(8,128)(2,1)S(1)}, u32[]{:S(2)}, u32[]{:S(2)}) collective-permute-start(bf16[4,24,640]{2,1,0:T(8,128)(2,1)S(1)} %get-tuple-element.20), channel_id=1, source_target_pairs={{0,18},{1,19},{2,16},{3,17},{16,2},{17,3},{18,0},{19,1},{4,22},{5,... | collective-permute-start | bytes 368648 | tf_op jit(solution)/shard_map/ppermute | solution.py:260
  54.0 8.9 %collective-permute-start.9 = (bf16[4,24,640]{2,1,0:T(8,128)(2,1)S(1)}, bf16[4,24,640]{2,1,0:T(8,128)(2,1)S(1)}, u32[]{:S(2)}, u32[]{:S(2)}) collective-permute-start(bf16[4,24,640]{2,1,0:T(8,128)(2,1)S(1)} %get-tuple-element.21), channel_id=1, source_target_pairs={{0,3},{1,2},{2,1},{3,0},{16,19},{17,18},{18,17},{19,16},{4,7},{5,6... | collective-permute-start | bytes 368648 | tf_op jit(solution)/shard_map/ppermute | solution.py:260
  56.3 6.6 %collective-permute-start.10 = (bf16[4,24,640]{2,1,0:T(8,128)(2,1)S(1)}, bf16[4,24,640]{2,1,0:T(8,128)(2,1)S(1)}, u32[]{:S(2)}, u32[]{:S(2)}) collective-permute-start(bf16[4,24,640]{2,1,0:T(8,128)(2,1)S(1)} %get-tuple-element.22), channel_id=1, source_target_pairs={{0,19},{1,18},{2,17},{3,16},{16,3},{17,2},{18,1},{19,0},{4,23},{5,... | collective-permute-start | bytes 368648 | tf_op jit(solution)/shard_map/ppermute | solution.py:260
  56.3 6.6 %collective-permute-start.11 = (bf16[4,24,640]{2,1,0:T(8,128)(2,1)S(1)}, bf16[4,24,640]{2,1,0:T(8,128)(2,1)S(1)}, u32[]{:S(2)}, u32[]{:S(2)}) collective-permute-start(bf16[4,24,640]{2,1,0:T(8,128)(2,1)S(1)} %get-tuple-element.24), channel_id=1, source_target_pairs={{0,16},{1,17},{2,18},{3,19},{16,0},{17,1},{18,2},{19,3},{4,20},{5,... | collective-permute-start | bytes 368648 | tf_op jit(solution)/shard_map/ppermute | solution.py:260

commit v21 on v20

--- a/solution.py
+++ b/solution.py
@@ -73,8 +73,8 @@
     fields_ref = refs.pop(0)
     weight_refs = [refs.pop(0) for _ in range(counts[0])]
     mix_slots = [[refs.pop(0) for _ in range(n)] for n in counts[1]]
-    field_rows, total, mix_all, mixed = refs[-4:]
-    outs = refs[:-4]
+    field_rows, total, mix_all, mixed, partner_rows, arrived = refs[-6:]
+    outs = refs[:-6]
     late, owners, span, _ = fields_ref.shape
     depth, width = mix_slots[0][0].shape[1:]
     channels = owners * depth
@@ -84,12 +84,18 @@
     cells = span // groups
     member, owner, group = place_ref[0], place_ref[1], place_ref[2]
 
+    copies = [pltpu.make_async_copy(weight_refs[s], partner_rows.at[s - 1], arrived.at[s - 1]) for s in range(1, late)]
+    for copy in copies:
+        copy.start()
     read = pl.ds(HALO - halo, late * rows + 2 * halo)
     total[:, read] = jnp.zeros((bases, late * rows + 2 * halo) + total.shape[2:], total.dtype)
     upper = pl.ds(padded - LANES, LANES)
     field_rows[:, :, upper] = jnp.zeros(field_rows.shape[:2] + (LANES,), field_rows.dtype)
     for s in range(late):
         lat = partner_in_kernel(member, s, late)
+        if s:
+            copies[s - 1].wait()
+        kernel_rows = partner_rows.at[s - 1] if s else weight_refs[0]
         for p in range(owners):
             value = fields_ref[lat, p]
             for r in range(rows):
@@ -106,7 +112,7 @@
                     source = lax.rem(b + shift_ref[row, j] + nblocks, nblocks)
                     chosen.append(field_rows[r, pl.ds(pl.multiple_of(source * block, block), block)])
                 picked = jnp.concatenate(chosen, axis=0)
-                lhs = weight_refs[s][r, :, pl.ds(q, sub), :].reshape(bases * taps * sub, slots * block)
+                lhs = kernel_rows[r, :, pl.ds(q, sub), :].reshape(bases * taps * sub, slots * block)
                 product = jnp.dot(lhs, picked, preferred_element_type=jnp.float32)
                 for k in range(bases):
                     at = pl.ds(row + low_ref[k, row] + HALO, taps)
@@ -159,13 +165,18 @@
     return pl.pallas_call(
         functools.partial(conv_mix_kernel, (bases, taps, slots, halo, sub, groups), counts),
         out_shape=shapes,
-        in_specs=[SMEM_SPEC] * 3 + [VMEM_SPEC] * len(operands),
+        in_specs=[SMEM_SPEC] * 3
+        + [VMEM_SPEC] * 2
+        + [pl.BlockSpec(memory_space=pl.ANY)] * (late - 1)
+        + [VMEM_SPEC] * (len(operands) - 1 - late),
         out_specs=[VMEM_SPEC] * len(shapes),
         scratch_shapes=[
             VMEM((rows, owners * span, padded), jnp.bfloat16),
             VMEM((bases, all_rows + 2 * HALO, span, padded), jnp.float32),
             VMEM((owners, bases, depth, width), jnp.bfloat16),
             VMEM((all_rows, span, width), jnp.float32),
+            VMEM((max(late - 1, 1),) + weights[0].shape, jnp.bfloat16),
+            pltpu.SemaphoreType.DMA((max(late - 1, 1),)),
         ],
         compiler_params=pltpu.CompilerParams(vmem_limit_bytes=LIMIT),
         name="conv_mix",

time: 64.7 us -> 64.2 us (level)
  no operation moved by 1% of the time
where the time goes in v21:
time: 64.2 us; the launch traced here: 63.8 us
  waiting for transfers between devices  26 us (40%)
  starting transfers between devices  19.7 us (31%)
  Pallas kernels  9.35 us (15%)
  local copies, waits for them, and re-layouts  8.62 us (13%)
    ppermute x1, waiting for transfers between devices, gather_mix(): copied = lax.ppermute(third, 'late', [(1, 0)])  9.13 us
    ppermute x7, waiting for transfers between devices, per_device(): lax.ppermute(block, ('late', 'lonq'), route)  7.83 us
    pallas_call x1, Pallas kernels, conv_mix(): pl.pallas_call(functools.partial(conv_mix_kernel, (bases, taps, slots, ha...  6.55 us
    all_to_all x1, starting transfers between devices, per_device(): lax.all_to_all(packed, ('late', 'lonp', 'lonq'), split_axis=0, concat_axi...  6.55 us
    ppermute x7, starting transfers between devices, per_device(): lax.ppermute(block, ('late', 'lonq'), route)  4.85 us
    ppermute x1, waiting for transfers between devices, gather_mix(): first = lax.ppermute(mix, ('late', 'lonp'), route)  4.58 us
    all_to_all x1, waiting for transfers between devices, per_device(): lax.all_to_all(packed, ('late', 'lonp', 'lonq'), split_axis=0, concat_axi...  4.5 us
    transpose x1, local copies, waits for them, and re-layouts, both_kernels(): kernel.transpose(1, 0, 2, 5, 3, 4)  4.18 us
  transfers between devices with their start and end apart: 13, of which 5 were waited for; matrix products, arithmetic and copies ran while one was open for 12% of the time, Pallas kernels for 2%

profile of v21, /device:TPU:0, one launch (start us, length us, event | category | flops | bytes accessed | tf_op | source)
XLA Modules:
  0.0 63.8 jit_solution(5212551413415649711)
XLA Ops:
  0.0 3.0 %collective-permute-start = (bf16[5,40,640]{2,1,0:T(8,128)(2,1)}, bf16[5,40,640]{2,1,0:T(8,128)(2,1)S(1)}, u32[]{:S(2)}, u32[]{:S(2)}) collective-permute-start(bf16[5,40,640]{2,1,0:T(8,128)(2,1)} %refs_3_.1), channel_id=1, source_target_pairs={{0,4},{4,0},{8,12},{12,8},{16,24},{20,28},{24,16},{28,20},{1,5},{5... | collective-permute-start | bytes 768008 | tf_op jit(solution)/shard_map/ppermute | solution.py:219
  3.0 0.0 copy-start.1
  3.0 0.9 %copy-done.1 = bf16[2,4,640,24]{2,3,1,0:T(8,128)(2,1)S(1)} copy-done((bf16[2,4,640,24]{2,3,1,0:T(8,128)(2,1)S(1)}, bf16[2,4,640,24]{2,3,1,0:T(8,128)(2,1)}, u32[]{:S(2)}) %copy-start.1) | copy-done | bytes 245784
  4.0 1.3 %pack.1 = bf16[2,4,4,24,640]{4,3,2,1,0:T(8,128)(2,1)} custom-call(bf16[2,4,24,640]{3,2,1,0:T(8,128)(2,1)S(1)} %bitcast.12), custom_call_target="tpu_custom_call" | custom-call | tf_op jit(solution)/shard_map/pack/pallas_call | solution.py:53
  5.3 4.6 %collective-permute-done.refs_4_ = bf16[5,40,640]{2,1,0:T(8,128)(2,1)S(1)} collective-permute-done((bf16[5,40,640]{2,1,0:T(8,128)(2,1)}, bf16[5,40,640]{2,1,0:T(8,128)(2,1)S(1)}, u32[]{:S(2)}, u32[]{:S(2)}) %collective-permute-start) | collective-permute-done | bytes 256032 | tf_op jit(solution)/shard_map/ppermute | solution.py:219
  9.9 6.5 %all-to-all-start = ((bf16[32,24,640]{2,1,0:T(8,128)(2,1)}), bf16[32,24,640]{2,1,0:T(8,128)(2,1)S(1)}, u32[]{:S(2)}, u32[]{:S(2)}) async-start(bf16[32,24,640]{2,1,0:T(8,128)(2,1)} %bitcast.7), calls=%async_computation | async-start | bytes 1966080 | tf_op jit(solution)/shard_map/all_to_all | solution.py:240
  16.5 4.2 %copy.8 = bf16[4,5,3,64,3,64]{3,5,4,2,1,0:T(8,128)(2,1)} copy(bf16[4,5,3,64,3,64]{3,5,4,2,0,1:T(8,128)(2,1)} %bitcast.14) | data formatting | bytes 2949120 | tf_op jit(solution)/shard_map/transpose | solution.py:211
  20.6 0.0 copy-start.3
  20.6 0.0 copy-start
  20.6 0.0 copy-start.2
  20.6 3.3 %copy.11.refs_1_ = bf16[4,15,64,192]{3,2,1,0:T(8,128)(2,1)S(1)} copy(bf16[4,15,64,192]{2,3,1,0:T(8,128)(2,1)} %bitcast.13) | data formatting | bytes 2949120 | tf_op jit(solution)/shard_map/reshape | solution.py:211
  24.0 0.3 collective-permute-start.1
  24.3 1.4 %collective-permute-start.3 = (bf16[5,40,640]{2,1,0:T(8,128)(2,1)S(1)}, bf16[5,40,640]{2,1,0:T(8,128)(2,1)}, u32[]{:S(2)}, u32[]{:S(2)}) collective-permute-start(bf16[5,40,640]{2,1,0:T(8,128)(2,1)S(1)} %collective-permute-done.refs_4_), channel_id=1, source_target_pairs={{16,20},{20,16},{24,28},{28,24},{17,21},{21,17},{25,29},{29,25},{1... | collective-permute-start | bytes 768008 | tf_op jit(solution)/shard_map/ppermute | solution.py:221
  25.6 2.4 %collective-permute-start.2 = (bf16[5,40,640]{2,1,0:T(8,128)(2,1)S(1)}, bf16[5,40,640]{2,1,0:T(8,128)(2,1)}, u32[]{:S(2)}, u32[]{:S(2)}) collective-permute-start(bf16[5,40,640]{2,1,0:T(8,128)(2,1)S(1)} %collective-permute-done.refs_4_), channel_id=1, source_target_pairs={{0,16},{16,0},{1,17},{17,1},{2,18},{18,2},{3,19},{19,3},{4,20},{20... | collective-permute-start | bytes 768008 | tf_op jit(solution)/shard_map/ppermute | solution.py:33
  28.0 0.0 collective-permute-done.3.refs_6_
  28.0 1.3 %collective-permute-start.4 = (bf16[5,40,640]{2,1,0:T(8,128)(2,1)}, bf16[5,40,640]{2,1,0:T(8,128)(2,1)}, u32[]{:S(2)}, u32[]{:S(2)}) collective-permute-start(bf16[5,40,640]{2,1,0:T(8,128)(2,1)} %collective-permute-done.3.refs_6_), channel_id=1, source_target_pairs={{16,0},{17,1},{18,2},{19,3},{20,4},{21,5},{22,6},{23,7},{24,8},{25... | collective-permute-start | bytes 768008 | tf_op jit(solution)/shard_map/ppermute | solution.py:223
  29.3 0.0 copy-done.3
  29.3 0.1 copy.10.shift_ref
  29.4 0.1 stack.28.place_ref
  29.5 0.0 collective-permute-done.2.refs_5_
  29.5 9.1 %collective-permute-done.4.refs_7_ = bf16[5,40,640]{2,1,0:T(8,128)(2,1)} collective-permute-done((bf16[5,40,640]{2,1,0:T(8,128)(2,1)}, bf16[5,40,640]{2,1,0:T(8,128)(2,1)}, u32[]{:S(2)}, u32[]{:S(2)}) %collective-permute-start.4) | collective-permute-done | bytes 256032 | tf_op jit(solution)/shard_map/ppermute | solution.py:223
  38.6 0.0 collective-permute-done.1.refs_2_
  38.6 4.5 %all-to-all-done = bf16[32,24,640]{2,1,0:T(8,128)(2,1)S(1)} async-done(((bf16[32,24,640]{2,1,0:T(8,128)(2,1)}), bf16[32,24,640]{2,1,0:T(8,128)(2,1)S(1)}, u32[]{:S(2)}, u32[]{:S(2)}) %all-to-all-start) | async-done | bytes 983072 | tf_op jit(solution)/shard_map/all_to_all | solution.py:240
  43.1 0.0 copy-done
  43.1 0.0 copy-done.2
  43.1 6.6 %conv_mix.1 = (bf16[4,24,640]{2,1,0:T(8,128)(2,1)S(1)}, bf16[4,24,640]{2,1,0:T(8,128)(2,1)S(1)}, bf16[4,24,640]{2,1,0:T(8,128)(2,1)S(1)}, bf16[4,24,640]{2,1,0:T...) custom-call(s32[5,8]{1,0:T(8,128)S(1)} %copy-done.2, ...), custom_call_target="tpu_custom_call" | custom-call | tf_op jit(solution)/shard_map/conv_mix/pallas_call | solution.py:165
  49.7 0.1 collective-permute-start.5
  49.8 0.8 %collective-permute-start.6 = (bf16[4,24,640]{2,1,0:T(8,128)(2,1)S(1)}, bf16[4,24,640]{2,1,0:T(8,128)(2,1)S(1)}, u32[]{:S(2)}, u32[]{:S(2)}) collective-permute-start(bf16[4,24,640]{2,1,0:T(8,128)(2,1)S(1)} %get-tuple-element.18), channel_id=1, source_target_pairs={{0,2},{1,3},{2,0},{3,1},{16,18},{17,19},{18,16},{19,17},{4,6},{5,7... | collective-permute-start | bytes 368648 | tf_op jit(solution)/shard_map/ppermute | solution.py:271
  50.5 0.0 collective-permute-start.7
  50.5 3.0 %collective-permute-start.8 = (bf16[4,24,640]{2,1,0:T(8,128)(2,1)S(1)}, bf16[4,24,640]{2,1,0:T(8,128)(2,1)S(1)}, u32[]{:S(2)}, u32[]{:S(2)}) collective-permute-start(bf16[4,24,640]{2,1,0:T(8,128)(2,1)S(1)} %get-tuple-element.20), channel_id=1, source_target_pairs={{0,18},{1,19},{2,16},{3,17},{16,2},{17,3},{18,0},{19,1},{4,22},{5,... | collective-permute-start | bytes 368648 | tf_op jit(solution)/shard_map/ppermute | solution.py:271
  53.5 0.2 collective-permute-start.9
  53.7 2.0 %collective-permute-done.5.refs_0_ = bf16[4,24,640]{2,1,0:T(8,128)(2,1)S(1)} collective-permute-done((bf16[4,24,640]{2,1,0:T(8,128)(2,1)S(1)}, bf16[4,24,640]{2,1,0:T(8,128)(2,1)S(1)}, u32[]{:S(2)}, u32[]{:S(2)}) %collective-permute-start.5) | collective-permute-done | bytes 122912 | tf_op jit(solution)/shard_map/ppermute | solution.py:271
  55.7 0.0 collective-permute-start.10
  55.7 0.0 collective-permute-done.6.refs_1_
  55.8 0.8 %collective-permute-start.11 = (bf16[4,24,640]{2,1,0:T(8,128)(2,1)S(1)}, bf16[4,24,640]{2,1,0:T(8,128)(2,1)S(1)}, u32[]{:S(2)}, u32[]{:S(2)}) collective-permute-start(bf16[4,24,640]{2,1,0:T(8,128)(2,1)S(1)} %get-tuple-element.24), channel_id=1, source_target_pairs={{0,16},{1,17},{2,18},{3,19},{16,0},{17,1},{18,2},{19,3},{4,20},{5,... | collective-permute-start | bytes 368648 | tf_op jit(solution)/shard_map/ppermute | solution.py:271
  56.6 0.0 collective-permute-done.7.refs_2_
  56.6 5.8 %collective-permute-done.8.refs_3_ = bf16[4,24,640]{2,1,0:T(8,128)(2,1)S(1)} collective-permute-done((bf16[4,24,640]{2,1,0:T(8,128)(2,1)S(1)}, bf16[4,24,640]{2,1,0:T(8,128)(2,1)S(1)}, u32[]{:S(2)}, u32[]{:S(2)}) %collective-permute-start.8) | collective-permute-done | bytes 122912 | tf_op jit(solution)/shard_map/ppermute | solution.py:271
  62.4 0.0 collective-permute-done.9.refs_4_
  62.4 0.0 collective-permute-done.10.refs_5_
  62.4 0.0 collective-permute-done.11.refs_7_
  62.4 1.5 %finish.1 = bf16[2,4,24,640]{3,2,1,0:T(8,128)(2,1)} custom-call(s32[7]{0:T(128)S(1)} %stack.28.place_ref, bf16[4,24,640]{2,1,0:T(8,128)(2,1)S(1)} %collective-permute-done.5.refs_0_, bf16[4,24,640]{2,1,0:T(8,128)(2,1)S(1)} %collective-permute-done.6.refs_1_, bf16[4,24,640]{2,1,0:T(8,128)(2,1)S(1)} %collective-permute-done.7.refs_2_, ...), custom_call_target="tpu_custom_call" | custom-call | tf_op jit(solution)/shard_map/finish/pallas_call | solution.py:199
Async XLA Ops:
  0.0 9.9 %collective-permute-start = (bf16[5,40,640]{2,1,0:T(8,128)(2,1)}, bf16[5,40,640]{2,1,0:T(8,128)(2,1)S(1)}, u32[]{:S(2)}, u32[]{:S(2)}) collective-permute-start(bf16[5,40,640]{2,1,0:T(8,128)(2,1)} %refs_3_.1), channel_id=1, source_target_pairs={{0,4},{4,0},{8,12},{12,8},{16,24},{20,28},{24,16},{28,20},{1,5},{5... | collective-permute-start | bytes 768008 | tf_op jit(solution)/shard_map/ppermute | solution.py:219
  3.0 0.9 %copy-start.1 = (bf16[2,4,640,24]{2,3,1,0:T(8,128)(2,1)S(1)}, bf16[2,4,640,24]{2,3,1,0:T(8,128)(2,1)}, u32[]{:S(2)}) copy-start(bf16[2,4,640,24]{2,3,1,0:T(8,128)(2,1)} %param.5) | copy-start | bytes 737284
  9.9 33.2 %all-to-all-start = ((bf16[32,24,640]{2,1,0:T(8,128)(2,1)}), bf16[32,24,640]{2,1,0:T(8,128)(2,1)S(1)}, u32[]{:S(2)}, u32[]{:S(2)}) async-start(bf16[32,24,640]{2,1,0:T(8,128)(2,1)} %bitcast.7), calls=%async_computation | async-start | bytes 1966080 | tf_op jit(solution)/shard_map/all_to_all | solution.py:240
  20.6 8.7 %copy-start.3 = (s32[8,3]{0,1:T(4,128)S(1)}, s32[8,3]{0,1:T(4,128)}, u32[]{:S(2)}) copy-start(s32[8,3]{0,1:T(4,128)} %param.8) | copy-start | bytes 292
  20.6 22.5 %copy-start = (bf16[5,40,640]{2,1,0:T(8,128)(2,1)S(1)}, bf16[5,40,640]{2,1,0:T(8,128)(2,1)}, u32[]{:S(2)}) copy-start(bf16[5,40,640]{2,1,0:T(8,128)(2,1)} %refs_3_.1) | copy-start | bytes 768004
  20.6 22.5 %copy-start.2 = (s32[5,8]{1,0:T(8,128)S(1)}, s32[5,8]{1,0:T(8,128)}, u32[]{:S(2)}) copy-start(s32[5,8]{1,0:T(8,128)} %low_ref) | copy-start | bytes 484
  24.0 14.6 %collective-permute-start.1 = (bf16[4,15,64,192]{3,2,1,0:T(8,128)(2,1)S(1)}, bf16[4,15,64,192]{3,2,1,0:T(8,128)(2,1)}, u32[]{:S(2)}, u32[]{:S(2)}) collective-permute-start(bf16[4,15,64,192]{3,2,1,0:T(8,128)(2,1)S(1)} %copy.11.refs_1_), channel_id=1, source_target_pairs={{0,16},{16,0},{1,17},{17,1},{2,18},{18,2},{3,19},{19,3},{4,20},{20... | collective-permute-start | bytes 4423688 | tf_op jit(solution)/shard_map/ppermute | solution.py:33
  24.3 3.7 %collective-permute-start.3 = (bf16[5,40,640]{2,1,0:T(8,128)(2,1)S(1)}, bf16[5,40,640]{2,1,0:T(8,128)(2,1)}, u32[]{:S(2)}, u32[]{:S(2)}) collective-permute-start(bf16[5,40,640]{2,1,0:T(8,128)(2,1)S(1)} %collective-permute-done.refs_4_), channel_id=1, source_target_pairs={{16,20},{20,16},{24,28},{28,24},{17,21},{21,17},{25,29},{29,25},{1... | collective-permute-start | bytes 768008 | tf_op jit(solution)/shard_map/ppermute | solution.py:221
  25.6 3.8 %collective-permute-start.2 = (bf16[5,40,640]{2,1,0:T(8,128)(2,1)S(1)}, bf16[5,40,640]{2,1,0:T(8,128)(2,1)}, u32[]{:S(2)}, u32[]{:S(2)}) collective-permute-start(bf16[5,40,640]{2,1,0:T(8,128)(2,1)S(1)} %collective-permute-done.refs_4_), channel_id=1, source_target_pairs={{0,16},{16,0},{1,17},{17,1},{2,18},{18,2},{3,19},{19,3},{4,20},{20... | collective-permute-start | bytes 768008 | tf_op jit(solution)/shard_map/ppermute | solution.py:33
  28.0 10.6 %collective-permute-start.4 = (bf16[5,40,640]{2,1,0:T(8,128)(2,1)}, bf16[5,40,640]{2,1,0:T(8,128)(2,1)}, u32[]{:S(2)}, u32[]{:S(2)}) collective-permute-start(bf16[5,40,640]{2,1,0:T(8,128)(2,1)} %collective-permute-done.3.refs_6_), channel_id=1, source_target_pairs={{16,0},{17,1},{18,2},{19,3},{20,4},{21,5},{22,6},{23,7},{24,8},{25... | collective-permute-start | bytes 768008 | tf_op jit(solution)/shard_map/ppermute | solution.py:223
  49.7 6.1 %collective-permute-start.5 = (bf16[4,24,640]{2,1,0:T(8,128)(2,1)S(1)}, bf16[4,24,640]{2,1,0:T(8,128)(2,1)S(1)}, u32[]{:S(2)}, u32[]{:S(2)}) collective-permute-start(bf16[4,24,640]{2,1,0:T(8,128)(2,1)S(1)} %get-tuple-element.17), channel_id=1, source_target_pairs={{0,1},{1,0},{2,3},{3,2},{16,17},{17,16},{18,19},{19,18},{4,5},{5,4... | collective-permute-start | bytes 368648 | tf_op jit(solution)/shard_map/ppermute | solution.py:271
  49.8 6.0 %collective-permute-start.6 = (bf16[4,24,640]{2,1,0:T(8,128)(2,1)S(1)}, bf16[4,24,640]{2,1,0:T(8,128)(2,1)S(1)}, u32[]{:S(2)}, u32[]{:S(2)}) collective-permute-start(bf16[4,24,640]{2,1,0:T(8,128)(2,1)S(1)} %get-tuple-element.18), channel_id=1, source_target_pairs={{0,2},{1,3},{2,0},{3,1},{16,18},{17,19},{18,16},{19,17},{4,6},{5,7... | collective-permute-start | bytes 368648 | tf_op jit(solution)/shard_map/ppermute | solution.py:271
  50.5 6.1 %collective-permute-start.7 = (bf16[4,24,640]{2,1,0:T(8,128)(2,1)S(1)}, bf16[4,24,640]{2,1,0:T(8,128)(2,1)S(1)}, u32[]{:S(2)}, u32[]{:S(2)}) collective-permute-start(bf16[4,24,640]{2,1,0:T(8,128)(2,1)S(1)} %get-tuple-element.19), channel_id=1, source_target_pairs={{0,17},{1,16},{2,19},{3,18},{16,1},{17,0},{18,3},{19,2},{4,21},{5,... | collective-permute-start | bytes 368648 | tf_op jit(solution)/shard_map/ppermute | solution.py:271
  50.5 11.9 %collective-permute-start.8 = (bf16[4,24,640]{2,1,0:T(8,128)(2,1)S(1)}, bf16[4,24,640]{2,1,0:T(8,128)(2,1)S(1)}, u32[]{:S(2)}, u32[]{:S(2)}) collective-permute-start(bf16[4,24,640]{2,1,0:T(8,128)(2,1)S(1)} %get-tuple-element.20), channel_id=1, source_target_pairs={{0,18},{1,19},{2,16},{3,17},{16,2},{17,3},{18,0},{19,1},{4,22},{5,... | collective-permute-start | bytes 368648 | tf_op jit(solution)/shard_map/ppermute | solution.py:271
  53.5 8.9 %collective-permute-start.9 = (bf16[4,24,640]{2,1,0:T(8,128)(2,1)S(1)}, bf16[4,24,640]{2,1,0:T(8,128)(2,1)S(1)}, u32[]{:S(2)}, u32[]{:S(2)}) collective-permute-start(bf16[4,24,640]{2,1,0:T(8,128)(2,1)S(1)} %get-tuple-element.21), channel_id=1, source_target_pairs={{0,3},{1,2},{2,1},{3,0},{16,19},{17,18},{18,17},{19,16},{4,7},{5,6... | collective-permute-start | bytes 368648 | tf_op jit(solution)/shard_map/ppermute | solution.py:271
  55.7 6.6 %collective-permute-start.10 = (bf16[4,24,640]{2,1,0:T(8,128)(2,1)S(1)}, bf16[4,24,640]{2,1,0:T(8,128)(2,1)S(1)}, u32[]{:S(2)}, u32[]{:S(2)}) collective-permute-start(bf16[4,24,640]{2,1,0:T(8,128)(2,1)S(1)} %get-tuple-element.22), channel_id=1, source_target_pairs={{0,19},{1,18},{2,17},{3,16},{16,3},{17,2},{18,1},{19,0},{4,23},{5,... | collective-permute-start | bytes 368648 | tf_op jit(solution)/shard_map/ppermute | solution.py:271
  55.8 6.6 %collective-permute-start.11 = (bf16[4,24,640]{2,1,0:T(8,128)(2,1)S(1)}, bf16[4,24,640]{2,1,0:T(8,128)(2,1)S(1)}, u32[]{:S(2)}, u32[]{:S(2)}) collective-permute-start(bf16[4,24,640]{2,1,0:T(8,128)(2,1)S(1)} %get-tuple-element.24), channel_id=1, source_target_pairs={{0,16},{1,17},{2,18},{3,19},{16,0},{17,1},{18,2},{19,3},{4,20},{5,... | collective-permute-start | bytes 368648 | tf_op jit(solution)/shard_map/ppermute | solution.py:271

commit v22 on v21

--- a/solution.py
+++ b/solution.py
@@ -259,7 +259,7 @@
                 group = partner(lax.axis_index("lonq"), dq, groups)
                 partial[dl * groups + dq] += extra[lat, :, group]
     order = [(dl, dq) for dl in range(late) for dq in range(groups)]
-    order.sort(key=lambda at: (at[1] == 0, bin(at[1]).count("1"), at))
+    order.sort(key=lambda at: (at[1] == 0, at))
     parts = []
     for dl, dq in order:
         route = [

time: 64.2 us -> 64 us (level)
  starting transfers between devices: 19.7 us -> 18.9 us
  waiting for transfers between devices: 26 us -> 26.7 us
    ppermute x7, starting transfers between devices: 4.85 us -> 4.04 us  [per_device(): lax.ppermute(block, ('late', 'lonq'), route)]
  transfers between devices with their start and end apart: 13 -> 13, of which waited for: 5 -> 7; matrix products, arithmetic and copies ran while one was open for 12% -> 12% of each run, Pallas kernels for 2% -> 2%
where the time goes in v22:
time: 64 us; the launch traced here: 63.7 us
  waiting for transfers between devices  26.7 us (42%)
  starting transfers between devices  18.9 us (30%)
  Pallas kernels  9.35 us (15%)
  local copies, waits for them, and re-layouts  8.62 us (13%)
    ppermute x1, waiting for transfers between devices, gather_mix(): copied = lax.ppermute(third, 'late', [(1, 0)])  9.13 us
    ppermute x7, waiting for transfers between devices, per_device(): lax.ppermute(block, ('late', 'lonq'), route)  8.47 us
    pallas_call x1, Pallas kernels, conv_mix(): pl.pallas_call(functools.partial(conv_mix_kernel, (bases, taps, slots, ha...  6.55 us
    all_to_all x1, starting transfers between devices, per_device(): lax.all_to_all(packed, ('late', 'lonp', 'lonq'), split_axis=0, concat_axi...  6.55 us
    ppermute x1, waiting for transfers between devices, gather_mix(): first = lax.ppermute(mix, ('late', 'lonp'), route)  4.58 us
    all_to_all x1, waiting for transfers between devices, per_device(): lax.all_to_all(packed, ('late', 'lonp', 'lonq'), split_axis=0, concat_axi...  4.5 us
    transpose x1, local copies, waits for them, and re-layouts, both_kernels(): kernel.transpose(1, 0, 2, 5, 3, 4)  4.18 us
    ppermute x7, starting transfers between devices, per_device(): lax.ppermute(block, ('late', 'lonq'), route)  4.04 us
  transfers between devices with their start and end apart: 13, of which 7 were waited for; matrix products, arithmetic and copies ran while one was open for 12% of the time, Pallas kernels for 2%

profile of v22, /device:TPU:0, one launch (start us, length us, event | category | flops | bytes accessed | tf_op | source)
XLA Modules:
  0.0 63.7 jit_solution(1547983662197612726)
XLA Ops:
  0.0 3.0 %collective-permute-start = (bf16[5,40,640]{2,1,0:T(8,128)(2,1)}, bf16[5,40,640]{2,1,0:T(8,128)(2,1)S(1)}, u32[]{:S(2)}, u32[]{:S(2)}) collective-permute-start(bf16[5,40,640]{2,1,0:T(8,128)(2,1)} %refs_3_.1), channel_id=1, source_target_pairs={{0,4},{4,0},{8,12},{12,8},{16,24},{20,28},{24,16},{28,20},{1,5},{5... | collective-permute-start | bytes 768008 | tf_op jit(solution)/shard_map/ppermute | solution.py:219
  3.0 0.0 copy-start.1
  3.0 0.9 %copy-done.1 = bf16[2,4,640,24]{2,3,1,0:T(8,128)(2,1)S(1)} copy-done((bf16[2,4,640,24]{2,3,1,0:T(8,128)(2,1)S(1)}, bf16[2,4,640,24]{2,3,1,0:T(8,128)(2,1)}, u32[]{:S(2)}) %copy-start.1) | copy-done | bytes 245784
  4.0 1.3 %pack.1 = bf16[2,4,4,24,640]{4,3,2,1,0:T(8,128)(2,1)} custom-call(bf16[2,4,24,640]{3,2,1,0:T(8,128)(2,1)S(1)} %bitcast.12), custom_call_target="tpu_custom_call" | custom-call | tf_op jit(solution)/shard_map/pack/pallas_call | solution.py:53
  5.3 4.6 %collective-permute-done.refs_4_ = bf16[5,40,640]{2,1,0:T(8,128)(2,1)S(1)} collective-permute-done((bf16[5,40,640]{2,1,0:T(8,128)(2,1)}, bf16[5,40,640]{2,1,0:T(8,128)(2,1)S(1)}, u32[]{:S(2)}, u32[]{:S(2)}) %collective-permute-start) | collective-permute-done | bytes 256032 | tf_op jit(solution)/shard_map/ppermute | solution.py:219
  9.9 6.5 %all-to-all-start = ((bf16[32,24,640]{2,1,0:T(8,128)(2,1)}), bf16[32,24,640]{2,1,0:T(8,128)(2,1)S(1)}, u32[]{:S(2)}, u32[]{:S(2)}) async-start(bf16[32,24,640]{2,1,0:T(8,128)(2,1)} %bitcast.7), calls=%async_computation | async-start | bytes 1966080 | tf_op jit(solution)/shard_map/all_to_all | solution.py:240
  16.5 4.2 %copy.8 = bf16[4,5,3,64,3,64]{3,5,4,2,1,0:T(8,128)(2,1)} copy(bf16[4,5,3,64,3,64]{3,5,4,2,0,1:T(8,128)(2,1)} %bitcast.14) | data formatting | bytes 2949120 | tf_op jit(solution)/shard_map/transpose | solution.py:211
  20.6 0.0 copy-start.3
  20.6 0.0 copy-start
  20.6 0.0 copy-start.2
  20.6 3.3 %copy.11.refs_1_ = bf16[4,15,64,192]{3,2,1,0:T(8,128)(2,1)S(1)} copy(bf16[4,15,64,192]{2,3,1,0:T(8,128)(2,1)} %bitcast.13) | data formatting | bytes 2949120 | tf_op jit(solution)/shard_map/reshape | solution.py:211
  24.0 0.3 collective-permute-start.1
  24.3 1.4 %collective-permute-start.3 = (bf16[5,40,640]{2,1,0:T(8,128)(2,1)S(1)}, bf16[5,40,640]{2,1,0:T(8,128)(2,1)}, u32[]{:S(2)}, u32[]{:S(2)}) collective-permute-start(bf16[5,40,640]{2,1,0:T(8,128)(2,1)S(1)} %collective-permute-done.refs_4_), channel_id=1, source_target_pairs={{16,20},{20,16},{24,28},{28,24},{17,21},{21,17},{25,29},{29,25},{1... | collective-permute-start | bytes 768008 | tf_op jit(solution)/shard_map/ppermute | solution.py:221
  25.6 2.4 %collective-permute-start.2 = (bf16[5,40,640]{2,1,0:T(8,128)(2,1)S(1)}, bf16[5,40,640]{2,1,0:T(8,128)(2,1)}, u32[]{:S(2)}, u32[]{:S(2)}) collective-permute-start(bf16[5,40,640]{2,1,0:T(8,128)(2,1)S(1)} %collective-permute-done.refs_4_), channel_id=1, source_target_pairs={{0,16},{16,0},{1,17},{17,1},{2,18},{18,2},{3,19},{19,3},{4,20},{20... | collective-permute-start | bytes 768008 | tf_op jit(solution)/shard_map/ppermute | solution.py:33
  28.0 0.0 collective-permute-done.3.refs_6_
  28.0 1.3 %collective-permute-start.4 = (bf16[5,40,640]{2,1,0:T(8,128)(2,1)}, bf16[5,40,640]{2,1,0:T(8,128)(2,1)}, u32[]{:S(2)}, u32[]{:S(2)}) collective-permute-start(bf16[5,40,640]{2,1,0:T(8,128)(2,1)} %collective-permute-done.3.refs_6_), channel_id=1, source_target_pairs={{16,0},{17,1},{18,2},{19,3},{20,4},{21,5},{22,6},{23,7},{24,8},{25... | collective-permute-start | bytes 768008 | tf_op jit(solution)/shard_map/ppermute | solution.py:223
  29.3 0.0 copy-done.3
  29.3 0.1 copy.10.shift_ref
  29.4 0.1 stack.28.place_ref
  29.5 0.0 collective-permute-done.2.refs_5_
  29.5 9.1 %collective-permute-done.4.refs_7_ = bf16[5,40,640]{2,1,0:T(8,128)(2,1)} collective-permute-done((bf16[5,40,640]{2,1,0:T(8,128)(2,1)}, bf16[5,40,640]{2,1,0:T(8,128)(2,1)}, u32[]{:S(2)}, u32[]{:S(2)}) %collective-permute-start.4) | collective-permute-done | bytes 256032 | tf_op jit(solution)/shard_map/ppermute | solution.py:223
  38.6 0.0 collective-permute-done.1.refs_2_
  38.6 4.5 %all-to-all-done = bf16[32,24,640]{2,1,0:T(8,128)(2,1)S(1)} async-done(((bf16[32,24,640]{2,1,0:T(8,128)(2,1)}), bf16[32,24,640]{2,1,0:T(8,128)(2,1)S(1)}, u32[]{:S(2)}, u32[]{:S(2)}) %all-to-all-start) | async-done | bytes 983072 | tf_op jit(solution)/shard_map/all_to_all | solution.py:240
  43.1 0.0 copy-done
  43.1 0.0 copy-done.2
  43.1 6.6 %conv_mix.1 = (bf16[4,24,640]{2,1,0:T(8,128)(2,1)S(1)}, bf16[4,24,640]{2,1,0:T(8,128)(2,1)S(1)}, bf16[4,24,640]{2,1,0:T(8,128)(2,1)S(1)}, bf16[4,24,640]{2,1,0:T...) custom-call(s32[5,8]{1,0:T(8,128)S(1)} %copy-done.2, ...), custom_call_target="tpu_custom_call" | custom-call | tf_op jit(solution)/shard_map/conv_mix/pallas_call | solution.py:165
  49.7 0.1 collective-permute-start.5
  49.8 0.8 %collective-permute-start.6 = (bf16[4,24,640]{2,1,0:T(8,128)(2,1)S(1)}, bf16[4,24,640]{2,1,0:T(8,128)(2,1)S(1)}, u32[]{:S(2)}, u32[]{:S(2)}) collective-permute-start(bf16[4,24,640]{2,1,0:T(8,128)(2,1)S(1)} %get-tuple-element.18), channel_id=1, source_target_pairs={{0,2},{1,3},{2,0},{3,1},{16,18},{17,19},{18,16},{19,17},{4,6},{5,7... | collective-permute-start | bytes 368648 | tf_op jit(solution)/shard_map/ppermute | solution.py:271
  50.5 2.7 %collective-permute-start.7 = (bf16[4,24,640]{2,1,0:T(8,128)(2,1)S(1)}, bf16[4,24,640]{2,1,0:T(8,128)(2,1)S(1)}, u32[]{:S(2)}, u32[]{:S(2)}) collective-permute-start(bf16[4,24,640]{2,1,0:T(8,128)(2,1)S(1)} %get-tuple-element.19), channel_id=1, source_target_pairs={{0,3},{1,2},{2,1},{3,0},{16,19},{17,18},{18,17},{19,16},{4,7},{5,6... | collective-permute-start | bytes 368648 | tf_op jit(solution)/shard_map/ppermute | solution.py:271
  53.2 0.0 collective-permute-start.8
  53.2 0.5 collective-permute-start.9
  53.7 1.9 %collective-permute-done.5.refs_0_ = bf16[4,24,640]{2,1,0:T(8,128)(2,1)S(1)} collective-permute-done((bf16[4,24,640]{2,1,0:T(8,128)(2,1)S(1)}, bf16[4,24,640]{2,1,0:T(8,128)(2,1)S(1)}, u32[]{:S(2)}, u32[]{:S(2)}) %collective-permute-start.5) | collective-permute-done | bytes 122912 | tf_op jit(solution)/shard_map/ppermute | solution.py:271
  55.6 0.0 collective-permute-start.10
  55.6 2.1 %collective-permute-done.6.refs_1_ = bf16[4,24,640]{2,1,0:T(8,128)(2,1)S(1)} collective-permute-done((bf16[4,24,640]{2,1,0:T(8,128)(2,1)S(1)}, bf16[4,24,640]{2,1,0:T(8,128)(2,1)S(1)}, u32[]{:S(2)}, u32[]{:S(2)}) %collective-permute-start.6) | collective-permute-done | bytes 122912 | tf_op jit(solution)/shard_map/ppermute | solution.py:271
  57.7 0.0 collective-permute-start.11
  57.7 0.0 collective-permute-done.7.refs_2_
  57.8 1.2 %collective-permute-done.8.refs_3_ = bf16[4,24,640]{2,1,0:T(8,128)(2,1)S(1)} collective-permute-done((bf16[4,24,640]{2,1,0:T(8,128)(2,1)S(1)}, bf16[4,24,640]{2,1,0:T(8,128)(2,1)S(1)}, u32[]{:S(2)}, u32[]{:S(2)}) %collective-permute-start.8) | collective-permute-done | bytes 122912 | tf_op jit(solution)/shard_map/ppermute | solution.py:271
  58.9 3.3 %collective-permute-done.9.refs_4_ = bf16[4,24,640]{2,1,0:T(8,128)(2,1)S(1)} collective-permute-done((bf16[4,24,640]{2,1,0:T(8,128)(2,1)S(1)}, bf16[4,24,640]{2,1,0:T(8,128)(2,1)S(1)}, u32[]{:S(2)}, u32[]{:S(2)}) %collective-permute-start.9) | collective-permute-done | bytes 122912 | tf_op jit(solution)/shard_map/ppermute | solution.py:271
  62.2 0.0 collective-permute-done.10.refs_5_
  62.2 0.0 collective-permute-done.11.refs_7_
  62.2 1.5 %finish.1 = bf16[2,4,24,640]{3,2,1,0:T(8,128)(2,1)} custom-call(s32[7]{0:T(128)S(1)} %stack.28.place_ref, bf16[4,24,640]{2,1,0:T(8,128)(2,1)S(1)} %collective-permute-done.5.refs_0_, bf16[4,24,640]{2,1,0:T(8,128)(2,1)S(1)} %collective-permute-done.6.refs_1_, bf16[4,24,640]{2,1,0:T(8,128)(2,1)S(1)} %collective-permute-done.7.refs_2_, ...), custom_call_target="tpu_custom_call" | custom-call | tf_op jit(solution)/shard_map/finish/pallas_call | solution.py:199
Async XLA Ops:
  0.0 9.9 %collective-permute-start = (bf16[5,40,640]{2,1,0:T(8,128)(2,1)}, bf16[5,40,640]{2,1,0:T(8,128)(2,1)S(1)}, u32[]{:S(2)}, u32[]{:S(2)}) collective-permute-start(bf16[5,40,640]{2,1,0:T(8,128)(2,1)} %refs_3_.1), channel_id=1, source_target_pairs={{0,4},{4,0},{8,12},{12,8},{16,24},{20,28},{24,16},{28,20},{1,5},{5... | collective-permute-start | bytes 768008 | tf_op jit(solution)/shard_map/ppermute | solution.py:219
  3.0 0.9 %copy-start.1 = (bf16[2,4,640,24]{2,3,1,0:T(8,128)(2,1)S(1)}, bf16[2,4,640,24]{2,3,1,0:T(8,128)(2,1)}, u32[]{:S(2)}) copy-start(bf16[2,4,640,24]{2,3,1,0:T(8,128)(2,1)} %param.5) | copy-start | bytes 737284
  9.9 33.2 %all-to-all-start = ((bf16[32,24,640]{2,1,0:T(8,128)(2,1)}), bf16[32,24,640]{2,1,0:T(8,128)(2,1)S(1)}, u32[]{:S(2)}, u32[]{:S(2)}) async-start(bf16[32,24,640]{2,1,0:T(8,128)(2,1)} %bitcast.7), calls=%async_computation | async-start | bytes 1966080 | tf_op jit(solution)/shard_map/all_to_all | solution.py:240
  20.6 8.7 %copy-start.3 = (s32[8,3]{0,1:T(4,128)S(1)}, s32[8,3]{0,1:T(4,128)}, u32[]{:S(2)}) copy-start(s32[8,3]{0,1:T(4,128)} %param.8) | copy-start | bytes 292
  20.6 22.5 %copy-start = (bf16[5,40,640]{2,1,0:T(8,128)(2,1)S(1)}, bf16[5,40,640]{2,1,0:T(8,128)(2,1)}, u32[]{:S(2)}) copy-start(bf16[5,40,640]{2,1,0:T(8,128)(2,1)} %refs_3_.1) | copy-start | bytes 768004
  20.6 22.5 %copy-start.2 = (s32[5,8]{1,0:T(8,128)S(1)}, s32[5,8]{1,0:T(8,128)}, u32[]{:S(2)}) copy-start(s32[5,8]{1,0:T(8,128)} %low_ref) | copy-start | bytes 484
  24.0 14.6 %collective-permute-start.1 = (bf16[4,15,64,192]{3,2,1,0:T(8,128)(2,1)S(1)}, bf16[4,15,64,192]{3,2,1,0:T(8,128)(2,1)}, u32[]{:S(2)}, u32[]{:S(2)}) collective-permute-start(bf16[4,15,64,192]{3,2,1,0:T(8,128)(2,1)S(1)} %copy.11.refs_1_), channel_id=1, source_target_pairs={{0,16},{16,0},{1,17},{17,1},{2,18},{18,2},{3,19},{19,3},{4,20},{20... | collective-permute-start | bytes 4423688 | tf_op jit(solution)/shard_map/ppermute | solution.py:33
  24.3 3.7 %collective-permute-start.3 = (bf16[5,40,640]{2,1,0:T(8,128)(2,1)S(1)}, bf16[5,40,640]{2,1,0:T(8,128)(2,1)}, u32[]{:S(2)}, u32[]{:S(2)}) collective-permute-start(bf16[5,40,640]{2,1,0:T(8,128)(2,1)S(1)} %collective-permute-done.refs_4_), channel_id=1, source_target_pairs={{16,20},{20,16},{24,28},{28,24},{17,21},{21,17},{25,29},{29,25},{1... | collective-permute-start | bytes 768008 | tf_op jit(solution)/shard_map/ppermute | solution.py:221
  25.6 3.8 %collective-permute-start.2 = (bf16[5,40,640]{2,1,0:T(8,128)(2,1)S(1)}, bf16[5,40,640]{2,1,0:T(8,128)(2,1)}, u32[]{:S(2)}, u32[]{:S(2)}) collective-permute-start(bf16[5,40,640]{2,1,0:T(8,128)(2,1)S(1)} %collective-permute-done.refs_4_), channel_id=1, source_target_pairs={{0,16},{16,0},{1,17},{17,1},{2,18},{18,2},{3,19},{19,3},{4,20},{20... | collective-permute-start | bytes 768008 | tf_op jit(solution)/shard_map/ppermute | solution.py:33
  28.0 10.6 %collective-permute-start.4 = (bf16[5,40,640]{2,1,0:T(8,128)(2,1)}, bf16[5,40,640]{2,1,0:T(8,128)(2,1)}, u32[]{:S(2)}, u32[]{:S(2)}) collective-permute-start(bf16[5,40,640]{2,1,0:T(8,128)(2,1)} %collective-permute-done.3.refs_6_), channel_id=1, source_target_pairs={{16,0},{17,1},{18,2},{19,3},{20,4},{21,5},{22,6},{23,7},{24,8},{25... | collective-permute-start | bytes 768008 | tf_op jit(solution)/shard_map/ppermute | solution.py:223
  49.7 6.0 %collective-permute-start.5 = (bf16[4,24,640]{2,1,0:T(8,128)(2,1)S(1)}, bf16[4,24,640]{2,1,0:T(8,128)(2,1)S(1)}, u32[]{:S(2)}, u32[]{:S(2)}) collective-permute-start(bf16[4,24,640]{2,1,0:T(8,128)(2,1)S(1)} %get-tuple-element.17), channel_id=1, source_target_pairs={{0,1},{1,0},{2,3},{3,2},{16,17},{17,16},{18,19},{19,18},{4,5},{5,4... | collective-permute-start | bytes 368648 | tf_op jit(solution)/shard_map/ppermute | solution.py:271
  49.8 8.0 %collective-permute-start.6 = (bf16[4,24,640]{2,1,0:T(8,128)(2,1)S(1)}, bf16[4,24,640]{2,1,0:T(8,128)(2,1)S(1)}, u32[]{:S(2)}, u32[]{:S(2)}) collective-permute-start(bf16[4,24,640]{2,1,0:T(8,128)(2,1)S(1)} %get-tuple-element.18), channel_id=1, source_target_pairs={{0,2},{1,3},{2,0},{3,1},{16,18},{17,19},{18,16},{19,17},{4,6},{5,7... | collective-permute-start | bytes 368648 | tf_op jit(solution)/shard_map/ppermute | solution.py:271
  50.5 7.2 %collective-permute-start.7 = (bf16[4,24,640]{2,1,0:T(8,128)(2,1)S(1)}, bf16[4,24,640]{2,1,0:T(8,128)(2,1)S(1)}, u32[]{:S(2)}, u32[]{:S(2)}) collective-permute-start(bf16[4,24,640]{2,1,0:T(8,128)(2,1)S(1)} %get-tuple-element.19), channel_id=1, source_target_pairs={{0,3},{1,2},{2,1},{3,0},{16,19},{17,18},{18,17},{19,16},{4,7},{5,6... | collective-permute-start | bytes 368648 | tf_op jit(solution)/shard_map/ppermute | solution.py:271
  53.2 5.7 %collective-permute-start.8 = (bf16[4,24,640]{2,1,0:T(8,128)(2,1)S(1)}, bf16[4,24,640]{2,1,0:T(8,128)(2,1)S(1)}, u32[]{:S(2)}, u32[]{:S(2)}) collective-permute-start(bf16[4,24,640]{2,1,0:T(8,128)(2,1)S(1)} %get-tuple-element.20), channel_id=1, source_target_pairs={{0,17},{1,16},{2,19},{3,18},{16,1},{17,0},{18,3},{19,2},{4,21},{5,... | collective-permute-start | bytes 368648 | tf_op jit(solution)/shard_map/ppermute | solution.py:271
  53.2 9.0 %collective-permute-start.9 = (bf16[4,24,640]{2,1,0:T(8,128)(2,1)S(1)}, bf16[4,24,640]{2,1,0:T(8,128)(2,1)S(1)}, u32[]{:S(2)}, u32[]{:S(2)}) collective-permute-start(bf16[4,24,640]{2,1,0:T(8,128)(2,1)S(1)} %get-tuple-element.21), channel_id=1, source_target_pairs={{0,18},{1,19},{2,16},{3,17},{16,2},{17,3},{18,0},{19,1},{4,22},{5,... | collective-permute-start | bytes 368648 | tf_op jit(solution)/shard_map/ppermute | solution.py:271
  55.6 6.6 %collective-permute-start.10 = (bf16[4,24,640]{2,1,0:T(8,128)(2,1)S(1)}, bf16[4,24,640]{2,1,0:T(8,128)(2,1)S(1)}, u32[]{:S(2)}, u32[]{:S(2)}) collective-permute-start(bf16[4,24,640]{2,1,0:T(8,128)(2,1)S(1)} %get-tuple-element.22), channel_id=1, source_target_pairs={{0,19},{1,18},{2,17},{3,16},{16,3},{17,2},{18,1},{19,0},{4,23},{5,... | collective-permute-start | bytes 368648 | tf_op jit(solution)/shard_map/ppermute | solution.py:271
  57.7 4.5 %collective-permute-start.11 = (bf16[4,24,640]{2,1,0:T(8,128)(2,1)S(1)}, bf16[4,24,640]{2,1,0:T(8,128)(2,1)S(1)}, u32[]{:S(2)}, u32[]{:S(2)}) collective-permute-start(bf16[4,24,640]{2,1,0:T(8,128)(2,1)S(1)} %get-tuple-element.24), channel_id=1, source_target_pairs={{0,16},{1,17},{2,18},{3,19},{16,0},{17,1},{18,2},{19,3},{4,20},{5,... | collective-permute-start | bytes 368648 | tf_op jit(solution)/shard_map/ppermute | solution.py:271
